TPU v7x, 32 devices: a whole 2x2x4 slice. The times are simulated.
32 devices in a mesh: batch: 4 (over y, core), seq: 8 (over z, x).
Axes of the slice: x: 2, y: 2, z: 4, core: 2. Of those that a mesh axis runs over, the one named last changes fastest.
Arguments:
- inputs: bfloat16 [4, 2048, 2048], P('batch', 'seq'), may hold values from -6 to 6
- exit_layers: int32 [4, 2048], P('batch'), may hold values from 1 to 24, as said below
- lengths: int32 [4, 7], P('batch'), may hold values from 1 to 512, as said below
- layer_index: int32 [1], replicated, may hold values from 8 to 15
- out_grad: bfloat16 [4, 2048, 2048], P('batch', 'seq'), may hold values from -6 to 6
- ln1_gain: bfloat16 [2048], P(('batch', 'seq')), may hold values from 0.5 to 1.5
- ln1_bias: bfloat16 [2048], P(('batch', 'seq')), may hold values from -1.75 to 1.75
- q_weight: bfloat16 [2048, 2048], P(('batch', 'seq')), may hold values from -0.125 to 0.125
- q_bias: bfloat16 [2048], P(('batch', 'seq')), may hold values from -1.75 to 1.75
- k_weight: bfloat16 [2048, 2048], P(('batch', 'seq')), may hold values from -0.125 to 0.125
- v_weight: bfloat16 [2048, 2048], P(('batch', 'seq')), may hold values from -0.125 to 0.125
- v_bias: bfloat16 [2048], P(('batch', 'seq')), may hold values from -1.75 to 1.75
- o_weight: bfloat16 [2048, 2048], P(('batch', 'seq')), may hold values from -0.5 to 0.5
- o_bias: bfloat16 [2048], P(('batch', 'seq')), may hold values from -1.75 to 1.75
- ln2_gain: bfloat16 [2048], P(('batch', 'seq')), may hold values from 0.5 to 1.5
- ln2_bias: bfloat16 [2048], P(('batch', 'seq')), may hold values from -1.75 to 1.75
- fc1_weight: bfloat16 [2048, 8192], P(None, ('batch', 'seq')), may hold values from -0.125 to 0.125
- fc1_bias: bfloat16 [8192], P(('batch', 'seq')), may hold values from -1.75 to 1.75
- fc2_weight: bfloat16 [8192, 2048], P(('batch', 'seq')), may hold values from -0.09375 to 0.09375
- fc2_bias: bfloat16 [2048], P(('batch', 'seq')), may hold values from -1.75 to 1.75
Outputs:
- outputs: bfloat16 [4, 2048, 2048], P('batch', 'seq')
- input_grad: bfloat16 [4, 2048, 2048], P('batch', 'seq')
- ln1_gain_grad: float32 [2048], P(('batch', 'seq'))
- ln1_bias_grad: float32 [2048], P(('batch', 'seq'))
- q_weight_grad: float32 [2048, 2048], P(('batch', 'seq'))
- q_bias_grad: float32 [2048], P(('batch', 'seq'))
- k_weight_grad: float32 [2048, 2048], P(('batch', 'seq'))
- v_weight_grad: float32 [2048, 2048], P(('batch', 'seq'))
- v_bias_grad: float32 [2048], P(('batch', 'seq'))
- o_weight_grad: float32 [2048, 2048], P(('batch', 'seq'))
- o_bias_grad: float32 [2048], P(('batch', 'seq'))
- ln2_gain_grad: float32 [2048], P(('batch', 'seq'))
- ln2_bias_grad: float32 [2048], P(('batch', 'seq'))
- fc1_weight_grad: float32 [2048, 8192], P(None, ('batch', 'seq'))
- fc1_bias_grad: float32 [8192], P(('batch', 'seq'))
- fc2_weight_grad: float32 [8192, 2048], P(('batch', 'seq'))
- fc2_bias_grad: float32 [2048], P(('batch', 'seq'))
Inputs may be any that keep to these rules, and one draw needn't show every extreme that they name: Each group's 7 lengths sum to 2048; in every group the largest is exactly 512. `exit_layers`: along each sequence the exit layer never rises from one position to the next; the first position of every sequence exits above every drawn layer index.
All inputs are finite; a program needn't handle non-finite values.
Results may differ from a plain program's by a relative error of at most 0.013.
Values may be sent and summed in bfloat16 or wider, within the bound.
A program may use at most 448 MiB of HBM per device.

v0:
```python
from functools import partial

import jax
import jax.numpy as jnp
from jax import lax
from jax.sharding import PartitionSpec as P

HEAD_DIM = 64


bfloat = jnp.bfloat16
single = jnp.float32


def layer_norm(values, gain_vec, shift_vec):
    center = jnp.mean(values, axis=-1, keepdims=True)
    centered = values - center
    spread = jnp.mean(centered * centered, axis=-1, keepdims=True)
    return centered * lax.rsqrt(spread + 1e-05) * gain_vec + shift_vec


def block_scores(query_heads, key_heads, segment, row_start, block_rows, window):
    group_tok = key_heads.shape[0]
    key_start = jnp.clip(row_start + block_rows - window, 0, group_tok - window)
    query_blk = lax.dynamic_slice_in_dim(query_heads, row_start, block_rows, 0)
    key_blk = lax.dynamic_slice_in_dim(key_heads, key_start, window, 0)
    query_pos = row_start + jnp.arange(block_rows, dtype=jnp.int32)
    key_pos = key_start + jnp.arange(window, dtype=jnp.int32)
    query_seg = lax.dynamic_slice_in_dim(segment, row_start, block_rows, 0)
    key_seg = lax.dynamic_slice_in_dim(segment, key_start, window, 0)
    allowed = (query_seg[:, None] == key_seg[None, :]) & (key_pos[None, :] <= query_pos[:, None])
    scores = jnp.einsum(
        "qhd,khd->hqk", query_blk, key_blk, preferred_element_type=single
    ) * HEAD_DIM ** (-0.5)
    return (jnp.where(allowed[None], scores, -1e30), key_start, query_blk, key_blk)


def attention_forward(query_heads, key_heads, value_heads, segment, block_rows, window):
    group_tok = query_heads.shape[0]

    def one_block(block_id):
        row_start = block_id * block_rows
        scores, key_start, query_blk, key_blk = block_scores(
            query_heads, key_heads, segment, row_start, block_rows, window
        )
        value_blk = lax.dynamic_slice_in_dim(value_heads, key_start, window, 0)
        row_peak = jnp.max(scores, axis=-1, keepdims=True)
        weights_exp = jnp.exp(scores - row_peak)
        row_total = jnp.sum(weights_exp, axis=-1, keepdims=True)
        prob_low = (weights_exp / row_total).astype(bfloat)
        context = jnp.einsum("hqk,khd->qhd", prob_low, value_blk, preferred_element_type=single)
        return (context.astype(bfloat), (row_peak + jnp.log(row_total))[..., 0])

    contexts, logsum = lax.map(one_block, jnp.arange(group_tok // block_rows, dtype=jnp.int32))
    return (contexts.reshape(group_tok, -1), logsum)


def attention_backward(
    query_heads, key_heads, value_heads, grad_heads, logsum, segment, block_rows, window
):
    group_tok = query_heads.shape[0]

    def one_block(carried, block_id):
        key_acc, value_acc = carried
        row_start = block_id * block_rows
        scores, key_start, query_blk, key_blk = block_scores(
            query_heads, key_heads, segment, row_start, block_rows, window
        )
        value_blk = lax.dynamic_slice_in_dim(value_heads, key_start, window, 0)
        grad_blk = lax.dynamic_slice_in_dim(grad_heads, row_start, block_rows, 0)
        prob_rows = jnp.exp(scores - logsum[block_id][..., None])
        prob_grad = jnp.einsum("qhd,khd->hqk", grad_blk, value_blk, preferred_element_type=single)
        row_dot = jnp.sum(prob_rows * prob_grad, axis=-1, keepdims=True)
        score_grad = (prob_rows * (prob_grad - row_dot)).astype(bfloat)
        query_part = jnp.einsum(
            "hqk,khd->qhd", score_grad, key_blk, preferred_element_type=single
        ) * HEAD_DIM ** (-0.5)
        key_part = jnp.einsum(
            "hqk,qhd->khd", score_grad, query_blk, preferred_element_type=single
        ) * HEAD_DIM ** (-0.5)
        value_part = jnp.einsum(
            "hqk,qhd->khd", prob_rows.astype(bfloat), grad_blk, preferred_element_type=single
        )
        key_acc = lax.dynamic_update_slice_in_dim(
            key_acc,
            lax.dynamic_slice_in_dim(key_acc, key_start, window, 0) + key_part,
            key_start,
            0,
        )
        value_acc = lax.dynamic_update_slice_in_dim(
            value_acc,
            lax.dynamic_slice_in_dim(value_acc, key_start, window, 0) + value_part,
            key_start,
            0,
        )
        return ((key_acc, value_acc), query_part)

    zero_acc = jnp.zeros(key_heads.shape, single)
    (key_acc, value_acc), query_parts = lax.scan(
        one_block, (zero_acc, zero_acc), jnp.arange(group_tok // block_rows, dtype=jnp.int32)
    )
    col_count = query_heads.shape[1] * query_heads.shape[2]
    return (
        query_parts.reshape(group_tok, col_count).astype(bfloat),
        key_acc.reshape(group_tok, col_count).astype(bfloat),
        value_acc.reshape(group_tok, col_count).astype(bfloat),
    )


def column_sums(matrix):
    return jnp.sum(matrix.astype(single), axis=0)


def on_device(
    inputs,
    exit_layers,
    lengths,
    layer_index,
    out_grad,
    ln1_gain,
    ln1_bias,
    q_weight,
    q_bias,
    k_weight,
    v_weight,
    v_bias,
    o_weight,
    o_bias,
    ln2_gain,
    ln2_bias,
    fc1_weight,
    fc1_bias,
    fc2_weight,
    fc2_bias,
):
    local = inputs[0].astype(single)
    tok_dev = local.shape[0]
    group_tok = tok_dev * lax.axis_size("seq")
    my_start = lax.axis_index("seq") * tok_dev
    block_rows = min(512, group_tok)
    window = min(group_tok, group_tok // 4 + block_rows)
    group_active = (exit_layers[0] > layer_index[0]).astype(single)
    active_total = jnp.sum(group_active)
    active = lax.dynamic_slice_in_dim(group_active, my_start, tok_dev, 0)[:, None]
    seq_ends = jnp.cumsum(lengths[0])
    places = jnp.arange(group_tok, dtype=jnp.int32)
    segment = jnp.sum((places[:, None] >= seq_ends[None, :]).astype(jnp.int32), axis=1)
    dense_full = (
        lax.all_gather(ln1_gain, ("batch", "seq"), axis=0, tiled=True),
        lax.all_gather(ln1_bias, ("batch", "seq"), axis=0, tiled=True),
        lax.all_gather(q_weight, ("batch", "seq"), axis=0, tiled=True),
        lax.all_gather(q_bias, ("batch", "seq"), axis=0, tiled=True),
        lax.all_gather(k_weight, ("batch", "seq"), axis=0, tiled=True),
        lax.all_gather(v_weight, ("batch", "seq"), axis=0, tiled=True),
        lax.all_gather(v_bias, ("batch", "seq"), axis=0, tiled=True),
        lax.all_gather(o_weight, ("batch", "seq"), axis=0, tiled=True),
        lax.all_gather(o_bias, ("batch", "seq"), axis=0, tiled=True),
        lax.all_gather(ln2_gain, ("batch", "seq"), axis=0, tiled=True),
        lax.all_gather(ln2_bias, ("batch", "seq"), axis=0, tiled=True),
        lax.all_gather(fc2_bias, ("batch", "seq"), axis=0, tiled=True),
    )
    (
        gain_one,
        bias_one,
        weight_q,
        bias_q,
        weight_k,
        weight_v,
        bias_v,
        weight_o,
        bias_o,
        gain_two,
        bias_two,
        bias_down,
    ) = dense_full
    normed = layer_norm(local, gain_one.astype(single), bias_one.astype(single))
    normed_low = normed.astype(bfloat)
    queries = (
        jnp.dot(normed_low, weight_q, preferred_element_type=single) + bias_q.astype(single)
    ).astype(bfloat)
    keys_all = jnp.dot(normed_low, weight_k, preferred_element_type=single).astype(bfloat)
    values = (
        jnp.dot(normed_low, weight_v, preferred_element_type=single) + bias_v.astype(single)
    ).astype(bfloat)
    query_cols, key_cols, value_cols = (
        lax.all_to_all(queries, "seq", split_axis=1, concat_axis=0, tiled=True),
        lax.all_to_all(keys_all, "seq", split_axis=1, concat_axis=0, tiled=True),
        lax.all_to_all(values, "seq", split_axis=1, concat_axis=0, tiled=True),
    )
    query_heads = query_cols.reshape(group_tok, -1, HEAD_DIM)
    key_heads = key_cols.reshape(group_tok, -1, HEAD_DIM)
    value_heads = value_cols.reshape(group_tok, -1, HEAD_DIM)
    context_cols, logsum = attention_forward(
        query_heads, key_heads, value_heads, segment, block_rows, window
    )
    context = lax.all_to_all(context_cols, "seq", split_axis=0, concat_axis=1, tiled=True)
    attended = jnp.dot(context, weight_o, preferred_element_type=single) + bias_o.astype(single)
    middle = local + active * attended
    gain_two_f = gain_two.astype(single)
    bias_two_f = bias_two.astype(single)
    normed_two = layer_norm(middle, gain_two_f, bias_two_f).astype(bfloat)
    cotangent = out_grad[0].astype(single) * (group_tok / active_total)
    branch_grad = (active * cotangent).astype(bfloat)
    down_b_grad = column_sums(branch_grad)
    weight_up, bias_up, weight_down = (
        lax.all_gather(fc1_weight, "batch", axis=1, tiled=True),
        lax.all_gather(fc1_bias, "batch", axis=0, tiled=True),
        lax.all_gather(fc2_weight, "batch", axis=0, tiled=True),
    )
    normed_group = lax.all_gather(normed_two, "seq", axis=0, tiled=True)
    hidden_pre = jnp.dot(normed_group, weight_up, preferred_element_type=single) + bias_up.astype(
        single
    )
    gelu_value, gelu_pull = jax.vjp(partial(jax.nn.gelu, approximate=True), hidden_pre)
    hidden = gelu_value.astype(bfloat)
    rows = lax.slice_in_dim(hidden, 0, tok_dev * lax.axis_size("seq"), axis=0)
    branch = lax.psum_scatter(
        jnp.dot(rows, weight_down, preferred_element_type=single).astype(jnp.bfloat16),
        "seq",
        scatter_dimension=0,
        tiled=True,
    ).astype(jnp.float32) + bias_down.astype(single)
    outputs = middle + active * branch
    branch_group = lax.all_gather(branch_grad, "seq", axis=0, tiled=True)
    down_w_grad = jnp.einsum("tf,td->fd", hidden, branch_group, preferred_element_type=single)
    hidden_grad = jnp.einsum("td,fd->tf", branch_group, weight_down, preferred_element_type=single)
    pre_grad = gelu_pull(hidden_grad)[0].astype(bfloat)
    up_w_grad = jnp.einsum("td,tf->df", normed_group, pre_grad, preferred_element_type=single)
    up_b_grad = column_sums(pre_grad)
    rows = pre_grad
    normed_two_grad = lax.psum_scatter(
        jnp.einsum("tf,df->td", rows, weight_up, preferred_element_type=single),
        "seq",
        scatter_dimension=0,
        tiled=True,
    )
    ffn_shards = (
        lax.psum_scatter(
            up_w_grad.astype(jnp.bfloat16), "batch", scatter_dimension=1, tiled=True
        ).astype(jnp.float32),
        lax.psum_scatter(
            up_b_grad.astype(jnp.bfloat16), "batch", scatter_dimension=0, tiled=True
        ).astype(jnp.float32),
        lax.psum_scatter(
            down_w_grad.astype(jnp.bfloat16), "batch", scatter_dimension=0, tiled=True
        ).astype(jnp.float32),
    )
    norm_value, norm_pull = jax.vjp(layer_norm, middle, gain_two_f, bias_two_f)
    middle_part, gain_two_grad, bias_two_grad = norm_pull(normed_two_grad)
    middle_grad = cotangent + middle_part
    attended_grad = (active * middle_grad).astype(bfloat)
    out_w_grad = jnp.einsum("td,te->de", context, attended_grad, preferred_element_type=single)
    out_b_grad = column_sums(attended_grad)
    context_grad = jnp.einsum(
        "te,de->td", attended_grad, weight_o, preferred_element_type=single
    ).astype(bfloat)
    grad_cols = lax.all_to_all(context_grad, "seq", split_axis=1, concat_axis=0, tiled=True)
    grad_heads = grad_cols.reshape(group_tok, -1, HEAD_DIM)
    query_grad_cols, key_grad_cols, value_grad_cols = attention_backward(
        query_heads, key_heads, value_heads, grad_heads, logsum, segment, block_rows, window
    )
    query_grad, key_grad, value_grad = (
        lax.all_to_all(query_grad_cols, "seq", split_axis=0, concat_axis=1, tiled=True),
        lax.all_to_all(key_grad_cols, "seq", split_axis=0, concat_axis=1, tiled=True),
        lax.all_to_all(value_grad_cols, "seq", split_axis=0, concat_axis=1, tiled=True),
    )
    query_w_grad = jnp.einsum("td,te->de", normed_low, query_grad, preferred_element_type=single)
    query_b_grad = column_sums(query_grad)
    key_w_grad = jnp.einsum("td,te->de", normed_low, key_grad, preferred_element_type=single)
    value_w_grad = jnp.einsum("td,te->de", normed_low, value_grad, preferred_element_type=single)
    value_b_grad = column_sums(value_grad)
    normed_grad = (
        jnp.einsum("te,de->td", query_grad, weight_q, preferred_element_type=single)
        + jnp.einsum("te,de->td", key_grad, weight_k, preferred_element_type=single)
        + jnp.einsum("te,de->td", value_grad, weight_v, preferred_element_type=single)
    )
    first_value, first_pull = jax.vjp(
        layer_norm, local, gain_one.astype(single), bias_one.astype(single)
    )
    input_part, gain_one_grad, bias_one_grad = first_pull(normed_grad)
    input_grad = middle_grad + input_part
    shards = (
        lax.psum_scatter(gain_one_grad, ("batch", "seq"), scatter_dimension=0, tiled=True),
        lax.psum_scatter(bias_one_grad, ("batch", "seq"), scatter_dimension=0, tiled=True),
        lax.psum_scatter(query_w_grad, ("batch", "seq"), scatter_dimension=0, tiled=True),
        lax.psum_scatter(query_b_grad, ("batch", "seq"), scatter_dimension=0, tiled=True),
        lax.psum_scatter(key_w_grad, ("batch", "seq"), scatter_dimension=0, tiled=True),
        lax.psum_scatter(value_w_grad, ("batch", "seq"), scatter_dimension=0, tiled=True),
        lax.psum_scatter(value_b_grad, ("batch", "seq"), scatter_dimension=0, tiled=True),
        lax.psum_scatter(out_w_grad, ("batch", "seq"), scatter_dimension=0, tiled=True),
        lax.psum_scatter(out_b_grad, ("batch", "seq"), scatter_dimension=0, tiled=True),
        lax.psum_scatter(gain_two_grad, ("batch", "seq"), scatter_dimension=0, tiled=True),
        lax.psum_scatter(bias_two_grad, ("batch", "seq"), scatter_dimension=0, tiled=True),
        lax.psum_scatter(down_b_grad, ("batch", "seq"), scatter_dimension=0, tiled=True),
    )
    return (
        outputs.astype(bfloat)[None],
        input_grad.astype(bfloat)[None],
        shards[0],
        shards[1],
        shards[2],
        shards[3],
        shards[4],
        shards[5],
        shards[6],
        shards[7],
        shards[8],
        shards[9],
        shards[10],
        ffn_shards[0],
        ffn_shards[1],
        ffn_shards[2],
        shards[11],
    )


def solution(mesh):
    placed = (
        P("batch", "seq", None),
        P("batch", None),
        P("batch", None),
        P(),
        P("batch", "seq", None),
        P(("batch", "seq")),
        P(("batch", "seq")),
        P(("batch", "seq"), None),
        P(("batch", "seq")),
        P(("batch", "seq"), None),
        P(("batch", "seq"), None),
        P(("batch", "seq")),
        P(("batch", "seq"), None),
        P(("batch", "seq")),
        P(("batch", "seq")),
        P(("batch", "seq")),
        P(None, ("batch", "seq")),
        P(("batch", "seq")),
        P(("batch", "seq"), None),
        P(("batch", "seq")),
    )
    return jax.shard_map(
        on_device,
        mesh=mesh,
        in_specs=placed,
        out_specs=(
            P("batch", "seq", None),
            P("batch", "seq", None),
            P(("batch", "seq")),
            P(("batch", "seq")),
            P(("batch", "seq"), None),
            P(("batch", "seq")),
            P(("batch", "seq"), None),
            P(("batch", "seq"), None),
            P(("batch", "seq")),
            P(("batch", "seq"), None),
            P(("batch", "seq")),
            P(("batch", "seq")),
            P(("batch", "seq")),
            P(None, ("batch", "seq")),
            P(("batch", "seq")),
            P(("batch", "seq"), None),
            P(("batch", "seq")),
        ),
        check_vma=False,
    )
```

profile of v0, /device:TPU:0, one launch (start us, length us, event | category | flops | bytes accessed | tf_op | source)
XLA Modules:
  0.0 3043.8 jit_solution(15829281172894296803)
XLA Ops:
  16.8 43.4 %all-reduce.18 = (bf16[2048]{0:T(1024)(128)(2,1)S(1)}, bf16[2048]{0:T(1024)(128)(2,1)S(1)}, bf16[2048]{0:T(1024)(128)(2,1)S(1)}, bf16[2048]{0:T(1024)(128)(2,1)S...) all-reduce(bf16[2048]{0:T(1024)(128)(2,1)S(1)} %dynamic-update-slic, ...), channel_id=1, replica_groups=mesh['batch'=4,'seq'=8] {'batch','seq'}, use_global_device_ids=true, to_apply=%add.2 | all-reduce | flops 16384 | bytes 65536
  64.2 27.3 all-gather.12.cloned.1.call-done
  102.8 78.0 %all-gather.10.cloned.1.call-done = bf16[2048,2048]{1,0:T(8,128)(2,1)} async-done(((bf16[64,2048]{1,0:T(8,128)(2,1)}), bf16[2048,2048]{1,0:T(8,128)(2,1)}) %all-gather.10.cloned.1.call-update) | async-done | bytes 8388624 | tf_op jit(solution)/shard_map/all_gather | solution.py:154
  191.6 78.1 %all-gather.14.cloned.1.call-done = bf16[2048,2048]{1,0:T(8,128)(2,1)} async-done(((bf16[64,2048]{1,0:T(8,128)(2,1)}), bf16[2048,2048]{1,0:T(8,128)(2,1)}) %all-gather.14.cloned.1.call-update) | async-done | bytes 8388624 | tf_op jit(solution)/shard_map/all_gather | solution.py:153
  287.4 30.1 all-to-all-done.2
  321.7 42.6 %while.34 = (s32[]{:T(128)}, bf16[4,512,4,64]{1,3,2,0:T(8,128)(2,1)}, f32[4,4,512]{2,1,0:T(4,128)S(1)}, s32[4]{0:T(128)S(1)}, bf16[2048,4,64]{0,2,1:T(8,128)(2,1...) while((s32[]{:T(128)}, ...), condition=%wide.region_7.8_spmd, body=%wide.region_4.0_spmd.sunk | while | flops 563740160 | bytes 28932368 | solution.py:54
  378.0 24.3 all-to-all-done.3
  420.1 115.3 %all-gather.18.cloned.1.call-done = bf16[2048,2048]{1,0:T(8,128)(2,1)} async-done(((bf16[256,2048]{1,0:T(8,128)(2,1)}), bf16[2048,2048]{1,0:T(8,128)(2,1)}) %all-gather.18.cloned.1.call-update) | async-done | bytes 8388624 | tf_op jit(solution)/shard_map/all_gather | solution.py:210
  549.9 19.8 all-gather.22.cloned.1.call-done
  569.7 127.7 %all-gather.24.cloned.1.call-done = bf16[2048,2048]{1,0:T(8,128)(2,1)} async-done(((bf16[256,2048]{1,0:T(8,128)(2,1)}), bf16[2048,2048]{1,0:T(8,128)(2,1)}) %all-gather.24.cloned.1.call-update) | async-done | bytes 8388624 | tf_op jit(solution)/shard_map/all_gather | solution.py:224
  697.4 20.8 fusion.88
  732.4 15.4 convolution_convert_fusion
  747.9 16.8 convolution_convert_fusion.1
  765.4 247.8 %reduce-scatter.11.cloned.1.call-done = f32[256,2048]{1,0:T(8,128)} async-done(((f32[2048,2048]{1,0:T(8,128)}), f32[256,2048]{1,0:T(8,128)}) %reduce-scatter.11.cloned.1.call-update) | async-done | bytes 2097168 | tf_op jit(solution)/shard_map/reduce_scatter | solution.py:231
  1016.1 149.0 %reduce-scatter.9.cloned.1.call-done = bf16[256,2048]{1,0:T(8,128)(2,1)} async-done(((bf16[2048,2048]{1,0:T(8,128)(2,1)}), bf16[256,2048]{1,0:T(8,128)(2,1)}) %reduce-scatter.9.cloned.1.call-update) | async-done | bytes 1048592 | tf_op jit(solution)/shard_map/reduce_scatter | solution.py:217
  1214.9 150.5 %while.35 = (s32[]{:T(128)}, f32[2048,4,64]{0,2,1:T(8,128)}, f32[2048,4,64]{0,2,1:T(8,128)}, bf16[4,512,4,64]{1,3,2,0:T(8,128)(2,1)}, s32[4]{0:T(128)S(1)}, /*in...) while((s32[]{:T(128)}, f32[2048,4,64]{0,2,1:T(8,128)}, ...), condition=%wide.region_17.18_spmd, body=%wide.region_15.17_spmd.sunk | while | flops 1376124416 | bytes 160520640 | solution.py:99
  1376.4 22.6 all-to-all-done.5
  1404.9 24.0 all-to-all-done.7
  1442.7 15.5 all-to-all-done.6
  1529.0 65.5 %all-reduce.21.cloned.1.call-done = (f32[2048]{0:T(1024)}, f32[2048]{0:T(1024)}, f32[2048]{0:T(1024)}, f32[2048]{0:T(1024)}, f32[2048]{0:T(1024)}, /*index=5*/f32[2048]{0:T(1024)}, f32[2048]{0:T(1024)}, f32[2048]{0:T(1024)}) async-done(((f32[2048]{0:T(1024)}, f32[2048]{0:T(1024)}, f32[2048]{0:T(1024)}, f32[2048]{0:T(1024)}, f32[2048]{0:T(1024)}, /*index=5*/f32[2048]{0:T(1024)}, f32[2048]{0:T(1024)}, ...) | async-done | bytes 65552
  1604.6 351.8 %reduce-scatter.19.cloned.1.call-done = f32[64,2048]{1,0:T(8,128)} async-done(((f32[2048,2048]{1,0:T(8,128)}), f32[64,2048]{1,0:T(8,128)}) %reduce-scatter.19.cloned.1.call-update) | async-done | bytes 524304 | tf_op jit(solution)/shard_map/reduce_scatter | solution.py:290
  1956.4 360.2 %reduce-scatter.17.cloned.1.call-done = f32[64,2048]{1,0:T(8,128)} async-done(((f32[2048,2048]{1,0:T(8,128)}), f32[64,2048]{1,0:T(8,128)}) %reduce-scatter.17.cloned.1.call-update) | async-done | bytes 524304 | tf_op jit(solution)/shard_map/reduce_scatter | solution.py:288
  2316.6 360.2 %reduce-scatter.13.cloned.1.call-done = f32[64,2048]{1,0:T(8,128)} async-done(((f32[2048,2048]{1,0:T(8,128)}), f32[64,2048]{1,0:T(8,128)}) %reduce-scatter.13.cloned.1.call-update) | async-done | bytes 524304 | tf_op jit(solution)/shard_map/reduce_scatter | solution.py:285
  2676.8 360.2 %reduce-scatter.15.cloned.1.call-done = f32[64,2048]{1,0:T(8,128)} async-done(((f32[2048,2048]{1,0:T(8,128)}), f32[64,2048]{1,0:T(8,128)}) %reduce-scatter.15.cloned.1.call-update) | async-done | bytes 524304 | tf_op jit(solution)/shard_map/reduce_scatter | solution.py:287
  (359 shorter events, 459.5 us)
Async XLA Ops:
  7.2 84.4 %all-gather.12.cloned.1.call-start = ((), (), s32[]{:S(2)}) async-start(), calls=%async_computation.17 | async-start | bytes 8650752 | tf_op jit(solution)/shard_map/all_gather | solution.py:151
  7.9 172.8 %all-gather.10.cloned.1.call-start = ((), (), s32[]{:S(2)}) async-start(), calls=%async_computation.16 | async-start | bytes 8650752 | tf_op jit(solution)/shard_map/all_gather | solution.py:154
  8.7 261.0 %all-gather.14.cloned.1.call-start = ((), (), s32[]{:S(2)}) async-start(), calls=%async_computation.18 | async-start | bytes 8650752 | tf_op jit(solution)/shard_map/all_gather | solution.py:153
  9.4 368.6 %all-gather.16.cloned.1.call-start = ((), (), s32[]{:S(2)}) async-start(), calls=%async_computation.19 | async-start | bytes 8650752 | tf_op jit(solution)/shard_map/all_gather | solution.py:156
  98.7 88.8 %all-to-all-start.1 = ((bf16[256,8,256]{2,0,1:T(8,128)(2,1)}), bf16[256,8,256]{2,0,1:T(8,128)(2,1)S(1)}, u32[]{:S(2)}, u32[]{:S(2)}) async-start(bf16[256,8,256]{2,0,1:T(8,128)(2,1)} %bitcast.179), calls=%async_computation.1 | async-start | bytes 2097152 | tf_op jit(solution)/shard_map/all_to_all | solution.py:186
  187.5 89.0 %all-to-all-start = ((bf16[256,8,256]{2,0,1:T(8,128)(2,1)}), bf16[256,8,256]{2,0,1:T(8,128)(2,1)S(1)}, u32[]{:S(2)}, u32[]{:S(2)}) async-start(bf16[256,8,256]{2,0,1:T(8,128)(2,1)} %bitcast.212), calls=%async_computation | async-start | bytes 2097152 | tf_op jit(solution)/shard_map/all_to_all | solution.py:188
  276.5 40.9 %all-to-all-start.2 = ((bf16[256,8,256]{2,0,1:T(8,128)(2,1)}), bf16[256,8,256]{2,0,1:T(8,128)(2,1)}, u32[]{:S(2)}, u32[]{:S(2)}) async-start(bf16[256,8,256]{2,0,1:T(8,128)(2,1)} %bitcast.210), calls=%async_computation.2 | async-start | bytes 2097152 | tf_op jit(solution)/shard_map/all_to_all | solution.py:187
  280.8 139.3 %all-gather.20.cloned.1.call-start = ((), (), s32[]{:S(2)}) async-start(), calls=%async_computation.21 | async-start | bytes 5242880 | tf_op jit(solution)/shard_map/all_gather | solution.py:206
  372.4 29.9 all-to-all-start.3
  376.7 158.8 %all-gather.18.cloned.1.call-start = ((), (), s32[]{:S(2)}) async-start(), calls=%async_computation.20 | async-start | bytes 9437184 | tf_op jit(solution)/shard_map/all_gather | solution.py:210
  411.4 158.4 %all-gather.22.cloned.1.call-start = ((), (), s32[]{:S(2)}) async-start(), calls=%async_computation.22 | async-start | bytes 5242880 | tf_op jit(solution)/shard_map/all_gather | solution.py:208
  412.1 285.3 %all-gather.24.cloned.1.call-start = ((), (), s32[]{:S(2)}) async-start(), calls=%async_computation.24 | async-start | bytes 9437184 | tf_op jit(solution)/shard_map/all_gather | solution.py:224
  415.0 598.2 %reduce-scatter.11.cloned.1.call-start = ((), (), s32[]{:S(2)}) async-start(), calls=%async_computation.25 | async-start | bytes 18874368 | tf_op jit(solution)/shard_map/reduce_scatter | solution.py:231
  732.3 432.8 %reduce-scatter.9.cloned.1.call-start = ((), (), s32[]{:S(2)}) async-start(), calls=%async_computation.23 | async-start | bytes 9437184 | tf_op jit(solution)/shard_map/reduce_scatter | solution.py:217
  747.8 772.3 %reduce-scatter.23.cloned.1.call-start = ((), (), s32[]{:S(2)}) async-start(), calls=%async_computation.31 | async-start | bytes 5242880 | tf_op jit(solution)/shard_map/reduce_scatter | solution.py:244
  1179.6 29.9 all-to-all-start.4
  1183.2 339.8 %reduce-scatter.21.cloned.1.call-start = ((), (), s32[]{:S(2)}) async-start(), calls=%async_computation.30 | async-start | bytes 5242880 | tf_op jit(solution)/shard_map/reduce_scatter | solution.py:238
  1368.9 30.1 all-to-all-start.5
  1399.0 29.9 all-to-all-start.7
  1432.5 162.0 %all-reduce.21.cloned.1.call-start = ((), (), s32[]{:S(2)}) async-start(), calls=%async_computation.32 | async-start | bytes 131072
  1474.8 481.6 %reduce-scatter.19.cloned.1.call-start = ((), (), s32[]{:S(2)}) async-start(), calls=%async_computation.29 | async-start | bytes 17301504 | tf_op jit(solution)/shard_map/reduce_scatter | solution.py:290
  1484.7 831.9 %reduce-scatter.17.cloned.1.call-start = ((), (), s32[]{:S(2)}) async-start(), calls=%async_computation.28 | async-start | bytes 17301504 | tf_op jit(solution)/shard_map/reduce_scatter | solution.py:288
  1494.9 1181.9 %reduce-scatter.13.cloned.1.call-start = ((), (), s32[]{:S(2)}) async-start(), calls=%async_computation.26 | async-start | bytes 17301504 | tf_op jit(solution)/shard_map/reduce_scatter | solution.py:285
  1503.2 1533.8 %reduce-scatter.15.cloned.1.call-start = ((), (), s32[]{:S(2)}) async-start(), calls=%async_computation.27 | async-start | bytes 17301504 | tf_op jit(solution)/shard_map/reduce_scatter | solution.py:287
  (50 other events, 1455.8 us)
Sparse Core Ops, SparseCore 0:
  11.0 80.5 all-gather.11
  94.5 86.1 all-gather.9
  183.7 85.9 all-gather.13
  272.5 85.7 all-gather.15
  359.7 33.6 all-gather.19
  411.5 123.9 all-gather.17
  537.0 32.6 all-gather.21
  572.4 124.9 all-gather.23
  732.5 280.7 reduce-scatter.10
  1017.1 147.9 reduce-scatter.8
  1167.7 43.5 reduce-scatter.22
  1213.8 44.5 reduce-scatter.20
  1474.9 119.5 all-reduce.20
  1597.3 359.0 reduce-scatter.18
  1959.2 357.3 reduce-scatter.16
  2319.5 357.3 reduce-scatter.12
  2679.7 357.3 reduce-scatter.14
where the time goes:
time: 3050 us; the launch traced here: 3040 us
  waiting for transfers between devices  2470 us (81%)
  matrix products  275 us (9%)
  local copies, waits for them, and re-layouts  124 us (4%)
  blocking collectives  54.6 us (2%)
  other arithmetic  53.6 us (2%)
  starting transfers between devices  33.3 us (1%)
    reduce_scatter x1, waiting for transfers between devices, on_device(): lax.psum_scatter(value_w_grad, ('batch', 'seq'), scatter_dimension=0, til...  360 us
    reduce_scatter x1, waiting for transfers between devices, on_device(): lax.psum_scatter(key_w_grad, ('batch', 'seq'), scatter_dimension=0, tiled...  360 us
    reduce_scatter x1, waiting for transfers between devices, on_device(): lax.psum_scatter(query_w_grad, ('batch', 'seq'), scatter_dimension=0, til...  360 us
    reduce_scatter x1, waiting for transfers between devices, on_device(): lax.psum_scatter(out_w_grad, ('batch', 'seq'), scatter_dimension=0, tiled...  352 us
    reduce_scatter x1, waiting for transfers between devices, on_device(): lax.psum_scatter(jnp.einsum('tf,df->td', rows, weight_up, preferred_eleme...  248 us
    reduce_scatter x1, waiting for transfers between devices, on_device(): lax.psum_scatter(jnp.dot(rows, weight_down, preferred_element_type=single...  149 us
    all_gather x1, waiting for transfers between devices, on_device(): branch_group = lax.all_gather(branch_grad, 'seq', axis=0, tiled=True)  128 us
    all_gather x1, waiting for transfers between devices, on_device(): normed_group = lax.all_gather(normed_two, 'seq', axis=0, tiled=True)  115 us
  transfers between devices with their start and end apart: 25, of which 19 were waited for; matrix products, arithmetic and copies ran while one was open for 13% of the time, Pallas kernels for 0%

commit v1 on v0

v1 whole, which is shorter than its diff:
```python
from functools import partial

import jax
import jax.numpy as jnp
from jax import lax
from jax.sharding import Mesh
from jax.sharding import PartitionSpec as P

HEAD_DIM = 64
SPANS = 4

bfloat = jnp.bfloat16
single = jnp.float32

PLANE = ("b", "x")
ALL = ("b", "z", "x")


def dot(left, right):
    return jnp.dot(left, right, preferred_element_type=single)


def dot_tn(left, right):
    return lax.dot_general(left, right, (((0,), (0,)), ((), ())), preferred_element_type=single)


def dot_nt(left, right):
    return lax.dot_general(left, right, (((1,), (1,)), ((), ())), preferred_element_type=single)


def layer_norm(values, gain_vec, shift_vec):
    center = jnp.mean(values, axis=-1, keepdims=True)
    centered = values - center
    spread = jnp.mean(centered * centered, axis=-1, keepdims=True)
    return centered * lax.rsqrt(spread + 1e-05) * gain_vec + shift_vec


def column_sums(matrix):
    return jnp.sum(matrix.astype(single), axis=0)


def attention_forward(query, key_two, value_two, allowed):
    scores = jnp.einsum("gqhd,gkhd->ghqk", query, key_two, preferred_element_type=single) * HEAD_DIM ** (-0.5)
    scores = jnp.where(allowed[:, None], scores, -1e30)
    row_peak = jnp.max(scores, axis=-1, keepdims=True)
    weights_exp = jnp.exp(scores - row_peak)
    row_total = jnp.sum(weights_exp, axis=-1, keepdims=True)
    prob_low = (weights_exp / row_total).astype(bfloat)
    context = jnp.einsum("ghqk,gkhd->gqhd", prob_low, value_two, preferred_element_type=single)
    return context.astype(bfloat), row_peak + jnp.log(row_total)


def attention_backward(query, key_two, value_two, grad, logsum, allowed):
    scores = jnp.einsum("gqhd,gkhd->ghqk", query, key_two, preferred_element_type=single) * HEAD_DIM ** (-0.5)
    probs = jnp.exp(jnp.where(allowed[:, None], scores, -1e30) - logsum)
    prob_grad = jnp.einsum("gqhd,gkhd->ghqk", grad, value_two, preferred_element_type=single)
    row_dot = jnp.sum(probs * prob_grad, axis=-1, keepdims=True)
    score_grad = (probs * (prob_grad - row_dot)).astype(bfloat)
    query_grad = jnp.einsum("ghqk,gkhd->gqhd", score_grad, key_two, preferred_element_type=single) * HEAD_DIM ** (-0.5)
    key_grad = jnp.einsum("ghqk,gqhd->gkhd", score_grad, query, preferred_element_type=single) * HEAD_DIM ** (-0.5)
    value_grad = jnp.einsum("ghqk,gqhd->gkhd", probs.astype(bfloat), grad, preferred_element_type=single)
    return query_grad, key_grad, value_grad


def norm_backward(values, out_grad, gain_vec):
    center = jnp.mean(values, axis=-1, keepdims=True)
    centered = values - center
    rs = lax.rsqrt(jnp.mean(centered * centered, axis=-1, keepdims=True) + 1e-05)
    xhat = centered * rs
    g = out_grad * gain_vec
    part = rs * (g - jnp.mean(g, axis=-1, keepdims=True) - xhat * jnp.mean(g * xhat, axis=-1, keepdims=True))
    return part, jnp.sum(out_grad * xhat, axis=0), jnp.sum(out_grad, axis=0)


def on_device(
    inputs,
    exit_layers,
    lengths,
    layer_index,
    out_grad,
    ln1_gain,
    ln1_bias,
    q_weight,
    q_bias,
    k_weight,
    v_weight,
    v_bias,
    o_weight,
    o_bias,
    ln2_gain,
    ln2_bias,
    fc1_weight,
    fc1_bias,
    fc2_weight,
    fc2_bias,
):
    B, Z, X = lax.axis_size("b"), lax.axis_size("z"), lax.axis_size("x")
    R = B * X
    local = inputs[0].astype(single)
    tok, D = local.shape
    span = X * tok
    group_tok = Z * span
    at_z, at_x = lax.axis_index("z"), lax.axis_index("x")
    rank = lax.axis_index("b") * X + at_x
    rows_dev = q_weight.shape[0]
    cols = D // R
    heads = cols // HEAD_DIM
    whole_heads = rows_dev % HEAD_DIM == 0

    group_active = (exit_layers[0] > layer_index[0]).astype(single)
    active_total = jnp.sum(group_active)
    active = lax.dynamic_slice_in_dim(group_active, at_z * span + at_x * tok, tok, 0)[:, None]

    ends = jnp.cumsum(lax.all_gather(lengths[0], "b", axis=0), axis=1)
    places = at_z * span + jnp.arange(span, dtype=jnp.int32)
    starts = jnp.max(jnp.where(ends[:, None, :] <= places[None, :, None], ends[:, None, :], 0), axis=2)
    key_places = (at_z - 1) * span + jnp.arange(2 * span, dtype=jnp.int32)
    allowed = (key_places[None, None, :] >= starts[:, :, None]) & (key_places[None, None, :] <= places[None, :, None])

    small = jnp.stack([ln1_gain, ln1_bias, q_bias, v_bias, o_bias, ln2_gain, ln2_bias, fc2_bias])
    small = lax.all_gather(small, ALL, axis=1, tiled=True).astype(single)
    gain_one, bias_one, bias_q, bias_v, bias_o, gain_two, bias_two, bias_down = [small[i] for i in range(8)]

    def to_ranks(matrix):
        lead = matrix.shape[:-1]
        if whole_heads:
            matrix = matrix.reshape(*lead, B, Z, X, rows_dev)
            k = len(lead)
            return matrix.transpose(k, k + 2, *range(k), k + 1, k + 3).reshape(R, *lead, cols)
        return jnp.moveaxis(matrix.reshape(*lead, R, cols), -2, 0)

    def from_ranks(parts):
        if whole_heads:
            parts = parts.reshape(B, X, -1, Z, rows_dev)
            return parts.transpose(2, 0, 3, 1, 4).reshape(-1, D)
        return parts.transpose(1, 0, 2).reshape(-1, D)

    def mine(vector):
        return lax.dynamic_index_in_dim(to_ranks(vector), rank, 0, keepdims=False)

    qkv_parts = jnp.concatenate([to_ranks(q_weight), to_ranks(k_weight), to_ranks(v_weight)], axis=2)
    qkv_mine = lax.all_to_all(qkv_parts, PLANE, split_axis=0, concat_axis=0, tiled=True)
    weight_qkv = lax.all_gather(qkv_mine, "z", axis=0)
    weight_qkv = weight_qkv.reshape(Z, B, X, rows_dev, 3 * cols).transpose(1, 0, 2, 3, 4).reshape(D, 3 * cols)
    bias_qkv = jnp.concatenate([mine(bias_q), jnp.zeros((cols,), single), mine(bias_v)])
    if whole_heads:
        weight_o = lax.all_gather(o_weight, "z", axis=0, tiled=True)
    else:
        weight_o = lax.dynamic_slice_in_dim(lax.all_gather(o_weight, ALL, axis=0, tiled=True), rank * cols, cols, 0)
    weight_up = lax.all_gather(fc1_weight, "z", axis=1, tiled=True)
    weight_down = lax.all_gather(fc2_weight, "z", axis=0, tiled=True)
    bias_up = lax.all_gather(fc1_bias, "z", axis=0, tiled=True).astype(single)

    normed_low = layer_norm(local, gain_one, bias_one).astype(bfloat)
    normed_all = lax.all_gather(normed_low, PLANE, axis=0, tiled=True)
    qkv = (dot(normed_all, weight_qkv) + bias_qkv).astype(bfloat)
    query = qkv[:, :cols].reshape(B, span, heads, HEAD_DIM)
    key_value = qkv[:, cols:]
    up = [(i, i + 1) for i in range(Z - 1)]
    down = [(i + 1, i) for i in range(Z - 1)]
    before = lax.ppermute(key_value, "z", up)
    both = jnp.concatenate([before.reshape(B, span, 2 * cols), key_value.reshape(B, span, 2 * cols)], axis=1)
    key_two = both[..., :cols].reshape(B, 2 * span, heads, HEAD_DIM)
    value_two = both[..., cols:].reshape(B, 2 * span, heads, HEAD_DIM)
    context, logsum = attention_forward(query, key_two, value_two, allowed)
    context = context.reshape(B * span, cols)

    def reduce_plane(partial_sums):
        return lax.psum_scatter(partial_sums.astype(bfloat), PLANE, scatter_dimension=0, tiled=True).astype(single)

    attended = reduce_plane(dot(context, weight_o)) + bias_o
    middle = local + active * attended
    normed_two = layer_norm(middle, gain_two, bias_two).astype(bfloat)
    cotangent = out_grad[0].astype(single) * (group_tok / active_total)
    branch_grad = (active * cotangent).astype(bfloat)
    down_b_grad = column_sums(branch_grad)
    branch_all = lax.all_gather(branch_grad, PLANE, axis=0, tiled=True)
    two_all = lax.all_gather(normed_two, PLANE, axis=0, tiled=True)
    hidden_pre = dot(two_all, weight_up) + bias_up
    gelu_value, gelu_pull = jax.vjp(partial(jax.nn.gelu, approximate=True), hidden_pre)
    hidden = gelu_value.astype(bfloat)
    hidden_grad = dot_nt(branch_all, weight_down)
    pre_grad = gelu_pull(hidden_grad)[0].astype(bfloat)
    normed_two_grad = reduce_plane(dot_nt(pre_grad, weight_up))
    branch = reduce_plane(dot(hidden, weight_down)) + bias_down
    outputs = middle + active * branch
    down_w_grad = dot_tn(hidden, branch_all)
    up_w_grad = dot_tn(two_all, pre_grad)
    up_b_grad = column_sums(pre_grad)
    down_w_shard = lax.psum_scatter(down_w_grad.astype(bfloat), "z", scatter_dimension=0, tiled=True).astype(single)
    up_w_shard = lax.psum_scatter(up_w_grad.astype(bfloat), "z", scatter_dimension=1, tiled=True).astype(single)
    up_b_shard = lax.psum_scatter(up_b_grad, "z", scatter_dimension=0, tiled=True)

    middle_part, gain_two_grad, bias_two_grad = norm_backward(middle, normed_two_grad, gain_two)
    middle_grad = cotangent + middle_part
    attended_grad = (active * middle_grad).astype(bfloat)
    out_b_grad = column_sums(attended_grad)
    attended_all = lax.all_gather(attended_grad, PLANE, axis=0, tiled=True)
    context_grad = dot_nt(attended_all, weight_o).astype(bfloat)
    out_w_grad = dot_tn(context, attended_all)
    query_grad, key_grad, value_grad = attention_backward(
        query, key_two, value_two, context_grad.reshape(B, span, heads, HEAD_DIM), logsum, allowed
    )
    pair = jnp.concatenate(
        [key_grad.reshape(B, 2 * span, cols), value_grad.reshape(B, 2 * span, cols)], axis=2
    )
    after = lax.ppermute(pair[:, :span].astype(bfloat), "z", down).astype(single)
    pair_grad = (pair[:, span:] + after).astype(bfloat).reshape(B * span, 2 * cols)
    qkv_grad = jnp.concatenate([query_grad.astype(bfloat).reshape(B * span, cols), pair_grad], axis=1)
    normed_grad = reduce_plane(dot_nt(qkv_grad, weight_qkv))
    qkv_w_grad = dot_tn(normed_all, qkv_grad)
    qkv_b_grad = column_sums(qkv_grad)
    input_part, gain_one_grad, bias_one_grad = norm_backward(local, normed_grad, gain_one)
    input_grad = middle_grad + input_part

    qkv_w_grad = qkv_w_grad.astype(bfloat).reshape(B, Z, X, rows_dev, 3 * cols)
    qkv_w_grad = lax.psum_scatter(qkv_w_grad.transpose(1, 0, 2, 3, 4), "z", scatter_dimension=0, tiled=True)
    qkv_w_grad = lax.all_to_all(qkv_w_grad.reshape(R, rows_dev, 3 * cols), PLANE, split_axis=0, concat_axis=0, tiled=True)
    qkv_w_grad = qkv_w_grad.astype(single)
    q_w_shard, k_w_shard, v_w_shard = [from_ranks(qkv_w_grad[..., i * cols : (i + 1) * cols]) for i in range(3)]
    if whole_heads:
        out_w_shard = lax.psum_scatter(out_w_grad.astype(bfloat), "z", scatter_dimension=0, tiled=True).astype(single)
        q_b_shard = lax.psum_scatter(qkv_b_grad[:cols], "z", scatter_dimension=0, tiled=True)
        v_b_shard = lax.psum_scatter(qkv_b_grad[2 * cols :], "z", scatter_dimension=0, tiled=True)
    else:

        def placed(rows):
            full = jnp.zeros((D,) + rows.shape[1:], rows.dtype)
            full = lax.dynamic_update_slice_in_dim(full, rows, rank * cols, 0)
            return lax.psum_scatter(full, ALL, scatter_dimension=0, tiled=True).astype(single)

        out_w_shard = placed(out_w_grad.astype(bfloat))
        q_b_shard = placed(qkv_b_grad[:cols])
        v_b_shard = placed(qkv_b_grad[2 * cols :])
    sums = jnp.stack([gain_one_grad, bias_one_grad, out_b_grad, gain_two_grad, bias_two_grad, down_b_grad])
    sums = lax.psum_scatter(sums, ALL, scatter_dimension=1, tiled=True)
    return (
        outputs.astype(bfloat)[None],
        input_grad.astype(bfloat)[None],
        sums[0],
        sums[1],
        q_w_shard,
        q_b_shard,
        k_w_shard,
        v_w_shard,
        v_b_shard,
        out_w_shard,
        sums[2],
        sums[3],
        sums[4],
        up_w_shard,
        up_b_shard,
        down_w_shard,
        sums[5],
    )


def solution(mesh):
    groups, parts = mesh.shape["batch"], mesh.shape["seq"]
    inner = Mesh(mesh.devices.reshape(groups, SPANS, parts // SPANS), ("b", "z", "x"))
    token = P("b", ("z", "x"), None)
    vector = P(ALL)
    rows = P(ALL, None)
    columns = P(None, ALL)
    return jax.shard_map(
        on_device,
        mesh=inner,
        in_specs=(
            token,
            P("b", None),
            P("b", None),
            P(),
            token,
            vector,
            vector,
            rows,
            vector,
            rows,
            rows,
            vector,
            rows,
            vector,
            vector,
            vector,
            columns,
            vector,
            rows,
            vector,
        ),
        out_specs=(
            token,
            token,
            vector,
            vector,
            rows,
            vector,
            rows,
            rows,
            vector,
            rows,
            vector,
            vector,
            vector,
            columns,
            vector,
            rows,
            vector,
        ),
        check_vma=False,
    )
```

time: 3050 us -> 1580 us (0.52)
  waiting for transfers between devices: 2470 us -> 1040 us
  blocking collectives: 54.6 us -> 113 us
  local copies, waits for them, and re-layouts: 124 us -> 76.3 us
  matrix products: 275 us -> 232 us
  other arithmetic: 53.6 us -> 88.3 us
    reduce_scatter x8 -> x7, waiting for transfers between devices: 1830 us -> 412 us  [the longest x4 253 us: reduce_plane(): lax.psum_scatter(partial_sums.astype(bfloat), PLANE, scatter_dimension=0,...]
    unnamed x18 -> x19, waiting for transfers between devices: 69.3 us -> 203 us
    all_to_all x8 -> x1, waiting for transfers between devices: 128 us -> 0.01 us  [on_device(): lax.all_to_all(qkv_w_grad.reshape(R, rows_dev, 3 * cols), PLANE, split_ax...]
    all_gather x8, waiting for transfers between devices: 446 us -> 342 us  [the longest x1 67.7 us: on_device(): weight_down = lax.all_gather(fc2_weight, 'z', axis=0, tiled=True)]
    all_gather x1 -> x3, blocking collectives: 5.07 us -> 85 us  [the longest x1 68.8 us: on_device(): small = lax.all_gather(small, ALL, axis=1, tiled=True).astype(single)]
    ppermute x0 -> x2, waiting for transfers between devices: none -> 79.1 us  [the longest x1 44.5 us: on_device(): before = lax.ppermute(key_value, 'z', up)]
    dynamic_update_slice x8 -> x0, local copies, waits for them, and re-layouts: 44 us -> none  [the longest x4 22 us: one_block(): lax.dynamic_update_slice_in_dim(value_acc, lax.dynamic_slice_in_dim(value...]
    dot_general x46 -> x18, matrix products: 275 us -> 232 us  [the longest x4 48.6 us: dot_nt(): lax.dot_general(left, right, (((1,), (1,)), ((), ())), preferred_element_...]
  transfers between devices with their start and end apart: 25 -> 20, of which waited for: 19 -> 17; matrix products, arithmetic and copies ran while one was open for 13% -> 13% of each run, Pallas kernels for 0% -> 0%
where the time goes in v1:
time: 1580 us
  waiting for transfers between devices  1040 us (66%)
  matrix products  232 us (15%)
  blocking collectives  113 us (7%)
  other arithmetic  88.3 us (6%)
  local copies, waits for them, and re-layouts  76.3 us (5%)
  between operations  17.7 us (1%)
    reduce_scatter x4, waiting for transfers between devices, reduce_plane(): lax.psum_scatter(partial_sums.astype(bfloat), PLANE, scatter_dimension=0,...  253 us
    unnamed x19, waiting for transfers between devices  203 us
    reduce_scatter x1, waiting for transfers between devices, on_device(): lax.psum_scatter(up_w_grad.astype(bfloat), 'z', scatter_dimension=1, tile...  76.6 us
    reduce_scatter x1, waiting for transfers between devices, on_device(): lax.psum_scatter(down_w_grad.astype(bfloat), 'z', scatter_dimension=0, ti...  70.4 us
    all_gather x1, blocking collectives, on_device(): small = lax.all_gather(small, ALL, axis=1, tiled=True).astype(single)  68.8 us
    all_gather x1, waiting for transfers between devices, on_device(): weight_down = lax.all_gather(fc2_weight, 'z', axis=0, tiled=True)  67.7 us
    all_gather x1, waiting for transfers between devices, on_device(): weight_up = lax.all_gather(fc1_weight, 'z', axis=1, tiled=True)  63 us
    all_gather x1, waiting for transfers between devices, on_device(): branch_all = lax.all_gather(branch_grad, PLANE, axis=0, tiled=True)  55.6 us
  transfers between devices with their start and end apart: 20, of which 17 were waited for; matrix products, arithmetic and copies ran while one was open for 13% of the time, Pallas kernels for 0%

profile of v1, /device:TPU:0, one launch (start us, length us, event | category | flops | bytes accessed | tf_op | source)
XLA Modules:
  0.0 1576.5 jit_solution(18308437619097238947)
XLA Ops:
  12.4 17.1 %all_to_all.10 = bf16[8,64,768]{2,1,0:T(8,128)(2,1)} all-to-all(bf16[8,64,768]{2,1,0:T(8,128)(2,1)S(1)} %pad_maximum_fusion.5), channel_id=1, replica_groups=mesh['b'=4,'z'=4,'x'=2] {'b','x'}, dimensions={0} | all-to-all | bytes 1572864 | tf_op jit(solution)/shard_map/all_to_all | solution.py:142
  29.7 68.8 %all-gather.1 = bf16[32,64,8]{1,2,0:T(8,128)(2,1)S(1)} all-gather(bf16[1,64,8]{1,2,0:T(8,128)(2,1)S(1)} %bitcast.246), channel_id=1, replica_groups=mesh['b'=4,'z'=4,'x'=2] {'b','z','x'}, dimensions={0}, use_global_device_ids=true | all-gather | bytes 33792 | tf_op jit(solution)/shard_map/all_gather | solution.py:121
  105.7 47.2 %all-gather.13.cloned.1.call-done = bf16[2048,2048]{1,0:T(8,128)(2,1)} async-done(((bf16[256,2048]{1,0:T(8,128)(2,1)}), bf16[2048,2048]{1,0:T(8,128)(2,1)}) %all-gather.13.cloned.1.call-update) | async-done | bytes 8388624 | tf_op jit(solution)/shard_map/all_gather | solution.py:155
  187.4 44.5 %collective-permute-done = bf16[2048,512]{1,0:T(8,128)(2,1)} collective-permute-done((bf16[2048,512]{1,0:T(8,128)(2,1)}, bf16[2048,512]{1,0:T(8,128)(2,1)}, u32[]{:S(2)}, u32[]{:S(2)}) %collective-permute-start) | collective-permute-done | bytes 2097184 | tf_op jit(solution)/shard_map/ppermute | solution.py:161
  243.2 15.9 %fusion.61 = (f32[4,4,512]{2,1,0:T(4,128)S(1)}, f32[4,4,512,1024]{3,2,1,0:T(8,128)}) fusion(bf16[4,512,4,64]{1,3,2,0:T(8,128)(2,1)} %copy.142, bf16[4,1024,4,64]{1,3,2,0:T(8,128)(2,1)S(1)} %bitcast.188, pred[4,512,1024]{2,1,0:T(8,128)(4,1)} %compare_and_fusion), kind=kOutput, calls=%fused_computation.130 | convolution fusion | flops 1098899456 | bytes 38830080 | tf_op jit(solution)/shard_map/gqhd,gkhd->ghqk/dot_general | solution.py:43
  297.5 69.8 %reduce-scatter.14.cloned.1.call-done = bf16[256,2048]{1,0:T(8,128)(2,1)} async-done(((bf16[2048,2048]{1,0:T(8,128)(2,1)}), bf16[256,2048]{1,0:T(8,128)(2,1)}) %reduce-scatter.14.cloned.1.call-update) | async-done | bytes 1048592 | tf_op jit(solution)/shard_map/reduce_scatter | solution.py:169
  386.4 63.0 %all-gather.19.cloned.1.call-done = bf16[2048,1024]{1,0:T(8,128)(2,1)} async-done(((bf16[2048,256]{1,0:T(8,128)(2,1)}), bf16[2048,1024]{1,0:T(8,128)(2,1)}) %all-gather.19.cloned.1.call-update) | async-done | bytes 4194320 | tf_op jit(solution)/shard_map/all_gather | solution.py:150
  449.3 54.5 %all-gather.17.cloned.1.call-done = bf16[2048,2048]{1,0:T(8,128)(2,1)} async-done(((bf16[256,2048]{1,0:T(8,128)(2,1)}), bf16[2048,2048]{1,0:T(8,128)(2,1)}) %all-gather.17.cloned.1.call-update) | async-done | bytes 8388624 | tf_op jit(solution)/shard_map/all_gather | solution.py:178
  518.6 67.7 %all-gather.21.cloned.1.call-done = bf16[1024,2048]{1,0:T(8,128)(2,1)} async-done(((bf16[256,2048]{1,0:T(8,128)(2,1)}), bf16[1024,2048]{1,0:T(8,128)(2,1)}) %all-gather.21.cloned.1.call-update) | async-done | bytes 4194320 | tf_op jit(solution)/shard_map/all_gather | solution.py:151
  586.3 55.6 %all-gather.23.cloned.1.call-done = bf16[2048,2048]{1,0:T(8,128)(2,1)} async-done(((bf16[256,2048]{1,0:T(8,128)(2,1)}), bf16[2048,2048]{1,0:T(8,128)(2,1)}) %all-gather.23.cloned.1.call-update) | async-done | bytes 8388624 | tf_op jit(solution)/shard_map/all_gather | solution.py:177
  641.9 20.8 %convert_reduce_fusion = (f32[1024]{0:T(1024)}, bf16[2048,1024]{1,0:T(8,128)(2,1)S(1)}) fusion(f32[2048,1024]{1,0:T(8,128)} %fusion.62, f32[1024]{0:T(1024)S(1)} %bitcast.248, bf16[2048,2048]{1,0:T(8,128)(2,1)} %all-gather.23.cloned.1.call-done, bf16[1024,2048]{1,0:T(8,128)(2,1)} %all-gather.21.cloned.1.call-done), kind=kOutput, calls=%fused_computation.22 | convolution fusion | flops 8638168064 | bytes 25174016 | tf_op jit(solution)/shard_map/dot_general | solution.py:28
  691.3 55.8 %reduce-scatter.18.cloned.1.call-done = bf16[256,2048]{1,0:T(8,128)(2,1)} async-done(((bf16[2048,2048]{1,0:T(8,128)(2,1)}), bf16[256,2048]{1,0:T(8,128)(2,1)}) %reduce-scatter.18.cloned.1.call-update) | async-done | bytes 1048592 | tf_op jit(solution)/shard_map/reduce_scatter | solution.py:169
  750.3 71.5 %reduce-scatter.16.cloned.1.call-done = bf16[256,2048]{1,0:T(8,128)(2,1)} async-done(((bf16[2048,2048]{1,0:T(8,128)(2,1)}), bf16[256,2048]{1,0:T(8,128)(2,1)}) %reduce-scatter.16.cloned.1.call-update) | async-done | bytes 1048592 | tf_op jit(solution)/shard_map/reduce_scatter | solution.py:169
  826.9 54.5 %all-gather.25.cloned.1.call-done = bf16[2048,2048]{1,0:T(8,128)(2,1)} async-done(((bf16[256,2048]{1,0:T(8,128)(2,1)}), bf16[2048,2048]{1,0:T(8,128)(2,1)}) %all-gather.25.cloned.1.call-update) | async-done | bytes 8388624 | tf_op jit(solution)/shard_map/all_gather | solution.py:198
  889.7 15.5 fusion.2
  905.2 22.2 %multiply_reduce_fusion = (f32[4,4,512]{2,1,0:T(4,128)S(1)}, f32[4,4,512,1024]{3,2,1,0:T(8,128)}) fusion(f32[4,4,512,1024]{3,2,1,0:T(8,128)} %get-tuple-element.63, f32[4,4,512]{2,1,0:T(4,128)S(1)} %bitcast.214, bf16[4,512,4,64]{1,3,2,0:T(8,128)(2,1)S(1)} %copy.145, bf16[4,1024,4,64]{1,3,2,0:T(8,128)(2,1)S(1)} %bitcast.193), kind=kOutput, calls=%fused_computation.1 | convolution fusion | flops 1098899456 | bytes 70320128 | tf_op jit(solution)/shard_map/gqhd,gkhd->ghqk/dot_general | solution.py:56
  932.7 27.8 %multiply_convert_fusion = bf16[4,4,512,1024]{3,2,1,0:T(8,128)(2,1)} fusion(f32[4,4,512,1024]{3,2,1,0:T(8,128)} %get-tuple-element.65, f32[4,4,512,1024]{3,2,1,0:T(8,128)} %get-tuple-element.63, f32[4,4,512]{2,1,0:T(4,128)S(1)} %get-tuple-element.64, f32[4,4,512]{2,1,0:T(4,128)S(1)} %bitcast.215), kind=kLoop, calls=%fused_computation | loop fusion | flops 33554432 | bytes 83951616 | tf_op jit(solution)/shard_map/convert_element_type | solution.py:58
  996.0 34.6 %collective-permute-done.1 = bf16[4,512,512]{2,1,0:T(8,128)(2,1)} collective-permute-done((bf16[4,512,512]{2,1,0:T(8,128)(2,1)}, bf16[4,512,512]{2,1,0:T(8,128)(2,1)}, u32[]{:S(2)}, u32[]{:S(2)}) %collective-permute-start.1) | collective-permute-done | bytes 2097184 | tf_op jit(solution)/shard_map/ppermute | solution.py:207
  1044.7 16.7 %convolution_convert_fusion.4 = bf16[1024,2048]{1,0:T(8,128)(2,1)} fusion(bf16[2048,2048]{1,0:T(8,128)(2,1)} %all-gather.23.cloned.1.call-done, f32[2048,1024]{1,0:T(8,128)} %fusion.62, f32[1024]{0:T(1024)S(1)} %bitcast.250), kind=kOutput, calls=%fused_computation.38 | convolution fusion | flops 8613003264 | bytes 20975616 | tf_op jit(solution)/shard_map/dot_general | solution.py:24
  1095.8 69.0 %all-reduce.7.cloned.1.call-done = bf16[4,4,2,64,768]{4,3,2,0,1:T(8,128)(2,1)} async-done(((bf16[4,4,2,64,768]{4,3,2,0,1:T(8,128)(2,1)}), bf16[4,4,2,64,768]{4,3,2,0,1:T(8,128)(2,1)}) %all-reduce.7.cloned.1.call-update) | async-done | bytes 3145744
  1172.6 70.4 %reduce-scatter.26.cloned.1.call-done = bf16[256,2048]{1,0:T(8,128)(2,1)} async-done(((bf16[1024,2048]{1,0:T(8,128)(2,1)}), bf16[256,2048]{1,0:T(8,128)(2,1)}) %reduce-scatter.26.cloned.1.call-update) | async-done | bytes 1048592 | tf_op jit(solution)/shard_map/reduce_scatter | solution.py:190
  1245.8 76.6 %reduce-scatter.24.cloned.1.call-done = bf16[2048,256]{1,0:T(8,128)(2,1)} async-done(((bf16[2048,1024]{1,0:T(8,128)(2,1)}), bf16[2048,256]{1,0:T(8,128)(2,1)}) %reduce-scatter.24.cloned.1.call-update) | async-done | bytes 1048592 | tf_op jit(solution)/shard_map/reduce_scatter | solution.py:191
  1370.4 55.5 %reduce-scatter.20.cloned.1.call-done = bf16[256,2048]{1,0:T(8,128)(2,1)} async-done(((bf16[2048,2048]{1,0:T(8,128)(2,1)}), bf16[256,2048]{1,0:T(8,128)(2,1)}) %reduce-scatter.20.cloned.1.call-update) | async-done | bytes 1048592 | tf_op jit(solution)/shard_map/reduce_scatter | solution.py:169
  1432.8 132.3 %reduce-scatter.28.cloned.1.call-done = f32[64,6]{1,0:T(8,128)} async-done(((f32[2048,6]{1,0:T(8,128)}), f32[64,6]{1,0:T(8,128)}) %reduce-scatter.28.cloned.1.call-update) | async-done | bytes 1552
  (240 shorter events, 331.4 us)
Async XLA Ops:
  7.2 94.7 %all-gather.27.cloned.1.call-start = ((), (), s32[]{:S(2)}) async-start(), calls=%async_computation.24 | async-start | bytes 3932160 | tf_op jit(solution)/shard_map/all_gather | solution.py:143
  10.8 87.8 %copy-start = (bf16[1,256,2048]{2,1,0:T(8,128)(2,1)S(1)}, bf16[1,256,2048]{2,1,0:T(8,128)(2,1)}, u32[]{:S(2)}) copy-start(bf16[1,256,2048]{2,1,0:T(8,128)(2,1)} %param.20) | copy-start | bytes 3145732
  29.6 123.4 %all-gather.13.cloned.1.call-start = ((), (), s32[]{:S(2)}) async-start(), calls=%async_computation.10 | async-start | bytes 9437184 | tf_op jit(solution)/shard_map/all_gather | solution.py:155
  101.4 186.2 %all-gather.15.cloned.1.call-start = ((), (), s32[]{:S(2)}) async-start(), calls=%async_computation.11 | async-start | bytes 1310720 | tf_op jit(solution)/shard_map/all_gather | solution.py:147
  166.1 65.8 %collective-permute-start = (bf16[2048,512]{1,0:T(8,128)(2,1)}, bf16[2048,512]{1,0:T(8,128)(2,1)}, u32[]{:S(2)}, u32[]{:S(2)}) collective-permute-start(bf16[2048,512]{1,0:T(8,128)(2,1)} %slice.105), channel_id=1, source_target_pairs={{0,2},{2,4},{4,6},{1,3},{3,5},{5,7},{8,10},{10,12},{12,14},{9,11},... | collective-permute-start | bytes 6291464 | tf_op jit(solution)/shard_map/ppermute | solution.py:161
  170.8 196.5 %reduce-scatter.14.cloned.1.call-start = ((), (), s32[]{:S(2)}) async-start(), calls=%async_computation.12 | async-start | bytes 9437184 | tf_op jit(solution)/shard_map/reduce_scatter | solution.py:169
  294.9 76.2 %copy-start.12 = (bf16[1,256,2048]{2,1,0:T(8,128)(2,1)S(1)}, bf16[1,256,2048]{2,1,0:T(8,128)(2,1)}, u32[]{:S(2)}) copy-start(bf16[1,256,2048]{2,1,0:T(8,128)(2,1)} %param.24) | copy-start | bytes 3145732
  294.9 154.5 %all-gather.19.cloned.1.call-start = ((), (), s32[]{:S(2)}) async-start(), calls=%async_computation.14 | async-start | bytes 5242880 | tf_op jit(solution)/shard_map/all_gather | solution.py:150
  295.5 208.4 %all-gather.17.cloned.1.call-start = ((), (), s32[]{:S(2)}) async-start(), calls=%async_computation.13 | async-start | bytes 9437184 | tf_op jit(solution)/shard_map/all_gather | solution.py:178
  373.8 212.5 %all-gather.21.cloned.1.call-start = ((), (), s32[]{:S(2)}) async-start(), calls=%async_computation.15 | async-start | bytes 5242880 | tf_op jit(solution)/shard_map/all_gather | solution.py:151
  374.6 267.3 %all-gather.23.cloned.1.call-start = ((), (), s32[]{:S(2)}) async-start(), calls=%async_computation.17 | async-start | bytes 9437184 | tf_op jit(solution)/shard_map/all_gather | solution.py:177
  375.3 371.8 %reduce-scatter.18.cloned.1.call-start = ((), (), s32[]{:S(2)}) async-start(), calls=%async_computation.18 | async-start | bytes 9437184 | tf_op jit(solution)/shard_map/reduce_scatter | solution.py:169
  675.7 146.1 %reduce-scatter.16.cloned.1.call-start = ((), (), s32[]{:S(2)}) async-start(), calls=%async_computation.16 | async-start | bytes 9437184 | tf_op jit(solution)/shard_map/reduce_scatter | solution.py:169
  691.2 130.5 %copy-start.21 = (f32[1,2048]{1,0:T(1,128)S(1)}, f32[1,2048]{1,0:T(1,128)}, u32[]{:S(2)}) copy-start(f32[1,2048]{1,0:T(1,128)} %get-tuple-element.45) | copy-start | bytes 24580
  691.3 190.1 %all-gather.25.cloned.1.call-start = ((), (), s32[]{:S(2)}) async-start(), calls=%async_computation.19 | async-start | bytes 9437184 | tf_op jit(solution)/shard_map/all_gather | solution.py:198
  826.8 338.0 %all-reduce.7.cloned.1.call-start = ((), (), s32[]{:S(2)}) async-start(), calls=%async_computation.26 | async-start | bytes 6291456
  980.6 50.0 %collective-permute-start.1 = (bf16[4,512,512]{2,1,0:T(8,128)(2,1)}, bf16[4,512,512]{2,1,0:T(8,128)(2,1)}, u32[]{:S(2)}, u32[]{:S(2)}) collective-permute-start(bf16[4,512,512]{2,1,0:T(8,128)(2,1)} %fusion.16), channel_id=1, source_target_pairs={{2,0},{4,2},{6,4},{3,1},{5,3},{7,5},{10,8},{12,10},{14,12},{11,9},... | collective-permute-start | bytes 6291464 | tf_op jit(solution)/shard_map/ppermute | solution.py:207
  1044.5 198.5 %reduce-scatter.26.cloned.1.call-start = ((), (), s32[]{:S(2)}) async-start(), calls=%async_computation.23 | async-start | bytes 5242880 | tf_op jit(solution)/shard_map/reduce_scatter | solution.py:190
  1061.5 261.0 %reduce-scatter.24.cloned.1.call-start = ((), (), s32[]{:S(2)}) async-start(), calls=%async_computation.22 | async-start | bytes 5242880 | tf_op jit(solution)/shard_map/reduce_scatter | solution.py:191
  1075.6 277.0 %reduce-scatter.22.cloned.1.call-start = ((), (), s32[]{:S(2)}) async-start(), calls=%async_computation.21 | async-start | bytes 1310720 | tf_op jit(solution)/shard_map/reduce_scatter | solution.py:222
  1083.6 342.4 %reduce-scatter.20.cloned.1.call-start = ((), (), s32[]{:S(2)}) async-start(), calls=%async_computation.20 | async-start | bytes 9437184 | tf_op jit(solution)/shard_map/reduce_scatter | solution.py:169
  1167.6 186.8 %all-to-all-start.1 = ((bf16[8,64,768]{2,1,0:T(8,128)(2,1)}), bf16[8,64,768]{2,1,0:T(8,128)(2,1)S(1)}, u32[]{:S(2)}, u32[]{:S(2)}) async-start(bf16[8,64,768]{2,1,0:T(8,128)(2,1)} %bitcast.208), calls=%async_computation.5 | async-start | bytes 1572864 | tf_op jit(solution)/shard_map/all_to_all | solution.py:218
  1171.2 393.9 %reduce-scatter.28.cloned.1.call-start = ((), (), s32[]{:S(2)}) async-start(), calls=%async_computation.25 | async-start | bytes 1081344
  1172.6 154.3 %copy-start.27 = (f32[1024]{0:T(1024)S(1)}, f32[1024]{0:T(1024)}, u32[]{:S(2)}) copy-start(f32[1024]{0:T(1024)} %get-tuple-element.30) | copy-start | bytes 12292
  (37 other events, 951.6 us)
Sparse Core Ops, SparseCore 0:
  29.7 63.7 all-gather.26
  101.5 51.3 all-gather.12
  170.9 39.7 all-gather.14
  295.0 72.2 reduce-scatter.13
  368.8 80.5 all-gather.18
  451.2 52.6 all-gather.16
  505.5 80.7 all-gather.20
  588.9 52.9 all-gather.22
  675.8 71.2 reduce-scatter.17
  750.4 71.2 reduce-scatter.15
  827.0 54.3 all-gather.24
  1044.6 120.1 all-reduce.6
  1167.2 75.7 reduce-scatter.25
  1245.2 77.2 reduce-scatter.23
  1324.7 27.8 reduce-scatter.21
  1355.9 70.0 reduce-scatter.19
  1429.9 135.2 reduce-scatter.27

commit v2 on v1

--- a/solution.py
+++ b/solution.py
@@ -1,8 +1,11 @@
+import functools
 from functools import partial
 
 import jax
 import jax.numpy as jnp
 from jax import lax
+from jax.experimental import pallas as pl
+from jax.experimental.pallas import tpu as pltpu
 from jax.sharding import Mesh
 from jax.sharding import PartitionSpec as P
 
@@ -14,6 +17,200 @@
 
 PLANE = ("b", "x")
 ALL = ("b", "z", "x")
+MESH = pl.DeviceIdType.MESH
+TILE = 512
+
+def plane_place():
+    b, z, x = lax.axis_index("b"), lax.axis_index("z"), lax.axis_index("x")
+    sib_b = b + 1 - 2 * lax.rem(b, 2)
+    far_b = lax.rem(b + 2, 4)
+    far_sib_b = lax.rem(sib_b + 2, 4)
+    ids = {"s": (sib_b, z, x), "x": (b, z, 1 - x), "y": (far_b, z, x)}
+    ranks = {
+        "o": b * 2 + x,
+        "s": sib_b * 2 + x,
+        "x": b * 2 + 1 - x,
+        "xs": sib_b * 2 + 1 - x,
+        "y": far_b * 2 + x,
+        "ys": far_sib_b * 2 + x,
+        "d": far_b * 2 + 1 - x,
+        "ds": far_sib_b * 2 + 1 - x,
+    }
+    return ids, ranks
+
+def greet(ids):
+    barrier = pltpu.get_barrier_semaphore()
+    for device in ids.values():
+        pl.semaphore_signal(barrier, inc=1, device_id=device, device_id_type=MESH)
+    pl.semaphore_wait(barrier, len(ids))
+
+def tiles(lo, hi, body):
+    def step(i, _):
+        body(pl.ds(pl.multiple_of(i * TILE, TILE), TILE))
+        return 0
+    lax.fori_loop(lo // TILE, hi // TILE, step, 0)
+
+def gather_kernel(body_of, n_in, n_out, x_ref, *refs):
+    ins = refs[:n_in]; all_ref = refs[n_in]; outs = refs[n_in + 1 : n_in + 1 + n_out]
+    held, send, recv, keep = refs[n_in + 1 + n_out :]
+    ids, at = plane_place()
+    half = x_ref.shape[0] // 2
+    parts = (pl.ds(0, half), pl.ds(half, half))
+    greet(ids)
+    count = [0]
+    started = []
+    def ship(src, dst, to):
+        n = count[0]; count[0] += 1
+        c = pltpu.make_async_remote_copy(src_ref=src, dst_ref=dst, send_sem=send.at[n], recv_sem=recv.at[n], device_id=ids[to], device_id_type=MESH)
+        c.start(); started.append(c)
+        return c
+    own = at["o"]
+    x0 = ship(x_ref.at[parts[0]], held.at[own, parts[0]], "x")
+    y1 = ship(x_ref.at[parts[1]], held.at[own, parts[1]], "y")
+    x1 = ship(x_ref.at[parts[1]], held.at[own, parts[1]], "x")
+    y0 = ship(x_ref.at[parts[0]], held.at[own, parts[0]], "y")
+    s0 = ship(x_ref, held.at[own], "s")
+    kept = []
+    def done(rank, src):
+        c = pltpu.make_async_copy(src, all_ref.at[rank], keep.at[len(kept)])
+        c.start(); kept.append(c)
+        if body_of is not None:
+            body_of(rank, src, ins, outs)
+    done(own, x_ref)
+    s0.wait_recv()
+    done(at["s"], held.at[at["s"]])
+    x0.wait_recv()
+    ry = ship(held.at[at["x"], parts[0]], held.at[at["x"], parts[0]], "y")
+    y1.wait_recv()
+    rx = ship(held.at[at["y"], parts[1]], held.at[at["y"], parts[1]], "x")
+    x1.wait_recv()
+    sx = ship(held.at[at["x"]], held.at[at["x"]], "s")
+    y0.wait_recv()
+    sy = ship(held.at[at["y"]], held.at[at["y"]], "s")
+    done(at["x"], held.at[at["x"]])
+    done(at["y"], held.at[at["y"]])
+    sx.wait_recv()
+    done(at["xs"], held.at[at["xs"]])
+    sy.wait_recv()
+    done(at["ys"], held.at[at["ys"]])
+    ry.wait_recv(); rx.wait_recv()
+    sd = ship(held.at[at["d"]], held.at[at["d"]], "s")
+    done(at["d"], held.at[at["d"]])
+    sd.wait_recv()
+    done(at["ds"], held.at[at["ds"]])
+    for c in started: c.wait_send()
+    for c in kept: c.wait()
+
+def vmem(n): return [pl.BlockSpec(memory_space=pltpu.VMEM)] * n
+
+def plane_gather(x, ins, out_types, body_of, cid, name, ranks=8):
+    tok, D = x.shape
+    res = pl.pallas_call(
+        functools.partial(gather_kernel, body_of, len(ins), len(out_types)),
+        out_shape=[jax.ShapeDtypeStruct((ranks, tok, D), x.dtype), *out_types],
+        in_specs=vmem(1 + len(ins)),
+        out_specs=[pl.BlockSpec(memory_space=pl.ANY)] + vmem(len(out_types)),
+        scratch_shapes=[pltpu.VMEM((ranks, tok, D), x.dtype), pltpu.SemaphoreType.DMA((10,)), pltpu.SemaphoreType.DMA((10,)), pltpu.SemaphoreType.DMA((8,))],
+        compiler_params=pltpu.CompilerParams(collective_id=cid, has_side_effects=True, vmem_limit_bytes=60 << 20),
+        name=name,
+    )(x, *ins)
+    return res[0].reshape(ranks * tok, D), *res[1:]
+
+def gather_dot(x, w, bias, out_dtype, turned, cid, name):
+    ranks, tok, D = 8, *x.shape
+    N = w.shape[0] if turned else w.shape[1]
+    tile = min(N, 512) if N % 512 == 0 else 256
+    def body(rank, src, ins, outs):
+        w_ref, b_ref = ins
+        def step(i, _):
+            cols = pl.ds(pl.multiple_of(i * tile, tile), tile)
+            if turned:
+                y = lax.dot_general(src[...], w_ref[cols, :], (((1,), (1,)), ((), ())), preferred_element_type=single)
+            else:
+                y = jnp.dot(src[...], w_ref[:, cols], preferred_element_type=single)
+            outs[0][rank, :, cols] = (y + b_ref[:, cols]).astype(out_dtype)
+            return 0
+        lax.fori_loop(0, N // tile, step, 0)
+    all_, y = plane_gather(x, (w, bias), [jax.ShapeDtypeStruct((ranks, tok, N), out_dtype)], body, cid, name)
+    return all_, y.reshape(ranks * tok, N)
+
+def reduce_kernel(turned, a_ref, w_ref, out_ref, sib_out, sib_in, stage, landed, send, recv):
+    ids, at = plane_place()
+    ranks, tok, _ = a_ref.shape
+    D = out_ref.shape[1]
+    mid = D // 2
+    greet(ids)
+    count = [0]; started = []
+    def ship(src, dst, to):
+        n = count[0]; count[0] += 1
+        c = pltpu.make_async_remote_copy(src_ref=src, dst_ref=dst, send_sem=send.at[n], recv_sem=recv.at[n], device_id=ids[to], device_id_type=MESH)
+        c.start(); started.append(c)
+        return c
+    def term(rank, cols):
+        if turned:
+            return lax.dot_general(a_ref[rank], w_ref[cols, :], (((1,), (1,)), ((), ())), preferred_element_type=single)
+        return jnp.dot(a_ref[rank], w_ref[:, cols], preferred_element_type=single)
+    order = ("d", "x", "y", "o")
+    twin = {"d": "ds", "x": "xs", "y": "ys", "o": "s"}
+    sib = []
+    for j, d in enumerate(order):
+        def fill(cols, j=j, d=d):
+            sib_out[j, :, cols] = term(at[twin[d]], cols).astype(bfloat)
+        tiles(0, D, fill)
+        sib.append(ship(sib_out.at[j], sib_in.at[j], "s"))
+    def pair(j, cols):
+        return term(at[order[j]], cols) + sib_in[j, :, cols].astype(single)
+    def local(h, cols):
+        return pl.ds(pl.multiple_of(cols.start - h * mid, TILE), TILE)
+    def put(j, h, extra=None):
+        def fill(cols):
+            value = pair(j, cols)
+            if extra is not None:
+                value = value + landed[extra, :, local(h, cols)].astype(single)
+            stage[j, h, :, local(h, cols)] = value.astype(bfloat)
+        tiles(h * mid, (h + 1) * mid, fill)
+    sib[0].wait_recv()
+    put(0, 0)
+    d_a = ship(stage.at[0, 0], landed.at[0], "x")
+    put(0, 1)
+    d_b = ship(stage.at[0, 1], landed.at[1], "y")
+    sib[1].wait_recv()
+    put(1, 0)
+    x_a = ship(stage.at[1, 0], landed.at[2], "x")
+    sib[2].wait_recv()
+    put(2, 1)
+    y_b = ship(stage.at[2, 1], landed.at[3], "y")
+    sib[3].wait_recv()
+    def first(cols):
+        out_ref[:, cols] = pair(3, cols)
+    tiles(0, D, first)
+    d_b.wait_recv()
+    put(1, 1, extra=1)
+    x_b = ship(stage.at[1, 1], landed.at[5], "x")
+    d_a.wait_recv()
+    put(2, 0, extra=0)
+    y_a = ship(stage.at[2, 0], landed.at[4], "y")
+    x_a.wait_recv(); y_b.wait_recv(); x_b.wait_recv(); y_a.wait_recv()
+    for h, (n, m) in enumerate(((2, 4), (3, 5))):
+        def add(cols, h=h, n=n, m=m):
+            c = local(h, cols)
+            out_ref[:, cols] = out_ref[:, cols] + landed[n, :, c].astype(single) + landed[m, :, c].astype(single)
+        tiles(h * mid, (h + 1) * mid, add)
+    for c in started: c.wait_send()
+
+def dot_reduce(a, w, turned, cid, name):
+    ranks = 8
+    D = w.shape[0] if turned else w.shape[1]
+    tok = a.shape[0] // ranks
+    return pl.pallas_call(
+        functools.partial(reduce_kernel, turned),
+        out_shape=jax.ShapeDtypeStruct((tok, D), single),
+        in_specs=vmem(2), out_specs=vmem(1)[0],
+        scratch_shapes=[pltpu.VMEM((4, tok, D), bfloat), pltpu.VMEM((4, tok, D), bfloat), pltpu.VMEM((3, 2, tok, D // 2), bfloat), pltpu.VMEM((6, tok, D // 2), bfloat),
+            pltpu.SemaphoreType.DMA((10,)), pltpu.SemaphoreType.DMA((10,))],
+        compiler_params=pltpu.CompilerParams(collective_id=cid, has_side_effects=True, vmem_limit_bytes=60 << 20),
+        name=name,
+    )(a.reshape(ranks, tok, -1), w)
 
 
 def dot(left, right):
@@ -111,7 +308,9 @@
     active_total = jnp.sum(group_active)
     active = lax.dynamic_slice_in_dim(group_active, at_z * span + at_x * tok, tok, 0)[:, None]
 
-    ends = jnp.cumsum(lax.all_gather(lengths[0], "b", axis=0), axis=1)
+    count = lengths.shape[1]
+    upto = jnp.arange(count)[:, None] <= jnp.arange(count)[None, :]
+    ends = jnp.sum(jnp.where(upto, lax.all_gather(lengths[0], "b", axis=0)[:, :, None], 0), axis=1)
     places = at_z * span + jnp.arange(span, dtype=jnp.int32)
     starts = jnp.max(jnp.where(ends[:, None, :] <= places[None, :, None], ends[:, None, :], 0), axis=2)
     key_places = (at_z - 1) * span + jnp.arange(2 * span, dtype=jnp.int32)
@@ -152,7 +351,26 @@
     bias_up = lax.all_gather(fc1_bias, "z", axis=0, tiled=True).astype(single)
 
     normed_low = layer_norm(local, gain_one, bias_one).astype(bfloat)
-    normed_all = lax.all_gather(normed_low, PLANE, axis=0, tiled=True)
+    fast = (B, X) == (4, 2)
+
+    def gather_plane(rows, cid, name):
+        if fast:
+            return plane_gather(rows, (), [], None, cid, name)[0]
+        return lax.all_gather(rows, PLANE, axis=0, tiled=True)
+
+    def gather_plane_dot(rows, weight, shift, out_type, turned, cid, name):
+        if fast:
+            return gather_dot(rows, weight, shift, out_type, turned, cid, name)
+        rows = lax.all_gather(rows, PLANE, axis=0, tiled=True)
+        return rows, ((dot_nt if turned else dot)(rows, weight) + shift).astype(out_type)
+
+    def reduce_plane(left, weight, turned, cid, name):
+        if fast:
+            return dot_reduce(left, weight, turned, cid, name)
+        terms = (dot_nt if turned else dot)(left, weight).astype(bfloat)
+        return lax.psum_scatter(terms, PLANE, scatter_dimension=0, tiled=True).astype(single)
+
+    normed_all = gather_plane(normed_low, 0, "gather_normed")
     qkv = (dot(normed_all, weight_qkv) + bias_qkv).astype(bfloat)
     query = qkv[:, :cols].reshape(B, span, heads, HEAD_DIM)
     key_value = qkv[:, cols:]
@@ -165,38 +383,34 @@
     context, logsum = attention_forward(query, key_two, value_two, allowed)
     context = context.reshape(B * span, cols)
 
-    def reduce_plane(partial_sums):
-        return lax.psum_scatter(partial_sums.astype(bfloat), PLANE, scatter_dimension=0, tiled=True).astype(single)
-
-    attended = reduce_plane(dot(context, weight_o)) + bias_o
+    attended = reduce_plane(context, weight_o, False, 1, "attended") + bias_o
     middle = local + active * attended
     normed_two = layer_norm(middle, gain_two, bias_two).astype(bfloat)
     cotangent = out_grad[0].astype(single) * (group_tok / active_total)
     branch_grad = (active * cotangent).astype(bfloat)
     down_b_grad = column_sums(branch_grad)
     branch_all = lax.all_gather(branch_grad, PLANE, axis=0, tiled=True)
-    two_all = lax.all_gather(normed_two, PLANE, axis=0, tiled=True)
-    hidden_pre = dot(two_all, weight_up) + bias_up
+    two_all, hidden_pre = gather_plane_dot(normed_two, weight_up, bias_up[None], single, False, 2, "up")
     gelu_value, gelu_pull = jax.vjp(partial(jax.nn.gelu, approximate=True), hidden_pre)
     hidden = gelu_value.astype(bfloat)
     hidden_grad = dot_nt(branch_all, weight_down)
     pre_grad = gelu_pull(hidden_grad)[0].astype(bfloat)
-    normed_two_grad = reduce_plane(dot_nt(pre_grad, weight_up))
-    branch = reduce_plane(dot(hidden, weight_down)) + bias_down
+    normed_two_grad = reduce_plane(pre_grad, weight_up, True, 3, "up_grad")
+    branch = reduce_plane(hidden, weight_down, False, 4, "down") + bias_down
     outputs = middle + active * branch
     down_w_grad = dot_tn(hidden, branch_all)
     up_w_grad = dot_tn(two_all, pre_grad)
     up_b_grad = column_sums(pre_grad)
     down_w_shard = lax.psum_scatter(down_w_grad.astype(bfloat), "z", scatter_dimension=0, tiled=True).astype(single)
     up_w_shard = lax.psum_scatter(up_w_grad.astype(bfloat), "z", scatter_dimension=1, tiled=True).astype(single)
-    up_b_shard = lax.psum_scatter(up_b_grad, "z", scatter_dimension=0, tiled=True)
 
     middle_part, gain_two_grad, bias_two_grad = norm_backward(middle, normed_two_grad, gain_two)
     middle_grad = cotangent + middle_part
     attended_grad = (active * middle_grad).astype(bfloat)
     out_b_grad = column_sums(attended_grad)
-    attended_all = lax.all_gather(attended_grad, PLANE, axis=0, tiled=True)
-    context_grad = dot_nt(attended_all, weight_o).astype(bfloat)
+    attended_all, context_grad = gather_plane_dot(
+        attended_grad, weight_o, jnp.zeros((1, cols), single), bfloat, True, 5, "attended_grad"
+    )
     out_w_grad = dot_tn(context, attended_all)
     query_grad, key_grad, value_grad = attention_backward(
         query, key_two, value_two, context_grad.reshape(B, span, heads, HEAD_DIM), logsum, allowed
@@ -207,21 +421,27 @@
     after = lax.ppermute(pair[:, :span].astype(bfloat), "z", down).astype(single)
     pair_grad = (pair[:, span:] + after).astype(bfloat).reshape(B * span, 2 * cols)
     qkv_grad = jnp.concatenate([query_grad.astype(bfloat).reshape(B * span, cols), pair_grad], axis=1)
-    normed_grad = reduce_plane(dot_nt(qkv_grad, weight_qkv))
+    normed_grad = reduce_plane(qkv_grad, weight_qkv, True, 6, "qkv_grad")
     qkv_w_grad = dot_tn(normed_all, qkv_grad)
     qkv_b_grad = column_sums(qkv_grad)
     input_part, gain_one_grad, bias_one_grad = norm_backward(local, normed_grad, gain_one)
     input_grad = middle_grad + input_part
 
+    def sum_to_owners(vectors, axes, parts):
+        split = jnp.concatenate([v.reshape(parts, -1) for v in vectors], axis=1)
+        summed = jnp.sum(lax.all_to_all(split, axes, split_axis=0, concat_axis=0, tiled=True), axis=0)
+        widths = [v.shape[0] // parts for v in vectors]
+        return [summed[sum(widths[:i]) : sum(widths[: i + 1])] for i in range(len(widths))]
+
     qkv_w_grad = qkv_w_grad.astype(bfloat).reshape(B, Z, X, rows_dev, 3 * cols)
-    qkv_w_grad = lax.psum_scatter(qkv_w_grad.transpose(1, 0, 2, 3, 4), "z", scatter_dimension=0, tiled=True)
+    qkv_w_grad = qkv_w_grad.transpose(1, 0, 2, 3, 4).reshape(D, 3 * cols)
+    qkv_w_grad = lax.psum_scatter(qkv_w_grad, "z", scatter_dimension=0, tiled=True)
     qkv_w_grad = lax.all_to_all(qkv_w_grad.reshape(R, rows_dev, 3 * cols), PLANE, split_axis=0, concat_axis=0, tiled=True)
     qkv_w_grad = qkv_w_grad.astype(single)
     q_w_shard, k_w_shard, v_w_shard = [from_ranks(qkv_w_grad[..., i * cols : (i + 1) * cols]) for i in range(3)]
     if whole_heads:
         out_w_shard = lax.psum_scatter(out_w_grad.astype(bfloat), "z", scatter_dimension=0, tiled=True).astype(single)
-        q_b_shard = lax.psum_scatter(qkv_b_grad[:cols], "z", scatter_dimension=0, tiled=True)
-        v_b_shard = lax.psum_scatter(qkv_b_grad[2 * cols :], "z", scatter_dimension=0, tiled=True)
+        q_b_shard, v_b_shard, up_b_shard = sum_to_owners([qkv_b_grad[:cols], qkv_b_grad[2 * cols :], up_b_grad], "z", Z)
     else:
 
         def placed(rows):
@@ -232,8 +452,10 @@
         out_w_shard = placed(out_w_grad.astype(bfloat))
         q_b_shard = placed(qkv_b_grad[:cols])
         v_b_shard = placed(qkv_b_grad[2 * cols :])
-    sums = jnp.stack([gain_one_grad, bias_one_grad, out_b_grad, gain_two_grad, bias_two_grad, down_b_grad])
-    sums = lax.psum_scatter(sums, ALL, scatter_dimension=1, tiled=True)
+        [up_b_shard] = sum_to_owners([up_b_grad], "z", Z)
+    sums = sum_to_owners(
+        [gain_one_grad, bias_one_grad, out_b_grad, gain_two_grad, bias_two_grad, down_b_grad], ALL, R * Z
+    )
     return (
         outputs.astype(bfloat)[None],
         input_grad.astype(bfloat)[None],

time: 1580 us -> 1050 us (0.66)
  waiting for transfers between devices: 1040 us -> 228 us
  Pallas kernels: 0 us -> 348 us
  matrix products: 232 us -> 166 us
    pallas_call x0 -> x7, Pallas kernels: none -> 348 us  [the longest x4 198 us: dot_reduce(): pl.pallas_call(functools.partial(reduce_kernel, turned), out_shape=jax.Sh...]
    reduce_scatter x4 -> x1, waiting for transfers between devices: 253 us -> 0.01 us  [on_device(): lax.psum_scatter(qkv_w_grad, 'z', scatter_dimension=0, tiled=True)]
    unnamed x19 -> x9, waiting for transfers between devices: 203 us -> 1.49 us
    all_gather x3 -> x0, waiting for transfers between devices: 156 us -> none  [the longest x1 54.5 us: on_device(): two_all = lax.all_gather(normed_two, PLANE, axis=0, tiled=True)]
    all_gather x1, waiting for transfers between devices: 67.7 us -> 0.01 us  [on_device(): weight_down = lax.all_gather(fc2_weight, 'z', axis=0, tiled=True)]
    all_gather x1, waiting for transfers between devices: 63 us -> 0.01 us  [on_device(): weight_up = lax.all_gather(fc1_weight, 'z', axis=1, tiled=True)]
    all_gather x1, waiting for transfers between devices: 55.6 us -> 0.02 us  [on_device(): branch_all = lax.all_gather(branch_grad, PLANE, axis=0, tiled=True)]
    reduce_scatter x1, waiting for transfers between devices: 76.6 us -> 38.6 us  [on_device(): lax.psum_scatter(up_w_grad.astype(bfloat), 'z', scatter_dimension=1, tile...]
  transfers between devices with their start and end apart: 20 -> 14, of which waited for: 17 -> 6; matrix products, arithmetic and copies ran while one was open for 13% -> 17% of each run, Pallas kernels for 0% -> 24%
where the time goes in v2:
time: 1050 us; the launch traced here: 1040 us
  Pallas kernels  348 us (33%)
  waiting for transfers between devices  228 us (22%)
  matrix products  166 us (16%)
  blocking collectives  103 us (10%)
  other arithmetic  97.7 us (9%)
  local copies, waits for them, and re-layouts  68.4 us (7%)
  between operations  16.6 us (2%)
  starting transfers between devices  16 us (2%)
    pallas_call x4, Pallas kernels, dot_reduce(): pl.pallas_call(functools.partial(reduce_kernel, turned), out_shape=jax.Sh...  198 us
    pallas_call x3, Pallas kernels, plane_gather(): pl.pallas_call(functools.partial(gather_kernel, body_of, len(ins), len(ou...  149 us
    reduce_scatter x1, waiting for transfers between devices, on_device(): lax.psum_scatter(down_w_grad.astype(bfloat), 'z', scatter_dimension=0, ti...  76.9 us
    all_gather x1, blocking collectives, on_device(): small = lax.all_gather(small, ALL, axis=1, tiled=True).astype(single)  68.8 us
    ppermute x1, waiting for transfers between devices, on_device(): before = lax.ppermute(key_value, 'z', up)  64.7 us
    dot_general x4, matrix products, dot_tn(): lax.dot_general(left, right, (((0,), (0,)), ((), ())), preferred_element_...  45.3 us
    reduce_scatter x1, waiting for transfers between devices, on_device(): lax.psum_scatter(up_w_grad.astype(bfloat), 'z', scatter_dimension=1, tile...  38.6 us
    ppermute x1, waiting for transfers between devices, on_device(): lax.ppermute(pair[:, :span].astype(bfloat), 'z', down).astype(single)  35.2 us
  transfers between devices with their start and end apart: 14, of which 6 were waited for; matrix products, arithmetic and copies ran while one was open for 17% of the time, Pallas kernels for 24%

profile of v2, /device:TPU:0, one launch (start us, length us, event | category | flops | bytes accessed | tf_op | source)
XLA Modules:
  0.0 1044.3 jit_solution(18171363442162089999)
XLA Ops:
  12.4 17.3 %all_to_all.28 = bf16[8,64,768]{2,1,0:T(8,128)(2,1)} all-to-all(bf16[8,64,768]{2,1,0:T(8,128)(2,1)S(1)} %pad_maximum_fusion.5), channel_id=1, replica_groups=mesh['b'=4,'z'=4,'x'=2] {'b','x'}, dimensions={0} | all-to-all | bytes 1572864 | tf_op jit(solution)/shard_map/all_to_all | solution.py:341
  31.3 68.8 %all-gather.1 = bf16[32,64,8]{1,2,0:T(8,128)(2,1)S(1)} all-gather(bf16[1,64,8]{1,2,0:T(8,128)(2,1)S(1)} %bitcast.217), channel_id=1, replica_groups=mesh['b'=4,'z'=4,'x'=2] {'b','z','x'}, dimensions={0}, use_global_device_ids=true | all-gather | bytes 33792 | tf_op jit(solution)/shard_map/all_gather | solution.py:320
  102.8 40.4 %gather_normed.1 = bf16[8,256,2048]{2,1,0:T(8,128)(2,1)} custom-call(bf16[256,2048]{1,0:T(8,128)(2,1)} %fusion.37.x_ref), custom_call_target="tpu_custom_call" | custom-call | tf_op jit(solution)/shard_map/gather_normed/pallas_call | solution.py:108
  179.4 64.7 %collective-permute-done = bf16[2048,512]{1,0:T(8,128)(2,1)} collective-permute-done((bf16[2048,512]{1,0:T(8,128)(2,1)}, bf16[2048,512]{1,0:T(8,128)(2,1)}, u32[]{:S(2)}, u32[]{:S(2)}) %collective-permute-start) | collective-permute-done | bytes 2097184 | tf_op jit(solution)/shard_map/ppermute | solution.py:379
  250.9 16.8 %fusion.63 = (f32[4,4,512]{2,1,0:T(4,128)S(1)}, f32[4,4,512,1024]{3,2,1,0:T(8,128)}) fusion(bf16[4,512,4,64]{1,3,2,0:T(8,128)(2,1)} %copy.140, bf16[4,1024,4,64]{1,3,2,0:T(8,128)(2,1)S(1)} %bitcast.169, pred[4,512,1024]{2,1,0:T(8,128)(4,1)} %compare_and_fusion), kind=kOutput, calls=%fused_computation.131 | convolution fusion | flops 1098899456 | bytes 38830080 | tf_op jit(solution)/shard_map/gqhd,gkhd->ghqk/dot_general | solution.py:240
  270.7 15.0 %fusion = f32[4,4,512]{2,1,0:T(4,128)S(1)} fusion(f32[4,4,512,1024]{3,2,1,0:T(8,128)} %get-tuple-element.74, f32[4,4,512]{2,1,0:T(4,128)S(1)} %get-tuple-element.73), kind=kLoop, calls=%fused_computation.6 | loop fusion | flops 16769024 | bytes 33619968 | tf_op jit(solution)/shard_map/reduce_sum | solution.py:244
  285.8 13.8 %fusion.49 = bf16[4,512,4,64]{1,3,2,0:T(8,128)(2,1)} fusion(bf16[4,1024,4,64]{1,3,2,0:T(8,128)(2,1)S(1)} %bitcast.179, f32[4,4,512,1024]{3,2,1,0:T(8,128)} %get-tuple-element.74, f32[4,4,512]{2,1,0:T(4,128)S(1)} %fusion, f32[4,4,512]{2,1,0:T(4,128)S(1)} %get-tuple-element.73), kind=kOutput, calls=%fused_computation.93 | convolution fusion | flops 1099431936 | bytes 36765696 | tf_op jit(solution)/shard_map/ghqk,gkhd->gqhd/dot_general | solution.py:246
  304.6 46.1 %attended.1 = f32[256,2048]{1,0:T(8,128)} custom-call(bf16[8,256,256]{2,1,0:T(8,128)(2,1)} %reshape.338.a_ref, bf16[256,2048]{1,0:T(8,128)(2,1)} %all-gather.10.cloned.1.call-done.w_ref.refs_0_), custom_call_target="tpu_custom_call" | custom-call | tf_op jit(solution)/shard_map/attended/pallas_call | solution.py:205
  355.1 11.8 %all-gather.3 = bf16[4,1,256]{2,1,0:T(2,128)(2,1)S(1)} all-gather(bf16[1,1,256]{2,1,0:T(2,128)(2,1)S(1)} %reshape.333), channel_id=1, replica_groups=mesh['b'=4,'z'=4,'x'=2] {'z'}, dimensions={0}, use_global_device_ids=true | all-gather | bytes 2560 | tf_op jit(solution)/shard_map/all_gather | solution.py:351
  369.3 67.7 %up.1 = (bf16[8,256,2048]{2,1,0:T(8,128)(2,1)}, f32[8,256,1024]{2,1,0:T(8,128)}) custom-call(bf16[256,2048]{1,0:T(8,128)(2,1)} %add_convert_fusion.2.x_ref, bf16[2048,1024]{1,0:T(8,128)(2,1)} %all-gather.12.cloned.1.call-done.refs_0_.w_ref, f32[1,1024]{1,0:T(1,128)} %convert.5.refs_1_), custom_call_target="tpu_custom_call" | custom-call | tf_op jit(solution)/shard_map/up/pallas_call | solution.py:108
  443.1 51.2 %down.1 = f32[256,2048]{1,0:T(8,128)} custom-call(bf16[8,256,1024]{2,1,0:T(8,128)(2,1)} %fusion.20.a_ref, bf16[1024,2048]{1,0:T(8,128)(2,1)} %all-gather.14.cloned.1.call-done.w_ref), custom_call_target="tpu_custom_call" | custom-call | tf_op jit(solution)/shard_map/down/pallas_call | solution.py:205
  494.3 20.9 %convert_reduce_fusion = (f32[1024]{0:T(1024)S(1)}, bf16[2048,1024]{1,0:T(8,128)(2,1)}, bf16[2048,1024]{1,0:T(8,128)(2,1)}) fusion(f32[8,256,1024]{2,1,0:T(8,128)} %get-tuple-element.21, bf16[2048,2048]{1,0:T(8,128)(2,1)} %all-gather.16.cloned.1.call-done, bf16[1024,2048]{1,0:T(8,128)(2,1)} %all-gather.14.cloned.1.call-done.w_ref), kind=kOutput, calls=%fused_computation.36 | convolution fusion | flops 8640265216 | bytes 29364224 | tf_op jit(solution)/shard_map/dot_general | solution.py:225
  515.2 51.8 %up_grad.1 = f32[256,2048]{1,0:T(8,128)} custom-call(bf16[8,256,1024]{2,1,0:T(8,128)(2,1)} %bitcast.183, bf16[2048,1024]{1,0:T(8,128)(2,1)} %all-gather.12.cloned.1.call-done.refs_0_.w_ref), custom_call_target="tpu_custom_call" | custom-call | tf_op jit(solution)/shard_map/up_grad/pallas_call | solution.py:205
  573.8 41.3 %attended_grad.1 = (bf16[8,256,2048]{2,1,0:T(8,128)(2,1)}, bf16[8,256,256]{2,1,0:T(8,128)(2,1)}) custom-call(bf16[256,2048]{1,0:T(8,128)(2,1)} %get-tuple-element.40.x_ref, bf16[256,2048]{1,0:T(8,128)(2,1)} %all-gather.10.cloned.1.call-done.w_ref.refs_0_, f32[1,256]{1,0:T(1,128)} %broadcast_in_dim.98.refs_1_), custom_call_target="tpu_custom_call" | custom-call | tf_op jit(solution)/shard_map/attended_grad/pallas_call | solution.py:108
  619.7 15.5 %fusion.2 = f32[4,4,64,1024]{3,2,1,0:T(8,128)} fusion(bf16[4,512,4,64]{1,3,2,0:T(8,128)(2,1)S(1)} %copy.144, f32[4,4,512,1024]{3,2,1,0:T(8,128)} %get-tuple-element.74, f32[4,4,512]{2,1,0:T(4,128)S(1)} %bitcast.195), kind=kOutput, calls=%fused_computation.8 | convolution fusion | flops 1090519040 | bytes 38830080 | tf_op jit(solution)/shard_map/ghqk,gqhd->gkhd/dot_general | solution.py:258
  635.2 22.1 %multiply_reduce_fusion = (f32[4,4,512]{2,1,0:T(4,128)S(1)}, f32[4,4,512,1024]{3,2,1,0:T(8,128)}) fusion(f32[4,4,512,1024]{3,2,1,0:T(8,128)} %get-tuple-element.74, f32[4,4,512]{2,1,0:T(4,128)S(1)} %bitcast.196, bf16[4,512,4,64]{1,3,2,0:T(8,128)(2,1)S(1)} %copy.144, bf16[4,1024,4,64]{1,3,2,0:T(8,128)(2,1)S(1)} %bitcast.180), kind=kOutput, calls=%fused_computation.1 | convolution fusion | flops 1098899456 | bytes 70320128 | tf_op jit(solution)/shard_map/gqhd,gkhd->ghqk/dot_general | solution.py:253
  662.7 28.1 %multiply_convert_fusion = bf16[4,4,512,1024]{3,2,1,0:T(8,128)(2,1)} fusion(f32[4,4,512,1024]{3,2,1,0:T(8,128)} %get-tuple-element.76, f32[4,4,512,1024]{3,2,1,0:T(8,128)} %get-tuple-element.74, f32[4,4,512]{2,1,0:T(4,128)S(1)} %get-tuple-element.75, f32[4,4,512]{2,1,0:T(4,128)S(1)} %bitcast.197), kind=kLoop, calls=%fused_computation | loop fusion | flops 33554432 | bytes 83951616 | tf_op jit(solution)/shard_map/convert_element_type | solution.py:255
  712.2 11.0 %fusion.48 = bf16[4,512,4,64]{1,3,2,0:T(8,128)(2,1)S(1)} fusion(bf16[4,1024,4,64]{1,3,2,0:T(8,128)(2,1)S(1)} %bitcast.170, bf16[4,4,512,1024]{3,2,1,0:T(8,128)(2,1)} %multiply_convert_fusion), kind=kOutput, calls=%fused_computation.92 | convolution fusion | flops 1074790400 | bytes 19922944 | tf_op jit(solution)/shard_map/ghqk,gkhd->gqhd/dot_general | solution.py:256
  726.1 35.2 %collective-permute-done.1 = bf16[4,512,512]{2,1,0:T(8,128)(2,1)} collective-permute-done((bf16[4,512,512]{2,1,0:T(8,128)(2,1)}, bf16[4,512,512]{2,1,0:T(8,128)(2,1)}, u32[]{:S(2)}, u32[]{:S(2)}) %collective-permute-start.1) | collective-permute-done | bytes 2097184 | tf_op jit(solution)/shard_map/ppermute | solution.py:421
  786.1 14.0 %convolution_convert_fusion.1 = bf16[2048,1024]{1,0:T(8,128)(2,1)} fusion(bf16[2048,2048]{1,0:T(8,128)(2,1)} %bitcast.229, bf16[2048,1024]{1,0:T(8,128)(2,1)} %get-tuple-element.36), kind=kOutput, calls=%fused_computation.48 | convolution fusion | flops 8592031744 | bytes 16777216 | tf_op jit(solution)/shard_map/dot_general | solution.py:221
  800.2 14.2 %convolution_convert_fusion = bf16[1024,2048]{1,0:T(8,128)(2,1)} fusion(bf16[2048,1024]{1,0:T(8,128)(2,1)} %get-tuple-element.46, bf16[2048,2048]{1,0:T(8,128)(2,1)} %all-gather.16.cloned.1.call-done), kind=kOutput, calls=%fused_computation.47 | convolution fusion | flops 8592031744 | bytes 16777216 | tf_op jit(solution)/shard_map/dot_general | solution.py:221
  820.2 49.2 %qkv_grad.1 = f32[256,2048]{1,0:T(8,128)} custom-call(bf16[8,256,768]{2,1,0:T(8,128)(2,1)} %pad_maximum_fusion.1.a_ref, bf16[2048,768]{1,0:T(8,128)(2,1)} %bitcast.178), custom_call_target="tpu_custom_call" | custom-call | tf_op jit(solution)/shard_map/qkv_grad/pallas_call | solution.py:205
  905.9 38.6 %reduce-scatter.9.cloned.1.call-done = bf16[2048,256]{1,0:T(8,128)(2,1)} async-done(((bf16[2048,1024]{1,0:T(8,128)(2,1)}), bf16[2048,256]{1,0:T(8,128)(2,1)}) %reduce-scatter.9.cloned.1.call-update) | async-done | bytes 1048592 | tf_op jit(solution)/shard_map/reduce_scatter | solution.py:405
  947.3 76.9 %reduce-scatter.11.cloned.1.call-done = bf16[256,2048]{1,0:T(8,128)(2,1)} async-done(((bf16[1024,2048]{1,0:T(8,128)(2,1)}), bf16[256,2048]{1,0:T(8,128)(2,1)}) %reduce-scatter.11.cloned.1.call-update) | async-done | bytes 1048592 | tf_op jit(solution)/shard_map/reduce_scatter | solution.py:404
  (223 shorter events, 195.3 us)
Async XLA Ops:
  7.2 136.0 %all-gather.18.cloned.1.call-start = ((), (), s32[]{:S(2)}) async-start(), calls=%async_computation.16 | async-start | bytes 3932160 | tf_op jit(solution)/shard_map/all_gather | solution.py:342
  11.9 19.4 %copy-start.26 = (bf16[64]{0:T(256)(128)(2,1)S(1)}, bf16[64]{0:T(256)(128)(2,1)}, u32[]{:S(2)}) copy-start(bf16[64]{0:T(256)(128)(2,1)} %param.25) | copy-start | bytes 388
  12.3 88.3 %copy-start = (bf16[1,256,2048]{2,1,0:T(8,128)(2,1)S(1)}, bf16[1,256,2048]{2,1,0:T(8,128)(2,1)}, u32[]{:S(2)}) copy-start(bf16[1,256,2048]{2,1,0:T(8,128)(2,1)} %param.20) | copy-start | bytes 3145732
  29.7 274.9 %all-gather.10.cloned.1.call-start = ((), (), s32[]{:S(2)}) async-start(), calls=%async_computation.8 | async-start | bytes 1310720 | tf_op jit(solution)/shard_map/all_gather | solution.py:346
  30.4 338.8 %all-gather.12.cloned.1.call-start = ((), (), s32[]{:S(2)}) async-start(), calls=%async_computation.9 | async-start | bytes 5242880 | tf_op jit(solution)/shard_map/all_gather | solution.py:349
  31.2 411.9 %all-gather.14.cloned.1.call-start = ((), (), s32[]{:S(2)}) async-start(), calls=%async_computation.10 | async-start | bytes 5242880 | tf_op jit(solution)/shard_map/all_gather | solution.py:350
  100.3 42.9 %copy-start.18 = (f32[1,2048]{1,0:T(1,128)}, f32[1,2048]{1,0:T(1,128)S(1)}, u32[]{:S(2)}) copy-start(f32[1,2048]{1,0:T(1,128)S(1)} %get-tuple-element.60) | copy-start | bytes 24580
  100.9 42.3 %copy-start.21 = (f32[256]{0:T(256)}, f32[256]{0:T(256)S(1)}, u32[]{:S(2)}) copy-start(f32[256]{0:T(256)S(1)} %broadcast_multiply_fusion.6) | copy-start | bytes 3076
  101.3 41.8 %copy-start.23 = (f32[256]{0:T(256)}, f32[256]{0:T(256)S(1)}, u32[]{:S(2)}) copy-start(f32[256]{0:T(256)S(1)} %add_rsqrt_fusion.1) | copy-start | bytes 3076
  158.0 86.1 %collective-permute-start = (bf16[2048,512]{1,0:T(8,128)(2,1)}, bf16[2048,512]{1,0:T(8,128)(2,1)}, u32[]{:S(2)}, u32[]{:S(2)}) collective-permute-start(bf16[2048,512]{1,0:T(8,128)(2,1)} %slice.133), channel_id=1, source_target_pairs={{0,2},{2,4},{4,6},{1,3},{3,5},{5,7},{8,10},{10,12},{12,14},{9,11},... | collective-permute-start | bytes 6291464 | tf_op jit(solution)/shard_map/ppermute | solution.py:379
  160.6 333.7 %all-gather.16.cloned.1.call-start = ((), (), s32[]{:S(2)}) async-start(), calls=%async_computation.11 | async-start | bytes 9437184 | tf_op jit(solution)/shard_map/all_gather | solution.py:392
  355.0 539.4 %reduce-scatter.5.cloned.1.call-start = ((), (), s32[]{:S(2)}) async-start(), calls=%async_computation.12 | async-start | bytes 3932160 | tf_op jit(solution)/shard_map/reduce_scatter | solution.py:438
  515.2 54.5 %copy-start.15 = (bf16[1,256,2048]{2,1,0:T(8,128)(2,1)S(1)}, bf16[1,256,2048]{2,1,0:T(8,128)(2,1)}, u32[]{:S(2)}) copy-start(bf16[1,256,2048]{2,1,0:T(8,128)(2,1)} %param.24) | copy-start | bytes 3145732
  662.7 28.1 %copy-start.9 = (bf16[4,512,4,64]{1,3,2,0:T(8,128)(2,1)S(1)}, bf16[4,512,4,64]{1,3,2,0:T(8,128)(2,1)}, u32[]{:S(2)}) copy-start(bf16[4,512,4,64]{1,3,2,0:T(8,128)(2,1)} %copy.140) | copy-start | bytes 3145732
  710.9 50.4 %collective-permute-start.1 = (bf16[4,512,512]{2,1,0:T(8,128)(2,1)}, bf16[4,512,512]{2,1,0:T(8,128)(2,1)}, u32[]{:S(2)}, u32[]{:S(2)}) collective-permute-start(bf16[4,512,512]{2,1,0:T(8,128)(2,1)} %fusion.27), channel_id=1, source_target_pairs={{2,0},{4,2},{6,4},{3,1},{5,3},{7,5},{10,8},{12,10},{14,12},{11,9},... | collective-permute-start | bytes 6291464 | tf_op jit(solution)/shard_map/ppermute | solution.py:421
  726.1 38.7 %copy-start.14 = (bf16[2048,256]{1,0:T(8,128)(2,1)}, bf16[2048,256]{1,0:T(8,128)(2,1)S(1)}, u32[]{:S(2)}) copy-start(bf16[2048,256]{1,0:T(8,128)(2,1)S(1)} %reshape.340) | copy-start | bytes 3145732
  776.7 125.6 %reduce-scatter.7.cloned.1.call-start = ((), (), s32[]{:S(2)}) async-start(), calls=%async_computation.13 | async-start | bytes 1310720 | tf_op jit(solution)/shard_map/reduce_scatter | solution.py:443
  786.1 158.5 %reduce-scatter.9.cloned.1.call-start = ((), (), s32[]{:S(2)}) async-start(), calls=%async_computation.14 | async-start | bytes 5242880 | tf_op jit(solution)/shard_map/reduce_scatter | solution.py:405
  800.2 224.0 %reduce-scatter.11.cloned.1.call-start = ((), (), s32[]{:S(2)}) async-start(), calls=%async_computation.15 | async-start | bytes 5242880 | tf_op jit(solution)/shard_map/reduce_scatter | solution.py:404
  820.2 49.2 %copy-start.6 = (bf16[4,512,512]{2,1,0:T(8,128)(2,1)S(1)}, bf16[4,512,512]{2,1,0:T(8,128)(2,1)}, u32[]{:S(2)}) copy-start(bf16[4,512,512]{2,1,0:T(8,128)(2,1)} %copy-done.5) | copy-start | bytes 6291460
  871.3 27.6 %copy-start.7 = (f32[256,2048]{1,0:T(8,128)S(1)}, f32[256,2048]{1,0:T(8,128)}, u32[]{:S(2)}) copy-start(f32[256,2048]{1,0:T(8,128)} %qkv_grad.1) | copy-start | bytes 6291460
  872.2 9.2 all-to-all-start.3
  881.4 13.0 %all-to-all-start.1 = ((f32[32,1,384]{2,1,0:T(1,128)}), f32[32,1,384]{2,1,0:T(1,128)S(1)}, u32[]{:S(2)}, u32[]{:S(2)}) async-start(f32[32,1,384]{2,1,0:T(1,128)} %all_to_all.19), calls=%async_computation.1 | async-start | bytes 98304 | tf_op jit(solution)/shard_map/all_to_all | solution.py:432
  894.4 132.5 %all-to-all-start.2 = ((bf16[8,64,768]{2,1,0:T(8,128)(2,1)}), bf16[8,64,768]{2,1,0:T(8,128)(2,1)}, u32[]{:S(2)}, u32[]{:S(2)}) async-start(bf16[8,64,768]{2,1,0:T(8,128)(2,1)} %bitcast.194), calls=%async_computation.3 | async-start | bytes 1572864 | tf_op jit(solution)/shard_map/all_to_all | solution.py:439
  (26 other events, 267.6 us)
Sparse Core Ops, SparseCore 0:
  29.8 63.8 all-gather.17
  95.2 26.5 all-gather.9
  123.4 114.4 all-gather.11
  239.3 82.4 all-gather.13
  355.1 81.3 all-gather.15
  776.8 59.4 reduce-scatter.4
  838.6 27.1 reduce-scatter.6
  868.2 76.3 reduce-scatter.8
  946.8 77.2 reduce-scatter.10

commit v3 on v2

--- a/solution.py
+++ b/solution.py
@@ -112,6 +112,7 @@
         out_specs=[pl.BlockSpec(memory_space=pl.ANY)] + vmem(len(out_types)),
         scratch_shapes=[pltpu.VMEM((ranks, tok, D), x.dtype), pltpu.SemaphoreType.DMA((10,)), pltpu.SemaphoreType.DMA((10,)), pltpu.SemaphoreType.DMA((8,))],
         compiler_params=pltpu.CompilerParams(collective_id=cid, has_side_effects=True, vmem_limit_bytes=60 << 20),
+        cost_estimate=pl.CostEstimate(flops=1 << 30, bytes_accessed=128 << 20, transcendentals=0),
         name=name,
     )(x, *ins)
     return res[0].reshape(ranks * tok, D), *res[1:]
@@ -209,6 +210,7 @@
         scratch_shapes=[pltpu.VMEM((4, tok, D), bfloat), pltpu.VMEM((4, tok, D), bfloat), pltpu.VMEM((3, 2, tok, D // 2), bfloat), pltpu.VMEM((6, tok, D // 2), bfloat),
             pltpu.SemaphoreType.DMA((10,)), pltpu.SemaphoreType.DMA((10,))],
         compiler_params=pltpu.CompilerParams(collective_id=cid, has_side_effects=True, vmem_limit_bytes=60 << 20),
+        cost_estimate=pl.CostEstimate(flops=1 << 30, bytes_accessed=128 << 20, transcendentals=0),
         name=name,
     )(a.reshape(ranks, tok, -1), w)
 
@@ -236,27 +238,144 @@
     return jnp.sum(matrix.astype(single), axis=0)
 
 
-def attention_forward(query, key_two, value_two, allowed):
+def windows(span):
+    block = span // 2
+    return [(i * block, i * block + block + span) for i in range(2)]
+
+def key_window(before, own, lo, hi, span):
+    return jnp.concatenate([before[lo:span], own[0 : hi - span]], axis=0)
+
+def hidden_bias(start_ref, i, block, lo, hi, span):
+    rows = span + i * block + lax.broadcasted_iota(jnp.int32, (block, hi - lo), 0)
+    keys = lo + lax.broadcasted_iota(jnp.int32, (block, hi - lo), 1)
+    start = start_ref[i * block : (i + 1) * block, :]
+    return jnp.where((keys >= start) & (keys <= rows), 0.0, -1e30).astype(single)
+
+def attend_kernel(start_ref, q_ref, k_ref, v_ref, kb_ref, vb_ref, out_ref):
+    span, cols = q_ref.shape
+    block = span // 2
+    lane = lax.broadcasted_iota(jnp.int32, (block, cols), 1) // HEAD_DIM
+    for i, (lo, hi) in enumerate(windows(span)):
+        rows = pl.ds(i * block, block)
+        bias = hidden_bias(start_ref, i, block, lo, hi, span)
+        keys = key_window(kb_ref, k_ref, lo, hi, span)
+        vals = key_window(vb_ref, v_ref, lo, hi, span)
+        query = q_ref[rows, :] * jnp.asarray(HEAD_DIM ** (-0.5), bfloat)
+        def head(h, total):
+            mine = lane == h
+            scores = dot_nt(jnp.where(mine, query, 0), keys) + bias
+            weights = jnp.exp(scores - jnp.max(scores, axis=1, keepdims=True))
+            part = jnp.dot(weights.astype(bfloat), vals, preferred_element_type=single)
+            part = part * (1.0 / jnp.sum(weights, axis=1, keepdims=True))
+            return jnp.where(mine, part, total)
+        total = lax.fori_loop(0, cols // HEAD_DIM, head, jnp.zeros((block, cols), single), unroll=True)
+        out_ref[rows, :] = total.astype(bfloat)
+
+def attend_back_kernel(start_ref, q_ref, k_ref, v_ref, kb_ref, vb_ref, do_ref, dq_ref, edge_ref, pair_ref, dk, dv):
+    span, cols = q_ref.shape
+    block = span // 2
+    scale = HEAD_DIM ** (-0.5)
+    dk[...] = jnp.zeros_like(dk)
+    dv[...] = jnp.zeros_like(dv)
+    lane = lax.broadcasted_iota(jnp.int32, (block, cols), 1) // HEAD_DIM
+    for i, (lo, hi) in enumerate(windows(span)):
+        rows = pl.ds(i * block, block)
+        bias = hidden_bias(start_ref, i, block, lo, hi, span)
+        keys = key_window(kb_ref, k_ref, lo, hi, span)
+        vals = key_window(vb_ref, v_ref, lo, hi, span)
+        query = q_ref[rows, :] * jnp.asarray(scale, bfloat)
+        grad = do_ref[rows, :]
+        def head(h, total):
+            mine = lane == h
+            query_h = jnp.where(mine, query, 0)
+            grad_h = jnp.where(mine, grad, 0)
+            scores = dot_nt(query_h, keys) + bias
+            weights = jnp.exp(scores - jnp.max(scores, axis=1, keepdims=True))
+            probs = weights * (1.0 / jnp.sum(weights, axis=1, keepdims=True))
+            prob_grad = dot_nt(grad_h, vals)
+            row_dot = jnp.sum(probs * prob_grad, axis=1, keepdims=True)
+            score_grad = (probs * (prob_grad - row_dot)).astype(bfloat)
+            dv[lo:hi, :] += dot_tn(probs.astype(bfloat), grad_h)
+            dk[lo:hi, :] += dot_tn(score_grad, query_h)
+            part = jnp.dot(score_grad, keys, preferred_element_type=single)
+            return jnp.where(mine, part, total)
+        total = lax.fori_loop(0, cols // HEAD_DIM, head, jnp.zeros((block, cols), single), unroll=True)
+        dq_ref[rows, :] = (total * scale).astype(bfloat)
+    edge_ref[:, :cols] = dk[:span, :].astype(bfloat)
+    edge_ref[:, cols:] = dv[:span, :].astype(bfloat)
+    pair_ref[:, :cols] = dk[span:, :]
+    pair_ref[:, cols:] = dv[span:, :]
+
+def attention_specs(span, cols):
+    def at(j):
+        return pl.BlockSpec((span, cols), lambda g: (g, j))
+    return [pl.BlockSpec((span, 1), lambda g: (g, 0)), at(0), at(1), at(2), at(0), at(1)]
+
+def attend(starts, qkv, before, groups):
+    span, cols = qkv.shape[0] // groups, qkv.shape[1] // 3
+    return pl.pallas_call(
+        attend_kernel,
+        grid=(groups,),
+        out_shape=jax.ShapeDtypeStruct((groups * span, cols), bfloat),
+        in_specs=attention_specs(span, cols),
+        out_specs=pl.BlockSpec((span, cols), lambda g: (g, 0)),
+        compiler_params=pltpu.CompilerParams(vmem_limit_bytes=60 << 20),
+        name="attend",
+    )(starts, qkv, qkv, qkv, before, before)
+
+def attend_back(starts, qkv, before, grad, groups):
+    span, cols = qkv.shape[0] // groups, qkv.shape[1] // 3
+    rows = groups * span
+    return pl.pallas_call(
+        attend_back_kernel,
+        grid=(groups,),
+        out_shape=[jax.ShapeDtypeStruct((rows, cols), bfloat), jax.ShapeDtypeStruct((rows, 2 * cols), bfloat), jax.ShapeDtypeStruct((rows, 2 * cols), single)],
+        in_specs=attention_specs(span, cols) + [pl.BlockSpec((span, cols), lambda g: (g, 0))],
+        out_specs=[pl.BlockSpec((span, cols), lambda g: (g, 0))] + [pl.BlockSpec((span, 2 * cols), lambda g: (g, 0))] * 2,
+        scratch_shapes=[pltpu.VMEM((2 * span, cols), single)] * 2,
+        compiler_params=pltpu.CompilerParams(vmem_limit_bytes=60 << 20),
+        name="attend_back",
+    )(starts, qkv, qkv, qkv, before, before, grad)
+
+
+def attention_heads(starts, qkv, before, groups):
+    span, cols = qkv.shape[0] // groups, qkv.shape[1] // 3
+    both = jnp.concatenate([before.reshape(groups, span, -1), qkv[:, cols:].reshape(groups, span, -1)], axis=1)
+    key_two, value_two = [both[..., i * cols : (i + 1) * cols].reshape(groups, 2 * span, -1, HEAD_DIM) for i in (0, 1)]
+    query = qkv[:, :cols].reshape(groups, span, -1, HEAD_DIM)
+    keys = jnp.arange(2 * span)[None, None, :]
+    rows = span + jnp.arange(span)[None, :, None]
+    allowed = (keys >= starts.reshape(groups, span, 1)) & (keys <= rows)
     scores = jnp.einsum("gqhd,gkhd->ghqk", query, key_two, preferred_element_type=single) * HEAD_DIM ** (-0.5)
     scores = jnp.where(allowed[:, None], scores, -1e30)
-    row_peak = jnp.max(scores, axis=-1, keepdims=True)
-    weights_exp = jnp.exp(scores - row_peak)
-    row_total = jnp.sum(weights_exp, axis=-1, keepdims=True)
-    prob_low = (weights_exp / row_total).astype(bfloat)
-    context = jnp.einsum("ghqk,gkhd->gqhd", prob_low, value_two, preferred_element_type=single)
-    return context.astype(bfloat), row_peak + jnp.log(row_total)
-
-
-def attention_backward(query, key_two, value_two, grad, logsum, allowed):
-    scores = jnp.einsum("gqhd,gkhd->ghqk", query, key_two, preferred_element_type=single) * HEAD_DIM ** (-0.5)
-    probs = jnp.exp(jnp.where(allowed[:, None], scores, -1e30) - logsum)
+    weights = jnp.exp(scores - jnp.max(scores, axis=-1, keepdims=True))
+    return query, key_two, value_two, weights / jnp.sum(weights, axis=-1, keepdims=True)
+
+
+def attention_forward(starts, qkv, before, groups):
+    if qkv.shape[1] // 3 % 128 == 0:
+        return attend(starts, qkv, before, groups)
+    _, _, value_two, probs = attention_heads(starts, qkv, before, groups)
+    context = jnp.einsum("ghqk,gkhd->gqhd", probs.astype(bfloat), value_two, preferred_element_type=single)
+    return context.astype(bfloat).reshape(qkv.shape[0], -1)
+
+
+def attention_backward(starts, qkv, before, grad, groups):
+    if qkv.shape[1] // 3 % 128 == 0:
+        return attend_back(starts, qkv, before, grad, groups)
+    query, key_two, value_two, probs = attention_heads(starts, qkv, before, groups)
+    span = query.shape[1]
+    grad = grad.reshape(query.shape)
     prob_grad = jnp.einsum("gqhd,gkhd->ghqk", grad, value_two, preferred_element_type=single)
     row_dot = jnp.sum(probs * prob_grad, axis=-1, keepdims=True)
     score_grad = (probs * (prob_grad - row_dot)).astype(bfloat)
     query_grad = jnp.einsum("ghqk,gkhd->gqhd", score_grad, key_two, preferred_element_type=single) * HEAD_DIM ** (-0.5)
     key_grad = jnp.einsum("ghqk,gqhd->gkhd", score_grad, query, preferred_element_type=single) * HEAD_DIM ** (-0.5)
     value_grad = jnp.einsum("ghqk,gqhd->gkhd", probs.astype(bfloat), grad, preferred_element_type=single)
-    return query_grad, key_grad, value_grad
+    pair = jnp.concatenate([t.reshape(groups, 2 * span, -1) for t in (key_grad, value_grad)], axis=2)
+    rows = qkv.shape[0]
+    edge, pair = [t.reshape(rows, -1) for t in (pair[:, :span].astype(bfloat), pair[:, span:])]
+    return query_grad.astype(bfloat).reshape(rows, -1), edge, pair
 
 
 def norm_backward(values, out_grad, gain_vec):
@@ -310,15 +429,22 @@
 
     count = lengths.shape[1]
     upto = jnp.arange(count)[:, None] <= jnp.arange(count)[None, :]
-    ends = jnp.sum(jnp.where(upto, lax.all_gather(lengths[0], "b", axis=0)[:, :, None], 0), axis=1)
+    small = [ln1_gain, ln1_bias, q_bias, v_bias, o_bias, ln2_gain, ln2_bias, fc2_bias]
+    pack = jnp.concatenate([v.astype(single) for v in (*small, fc1_bias, lengths[0])])
+    pad = -pack.shape[0] % 128
+    pack = lax.all_gather(jnp.concatenate([pack, jnp.zeros((pad,), single)]), ALL, axis=0)
+    vectors = [pack[:, i * rows_dev : (i + 1) * rows_dev].reshape(-1) for i in range(len(small))]
+    gain_one, bias_one, bias_q, bias_v, bias_o, gain_two, bias_two, bias_down = vectors
+    pack = pack.reshape(B, Z, X, -1)[..., len(small) * rows_dev :]
+    up_dev = fc1_bias.shape[0]
+    bias_up = lax.dynamic_index_in_dim(
+        pack[..., :up_dev].transpose(0, 2, 1, 3).reshape(R, Z * up_dev), rank, 0, keepdims=False
+    )
+    group_lengths = pack[:, 0, 0, up_dev : up_dev + count].astype(jnp.int32)
+    ends = jnp.sum(jnp.where(upto, group_lengths[:, :, None], 0), axis=1)
     places = at_z * span + jnp.arange(span, dtype=jnp.int32)
     starts = jnp.max(jnp.where(ends[:, None, :] <= places[None, :, None], ends[:, None, :], 0), axis=2)
-    key_places = (at_z - 1) * span + jnp.arange(2 * span, dtype=jnp.int32)
-    allowed = (key_places[None, None, :] >= starts[:, :, None]) & (key_places[None, None, :] <= places[None, :, None])
-
-    small = jnp.stack([ln1_gain, ln1_bias, q_bias, v_bias, o_bias, ln2_gain, ln2_bias, fc2_bias])
-    small = lax.all_gather(small, ALL, axis=1, tiled=True).astype(single)
-    gain_one, bias_one, bias_q, bias_v, bias_o, gain_two, bias_two, bias_down = [small[i] for i in range(8)]
+    starts = starts - (at_z - 1) * span
 
     def to_ranks(matrix):
         lead = matrix.shape[:-1]
@@ -339,7 +465,7 @@
 
     qkv_parts = jnp.concatenate([to_ranks(q_weight), to_ranks(k_weight), to_ranks(v_weight)], axis=2)
     qkv_mine = lax.all_to_all(qkv_parts, PLANE, split_axis=0, concat_axis=0, tiled=True)
-    weight_qkv = lax.all_gather(qkv_mine, "z", axis=0)
+    weight_qkv = lax.all_gather(qkv_mine.reshape(D // Z, 3 * cols), "z", axis=0, tiled=True)
     weight_qkv = weight_qkv.reshape(Z, B, X, rows_dev, 3 * cols).transpose(1, 0, 2, 3, 4).reshape(D, 3 * cols)
     bias_qkv = jnp.concatenate([mine(bias_q), jnp.zeros((cols,), single), mine(bias_v)])
     if whole_heads:
@@ -348,7 +474,6 @@
         weight_o = lax.dynamic_slice_in_dim(lax.all_gather(o_weight, ALL, axis=0, tiled=True), rank * cols, cols, 0)
     weight_up = lax.all_gather(fc1_weight, "z", axis=1, tiled=True)
     weight_down = lax.all_gather(fc2_weight, "z", axis=0, tiled=True)
-    bias_up = lax.all_gather(fc1_bias, "z", axis=0, tiled=True).astype(single)
 
     normed_low = layer_norm(local, gain_one, bias_one).astype(bfloat)
     fast = (B, X) == (4, 2)
@@ -372,37 +497,33 @@
 
     normed_all = gather_plane(normed_low, 0, "gather_normed")
     qkv = (dot(normed_all, weight_qkv) + bias_qkv).astype(bfloat)
-    query = qkv[:, :cols].reshape(B, span, heads, HEAD_DIM)
-    key_value = qkv[:, cols:]
     up = [(i, i + 1) for i in range(Z - 1)]
     down = [(i + 1, i) for i in range(Z - 1)]
-    before = lax.ppermute(key_value, "z", up)
-    both = jnp.concatenate([before.reshape(B, span, 2 * cols), key_value.reshape(B, span, 2 * cols)], axis=1)
-    key_two = both[..., :cols].reshape(B, 2 * span, heads, HEAD_DIM)
-    value_two = both[..., cols:].reshape(B, 2 * span, heads, HEAD_DIM)
-    context, logsum = attention_forward(query, key_two, value_two, allowed)
-    context = context.reshape(B * span, cols)
+    cotangent = out_grad[0].astype(single) * (group_tok / active_total)
+    branch_grad = (active * cotangent).astype(bfloat)
+    down_b_grad = column_sums(branch_grad)
+    qkv, branch_grad = lax.optimization_barrier((qkv, branch_grad))
+    before = lax.ppermute(qkv[:, cols:], "z", up)
+    branch_all = gather_plane(branch_grad, 7, "gather_branch")
+    before, branch_all = lax.optimization_barrier((before, branch_all))
+    starts = starts.reshape(B * span, 1)
+    context = attention_forward(starts, qkv, before, B)
 
     attended = reduce_plane(context, weight_o, False, 1, "attended") + bias_o
     middle = local + active * attended
     normed_two = layer_norm(middle, gain_two, bias_two).astype(bfloat)
-    cotangent = out_grad[0].astype(single) * (group_tok / active_total)
-    branch_grad = (active * cotangent).astype(bfloat)
-    down_b_grad = column_sums(branch_grad)
-    branch_all = lax.all_gather(branch_grad, PLANE, axis=0, tiled=True)
     two_all, hidden_pre = gather_plane_dot(normed_two, weight_up, bias_up[None], single, False, 2, "up")
     gelu_value, gelu_pull = jax.vjp(partial(jax.nn.gelu, approximate=True), hidden_pre)
     hidden = gelu_value.astype(bfloat)
     hidden_grad = dot_nt(branch_all, weight_down)
     pre_grad = gelu_pull(hidden_grad)[0].astype(bfloat)
+    down_w_grad = dot_tn(hidden, branch_all).astype(bfloat)
+    up_w_grad = dot_tn(two_all, pre_grad).astype(bfloat)
+    up_b_grad = column_sums(pre_grad)
+    hidden, pre_grad, down_w_grad, up_w_grad = lax.optimization_barrier((hidden, pre_grad, down_w_grad, up_w_grad))
     normed_two_grad = reduce_plane(pre_grad, weight_up, True, 3, "up_grad")
-    branch = reduce_plane(hidden, weight_down, False, 4, "down") + bias_down
-    outputs = middle + active * branch
-    down_w_grad = dot_tn(hidden, branch_all)
-    up_w_grad = dot_tn(two_all, pre_grad)
-    up_b_grad = column_sums(pre_grad)
-    down_w_shard = lax.psum_scatter(down_w_grad.astype(bfloat), "z", scatter_dimension=0, tiled=True).astype(single)
-    up_w_shard = lax.psum_scatter(up_w_grad.astype(bfloat), "z", scatter_dimension=1, tiled=True).astype(single)
+    down_w_shard = lax.psum_scatter(down_w_grad, "z", scatter_dimension=0, tiled=True).astype(single)
+    up_w_shard = lax.psum_scatter(up_w_grad, "z", scatter_dimension=1, tiled=True).astype(single)
 
     middle_part, gain_two_grad, bias_two_grad = norm_backward(middle, normed_two_grad, gain_two)
     middle_grad = cotangent + middle_part
@@ -412,15 +533,14 @@
         attended_grad, weight_o, jnp.zeros((1, cols), single), bfloat, True, 5, "attended_grad"
     )
     out_w_grad = dot_tn(context, attended_all)
-    query_grad, key_grad, value_grad = attention_backward(
-        query, key_two, value_two, context_grad.reshape(B, span, heads, HEAD_DIM), logsum, allowed
-    )
-    pair = jnp.concatenate(
-        [key_grad.reshape(B, 2 * span, cols), value_grad.reshape(B, 2 * span, cols)], axis=2
-    )
-    after = lax.ppermute(pair[:, :span].astype(bfloat), "z", down).astype(single)
-    pair_grad = (pair[:, span:] + after).astype(bfloat).reshape(B * span, 2 * cols)
-    qkv_grad = jnp.concatenate([query_grad.astype(bfloat).reshape(B * span, cols), pair_grad], axis=1)
+    query_grad, edge, pair = attention_backward(starts, qkv, before, context_grad, B)
+    hidden, edge, pair = lax.optimization_barrier((hidden, edge, pair))
+    after = lax.ppermute(edge, "z", down)
+    branch = reduce_plane(hidden, weight_down, False, 4, "down")
+    branch, after = lax.optimization_barrier((branch, after))
+    outputs = middle + active * (branch + bias_down)
+    pair_grad = (pair + after.astype(single)).astype(bfloat)
+    qkv_grad = jnp.concatenate([query_grad, pair_grad], axis=1)
     normed_grad = reduce_plane(qkv_grad, weight_qkv, True, 6, "qkv_grad")
     qkv_w_grad = dot_tn(normed_all, qkv_grad)
     qkv_b_grad = column_sums(qkv_grad)

time: 1050 us -> 881 us (0.84)
  matrix products: 166 us -> 74.8 us
  Pallas kernels: 348 us -> 414 us
  other arithmetic: 97.7 us -> 40.7 us
  local copies, waits for them, and re-layouts: 68.4 us -> 29 us
  waiting for transfers between devices: 228 us -> 192 us
  blocking collectives: 103 us -> 86.6 us
    dot_general x6 -> x0, matrix products: 89.9 us -> none  [the longest x1 22.1 us: attention_backward(): jnp.einsum('gqhd,gkhd->ghqk', grad, value_two, preferred_element_type=sin...]
    ppermute x2, waiting for transfers between devices: 99.8 us -> 35.1 us  [the longest x1 35.1 us: on_device(): before = lax.ppermute(qkv[:, cols:], 'z', up)]
    pallas_call x0 -> x2, Pallas kernels: none -> 46.7 us  [the longest x1 33.5 us: attend_back(): pl.pallas_call(attend_back_kernel, grid=(groups,), out_shape=[jax.ShapeDt...]
    convert_element_type x5, other arithmetic: 43.2 us -> 9.16 us  [the longest x1 3.66 us: on_device(): pair_grad = (pair + after.astype(single)).astype(bfloat)]
    reduce_scatter x2, waiting for transfers between devices: 116 us -> 149 us  [the longest x1 76.9 us: on_device(): lax.psum_scatter(down_w_grad, 'z', scatter_dimension=0, tiled=True)]
    pallas_call x3 -> x4, Pallas kernels: 149 us -> 168 us  [plane_gather(): pl.pallas_call(functools.partial(gather_kernel, body_of, len(ins), len(ou...]
    reshape x5 -> x1, local copies, waits for them, and re-layouts: 17.8 us -> 0.07 us  [on_device(): pack = pack.reshape(B, Z, X, -1)[..., len(small) * rows_dev:]]
    all_gather x3 -> x1, blocking collectives: 85.8 us -> 69.3 us  [on_device(): lax.all_gather(jnp.concatenate([pack, jnp.zeros((pad,), single)]), ALL, a...]
  transfers between devices with their start and end apart: 14 -> 13, of which waited for: 6 -> 4; matrix products, arithmetic and copies ran while one was open for 17% -> 6% of each run, Pallas kernels for 24% -> 33%
where the time goes in v3:
time: 881 us; the launch traced here: 874 us
  Pallas kernels  414 us (47%)
  waiting for transfers between devices  192 us (22%)
  blocking collectives  86.6 us (10%)
  matrix products  74.8 us (8%)
  other arithmetic  40.7 us (5%)
  local copies, waits for them, and re-layouts  29 us (3%)
  starting transfers between devices  20.9 us (2%)
  between operations  16.7 us (2%)
    pallas_call x4, Pallas kernels, dot_reduce(): pl.pallas_call(functools.partial(reduce_kernel, turned), out_shape=jax.Sh...  199 us
    pallas_call x4, Pallas kernels, plane_gather(): pl.pallas_call(functools.partial(gather_kernel, body_of, len(ins), len(ou...  168 us
    reduce_scatter x1, waiting for transfers between devices, on_device(): lax.psum_scatter(down_w_grad, 'z', scatter_dimension=0, tiled=True)  76.9 us
    reduce_scatter x1, waiting for transfers between devices, on_device(): lax.psum_scatter(up_w_grad, 'z', scatter_dimension=1, tiled=True)  72 us
    all_gather x1, blocking collectives, on_device(): lax.all_gather(jnp.concatenate([pack, jnp.zeros((pad,), single)]), ALL, a...  69.3 us
    dot_general x4, matrix products, dot_tn(): lax.dot_general(left, right, (((0,), (0,)), ((), ())), preferred_element_...  44.2 us
    ppermute x1, waiting for transfers between devices, on_device(): before = lax.ppermute(qkv[:, cols:], 'z', up)  35.1 us
    pallas_call x1, Pallas kernels, attend_back(): pl.pallas_call(attend_back_kernel, grid=(groups,), out_shape=[jax.ShapeDt...  33.5 us
  transfers between devices with their start and end apart: 13, of which 4 were waited for; matrix products, arithmetic and copies ran while one was open for 6% of the time, Pallas kernels for 33%

profile of v3, /device:TPU:0, one launch (start us, length us, event | category | flops | bytes accessed | tf_op | source)
XLA Modules:
  0.0 874.3 jit_solution(805915724900913554)
XLA Ops:
  11.5 17.3 %all_to_all.28 = bf16[8,64,768]{2,1,0:T(8,128)(2,1)} all-to-all(bf16[8,64,768]{2,1,0:T(8,128)(2,1)S(1)} %pad_maximum_fusion.1), channel_id=1, replica_groups=mesh['b'=4,'z'=4,'x'=2] {'b','x'}, dimensions={0} | all-to-all | bytes 1572864 | tf_op jit(solution)/shard_map/all_to_all | solution.py:467
  31.1 69.3 %all-gather.1 = f32[32,1,896]{2,1,0:T(1,128)S(1)} all-gather(f32[1,1,896]{2,1,0:T(1,128)S(1)} %reshape.301), channel_id=2, replica_groups=mesh['b'=4,'z'=4,'x'=2] {'b','z','x'}, dimensions={0}, use_global_device_ids=true | all-gather | bytes 118272 | tf_op jit(solution)/shard_map/all_gather | solution.py:435
  106.3 39.9 %gather_normed.1 = bf16[8,256,2048]{2,1,0:T(8,128)(2,1)} custom-call(bf16[256,2048]{1,0:T(8,128)(2,1)} %fusion.19.x_ref), custom_call_target="tpu_custom_call" | custom-call | flops 1073741824 | bytes 134217728 | tf_op jit(solution)/shard_map/gather_normed/pallas_call | solution.py:108
  148.5 10.2 %add_convert_fusion.q_ref.k_ref.v_ref = bf16[2048,768]{1,0:T(8,128)(2,1)S(1)} fusion(f32[768]{0:T(1024)S(1)} %pad_maximum_fusion.3, bf16[2048,2048]{1,0:T(8,128)(2,1)} %bitcast.145, bf16[2048,768]{1,0:T(8,128)(2,1)S(1)} %bitcast.140), kind=kOutput, calls=%fused_computation.16 | convolution fusion | flops 6445596672 | bytes 14683136 | tf_op jit(solution)/shard_map/dot_general | solution.py:219
  166.1 42.3 %gather_branch.1 = bf16[8,256,2048]{2,1,0:T(8,128)(2,1)} custom-call(bf16[256,2048]{1,0:T(8,128)(2,1)} %get-tuple-element.38.x_ref), custom_call_target="tpu_custom_call" | custom-call | flops 1073741824 | bytes 134217728 | tf_op jit(solution)/shard_map/gather_branch/pallas_call | solution.py:108
  208.4 35.1 %collective-permute-done.kb_ref.vb_ref = bf16[2048,512]{1,0:T(8,128)(2,1)} collective-permute-done((bf16[2048,512]{1,0:T(8,128)(2,1)S(1)}, bf16[2048,512]{1,0:T(8,128)(2,1)}, u32[]{:S(2)}, u32[]{:S(2)}) %collective-permute-start) | collective-permute-done | bytes 2097184 | tf_op jit(solution)/shard_map/ppermute | solution.py:506
  243.5 13.2 %attend.1 = bf16[2048,256]{1,0:T(8,128)(2,1)} custom-call(s32[2048,1]{1,0:T(8,128)} %bitcast.143, bf16[2048,768]{1,0:T(8,128)(2,1)} %copy-done, bf16[2048,768]{1,0:T(8,128)(2,1)} %copy-done, bf16[2048,768]{1,0:T(8,128)(2,1)} %copy-done, bf16[2048,512]{1,0:T(8,128)(2,1)} %collective-permute-done.kb_ref.vb_ref, ...), custom_call_target="tpu_custom_call" | custom-call | tf_op jit(solution)/shard_map/attend/pallas_call | solution.py:316
  256.8 45.9 %attended.1 = f32[256,2048]{1,0:T(8,128)} custom-call(bf16[8,256,256]{2,1,0:T(8,128)(2,1)} %bitcast.138, bf16[256,2048]{1,0:T(8,128)(2,1)} %all-gather.9.cloned.1.call-done.w_ref.refs_0_), custom_call_target="tpu_custom_call" | custom-call | flops 1073741824 | bytes 134217728 | tf_op jit(solution)/shard_map/attended/pallas_call | solution.py:206
  306.6 44.8 %up.1 = (bf16[8,256,2048]{2,1,0:T(8,128)(2,1)}, f32[8,256,1024]{2,1,0:T(8,128)}) custom-call(bf16[256,2048]{1,0:T(8,128)(2,1)} %add_convert_fusion.3.x_ref, bf16[2048,1024]{1,0:T(8,128)(2,1)} %all-gather.11.cloned.1.call-done.refs_0_.w_ref, f32[1,1024]{1,0:T(1,128)} %constant_dynamic-slice_fusion.2.refs_1_), custom_call_target="tpu_custom_call" | custom-call | flops 1073741824 | bytes 134217728 | tf_op jit(solution)/shard_map/up/pallas_call | solution.py:108
  351.4 20.3 %convert_reduce_fusion = (f32[1024]{0:T(1024)S(1)}, bf16[2048,1024]{1,0:T(8,128)(2,1)}, bf16[2048,1024]{1,0:T(8,128)(2,1)S(1)}) fusion(f32[8,256,1024]{2,1,0:T(8,128)} %get-tuple-element.40, bf16[2048,2048]{1,0:T(8,128)(2,1)} %bitcast.147, bf16[1024,2048]{1,0:T(8,128)(2,1)} %all-gather.13.cloned.1.call-done.w_ref), kind=kOutput, calls=%fused_computation.14 | convolution fusion | flops 8640265216 | bytes 29364224 | tf_op jit(solution)/shard_map/dot_general | solution.py:227
  373.6 12.7 %convolution_convert_fusion = bf16[1024,2048]{1,0:T(8,128)(2,1)} fusion(bf16[2048,1024]{1,0:T(8,128)(2,1)S(1)} %get-tuple-element.48, bf16[2048,2048]{1,0:T(8,128)(2,1)} %bitcast.148), kind=kOutput, calls=%fused_computation.18 | convolution fusion | flops 8592031744 | bytes 16777216 | tf_op jit(solution)/shard_map/dot_general | solution.py:223
  386.4 14.4 %convolution_convert_fusion.1 = bf16[2048,1024]{1,0:T(8,128)(2,1)} fusion(bf16[2048,2048]{1,0:T(8,128)(2,1)} %bitcast.175, bf16[2048,1024]{1,0:T(8,128)(2,1)} %get-tuple-element.44), kind=kOutput, calls=%fused_computation.19 | convolution fusion | flops 8592031744 | bytes 16777216 | tf_op jit(solution)/shard_map/dot_general | solution.py:223
  400.7 52.5 %up_grad.1 = f32[256,2048]{1,0:T(8,128)} custom-call(bf16[8,256,1024]{2,1,0:T(8,128)(2,1)} %bitcast.150, bf16[2048,1024]{1,0:T(8,128)(2,1)} %all-gather.11.cloned.1.call-done.refs_0_.w_ref), custom_call_target="tpu_custom_call" | custom-call | flops 1073741824 | bytes 134217728 | tf_op jit(solution)/shard_map/up_grad/pallas_call | solution.py:206
  459.2 41.5 %attended_grad.1 = (bf16[8,256,2048]{2,1,0:T(8,128)(2,1)}, bf16[8,256,256]{2,1,0:T(8,128)(2,1)}) custom-call(bf16[256,2048]{1,0:T(8,128)(2,1)} %get-tuple-element.70.x_ref, bf16[256,2048]{1,0:T(8,128)(2,1)} %all-gather.9.cloned.1.call-done.w_ref.refs_0_, f32[1,256]{1,0:T(1,128)} %broadcast_in_dim.42.refs_1_), custom_call_target="tpu_custom_call" | custom-call | flops 1073741824 | bytes 134217728 | tf_op jit(solution)/shard_map/attended_grad/pallas_call | solution.py:108
  500.6 33.5 %attend_back.1 = (bf16[2048,256]{1,0:T(8,128)(2,1)}, bf16[2048,512]{1,0:T(8,128)(2,1)}, f32[2048,512]{1,0:T(8,128)}) custom-call(s32[2048,1]{1,0:T(8,128)} %bitcast.144, bf16[2048,768]{1,0:T(8,128)(2,1)} %copy-done, bf16[2048,768]{1,0:T(8,128)(2,1)} %copy-done, bf16[2048,768]{1,0:T(8,128)(2,1)} %copy-done, ...), custom_call_target="tpu_custom_call" | custom-call | tf_op jit(solution)/shard_map/attend_back/pallas_call | solution.py:329
  535.7 51.5 %down.1 = f32[256,2048]{1,0:T(8,128)} custom-call(bf16[8,256,1024]{2,1,0:T(8,128)(2,1)} %bitcast.149, bf16[1024,2048]{1,0:T(8,128)(2,1)} %all-gather.13.cloned.1.call-done.w_ref), custom_call_target="tpu_custom_call" | custom-call | flops 1073741824 | bytes 134217728 | tf_op jit(solution)/shard_map/down/pallas_call | solution.py:206
  590.9 10.1 %convolution_convert_fusion.2 = bf16[2048,768]{1,0:T(8,128)(2,1)S(1)} fusion(bf16[2048,2048]{1,0:T(8,128)(2,1)} %bitcast.146, bf16[2048,512]{1,0:T(8,128)(2,1)S(1)} %add_convert_fusion.1, bf16[2048,256]{1,0:T(8,128)(2,1)S(1)} %copy-done.7), kind=kOutput, calls=%fused_computation.20 | convolution fusion | flops 6450315264 | bytes 14680064 | tf_op jit(solution)/shard_map/dot_general | solution.py:223
  602.9 7.0 convolution_convert_fusion.3
  615.4 7.8 all-to-all-start.3
  626.9 48.9 %qkv_grad.1 = f32[256,2048]{1,0:T(8,128)} custom-call(bf16[8,256,768]{2,1,0:T(8,128)(2,1)} %bitcast.142, bf16[2048,768]{1,0:T(8,128)(2,1)} %bitcast.141), custom_call_target="tpu_custom_call" | custom-call | flops 1073741824 | bytes 134217728 | tf_op jit(solution)/shard_map/qkv_grad/pallas_call | solution.py:206
  679.3 5.1 all-to-all-start.1
  688.4 4.1 all-to-all-done.1
  702.5 72.0 %reduce-scatter.9.cloned.1.call-done = bf16[2048,256]{1,0:T(8,128)(2,1)} async-done(((bf16[2048,1024]{1,0:T(8,128)(2,1)}), bf16[2048,256]{1,0:T(8,128)(2,1)}) %reduce-scatter.9.cloned.1.call-update) | async-done | bytes 1048592 | tf_op jit(solution)/shard_map/reduce_scatter | solution.py:526
  777.3 76.9 %reduce-scatter.11.cloned.1.call-done = bf16[256,2048]{1,0:T(8,128)(2,1)} async-done(((bf16[1024,2048]{1,0:T(8,128)(2,1)}), bf16[256,2048]{1,0:T(8,128)(2,1)}) %reduce-scatter.11.cloned.1.call-update) | async-done | bytes 1048592 | tf_op jit(solution)/shard_map/reduce_scatter | solution.py:525
  (182 shorter events, 81.2 us)
Async XLA Ops:
  7.2 139.0 %all-gather.7.cloned.1.call-start = ((), (), s32[]{:S(2)}) async-start(), calls=%async_computation.8 | async-start | bytes 3932160 | tf_op jit(solution)/shard_map/all_gather | solution.py:468
  11.4 19.6 %copy-start.14 = (bf16[64]{0:T(256)(128)(2,1)S(1)}, bf16[64]{0:T(256)(128)(2,1)}, u32[]{:S(2)}) copy-start(bf16[64]{0:T(256)(128)(2,1)} %param.25) | copy-start | bytes 388
  11.4 19.6 %copy-start.15 = (bf16[64]{0:T(256)(128)(2,1)S(1)}, bf16[64]{0:T(256)(128)(2,1)}, u32[]{:S(2)}) copy-start(bf16[64]{0:T(256)(128)(2,1)} %param.26) | copy-start | bytes 388
  11.4 19.6 %copy-start.16 = (bf16[64]{0:T(256)(128)(2,1)S(1)}, bf16[64]{0:T(256)(128)(2,1)}, u32[]{:S(2)}) copy-start(bf16[64]{0:T(256)(128)(2,1)} %param.28) | copy-start | bytes 388
  11.4 19.6 %copy-start.17 = (bf16[64]{0:T(256)(128)(2,1)S(1)}, bf16[64]{0:T(256)(128)(2,1)}, u32[]{:S(2)}) copy-start(bf16[64]{0:T(256)(128)(2,1)} %param.31) | copy-start | bytes 388
  11.4 19.6 %copy-start.18 = (bf16[64]{0:T(256)(128)(2,1)S(1)}, bf16[64]{0:T(256)(128)(2,1)}, u32[]{:S(2)}) copy-start(bf16[64]{0:T(256)(128)(2,1)} %param.33) | copy-start | bytes 388
  11.4 19.6 %copy-start.19 = (bf16[64]{0:T(256)(128)(2,1)S(1)}, bf16[64]{0:T(256)(128)(2,1)}, u32[]{:S(2)}) copy-start(bf16[64]{0:T(256)(128)(2,1)} %param.34) | copy-start | bytes 388
  11.4 19.6 %copy-start.20 = (bf16[64]{0:T(256)(128)(2,1)S(1)}, bf16[64]{0:T(256)(128)(2,1)}, u32[]{:S(2)}) copy-start(bf16[64]{0:T(256)(128)(2,1)} %param.35) | copy-start | bytes 388
  11.4 19.6 %copy-start.21 = (bf16[64]{0:T(256)(128)(2,1)S(1)}, bf16[64]{0:T(256)(128)(2,1)}, u32[]{:S(2)}) copy-start(bf16[64]{0:T(256)(128)(2,1)} %param.39) | copy-start | bytes 388
  28.7 72.1 %copy-start.1 = (bf16[1,256,2048]{2,1,0:T(8,128)(2,1)S(1)}, bf16[1,256,2048]{2,1,0:T(8,128)(2,1)}, u32[]{:S(2)}) copy-start(bf16[1,256,2048]{2,1,0:T(8,128)(2,1)} %param.20) | copy-start | bytes 3145732
  28.8 228.0 %all-gather.9.cloned.1.call-start = ((), (), s32[]{:S(2)}) async-start(), calls=%async_computation.9 | async-start | bytes 1310720 | tf_op jit(solution)/shard_map/all_gather | solution.py:472
  29.5 277.1 %all-gather.11.cloned.1.call-start = ((), (), s32[]{:S(2)}) async-start(), calls=%async_computation.10 | async-start | bytes 5242880 | tf_op jit(solution)/shard_map/all_gather | solution.py:475
  30.3 72.0 %copy-start.13 = (s32[1,2048]{1,0:T(1,128)S(1)}, s32[1,2048]{1,0:T(1,128)}, u32[]{:S(2)}) copy-start(s32[1,2048]{1,0:T(1,128)} %param.21) | copy-start | bytes 24580
  30.3 321.2 %all-gather.13.cloned.1.call-start = ((), (), s32[]{:S(2)}) async-start(), calls=%async_computation.11 | async-start | bytes 5242880 | tf_op jit(solution)/shard_map/all_gather | solution.py:476
  30.8 661.6 %reduce-scatter.5.cloned.1.call-start = ((), (), s32[]{:S(2)}) async-start(), calls=%async_computation.12 | async-start | bytes 3932160 | tf_op jit(solution)/shard_map/reduce_scatter | solution.py:558
  160.4 83.2 %collective-permute-start = (bf16[2048,512]{1,0:T(8,128)(2,1)S(1)}, bf16[2048,512]{1,0:T(8,128)(2,1)}, u32[]{:S(2)}, u32[]{:S(2)}) collective-permute-start(bf16[2048,512]{1,0:T(8,128)(2,1)S(1)} %slice.99), channel_id=1, source_target_pairs={{0,2},{2,4},{4,6},{1,3},{3,5},{5,7},{8,10},{10,12},{12,14},{9,11},... | collective-permute-start | bytes 6291464 | tf_op jit(solution)/shard_map/ppermute | solution.py:506
  256.8 46.0 %copy-start.2 = (bf16[1,256,2048]{2,1,0:T(8,128)(2,1)S(1)}, bf16[1,256,2048]{2,1,0:T(8,128)(2,1)}, u32[]{:S(2)}) copy-start(bf16[1,256,2048]{2,1,0:T(8,128)(2,1)} %param.20) | copy-start | bytes 3145732
  534.1 53.0 %collective-permute-start.1 = (bf16[2048,512]{1,0:T(8,128)(2,1)}, bf16[2048,512]{1,0:T(8,128)(2,1)}, u32[]{:S(2)}, u32[]{:S(2)}) collective-permute-start(bf16[2048,512]{1,0:T(8,128)(2,1)} %get-tuple-element.49), channel_id=1, source_target_pairs={{2,0},{4,2},{6,4},{3,1},{5,3},{7,5},{10,8},{12,10},{14,12},{11,9},... | collective-permute-start | bytes 6291464 | tf_op jit(solution)/shard_map/ppermute | solution.py:538
  602.9 96.0 %reduce-scatter.7.cloned.1.call-start = ((), (), s32[]{:S(2)}) async-start(), calls=%async_computation.13 | async-start | bytes 1310720 | tf_op jit(solution)/shard_map/reduce_scatter | solution.py:563
  610.0 164.6 %reduce-scatter.9.cloned.1.call-start = ((), (), s32[]{:S(2)}) async-start(), calls=%async_computation.14 | async-start | bytes 5242880 | tf_op jit(solution)/shard_map/reduce_scatter | solution.py:526
  610.7 243.4 %reduce-scatter.11.cloned.1.call-start = ((), (), s32[]{:S(2)}) async-start(), calls=%async_computation.15 | async-start | bytes 5242880 | tf_op jit(solution)/shard_map/reduce_scatter | solution.py:525
  615.4 63.9 %all-to-all-start.3 = ((f32[4,1,384]{2,1,0:T(1,128)}), f32[4,1,384]{2,1,0:T(1,128)S(1)}, u32[]{:S(2)}, u32[]{:S(2)}) async-start(f32[4,1,384]{2,1,0:T(1,128)} %all_to_all.22), calls=%async_computation.4 | async-start | bytes 12288 | tf_op jit(solution)/shard_map/all_to_all | solution.py:552
  679.3 13.2 %all-to-all-start.1 = ((f32[32,1,384]{2,1,0:T(1,128)}), f32[32,1,384]{2,1,0:T(1,128)S(1)}, u32[]{:S(2)}, u32[]{:S(2)}) async-start(f32[32,1,384]{2,1,0:T(1,128)} %all_to_all.19), calls=%async_computation.1 | async-start | bytes 98304 | tf_op jit(solution)/shard_map/all_to_all | solution.py:552
  692.5 164.5 %all-to-all-start.2 = ((bf16[8,64,768]{2,1,0:T(8,128)(2,1)}), bf16[8,64,768]{2,1,0:T(8,128)(2,1)S(1)}, u32[]{:S(2)}, u32[]{:S(2)}) async-start(bf16[8,64,768]{2,1,0:T(8,128)(2,1)} %bitcast.161), calls=%async_computation.3 | async-start | bytes 1572864 | tf_op jit(solution)/shard_map/all_to_all | solution.py:559
  (13 other events, 82.4 us)
Sparse Core Ops, SparseCore 0:
  28.9 64.1 all-gather.6
  94.7 26.6 all-gather.8
  123.0 111.8 all-gather.10
  236.3 82.4 all-gather.12
  603.0 63.4 reduce-scatter.4
  668.7 27.9 reduce-scatter.6
  699.1 75.4 reduce-scatter.8
  776.8 77.2 reduce-scatter.10

commit v4 on v3

--- a/solution.py
+++ b/solution.py
@@ -309,10 +309,10 @@
 def attention_specs(span, cols):
     def at(j):
         return pl.BlockSpec((span, cols), lambda g: (g, j))
-    return [pl.BlockSpec((span, 1), lambda g: (g, 0)), at(0), at(1), at(2), at(0), at(1)]
-
-def attend(starts, qkv, before, groups):
-    span, cols = qkv.shape[0] // groups, qkv.shape[1] // 3
+    return [pl.BlockSpec((span, 1), lambda g: (g, 0)), at(0), at(0), at(1), at(0), at(1)]
+
+def attend(starts, query, key_value, before, groups):
+    span, cols = query.shape[0] // groups, query.shape[1]
     return pl.pallas_call(
         attend_kernel,
         grid=(groups,),
@@ -321,10 +321,10 @@
         out_specs=pl.BlockSpec((span, cols), lambda g: (g, 0)),
         compiler_params=pltpu.CompilerParams(vmem_limit_bytes=60 << 20),
         name="attend",
-    )(starts, qkv, qkv, qkv, before, before)
-
-def attend_back(starts, qkv, before, grad, groups):
-    span, cols = qkv.shape[0] // groups, qkv.shape[1] // 3
+    )(starts, query, key_value, key_value, before, before)
+
+def attend_back(starts, query, key_value, before, grad, groups):
+    span, cols = query.shape[0] // groups, query.shape[1]
     rows = groups * span
     return pl.pallas_call(
         attend_back_kernel,
@@ -335,14 +335,14 @@
         scratch_shapes=[pltpu.VMEM((2 * span, cols), single)] * 2,
         compiler_params=pltpu.CompilerParams(vmem_limit_bytes=60 << 20),
         name="attend_back",
-    )(starts, qkv, qkv, qkv, before, before, grad)
-
-
-def attention_heads(starts, qkv, before, groups):
-    span, cols = qkv.shape[0] // groups, qkv.shape[1] // 3
-    both = jnp.concatenate([before.reshape(groups, span, -1), qkv[:, cols:].reshape(groups, span, -1)], axis=1)
+    )(starts, query, key_value, key_value, before, before, grad)
+
+
+def attention_heads(starts, query, key_value, before, groups):
+    span, cols = query.shape[0] // groups, query.shape[1]
+    both = jnp.concatenate([before.reshape(groups, span, -1), key_value.reshape(groups, span, -1)], axis=1)
     key_two, value_two = [both[..., i * cols : (i + 1) * cols].reshape(groups, 2 * span, -1, HEAD_DIM) for i in (0, 1)]
-    query = qkv[:, :cols].reshape(groups, span, -1, HEAD_DIM)
+    query = query.reshape(groups, span, -1, HEAD_DIM)
     keys = jnp.arange(2 * span)[None, None, :]
     rows = span + jnp.arange(span)[None, :, None]
     allowed = (keys >= starts.reshape(groups, span, 1)) & (keys <= rows)
@@ -352,18 +352,19 @@
     return query, key_two, value_two, weights / jnp.sum(weights, axis=-1, keepdims=True)
 
 
-def attention_forward(starts, qkv, before, groups):
-    if qkv.shape[1] // 3 % 128 == 0:
-        return attend(starts, qkv, before, groups)
-    _, _, value_two, probs = attention_heads(starts, qkv, before, groups)
+def attention_forward(starts, query, key_value, before, groups):
+    if query.shape[1] % 128 == 0:
+        return attend(starts, query, key_value, before, groups)
+    _, _, value_two, probs = attention_heads(starts, query, key_value, before, groups)
     context = jnp.einsum("ghqk,gkhd->gqhd", probs.astype(bfloat), value_two, preferred_element_type=single)
-    return context.astype(bfloat).reshape(qkv.shape[0], -1)
-
-
-def attention_backward(starts, qkv, before, grad, groups):
-    if qkv.shape[1] // 3 % 128 == 0:
-        return attend_back(starts, qkv, before, grad, groups)
-    query, key_two, value_two, probs = attention_heads(starts, qkv, before, groups)
+    return context.astype(bfloat).reshape(query.shape)
+
+
+def attention_backward(starts, query, key_value, before, grad, groups):
+    if query.shape[1] % 128 == 0:
+        return attend_back(starts, query, key_value, before, grad, groups)
+    rows = query.shape[0]
+    query, key_two, value_two, probs = attention_heads(starts, query, key_value, before, groups)
     span = query.shape[1]
     grad = grad.reshape(query.shape)
     prob_grad = jnp.einsum("gqhd,gkhd->ghqk", grad, value_two, preferred_element_type=single)
@@ -373,7 +374,6 @@
     key_grad = jnp.einsum("ghqk,gqhd->gkhd", score_grad, query, preferred_element_type=single) * HEAD_DIM ** (-0.5)
     value_grad = jnp.einsum("ghqk,gqhd->gkhd", probs.astype(bfloat), grad, preferred_element_type=single)
     pair = jnp.concatenate([t.reshape(groups, 2 * span, -1) for t in (key_grad, value_grad)], axis=2)
-    rows = qkv.shape[0]
     edge, pair = [t.reshape(rows, -1) for t in (pair[:, :span].astype(bfloat), pair[:, span:])]
     return query_grad.astype(bfloat).reshape(rows, -1), edge, pair
 
@@ -463,51 +463,62 @@
     def mine(vector):
         return lax.dynamic_index_in_dim(to_ranks(vector), rank, 0, keepdims=False)
 
+    gain_one, q_weight, k_weight, v_weight = lax.optimization_barrier((gain_one, q_weight, k_weight, v_weight))
     qkv_parts = jnp.concatenate([to_ranks(q_weight), to_ranks(k_weight), to_ranks(v_weight)], axis=2)
     qkv_mine = lax.all_to_all(qkv_parts, PLANE, split_axis=0, concat_axis=0, tiled=True)
-    weight_qkv = lax.all_gather(qkv_mine.reshape(D // Z, 3 * cols), "z", axis=0, tiled=True)
-    weight_qkv = weight_qkv.reshape(Z, B, X, rows_dev, 3 * cols).transpose(1, 0, 2, 3, 4).reshape(D, 3 * cols)
-    bias_qkv = jnp.concatenate([mine(bias_q), jnp.zeros((cols,), single), mine(bias_v)])
+    qkv_mine = qkv_mine.reshape(D // Z, 3 * cols)
+
+    def feature_rows(mine):
+        full = lax.all_gather(mine, "z", axis=0, tiled=True)
+        return full.reshape(Z, B, X, rows_dev, -1).transpose(1, 0, 2, 3, 4).reshape(D, -1)
+
+    weight_kv = feature_rows(qkv_mine[:, cols:])
+    bias_kv = jnp.concatenate([jnp.zeros((cols,), single), mine(bias_v)])
+    normed_low = layer_norm(local, gain_one, bias_one).astype(bfloat)
+    fast = (B, X) == (4, 2)
+
+    def gather_plane(rows, cid, name):
+        if fast:
+            return plane_gather(rows, (), [], None, cid, name)[0]
+        return lax.all_gather(rows, PLANE, axis=0, tiled=True)
+
+    def gather_plane_dot(rows, weight, shift, out_type, turned, cid, name):
+        if fast:
+            return gather_dot(rows, weight, shift, out_type, turned, cid, name)
+        rows = lax.all_gather(rows, PLANE, axis=0, tiled=True)
+        return rows, ((dot_nt if turned else dot)(rows, weight) + shift).astype(out_type)
+
+    def reduce_plane(left, weight, turned, cid, name):
+        if fast:
+            return dot_reduce(left, weight, turned, cid, name)
+        terms = (dot_nt if turned else dot)(left, weight).astype(bfloat)
+        return lax.psum_scatter(terms, PLANE, scatter_dimension=0, tiled=True).astype(single)
+
+    normed_all = gather_plane(normed_low, 0, "gather_normed")
+    normed_all, weight_kv, query_mine, o_weight, fc1_weight, fc2_weight = lax.optimization_barrier(
+        (normed_all, weight_kv, qkv_mine[:, :cols], o_weight, fc1_weight, fc2_weight)
+    )
+    weight_q = feature_rows(query_mine)
     if whole_heads:
         weight_o = lax.all_gather(o_weight, "z", axis=0, tiled=True)
     else:
         weight_o = lax.dynamic_slice_in_dim(lax.all_gather(o_weight, ALL, axis=0, tiled=True), rank * cols, cols, 0)
     weight_up = lax.all_gather(fc1_weight, "z", axis=1, tiled=True)
     weight_down = lax.all_gather(fc2_weight, "z", axis=0, tiled=True)
-
-    normed_low = layer_norm(local, gain_one, bias_one).astype(bfloat)
-    fast = (B, X) == (4, 2)
-
-    def gather_plane(rows, cid, name):
-        if fast:
-            return plane_gather(rows, (), [], None, cid, name)[0]
-        return lax.all_gather(rows, PLANE, axis=0, tiled=True)
-
-    def gather_plane_dot(rows, weight, shift, out_type, turned, cid, name):
-        if fast:
-            return gather_dot(rows, weight, shift, out_type, turned, cid, name)
-        rows = lax.all_gather(rows, PLANE, axis=0, tiled=True)
-        return rows, ((dot_nt if turned else dot)(rows, weight) + shift).astype(out_type)
-
-    def reduce_plane(left, weight, turned, cid, name):
-        if fast:
-            return dot_reduce(left, weight, turned, cid, name)
-        terms = (dot_nt if turned else dot)(left, weight).astype(bfloat)
-        return lax.psum_scatter(terms, PLANE, scatter_dimension=0, tiled=True).astype(single)
-
-    normed_all = gather_plane(normed_low, 0, "gather_normed")
-    qkv = (dot(normed_all, weight_qkv) + bias_qkv).astype(bfloat)
+    key_value = (dot(normed_all, weight_kv) + bias_kv).astype(bfloat)
     up = [(i, i + 1) for i in range(Z - 1)]
     down = [(i + 1, i) for i in range(Z - 1)]
     cotangent = out_grad[0].astype(single) * (group_tok / active_total)
     branch_grad = (active * cotangent).astype(bfloat)
     down_b_grad = column_sums(branch_grad)
-    qkv, branch_grad = lax.optimization_barrier((qkv, branch_grad))
-    before = lax.ppermute(qkv[:, cols:], "z", up)
+    key_value, branch_grad = lax.optimization_barrier((key_value, branch_grad))
+    before = lax.ppermute(key_value, "z", up)
     branch_all = gather_plane(branch_grad, 7, "gather_branch")
-    before, branch_all = lax.optimization_barrier((before, branch_all))
+    branch_all, late_normed = lax.optimization_barrier((branch_all, normed_all))
+    query = (dot(late_normed, weight_q) + mine(bias_q)).astype(bfloat)
+    before, query = lax.optimization_barrier((before, query))
     starts = starts.reshape(B * span, 1)
-    context = attention_forward(starts, qkv, before, B)
+    context = attention_forward(starts, query, key_value, before, B)
 
     attended = reduce_plane(context, weight_o, False, 1, "attended") + bias_o
     middle = local + active * attended
@@ -522,8 +533,8 @@
     up_b_grad = column_sums(pre_grad)
     hidden, pre_grad, down_w_grad, up_w_grad = lax.optimization_barrier((hidden, pre_grad, down_w_grad, up_w_grad))
     normed_two_grad = reduce_plane(pre_grad, weight_up, True, 3, "up_grad")
-    down_w_shard = lax.psum_scatter(down_w_grad, "z", scatter_dimension=0, tiled=True).astype(single)
-    up_w_shard = lax.psum_scatter(up_w_grad, "z", scatter_dimension=1, tiled=True).astype(single)
+    down_w_shard = lax.psum_scatter(down_w_grad, "z", scatter_dimension=0, tiled=True)
+    up_w_shard = lax.psum_scatter(up_w_grad, "z", scatter_dimension=1, tiled=True)
 
     middle_part, gain_two_grad, bias_two_grad = norm_backward(middle, normed_two_grad, gain_two)
     middle_grad = cotangent + middle_part
@@ -532,15 +543,17 @@
     attended_all, context_grad = gather_plane_dot(
         attended_grad, weight_o, jnp.zeros((1, cols), single), bfloat, True, 5, "attended_grad"
     )
+    context_grad, down_w_shard = lax.optimization_barrier((context_grad, down_w_shard))
     out_w_grad = dot_tn(context, attended_all)
-    query_grad, edge, pair = attention_backward(starts, qkv, before, context_grad, B)
+    query_grad, edge, pair = attention_backward(starts, query, key_value, before, context_grad, B)
     hidden, edge, pair = lax.optimization_barrier((hidden, edge, pair))
     after = lax.ppermute(edge, "z", down)
     branch = reduce_plane(hidden, weight_down, False, 4, "down")
-    branch, after = lax.optimization_barrier((branch, after))
+    branch, after, up_w_shard = lax.optimization_barrier((branch, after, up_w_shard))
     outputs = middle + active * (branch + bias_down)
     pair_grad = (pair + after.astype(single)).astype(bfloat)
     qkv_grad = jnp.concatenate([query_grad, pair_grad], axis=1)
+    weight_qkv = jnp.concatenate([weight_q, weight_kv], axis=1)
     normed_grad = reduce_plane(qkv_grad, weight_qkv, True, 6, "qkv_grad")
     qkv_w_grad = dot_tn(normed_all, qkv_grad)
     qkv_b_grad = column_sums(qkv_grad)
@@ -590,9 +603,9 @@
         sums[2],
         sums[3],
         sums[4],
-        up_w_shard,
+        up_w_shard.astype(single),
         up_b_shard,
-        down_w_shard,
+        down_w_shard.astype(single),
         sums[5],
     )
 

time: 881 us -> 791 us (0.90)
  waiting for transfers between devices: 192 us -> 91.3 us
    reduce_scatter x1, waiting for transfers between devices: 76.9 us -> 0.02 us  [on_device(): lax.psum_scatter(down_w_grad, 'z', scatter_dimension=0, tiled=True)]
    reduce_scatter x1, waiting for transfers between devices: 72 us -> 0.02 us  [on_device(): lax.psum_scatter(up_w_grad, 'z', scatter_dimension=1, tiled=True)]
    all_gather x1, waiting for transfers between devices: 0.02 us -> 34.2 us  [on_device(): weight_down = lax.all_gather(fc2_weight, 'z', axis=0, tiled=True)]
    ppermute x1, waiting for transfers between devices: 0.01 us -> 20.4 us  [on_device(): after = lax.ppermute(edge, 'z', down)]
    ppermute x1, waiting for transfers between devices: 35.1 us -> 15.5 us  [on_device(): before = lax.ppermute(key_value, 'z', up)]
    all_gather x1, waiting for transfers between devices: 0.01 us -> 9.56 us  [on_device(): weight_up = lax.all_gather(fc1_weight, 'z', axis=1, tiled=True)]
  transfers between devices with their start and end apart: 13 -> 14, of which waited for: 4 -> 6; matrix products, arithmetic and copies ran while one was open for 6% -> 11% of each run, Pallas kernels for 33% -> 53%
where the time goes in v4:
time: 791 us; the launch traced here: 783 us
  Pallas kernels  415 us (52%)
  waiting for transfers between devices  91.3 us (12%)
  blocking collectives  84.9 us (11%)
  matrix products  80.2 us (10%)
  other arithmetic  42 us (5%)
  local copies, waits for them, and re-layouts  36.4 us (5%)
  starting transfers between devices  17.2 us (2%)
  between operations  16.3 us (2%)
    pallas_call x4, Pallas kernels, dot_reduce(): pl.pallas_call(functools.partial(reduce_kernel, turned), out_shape=jax.Sh...  200 us
    pallas_call x4, Pallas kernels, plane_gather(): pl.pallas_call(functools.partial(gather_kernel, body_of, len(ins), len(ou...  169 us
    all_gather x1, blocking collectives, on_device(): lax.all_gather(jnp.concatenate([pack, jnp.zeros((pad,), single)]), ALL, a...  70.2 us
    dot_general x4, matrix products, dot_tn(): lax.dot_general(left, right, (((0,), (0,)), ((), ())), preferred_element_...  44.2 us
    all_gather x1, waiting for transfers between devices, on_device(): weight_down = lax.all_gather(fc2_weight, 'z', axis=0, tiled=True)  34.2 us
    pallas_call x1, Pallas kernels, attend_back(): pl.pallas_call(attend_back_kernel, grid=(groups,), out_shape=[jax.ShapeDt...  33.7 us
    ppermute x1, waiting for transfers between devices, on_device(): after = lax.ppermute(edge, 'z', down)  20.4 us
    dot_general x1, matrix products, dot_nt(): lax.dot_general(left, right, (((1,), (1,)), ((), ())), preferred_element_...  20.3 us
  transfers between devices with their start and end apart: 14, of which 6 were waited for; matrix products, arithmetic and copies ran while one was open for 11% of the time, Pallas kernels for 53%

profile of v4, /device:TPU:0, one launch (start us, length us, event | category | flops | bytes accessed | tf_op | source)
XLA Modules:
  0.0 783.4 jit_solution(6311626376172310322)
XLA Ops:
  7.9 6.1 concatenate.21
  14.0 70.2 %all-gather.1 = f32[32,1,896]{2,1,0:T(1,128)S(1)} all-gather(f32[1,1,896]{2,1,0:T(1,128)S(1)} %reshape.313), channel_id=2, replica_groups=mesh['b'=4,'z'=4,'x'=2] {'b','z','x'}, dimensions={0}, use_global_device_ids=true | all-gather | bytes 118272 | tf_op jit(solution)/shard_map/all_gather | solution.py:435
  88.5 14.6 %all_to_all.28 = bf16[8,64,768]{2,1,0:T(8,128)(2,1)S(1)} all-to-all(bf16[8,64,768]{2,1,0:T(8,128)(2,1)S(1)} %pad_maximum_fusion.2), channel_id=1, replica_groups=mesh['b'=4,'z'=4,'x'=2] {'b','x'}, dimensions={0} | all-to-all | bytes 1572864 | tf_op jit(solution)/shard_map/all_to_all | solution.py:468
  106.2 40.4 %gather_normed.1 = bf16[8,256,2048]{2,1,0:T(8,128)(2,1)} custom-call(bf16[256,2048]{1,0:T(8,128)(2,1)} %fusion.20.x_ref), custom_call_target="tpu_custom_call" | custom-call | flops 1073741824 | bytes 134217728 | tf_op jit(solution)/shard_map/gather_normed/pallas_call | solution.py:108
  156.3 8.6 %add_convert_fusion.1.k_ref.v_ref = bf16[2048,512]{1,0:T(8,128)(2,1)S(1)} fusion(bf16[2048,2048]{1,0:T(8,128)(2,1)} %bitcast.151, bf16[2048,512]{1,0:T(8,128)(2,1)} %bitcast.149, f32[512]{0:T(512)S(1)} %concatenate.23), kind=kOutput, calls=%fused_computation.17 | convolution fusion | flops 4297064448 | bytes 12584960 | tf_op jit(solution)/shard_map/dot_general | solution.py:219
  170.6 41.0 %gather_branch.1 = bf16[8,256,2048]{2,1,0:T(8,128)(2,1)} custom-call(bf16[256,2048]{1,0:T(8,128)(2,1)} %get-tuple-element.59.x_ref), custom_call_target="tpu_custom_call" | custom-call | flops 1073741824 | bytes 134217728 | tf_op jit(solution)/shard_map/gather_branch/pallas_call | solution.py:108
  212.9 7.1 fusion.12.q_ref
  220.0 15.5 %collective-permute-done.kb_ref.vb_ref = bf16[2048,512]{1,0:T(8,128)(2,1)} collective-permute-done((bf16[2048,512]{1,0:T(8,128)(2,1)S(1)}, bf16[2048,512]{1,0:T(8,128)(2,1)}, u32[]{:S(2)}, u32[]{:S(2)}) %collective-permute-start) | collective-permute-done | bytes 2097184 | tf_op jit(solution)/shard_map/ppermute | solution.py:515
  235.5 13.1 %attend.1 = bf16[2048,256]{1,0:T(8,128)(2,1)} custom-call(s32[2048,1]{1,0:T(8,128)} %bitcast.147, bf16[2048,256]{1,0:T(8,128)(2,1)} %fusion.12.q_ref, bf16[2048,512]{1,0:T(8,128)(2,1)} %copy-done.1, bf16[2048,512]{1,0:T(8,128)(2,1)} %copy-done.1, bf16[2048,512]{1,0:T(8,128)(2,1)} %collective-permute-done.kb_ref.vb_ref, ...), custom_call_target="tpu_custom_call" | custom-call | tf_op jit(solution)/shard_map/attend/pallas_call | solution.py:316
  248.7 45.7 %attended.1 = f32[256,2048]{1,0:T(8,128)} custom-call(bf16[8,256,256]{2,1,0:T(8,128)(2,1)} %bitcast.144, bf16[256,2048]{1,0:T(8,128)(2,1)} %all-gather.12.cloned.1.call-done.w_ref.refs_0_), custom_call_target="tpu_custom_call" | custom-call | flops 1073741824 | bytes 134217728 | tf_op jit(solution)/shard_map/attended/pallas_call | solution.py:206
  298.3 9.6 %all-gather.14.cloned.1.call-done.refs_0_.w_ref = bf16[2048,1024]{1,0:T(8,128)(2,1)} async-done(((bf16[2048,256]{1,0:T(8,128)(2,1)}), bf16[2048,1024]{1,0:T(8,128)(2,1)}) %all-gather.14.cloned.1.call-update) | async-done | bytes 4194320 | tf_op jit(solution)/shard_map/all_gather | solution.py:506
  307.9 46.1 %up.1 = (bf16[8,256,2048]{2,1,0:T(8,128)(2,1)}, f32[8,256,1024]{2,1,0:T(8,128)}) custom-call(bf16[256,2048]{1,0:T(8,128)(2,1)} %add_convert_fusion.3.x_ref, bf16[2048,1024]{1,0:T(8,128)(2,1)} %all-gather.14.cloned.1.call-done.refs_0_.w_ref, f32[1,1024]{1,0:T(1,128)} %constant_dynamic-slice_fusion.2.refs_1_), custom_call_target="tpu_custom_call" | custom-call | flops 1073741824 | bytes 134217728 | tf_op jit(solution)/shard_map/up/pallas_call | solution.py:108
  354.0 34.2 %all-gather.16.cloned.1.call-done.w_ref = bf16[1024,2048]{1,0:T(8,128)(2,1)} async-done(((bf16[256,2048]{1,0:T(8,128)(2,1)}), bf16[1024,2048]{1,0:T(8,128)(2,1)}) %all-gather.16.cloned.1.call-update) | async-done | bytes 4194320 | tf_op jit(solution)/shard_map/all_gather | solution.py:507
  388.3 20.3 %convert_reduce_fusion = (f32[1024]{0:T(1024)S(1)}, bf16[2048,1024]{1,0:T(8,128)(2,1)}, bf16[2048,1024]{1,0:T(8,128)(2,1)S(1)}) fusion(f32[8,256,1024]{2,1,0:T(8,128)} %get-tuple-element.66, bf16[2048,2048]{1,0:T(8,128)(2,1)} %bitcast.154, bf16[1024,2048]{1,0:T(8,128)(2,1)} %all-gather.16.cloned.1.call-done.w_ref), kind=kOutput, calls=%fused_computation.14 | convolution fusion | flops 8640265216 | bytes 29364224 | tf_op jit(solution)/shard_map/dot_general | solution.py:227
  410.5 12.7 %convolution_convert_fusion = bf16[1024,2048]{1,0:T(8,128)(2,1)} fusion(bf16[2048,1024]{1,0:T(8,128)(2,1)S(1)} %get-tuple-element.77, bf16[2048,2048]{1,0:T(8,128)(2,1)} %bitcast.155), kind=kOutput, calls=%fused_computation.18 | convolution fusion | flops 8592031744 | bytes 16777216 | tf_op jit(solution)/shard_map/dot_general | solution.py:223
  423.3 14.4 %convolution_convert_fusion.1 = bf16[2048,1024]{1,0:T(8,128)(2,1)} fusion(bf16[2048,2048]{1,0:T(8,128)(2,1)} %bitcast.186, bf16[2048,1024]{1,0:T(8,128)(2,1)} %get-tuple-element.71), kind=kOutput, calls=%fused_computation.19 | convolution fusion | flops 8592031744 | bytes 16777216 | tf_op jit(solution)/shard_map/dot_general | solution.py:223
  438.4 51.9 %up_grad.1 = f32[256,2048]{1,0:T(8,128)} custom-call(bf16[8,256,1024]{2,1,0:T(8,128)(2,1)} %bitcast.157, bf16[2048,1024]{1,0:T(8,128)(2,1)} %all-gather.14.cloned.1.call-done.refs_0_.w_ref), custom_call_target="tpu_custom_call" | custom-call | flops 1073741824 | bytes 134217728 | tf_op jit(solution)/shard_map/up_grad/pallas_call | solution.py:206
  496.3 41.2 %attended_grad.1 = (bf16[8,256,2048]{2,1,0:T(8,128)(2,1)}, bf16[8,256,256]{2,1,0:T(8,128)(2,1)}) custom-call(bf16[256,2048]{1,0:T(8,128)(2,1)} %get-tuple-element.100.x_ref, bf16[256,2048]{1,0:T(8,128)(2,1)} %all-gather.12.cloned.1.call-done.w_ref.refs_0_, f32[1,256]{1,0:T(1,128)} %broadcast_in_dim.39.refs_1_), custom_call_target="tpu_custom_call" | custom-call | flops 1073741824 | bytes 134217728 | tf_op jit(solution)/shard_map/attended_grad/pallas_call | solution.py:108
  537.5 33.7 %attend_back.1 = (bf16[2048,256]{1,0:T(8,128)(2,1)}, bf16[2048,512]{1,0:T(8,128)(2,1)}, f32[2048,512]{1,0:T(8,128)}) custom-call(s32[2048,1]{1,0:T(8,128)} %bitcast.148, bf16[2048,256]{1,0:T(8,128)(2,1)} %fusion.12.q_ref, bf16[2048,512]{1,0:T(8,128)(2,1)} %copy-done.1, bf16[2048,512]{1,0:T(8,128)(2,1)} %copy-done.1, ...), custom_call_target="tpu_custom_call" | custom-call | tf_op jit(solution)/shard_map/attend_back/pallas_call | solution.py:329
  572.5 7.0 convolution_convert_fusion.3
  579.6 52.1 %down.1 = f32[256,2048]{1,0:T(8,128)} custom-call(bf16[8,256,1024]{2,1,0:T(8,128)(2,1)} %bitcast.156, bf16[1024,2048]{1,0:T(8,128)(2,1)} %all-gather.16.cloned.1.call-done.w_ref), custom_call_target="tpu_custom_call" | custom-call | flops 1073741824 | bytes 134217728 | tf_op jit(solution)/shard_map/down/pallas_call | solution.py:206
  631.8 20.4 %collective-permute-done.1 = bf16[2048,512]{1,0:T(8,128)(2,1)} collective-permute-done((bf16[2048,512]{1,0:T(8,128)(2,1)}, bf16[2048,512]{1,0:T(8,128)(2,1)}, u32[]{:S(2)}, u32[]{:S(2)}) %collective-permute-start.1) | collective-permute-done | bytes 2097184 | tf_op jit(solution)/shard_map/ppermute | solution.py:550
  655.9 10.1 %convolution_convert_fusion.2 = bf16[2048,768]{1,0:T(8,128)(2,1)S(1)} fusion(bf16[2048,2048]{1,0:T(8,128)(2,1)} %bitcast.153, bf16[2048,512]{1,0:T(8,128)(2,1)S(1)} %add_convert_fusion, bf16[2048,256]{1,0:T(8,128)(2,1)S(1)} %copy-done.7), kind=kOutput, calls=%fused_computation.20 | convolution fusion | flops 6450315264 | bytes 14680064 | tf_op jit(solution)/shard_map/dot_general | solution.py:223
  685.8 49.9 %qkv_grad.1 = f32[256,2048]{1,0:T(8,128)} custom-call(bf16[8,256,768]{2,1,0:T(8,128)(2,1)} %bitcast.146, bf16[2048,768]{1,0:T(8,128)(2,1)} %pad_maximum_fusion.1.w_ref), custom_call_target="tpu_custom_call" | custom-call | flops 1073741824 | bytes 134217728 | tf_op jit(solution)/shard_map/qkv_grad/pallas_call | solution.py:206
  (170 shorter events, 101.1 us)
Async XLA Ops:
  7.2 79.2 %copy-start.12 = (bf16[64,2048]{1,0:T(8,128)(2,1)S(1)}, bf16[64,2048]{1,0:T(8,128)(2,1)}, u32[]{:S(2)}) copy-start(bf16[64,2048]{1,0:T(8,128)(2,1)} %param.29) | copy-start | bytes 786436
  7.2 140.1 %all-gather.8.cloned.1.call-start = ((), (), s32[]{:S(2)}) async-start(), calls=%async_computation.8 | async-start | bytes 2621440 | tf_op jit(solution)/shard_map/all_gather | solution.py:472
  88.4 15.7 %copy-start = (bf16[1,256,2048]{2,1,0:T(8,128)(2,1)S(1)}, bf16[1,256,2048]{2,1,0:T(8,128)(2,1)}, u32[]{:S(2)}) copy-start(bf16[1,256,2048]{2,1,0:T(8,128)(2,1)} %param.20) | copy-start | bytes 3145732
  104.0 107.6 %all-gather.10.cloned.1.call-start = ((), (), s32[]{:S(2)}) async-start(), calls=%async_computation.9 | async-start | bytes 1310720 | tf_op jit(solution)/shard_map/all_gather | solution.py:472
  150.4 3.2 copy-start.14
  150.4 4.5 copy-start.9
  150.5 98.2 %all-gather.12.cloned.1.call-start = ((), (), s32[]{:S(2)}) async-start(), calls=%async_computation.10 | async-start | bytes 1310720 | tf_op jit(solution)/shard_map/all_gather | solution.py:503
  151.2 156.7 %all-gather.14.cloned.1.call-start = ((), (), s32[]{:S(2)}) async-start(), calls=%async_computation.11 | async-start | bytes 5242880 | tf_op jit(solution)/shard_map/all_gather | solution.py:506
  151.8 236.5 %all-gather.16.cloned.1.call-start = ((), (), s32[]{:S(2)}) async-start(), calls=%async_computation.12 | async-start | bytes 5242880 | tf_op jit(solution)/shard_map/all_gather | solution.py:507
  152.4 385.1 %reduce-scatter.5.cloned.1.call-start = ((), (), s32[]{:S(2)}) async-start(), calls=%async_computation.13 | async-start | bytes 5242880 | tf_op jit(solution)/shard_map/reduce_scatter | solution.py:536
  164.9 46.7 %copy-start.1 = (bf16[2048,512]{1,0:T(8,128)(2,1)}, bf16[2048,512]{1,0:T(8,128)(2,1)S(1)}, u32[]{:S(2)}) copy-start(bf16[2048,512]{1,0:T(8,128)(2,1)S(1)} %add_convert_fusion.1.k_ref.v_ref) | copy-start | bytes 6291460
  164.9 70.7 %collective-permute-start = (bf16[2048,512]{1,0:T(8,128)(2,1)S(1)}, bf16[2048,512]{1,0:T(8,128)(2,1)}, u32[]{:S(2)}, u32[]{:S(2)}) collective-permute-start(bf16[2048,512]{1,0:T(8,128)(2,1)S(1)} %add_convert_fusion.1.k_ref.v_ref), channel_id=1, source_target_pairs={{0,2},{2,4},{4,6},{1,3},{3,5},{5,7},{8,10},{10,12},{12,14},{9,11},... | collective-permute-start | bytes 6291464 | tf_op jit(solution)/shard_map/ppermute | solution.py:515
  212.9 7.1 copy-start.6
  437.6 194.2 %reduce-scatter.7.cloned.1.call-start = ((), (), s32[]{:S(2)}) async-start(), calls=%async_computation.14 | async-start | bytes 5242880 | tf_op jit(solution)/shard_map/reduce_scatter | solution.py:537
  438.4 233.6 %reduce-scatter.11.cloned.1.call-start = ((), (), s32[]{:S(2)}) async-start(), calls=%async_computation.16 | async-start | bytes 1310720 | tf_op jit(solution)/shard_map/reduce_scatter | solution.py:576
  571.2 81.0 %collective-permute-start.1 = (bf16[2048,512]{1,0:T(8,128)(2,1)}, bf16[2048,512]{1,0:T(8,128)(2,1)}, u32[]{:S(2)}, u32[]{:S(2)}) collective-permute-start(bf16[2048,512]{1,0:T(8,128)(2,1)} %get-tuple-element.78), channel_id=1, source_target_pairs={{2,0},{4,2},{6,4},{3,1},{5,3},{7,5},{10,8},{12,10},{14,12},{11,9},... | collective-permute-start | bytes 6291464 | tf_op jit(solution)/shard_map/ppermute | solution.py:550
  579.6 171.7 %reduce-scatter.9.cloned.1.call-start = ((), (), s32[]{:S(2)}) async-start(), calls=%async_computation.15 | async-start | bytes 3932160 | tf_op jit(solution)/shard_map/reduce_scatter | solution.py:571
  631.8 24.1 %copy-start.7 = (bf16[2048,256]{1,0:T(8,128)(2,1)S(1)}, bf16[2048,256]{1,0:T(8,128)(2,1)}, u32[]{:S(2)}) copy-start(bf16[2048,256]{1,0:T(8,128)(2,1)} %get-tuple-element.81) | copy-start | bytes 3145732
  655.9 10.1 %copy-start.3 = (bf16[2048,512]{1,0:T(8,128)(2,1)}, bf16[2048,512]{1,0:T(8,128)(2,1)S(1)}, u32[]{:S(2)}) copy-start(bf16[2048,512]{1,0:T(8,128)(2,1)S(1)} %add_convert_fusion) | copy-start | bytes 6291460
  672.0 4.8 copy-start.4
  672.0 4.8 copy-start.8
  678.1 61.1 %all-to-all-start.3 = ((f32[4,1,384]{2,1,0:T(1,128)}), f32[4,1,384]{2,1,0:T(1,128)S(1)}, u32[]{:S(2)}, u32[]{:S(2)}) async-start(f32[4,1,384]{2,1,0:T(1,128)} %all_to_all.22), calls=%async_computation.6 | async-start | bytes 12288 | tf_op jit(solution)/shard_map/all_to_all | solution.py:565
  739.2 12.0 %all-to-all-start.1 = ((f32[32,1,384]{2,1,0:T(1,128)}), f32[32,1,384]{2,1,0:T(1,128)S(1)}, u32[]{:S(2)}, u32[]{:S(2)}) async-start(f32[32,1,384]{2,1,0:T(1,128)} %all_to_all.19), calls=%async_computation.3 | async-start | bytes 98304 | tf_op jit(solution)/shard_map/all_to_all | solution.py:565
  751.3 15.9 %all-to-all-start.2 = ((bf16[8,64,768]{2,1,0:T(8,128)(2,1)}), bf16[8,64,768]{2,1,0:T(8,128)(2,1)S(1)}, u32[]{:S(2)}, u32[]{:S(2)}) async-start(bf16[8,64,768]{2,1,0:T(8,128)(2,1)} %bitcast.172), calls=%async_computation.5 | async-start | bytes 1572864 | tf_op jit(solution)/shard_map/all_to_all | solution.py:572
  (5 other events, 11.8 us)
Sparse Core Ops, SparseCore 0:
  104.1 42.7 all-gather.7
  150.6 29.6 all-gather.9
  181.8 43.4 all-gather.11
  226.7 81.1 all-gather.13
  309.3 78.9 all-gather.15
  437.8 75.2 reduce-scatter.4
  515.5 90.5 reduce-scatter.6
  608.9 46.7 reduce-scatter.10
  668.0 60.0 reduce-scatter.8

commit v5 on v4

--- a/solution.py
+++ b/solution.py
@@ -238,6 +238,196 @@
     return jnp.sum(matrix.astype(single), axis=0)
 
 
+def shipper(send, recv, ids):
+    started = []
+    def ship(src, dst, to):
+        n = len(started)
+        copy = pltpu.make_async_remote_copy(
+            src_ref=src, dst_ref=dst, send_sem=send.at[n], recv_sem=recv.at[n], device_id=ids[to], device_id_type=MESH
+        )
+        copy.start()
+        started.append(copy)
+        return copy
+    return ship, started
+
+def ffn_kernel(x_ref, bg_ref, w1_ref, w2_ref, b_ref, hid_ref, pb_ref, r_ref, down_ref, up_ref,
+               held, bg, pg_ref, sib_out, sib_in, stage, landed, rows_out, send, recv, keep, load, store):
+    ids, at = plane_place()
+    tok, D = x_ref.shape
+    F = w1_ref.shape[1]
+    mid = D // 2
+    half = tok // 2
+    parts = (pl.ds(0, half), pl.ds(half, half))
+    own = at["o"]
+    loads = {}
+    for n, name in enumerate(at):
+        loads[name] = pltpu.make_async_copy(bg_ref.at[at[name]], bg.at[at[name]], load.at[n])
+        loads[name].start()
+    kept = pltpu.make_async_copy(x_ref, held.at[own], keep)
+    kept.start()
+    pb_ref[...] = jnp.zeros_like(pb_ref)
+    greet(ids)
+    ship, started = shipper(send, recv, ids)
+    x0 = ship(x_ref.at[parts[0]], held.at[own, parts[0]], "x")
+    y1 = ship(x_ref.at[parts[1]], held.at[own, parts[1]], "y")
+    x1 = ship(x_ref.at[parts[1]], held.at[own, parts[1]], "x")
+    y0 = ship(x_ref.at[parts[0]], held.at[own, parts[0]], "y")
+    s0 = ship(x_ref, held.at[own], "s")
+
+    def units(name):
+        rank = at[name]
+        src = x_ref if name == "o" else held.at[rank]
+        loads[name].wait()
+        def body(cols):
+            pre = jnp.dot(src[...], w1_ref[:, cols], preferred_element_type=single) + b_ref[:, cols]
+            square = pre * pre
+            bend = jnp.tanh(0.7978845608028654 * (pre + 0.044715 * (pre * square)))
+            rise = 0.5 * (1.0 + bend)
+            hid_ref[rank, :, cols] = (pre * rise).astype(bfloat)
+            slope = rise + (0.5 * 0.7978845608028654) * pre * (1.0 - bend * bend) * (1.0 + 3 * 0.044715 * square)
+            grad = (dot_nt(bg[rank], w2_ref[cols, :]) * slope).astype(bfloat)
+            pg_ref[rank, :, cols] = grad
+            pb_ref[:, cols] += jnp.sum(grad.astype(single), axis=0, keepdims=True)
+        tiles(0, F, body)
+
+    def term(name, cols):
+        return dot_nt(pg_ref[at[name]], w1_ref[cols, :])
+    order = ("d", "x", "y", "o")
+    twin = {"d": "ds", "x": "xs", "y": "ys", "o": "s"}
+    def to_sibling(j):
+        def fill(cols):
+            sib_out[j, :, cols] = term(twin[order[j]], cols).astype(bfloat)
+        tiles(0, D, fill)
+        return ship(sib_out.at[j], sib_in.at[j], "s")
+    def pair(j, cols):
+        return term(order[j], cols) + sib_in[j, :, cols].astype(single)
+    def local(h, cols):
+        return pl.ds(pl.multiple_of(cols.start - h * mid, TILE), TILE)
+    def put(j, h, extra=None):
+        def fill(cols):
+            value = pair(j, cols)
+            if extra is not None:
+                value = value + landed[extra, :, local(h, cols)].astype(single)
+            stage[j, h, :, local(h, cols)] = value.astype(bfloat)
+        tiles(h * mid, (h + 1) * mid, fill)
+
+    units("o")
+    s0.wait_recv()
+    units("s")
+    x0.wait_recv()
+    ry = ship(held.at[at["x"], parts[0]], held.at[at["x"], parts[0]], "y")
+    y1.wait_recv()
+    rx = ship(held.at[at["y"], parts[1]], held.at[at["y"], parts[1]], "x")
+    own_sib = to_sibling(3)
+    x1.wait_recv()
+    sx = ship(held.at[at["x"]], held.at[at["x"]], "s")
+    y0.wait_recv()
+    sy = ship(held.at[at["y"]], held.at[at["y"]], "s")
+    units("x")
+    sx.wait_recv()
+    units("xs")
+    x_sib = to_sibling(1)
+    units("y")
+    sy.wait_recv()
+    units("ys")
+    y_sib = to_sibling(2)
+    ry.wait_recv()
+    rx.wait_recv()
+    sd = ship(held.at[at["d"]], held.at[at["d"]], "s")
+    x_sib.wait_recv()
+    put(1, 0)
+    x_a = ship(stage.at[1, 0], landed.at[2], "x")
+    y_sib.wait_recv()
+    put(2, 1)
+    y_b = ship(stage.at[2, 1], landed.at[3], "y")
+    sd.wait_recv()
+    units("ds")
+    d_sib = to_sibling(0)
+    units("d")
+    d_sib.wait_recv()
+    put(0, 0)
+    d_a = ship(stage.at[0, 0], landed.at[0], "x")
+    put(0, 1)
+    d_b = ship(stage.at[0, 1], landed.at[1], "y")
+    own_sib.wait_recv()
+    def first(cols):
+        r_ref[:, cols] = pair(3, cols)
+    tiles(0, D, first)
+
+    kept.wait()
+    wide = rows_out.shape[1]
+    def grads(out_ref, count, value):
+        def step(i, _):
+            slot = lax.rem(i, 2)
+            here = pl.ds(pl.multiple_of(i * wide, wide), wide)
+            copy = pltpu.make_async_copy(rows_out.at[slot, :, pl.ds(0, out_ref.shape[1])], out_ref.at[here], store.at[slot])
+            @pl.when(i >= 2)
+            def _():
+                copy.wait()
+            rows_out[slot, :, : out_ref.shape[1]] = value(here).astype(bfloat)
+            copy.start()
+            return 0
+        lax.fori_loop(0, count, step, 0)
+        for slot in range(2):
+            pltpu.make_async_copy(rows_out.at[slot, :, pl.ds(0, out_ref.shape[1])], out_ref.at[pl.ds(0, wide)], store.at[slot]).wait()
+    ranks = held.shape[0]
+    grads(down_ref, F // wide, lambda cols: dot_tn(hid_ref[:, :, cols].reshape(ranks * tok, wide), bg[...].reshape(ranks * tok, D)))
+    d_b.wait_recv()
+    put(1, 1, extra=1)
+    x_b = ship(stage.at[1, 1], landed.at[5], "x")
+    d_a.wait_recv()
+    put(2, 0, extra=0)
+    y_a = ship(stage.at[2, 0], landed.at[4], "y")
+    grads(up_ref, D // wide, lambda cols: dot_tn(held[:, :, cols].reshape(ranks * tok, wide), pg_ref[...].reshape(ranks * tok, F)))
+    for copy in (x_a, y_b, x_b, y_a):
+        copy.wait_recv()
+    for h, (n, m) in enumerate(((2, 4), (3, 5))):
+        def add(cols, h=h, n=n, m=m):
+            c = local(h, cols)
+            r_ref[:, cols] = r_ref[:, cols] + landed[n, :, c].astype(single) + landed[m, :, c].astype(single)
+        tiles(h * mid, (h + 1) * mid, add)
+    for copy in started:
+        copy.wait_send()
+
+def feed_forward(x, bg, w1, w2, bias, cid):
+    ranks = 8
+    tok, D = x.shape
+    F = w1.shape[1]
+    anywhere = pl.BlockSpec(memory_space=pl.ANY)
+    inside = pl.BlockSpec(memory_space=pltpu.VMEM)
+    hid, pb, r, down, up = pl.pallas_call(
+        ffn_kernel,
+        out_shape=[
+            jax.ShapeDtypeStruct((ranks, tok, F), bfloat),
+            jax.ShapeDtypeStruct((1, F), single),
+            jax.ShapeDtypeStruct((tok, D), single),
+            jax.ShapeDtypeStruct((F, D), bfloat),
+            jax.ShapeDtypeStruct((D, F), bfloat),
+        ],
+        in_specs=[inside, anywhere, inside, inside, inside],
+        out_specs=[inside, inside, inside, anywhere, anywhere],
+        scratch_shapes=[
+            pltpu.VMEM((ranks, tok, D), bfloat),
+            pltpu.VMEM((ranks, tok, D), bfloat),
+            pltpu.VMEM((ranks, tok, F), bfloat),
+            pltpu.VMEM((4, tok, D), bfloat),
+            pltpu.VMEM((4, tok, D), bfloat),
+            pltpu.VMEM((3, 2, tok, D // 2), bfloat),
+            pltpu.VMEM((6, tok, D // 2), bfloat),
+            pltpu.VMEM((2, 128, D), bfloat),
+            pltpu.SemaphoreType.DMA((20,)),
+            pltpu.SemaphoreType.DMA((20,)),
+            pltpu.SemaphoreType.DMA,
+            pltpu.SemaphoreType.DMA((8,)),
+            pltpu.SemaphoreType.DMA((2,)),
+        ],
+        compiler_params=pltpu.CompilerParams(collective_id=cid, has_side_effects=True, vmem_limit_bytes=63 << 20),
+        cost_estimate=pl.CostEstimate(flops=1 << 30, bytes_accessed=256 << 20, transcendentals=0),
+        name="feed_forward",
+    )(x, bg.reshape(ranks, tok, D), w1, w2, bias)
+    return hid.reshape(ranks * tok, F), pb[0], r, down, up
+
+
 def windows(span):
     block = span // 2
     return [(i * block, i * block + block + span) for i in range(2)]
@@ -432,7 +622,8 @@
     small = [ln1_gain, ln1_bias, q_bias, v_bias, o_bias, ln2_gain, ln2_bias, fc2_bias]
     pack = jnp.concatenate([v.astype(single) for v in (*small, fc1_bias, lengths[0])])
     pad = -pack.shape[0] % 128
-    pack = lax.all_gather(jnp.concatenate([pack, jnp.zeros((pad,), single)]), ALL, axis=0)
+    pack = jnp.concatenate([pack, jnp.zeros((pad,), single)])
+    pack = lax.all_to_all(jnp.broadcast_to(pack, (R * Z, pack.shape[0])), ALL, split_axis=0, concat_axis=0, tiled=True)
     vectors = [pack[:, i * rows_dev : (i + 1) * rows_dev].reshape(-1) for i in range(len(small))]
     gain_one, bias_one, bias_q, bias_v, bias_o, gain_two, bias_two, bias_down = vectors
     pack = pack.reshape(B, Z, X, -1)[..., len(small) * rows_dev :]
@@ -464,6 +655,10 @@
         return lax.dynamic_index_in_dim(to_ranks(vector), rank, 0, keepdims=False)
 
     gain_one, q_weight, k_weight, v_weight = lax.optimization_barrier((gain_one, q_weight, k_weight, v_weight))
+    if whole_heads:
+        weight_o = lax.all_gather(o_weight, "z", axis=0, tiled=True)
+    else:
+        weight_o = lax.dynamic_slice_in_dim(lax.all_gather(o_weight, ALL, axis=0, tiled=True), rank * cols, cols, 0)
     qkv_parts = jnp.concatenate([to_ranks(q_weight), to_ranks(k_weight), to_ranks(v_weight)], axis=2)
     qkv_mine = lax.all_to_all(qkv_parts, PLANE, split_axis=0, concat_axis=0, tiled=True)
     qkv_mine = qkv_mine.reshape(D // Z, 3 * cols)
@@ -475,6 +670,7 @@
     weight_kv = feature_rows(qkv_mine[:, cols:])
     bias_kv = jnp.concatenate([jnp.zeros((cols,), single), mine(bias_v)])
     normed_low = layer_norm(local, gain_one, bias_one).astype(bfloat)
+    normed_low, weight_o = lax.optimization_barrier((normed_low, weight_o))
     fast = (B, X) == (4, 2)
 
     def gather_plane(rows, cid, name):
@@ -495,14 +691,10 @@
         return lax.psum_scatter(terms, PLANE, scatter_dimension=0, tiled=True).astype(single)
 
     normed_all = gather_plane(normed_low, 0, "gather_normed")
-    normed_all, weight_kv, query_mine, o_weight, fc1_weight, fc2_weight = lax.optimization_barrier(
-        (normed_all, weight_kv, qkv_mine[:, :cols], o_weight, fc1_weight, fc2_weight)
+    normed_all, weight_kv, query_mine, fc1_weight, fc2_weight = lax.optimization_barrier(
+        (normed_all, weight_kv, qkv_mine[:, :cols], fc1_weight, fc2_weight)
     )
     weight_q = feature_rows(query_mine)
-    if whole_heads:
-        weight_o = lax.all_gather(o_weight, "z", axis=0, tiled=True)
-    else:
-        weight_o = lax.dynamic_slice_in_dim(lax.all_gather(o_weight, ALL, axis=0, tiled=True), rank * cols, cols, 0)
     weight_up = lax.all_gather(fc1_weight, "z", axis=1, tiled=True)
     weight_down = lax.all_gather(fc2_weight, "z", axis=0, tiled=True)
     key_value = (dot(normed_all, weight_kv) + bias_kv).astype(bfloat)
@@ -523,16 +715,20 @@
     attended = reduce_plane(context, weight_o, False, 1, "attended") + bias_o
     middle = local + active * attended
     normed_two = layer_norm(middle, gain_two, bias_two).astype(bfloat)
-    two_all, hidden_pre = gather_plane_dot(normed_two, weight_up, bias_up[None], single, False, 2, "up")
-    gelu_value, gelu_pull = jax.vjp(partial(jax.nn.gelu, approximate=True), hidden_pre)
-    hidden = gelu_value.astype(bfloat)
-    hidden_grad = dot_nt(branch_all, weight_down)
-    pre_grad = gelu_pull(hidden_grad)[0].astype(bfloat)
-    down_w_grad = dot_tn(hidden, branch_all).astype(bfloat)
-    up_w_grad = dot_tn(two_all, pre_grad).astype(bfloat)
-    up_b_grad = column_sums(pre_grad)
-    hidden, pre_grad, down_w_grad, up_w_grad = lax.optimization_barrier((hidden, pre_grad, down_w_grad, up_w_grad))
-    normed_two_grad = reduce_plane(pre_grad, weight_up, True, 3, "up_grad")
+    if fast:
+        hidden, up_b_grad, normed_two_grad, down_w_grad, up_w_grad = feed_forward(
+            normed_two, branch_all, weight_up, weight_down, bias_up[None], 2
+        )
+    else:
+        two_all = gather_plane(normed_two, 2, "gather_two")
+        hidden_pre = dot(two_all, weight_up) + bias_up
+        gelu_value, gelu_pull = jax.vjp(partial(jax.nn.gelu, approximate=True), hidden_pre)
+        hidden = gelu_value.astype(bfloat)
+        pre_grad = gelu_pull(dot_nt(branch_all, weight_down))[0].astype(bfloat)
+        down_w_grad = dot_tn(hidden, branch_all).astype(bfloat)
+        up_w_grad = dot_tn(two_all, pre_grad).astype(bfloat)
+        up_b_grad = column_sums(pre_grad)
+        normed_two_grad = reduce_plane(pre_grad, weight_up, True, 3, "up_grad")
     down_w_shard = lax.psum_scatter(down_w_grad, "z", scatter_dimension=0, tiled=True)
     up_w_shard = lax.psum_scatter(up_w_grad, "z", scatter_dimension=1, tiled=True)
 

time: 791 us -> 754 us (0.953)
  waiting for transfers between devices: 91.3 us -> 158 us
  blocking collectives: 84.9 us -> 32.9 us
  matrix products: 80.2 us -> 32.7 us
    pallas_call x0 -> x1, Pallas kernels: none -> 91.5 us  [feed_forward(): pl.pallas_call(ffn_kernel, out_shape=[jax.ShapeDtypeStruct((ranks, tok, F...]
    all_gather x1 -> x0, blocking collectives: 70.2 us -> none  [on_device(): lax.all_gather(jnp.concatenate([pack, jnp.zeros((pad,), single)]), ALL, a...]
    all_gather x1, waiting for transfers between devices: 9.56 us -> 62.7 us  [on_device(): weight_up = lax.all_gather(fc1_weight, 'z', axis=1, tiled=True)]
    pallas_call x4 -> x3, Pallas kernels: 200 us -> 147 us  [dot_reduce(): pl.pallas_call(functools.partial(reduce_kernel, turned), out_shape=jax.Sh...]
    pallas_call x4 -> x3, Pallas kernels: 169 us -> 123 us  [plane_gather(): pl.pallas_call(functools.partial(gather_kernel, body_of, len(ins), len(ou...]
    all_gather x1, waiting for transfers between devices: 34.2 us -> 0.01 us  [on_device(): weight_down = lax.all_gather(fc2_weight, 'z', axis=0, tiled=True)]
    dot_general x4 -> x2, matrix products: 44.2 us -> 16.8 us  [dot_tn(): lax.dot_general(left, right, (((0,), (0,)), ((), ())), preferred_element_...]
    reduce_scatter x1, waiting for transfers between devices: 0.02 us -> 25.4 us  [on_device(): lax.psum_scatter(down_w_grad, 'z', scatter_dimension=0, tiled=True)]
  transfers between devices with their start and end apart: 14 -> 14, of which waited for: 6 -> 8; matrix products, arithmetic and copies ran while one was open for 11% -> 13% of each run, Pallas kernels for 53% -> 42%
where the time goes in v5:
time: 754 us; the launch traced here: 746 us
  Pallas kernels  408 us (54%)
  waiting for transfers between devices  158 us (21%)
  other arithmetic  42 us (6%)
  local copies, waits for them, and re-layouts  38.9 us (5%)
  blocking collectives  32.9 us (4%)
  matrix products  32.7 us (4%)
  starting transfers between devices  17.4 us (2%)
  between operations  16.3 us (2%)
    pallas_call x3, Pallas kernels, dot_reduce(): pl.pallas_call(functools.partial(reduce_kernel, turned), out_shape=jax.Sh...  147 us
    pallas_call x3, Pallas kernels, plane_gather(): pl.pallas_call(functools.partial(gather_kernel, body_of, len(ins), len(ou...  123 us
    pallas_call x1, Pallas kernels, feed_forward(): pl.pallas_call(ffn_kernel, out_shape=[jax.ShapeDtypeStruct((ranks, tok, F...  91.5 us
    all_gather x1, waiting for transfers between devices, on_device(): weight_up = lax.all_gather(fc1_weight, 'z', axis=1, tiled=True)  62.7 us
    pallas_call x1, Pallas kernels, attend_back(): pl.pallas_call(attend_back_kernel, grid=(groups,), out_shape=[jax.ShapeDt...  33.7 us
    reduce_scatter x1, waiting for transfers between devices, on_device(): lax.psum_scatter(down_w_grad, 'z', scatter_dimension=0, tiled=True)  25.4 us
    ppermute x1, waiting for transfers between devices, on_device(): before = lax.ppermute(key_value, 'z', up)  23.5 us
    reduce_scatter x1, waiting for transfers between devices, on_device(): lax.psum_scatter(up_w_grad, 'z', scatter_dimension=1, tiled=True)  22.6 us
  transfers between devices with their start and end apart: 14, of which 8 were waited for; matrix products, arithmetic and copies ran while one was open for 13% of the time, Pallas kernels for 42%

profile of v5, /device:TPU:0, one launch (start us, length us, event | category | flops | bytes accessed | tf_op | source)
XLA Modules:
  0.0 746.4 jit_solution(7434553660065493366)
XLA Ops:
  8.6 6.1 concatenate.21
  14.8 18.3 %all_to_all.37 = f32[32,1,896]{2,1,0:T(1,128)S(1)} all-to-all(f32[32,1,896]{2,1,0:T(1,128)S(1)} %broadcast_in_dim.38), channel_id=1, replica_groups=mesh['b'=4,'z'=4,'x'=2] {'b','z','x'}, dimensions={0} | all-to-all | bytes 229376 | tf_op jit(solution)/shard_map/all_to_all | solution.py:626
  37.3 14.6 %all_to_all.38 = bf16[8,64,768]{2,1,0:T(8,128)(2,1)S(1)} all-to-all(bf16[8,64,768]{2,1,0:T(8,128)(2,1)S(1)} %pad_maximum_fusion.2), channel_id=1, replica_groups=mesh['b'=4,'z'=4,'x'=2] {'b','x'}, dimensions={0} | all-to-all | bytes 1572864 | tf_op jit(solution)/shard_map/all_to_all | solution.py:663
  55.8 40.4 %gather_normed.1 = bf16[8,256,2048]{2,1,0:T(8,128)(2,1)} custom-call(bf16[256,2048]{1,0:T(8,128)(2,1)} %fusion.10.x_ref), custom_call_target="tpu_custom_call" | custom-call | flops 1073741824 | bytes 134217728 | tf_op jit(solution)/shard_map/gather_normed/pallas_call | solution.py:108
  104.0 8.7 %add_convert_fusion.1.k_ref.v_ref = bf16[2048,512]{1,0:T(8,128)(2,1)S(1)} fusion(bf16[2048,2048]{1,0:T(8,128)(2,1)} %bitcast.127, bf16[2048,512]{1,0:T(8,128)(2,1)} %bitcast.125, f32[512]{0:T(512)S(1)} %concatenate.23), kind=kOutput, calls=%fused_computation.2 | convolution fusion | flops 4297064448 | bytes 12584960 | tf_op jit(solution)/shard_map/dot_general | solution.py:219
  119.5 41.9 %gather_branch.1 = bf16[8,256,2048]{2,1,0:T(8,128)(2,1)} custom-call(bf16[256,2048]{1,0:T(8,128)(2,1)} %get-tuple-element.60.x_ref), custom_call_target="tpu_custom_call" | custom-call | flops 1073741824 | bytes 134217728 | tf_op jit(solution)/shard_map/gather_branch/pallas_call | solution.py:108
  162.8 7.1 fusion.2.q_ref
  169.9 23.5 %collective-permute-done.kb_ref.vb_ref = bf16[2048,512]{1,0:T(8,128)(2,1)} collective-permute-done((bf16[2048,512]{1,0:T(8,128)(2,1)S(1)}, bf16[2048,512]{1,0:T(8,128)(2,1)}, u32[]{:S(2)}, u32[]{:S(2)}) %collective-permute-start) | collective-permute-done | bytes 2097184 | tf_op jit(solution)/shard_map/ppermute | solution.py:707
  193.5 13.1 %attend.1 = bf16[2048,256]{1,0:T(8,128)(2,1)} custom-call(s32[2048,1]{1,0:T(8,128)} %bitcast.123, bf16[2048,256]{1,0:T(8,128)(2,1)} %fusion.2.q_ref, bf16[2048,512]{1,0:T(8,128)(2,1)} %copy-done.4, bf16[2048,512]{1,0:T(8,128)(2,1)} %copy-done.4, bf16[2048,512]{1,0:T(8,128)(2,1)} %collective-permute-done.kb_ref.vb_ref, ...), custom_call_target="tpu_custom_call" | custom-call | tf_op jit(solution)/shard_map/attend/pallas_call | solution.py:506
  206.5 45.9 %attended.1 = f32[256,2048]{1,0:T(8,128)} custom-call(bf16[8,256,256]{2,1,0:T(8,128)(2,1)} %bitcast.120, bf16[256,2048]{1,0:T(8,128)(2,1)} %all-gather.6.cloned.1.call-done.w_ref.refs_0_), custom_call_target="tpu_custom_call" | custom-call | flops 1073741824 | bytes 134217728 | tf_op jit(solution)/shard_map/attended/pallas_call | solution.py:206
  257.3 62.7 %all-gather.12.cloned.1.call-done.w1_ref = bf16[2048,1024]{1,0:T(8,128)(2,1)} async-done(((bf16[2048,256]{1,0:T(8,128)(2,1)}), bf16[2048,1024]{1,0:T(8,128)(2,1)}) %all-gather.12.cloned.1.call-update) | async-done | bytes 4194320 | tf_op jit(solution)/shard_map/all_gather | solution.py:698
  320.0 91.5 %feed_forward.1 = (bf16[8,256,1024]{2,1,0:T(8,128)(2,1)}, f32[1,1024]{1,0:T(1,128)}, f32[256,2048]{1,0:T(8,128)}, bf16[1024,2048]{1,0:T(8,128)(2,1)}, bf16[2048,1024]{1,0:T(8,128)(2,1)}) custom-call(bf16[256,2048]{1,0:T(8,128)(2,1)} %add_convert_fusion.3.x_ref, bf16[8,256,2048]{2,1,0:T(8,128)(2,1)} %gather_branch.1, ...), custom_call_target="tpu_custom_call" | custom-call | flops 1073741824 | bytes 268435456 | tf_op jit(solution)/shard_map/feed_forward/pallas_call | solution.py:398
  419.6 40.8 %attended_grad.1 = (bf16[8,256,2048]{2,1,0:T(8,128)(2,1)}, bf16[8,256,256]{2,1,0:T(8,128)(2,1)}) custom-call(bf16[256,2048]{1,0:T(8,128)(2,1)} %get-tuple-element.98.x_ref, bf16[256,2048]{1,0:T(8,128)(2,1)} %all-gather.6.cloned.1.call-done.w_ref.refs_0_, f32[1,256]{1,0:T(1,128)} %broadcast_in_dim.42.refs_1_), custom_call_target="tpu_custom_call" | custom-call | flops 1073741824 | bytes 134217728 | tf_op jit(solution)/shard_map/attended_grad/pallas_call | solution.py:108
  460.4 25.4 %reduce-scatter.5.cloned.1.call-done = bf16[256,2048]{1,0:T(8,128)(2,1)} async-done(((bf16[1024,2048]{1,0:T(8,128)(2,1)}), bf16[256,2048]{1,0:T(8,128)(2,1)}) %reduce-scatter.5.cloned.1.call-update) | async-done | bytes 1048592 | tf_op jit(solution)/shard_map/reduce_scatter | solution.py:732
  485.8 33.7 %attend_back.1 = (bf16[2048,256]{1,0:T(8,128)(2,1)}, bf16[2048,512]{1,0:T(8,128)(2,1)}, f32[2048,512]{1,0:T(8,128)}) custom-call(s32[2048,1]{1,0:T(8,128)} %bitcast.124, bf16[2048,256]{1,0:T(8,128)(2,1)} %fusion.2.q_ref, bf16[2048,512]{1,0:T(8,128)(2,1)} %copy-done.4, bf16[2048,512]{1,0:T(8,128)(2,1)} %copy-done.4, ...), custom_call_target="tpu_custom_call" | custom-call | tf_op jit(solution)/shard_map/attend_back/pallas_call | solution.py:519
  521.0 6.8 convolution_convert_fusion.1
  527.8 51.3 %down.1 = f32[256,2048]{1,0:T(8,128)} custom-call(bf16[8,256,1024]{2,1,0:T(8,128)(2,1)} %get-tuple-element.69, bf16[1024,2048]{1,0:T(8,128)(2,1)} %all-gather.14.cloned.1.call-done.w2_ref.w_ref), custom_call_target="tpu_custom_call" | custom-call | flops 1073741824 | bytes 134217728 | tf_op jit(solution)/shard_map/down/pallas_call | solution.py:206
  579.2 22.6 %reduce-scatter.7.cloned.1.call-done = bf16[2048,256]{1,0:T(8,128)(2,1)} async-done(((bf16[2048,1024]{1,0:T(8,128)(2,1)}), bf16[2048,256]{1,0:T(8,128)(2,1)}) %reduce-scatter.7.cloned.1.call-update) | async-done | bytes 1048592 | tf_op jit(solution)/shard_map/reduce_scatter | solution.py:733
  601.7 7.5 %collective-permute-done.1 = bf16[2048,512]{1,0:T(8,128)(2,1)} collective-permute-done((bf16[2048,512]{1,0:T(8,128)(2,1)}, bf16[2048,512]{1,0:T(8,128)(2,1)}, u32[]{:S(2)}, u32[]{:S(2)}) %collective-permute-start.1) | collective-permute-done | bytes 2097184 | tf_op jit(solution)/shard_map/ppermute | solution.py:746
  612.8 10.1 %convolution_convert_fusion = bf16[2048,768]{1,0:T(8,128)(2,1)S(1)} fusion(bf16[2048,2048]{1,0:T(8,128)(2,1)} %bitcast.129, bf16[2048,512]{1,0:T(8,128)(2,1)S(1)} %add_convert_fusion, bf16[2048,256]{1,0:T(8,128)(2,1)S(1)} %copy-done.11), kind=kOutput, calls=%fused_computation.3 | convolution fusion | flops 6450315264 | bytes 14680064 | tf_op jit(solution)/shard_map/dot_general | solution.py:223
  630.9 4.4 reduce-scatter.11.cloned.1.call-done
  648.4 49.9 %qkv_grad.1 = f32[256,2048]{1,0:T(8,128)} custom-call(bf16[8,256,768]{2,1,0:T(8,128)(2,1)} %bitcast.122, bf16[2048,768]{1,0:T(8,128)(2,1)} %pad_maximum_fusion.1.w_ref), custom_call_target="tpu_custom_call" | custom-call | flops 1073741824 | bytes 134217728 | tf_op jit(solution)/shard_map/qkv_grad/pallas_call | solution.py:206
  701.8 4.7 all-to-all-start.2
  723.6 5.8 all-to-all-done.3
  (180 shorter events, 93.3 us)
Async XLA Ops:
  7.2 28.0 %copy-start.17 = (bf16[64,2048]{1,0:T(8,128)(2,1)S(1)}, bf16[64,2048]{1,0:T(8,128)(2,1)}, u32[]{:S(2)}) copy-start(bf16[64,2048]{1,0:T(8,128)(2,1)} %param.29) | copy-start | bytes 786436
  7.2 48.6 %all-gather.6.cloned.1.call-start = ((), (), s32[]{:S(2)}) async-start(), calls=%async_computation.9 | async-start | bytes 1310720 | tf_op jit(solution)/shard_map/all_gather | solution.py:659
  7.9 88.3 %all-gather.8.cloned.1.call-start = ((), (), s32[]{:S(2)}) async-start(), calls=%async_computation.10 | async-start | bytes 2621440 | tf_op jit(solution)/shard_map/all_gather | solution.py:667
  37.3 15.6 %copy-start.2 = (bf16[1,256,2048]{2,1,0:T(8,128)(2,1)S(1)}, bf16[1,256,2048]{2,1,0:T(8,128)(2,1)}, u32[]{:S(2)}) copy-start(bf16[1,256,2048]{2,1,0:T(8,128)(2,1)} %param.20) | copy-start | bytes 3145732
  52.8 108.6 %all-gather.10.cloned.1.call-start = ((), (), s32[]{:S(2)}) async-start(), calls=%async_computation.11 | async-start | bytes 1310720 | tf_op jit(solution)/shard_map/all_gather | solution.py:667
  99.4 157.9 %all-gather.14.cloned.1.call-start = ((), (), s32[]{:S(2)}) async-start(), calls=%async_computation.13 | async-start | bytes 5242880 | tf_op jit(solution)/shard_map/all_gather | solution.py:699
  100.0 220.0 %all-gather.12.cloned.1.call-start = ((), (), s32[]{:S(2)}) async-start(), calls=%async_computation.12 | async-start | bytes 5242880 | tf_op jit(solution)/shard_map/all_gather | solution.py:698
  100.6 385.2 %reduce-scatter.5.cloned.1.call-start = ((), (), s32[]{:S(2)}) async-start(), calls=%async_computation.14 | async-start | bytes 5242880 | tf_op jit(solution)/shard_map/reduce_scatter | solution.py:732
  112.8 48.7 %copy-start.4 = (bf16[2048,512]{1,0:T(8,128)(2,1)}, bf16[2048,512]{1,0:T(8,128)(2,1)S(1)}, u32[]{:S(2)}) copy-start(bf16[2048,512]{1,0:T(8,128)(2,1)S(1)} %add_convert_fusion.1.k_ref.v_ref) | copy-start | bytes 6291460
  112.8 80.7 %collective-permute-start = (bf16[2048,512]{1,0:T(8,128)(2,1)S(1)}, bf16[2048,512]{1,0:T(8,128)(2,1)}, u32[]{:S(2)}, u32[]{:S(2)}) collective-permute-start(bf16[2048,512]{1,0:T(8,128)(2,1)S(1)} %add_convert_fusion.1.k_ref.v_ref), channel_id=1, source_target_pairs={{0,2},{2,4},{4,6},{1,3},{3,5},{5,7},{8,10},{10,12},{12,14},{9,11},... | collective-permute-start | bytes 6291464 | tf_op jit(solution)/shard_map/ppermute | solution.py:707
  162.8 7.2 copy-start.9
  411.6 190.1 %reduce-scatter.7.cloned.1.call-start = ((), (), s32[]{:S(2)}) async-start(), calls=%async_computation.15 | async-start | bytes 5242880 | tf_op jit(solution)/shard_map/reduce_scatter | solution.py:733
  412.3 223.0 %reduce-scatter.11.cloned.1.call-start = ((), (), s32[]{:S(2)}) async-start(), calls=%async_computation.17 | async-start | bytes 1310720 | tf_op jit(solution)/shard_map/reduce_scatter | solution.py:772
  485.8 35.2 %copy-start.7 = (bf16[2048,256]{1,0:T(8,128)(2,1)S(1)}, bf16[2048,256]{1,0:T(8,128)(2,1)}, u32[]{:S(2)}) copy-start(bf16[2048,256]{1,0:T(8,128)(2,1)} %attend.1) | copy-start | bytes 3145732
  519.5 89.7 %collective-permute-start.1 = (bf16[2048,512]{1,0:T(8,128)(2,1)}, bf16[2048,512]{1,0:T(8,128)(2,1)}, u32[]{:S(2)}, u32[]{:S(2)}) collective-permute-start(bf16[2048,512]{1,0:T(8,128)(2,1)} %get-tuple-element.77), channel_id=1, source_target_pairs={{2,0},{4,2},{6,4},{3,1},{5,3},{7,5},{10,8},{12,10},{14,12},{11,9},... | collective-permute-start | bytes 6291464 | tf_op jit(solution)/shard_map/ppermute | solution.py:746
  527.8 186.0 %reduce-scatter.9.cloned.1.call-start = ((), (), s32[]{:S(2)}) async-start(), calls=%async_computation.16 | async-start | bytes 3932160 | tf_op jit(solution)/shard_map/reduce_scatter | solution.py:767
  579.1 33.7 %copy-start.11 = (bf16[2048,256]{1,0:T(8,128)(2,1)S(1)}, bf16[2048,256]{1,0:T(8,128)(2,1)}, u32[]{:S(2)}) copy-start(bf16[2048,256]{1,0:T(8,128)(2,1)} %get-tuple-element.80) | copy-start | bytes 3145732
  612.8 10.1 %copy-start.5 = (bf16[2048,512]{1,0:T(8,128)(2,1)}, bf16[2048,512]{1,0:T(8,128)(2,1)S(1)}, u32[]{:S(2)}) copy-start(bf16[2048,512]{1,0:T(8,128)(2,1)S(1)} %add_convert_fusion) | copy-start | bytes 6291460
  629.5 10.5 %copy-start.12 = (bf16[2048,256]{1,0:T(8,128)(2,1)S(1)}, bf16[2048,256]{1,0:T(8,128)(2,1)}, u32[]{:S(2)}) copy-start(bf16[2048,256]{1,0:T(8,128)(2,1)} %get-tuple-element.80) | copy-start | bytes 3145732
  635.3 4.7 copy-start.6
  641.4 60.4 %all-to-all-start.4 = ((f32[4,1,384]{2,1,0:T(1,128)}), f32[4,1,384]{2,1,0:T(1,128)S(1)}, u32[]{:S(2)}, u32[]{:S(2)}) async-start(f32[4,1,384]{2,1,0:T(1,128)} %all_to_all.30), calls=%async_computation.7 | async-start | bytes 12288 | tf_op jit(solution)/shard_map/all_to_all | solution.py:761
  648.4 49.9 %copy-start.3 = (bf16[1,256,2048]{2,1,0:T(8,128)(2,1)S(1)}, bf16[1,256,2048]{2,1,0:T(8,128)(2,1)}, u32[]{:S(2)}) copy-start(bf16[1,256,2048]{2,1,0:T(8,128)(2,1)} %param.20) | copy-start | bytes 3145732
  701.8 12.0 %all-to-all-start.2 = ((f32[32,1,384]{2,1,0:T(1,128)}), f32[32,1,384]{2,1,0:T(1,128)S(1)}, u32[]{:S(2)}, u32[]{:S(2)}) async-start(f32[32,1,384]{2,1,0:T(1,128)} %all_to_all.27), calls=%async_computation.4 | async-start | bytes 98304 | tf_op jit(solution)/shard_map/all_to_all | solution.py:761
  713.8 15.6 %all-to-all-start.3 = ((bf16[8,64,768]{2,1,0:T(8,128)(2,1)}), bf16[8,64,768]{2,1,0:T(8,128)(2,1)S(1)}, u32[]{:S(2)}, u32[]{:S(2)}) async-start(bf16[8,64,768]{2,1,0:T(8,128)(2,1)} %bitcast.144), calls=%async_computation.6 | async-start | bytes 1572864 | tf_op jit(solution)/shard_map/all_to_all | solution.py:768
  (11 other events, 26.2 us)
Sparse Core Ops, SparseCore 0:
  9.6 33.6 all-gather.5
  52.9 43.1 all-gather.7
  99.5 30.6 all-gather.9
  131.7 104.1 all-gather.13
  237.3 82.7 all-gather.11
  411.7 74.0 reduce-scatter.4
  488.2 113.4 reduce-scatter.6
  604.6 30.6 reduce-scatter.10
  637.7 58.9 reduce-scatter.8

commit v6 on v5

--- a/solution.py
+++ b/solution.py
@@ -135,9 +135,10 @@
     all_, y = plane_gather(x, (w, bias), [jax.ShapeDtypeStruct((ranks, tok, N), out_dtype)], body, cid, name)
     return all_, y.reshape(ranks * tok, N)
 
-def reduce_kernel(turned, a_ref, w_ref, out_ref, sib_out, sib_in, stage, landed, send, recv):
+def reduce_kernel(turned, pairs, *refs):
+    left, right = refs[:pairs], refs[pairs : 2 * pairs]
+    out_ref, sib_out, sib_in, stage, landed, send, recv = refs[2 * pairs :]
     ids, at = plane_place()
-    ranks, tok, _ = a_ref.shape
     D = out_ref.shape[1]
     mid = D // 2
     greet(ids)
@@ -149,8 +150,8 @@
         return c
     def term(rank, cols):
         if turned:
-            return lax.dot_general(a_ref[rank], w_ref[cols, :], (((1,), (1,)), ((), ())), preferred_element_type=single)
-        return jnp.dot(a_ref[rank], w_ref[:, cols], preferred_element_type=single)
+            return sum(dot_nt(a[rank], w[cols, :]) for a, w in zip(left, right))
+        return sum(dot(a[rank], w[:, cols]) for a, w in zip(left, right))
     order = ("d", "x", "y", "o")
     twin = {"d": "ds", "x": "xs", "y": "ys", "o": "s"}
     sib = []
@@ -199,20 +200,20 @@
         tiles(h * mid, (h + 1) * mid, add)
     for c in started: c.wait_send()
 
-def dot_reduce(a, w, turned, cid, name):
+def dot_reduce(left, right, turned, cid, name):
     ranks = 8
-    D = w.shape[0] if turned else w.shape[1]
-    tok = a.shape[0] // ranks
+    D = right[0].shape[0] if turned else right[0].shape[1]
+    tok = left[0].size // left[0].shape[-1] // ranks
     return pl.pallas_call(
-        functools.partial(reduce_kernel, turned),
+        functools.partial(reduce_kernel, turned, len(left)),
         out_shape=jax.ShapeDtypeStruct((tok, D), single),
-        in_specs=vmem(2), out_specs=vmem(1)[0],
+        in_specs=vmem(2 * len(left)), out_specs=vmem(1)[0],
         scratch_shapes=[pltpu.VMEM((4, tok, D), bfloat), pltpu.VMEM((4, tok, D), bfloat), pltpu.VMEM((3, 2, tok, D // 2), bfloat), pltpu.VMEM((6, tok, D // 2), bfloat),
             pltpu.SemaphoreType.DMA((10,)), pltpu.SemaphoreType.DMA((10,))],
         compiler_params=pltpu.CompilerParams(collective_id=cid, has_side_effects=True, vmem_limit_bytes=60 << 20),
         cost_estimate=pl.CostEstimate(flops=1 << 30, bytes_accessed=128 << 20, transcendentals=0),
         name=name,
-    )(a.reshape(ranks, tok, -1), w)
+    )(*[a.reshape(ranks, tok, -1) for a in left], *right)
 
 
 def dot(left, right):
@@ -240,6 +241,7 @@
 
 def shipper(send, recv, ids):
     started = []
+
     def ship(src, dst, to):
         n = len(started)
         copy = pltpu.make_async_remote_copy(
@@ -248,14 +250,31 @@
         copy.start()
         started.append(copy)
         return copy
+
     return ship, started
 
-def ffn_kernel(x_ref, bg_ref, w1_ref, w2_ref, b_ref, hid_ref, pb_ref, r_ref, down_ref, up_ref,
-               held, bg, pg_ref, sib_out, sib_in, stage, landed, rows_out, send, recv, keep, load, store):
+
+TWIN = {"o": "s", "x": "xs", "y": "ys", "d": "ds"}
+
+
+def hidden_units(src, branch, w1_ref, w2_ref, b_ref, hid_ref, pg_ref, pb_ref, rank):
+    pre = jnp.dot(src[...], w1_ref[...], preferred_element_type=single) + b_ref[...]
+    square = pre * pre
+    bend = jnp.tanh(0.7978845608028654 * (pre + 0.044715 * (pre * square)))
+    rise = 0.5 * (1.0 + bend)
+    hid_ref[rank] = (pre * rise).astype(bfloat)
+    slope = rise + (0.5 * 0.7978845608028654) * pre * (1.0 - bend * bend) * (1.0 + 3 * 0.044715 * square)
+    grad = (dot_nt(branch[...], w2_ref[...]) * slope).astype(bfloat)
+    pg_ref[rank] = grad
+    pb_ref[...] += jnp.sum(grad.astype(single), axis=0, keepdims=True)
+
+
+def first_units_kernel(
+    x_ref, bg_ref, w1_ref, w2_ref, b_ref, all_ref, hid_ref, pg_ref, pb_ref, down_ref, up_ref,
+    held, bg, down_sum, up_sum, send, recv, keep, load,
+):
     ids, at = plane_place()
-    tok, D = x_ref.shape
-    F = w1_ref.shape[1]
-    mid = D // 2
+    tok = x_ref.shape[0]
     half = tok // 2
     parts = (pl.ds(0, half), pl.ds(half, half))
     own = at["o"]
@@ -263,9 +282,6 @@
     for n, name in enumerate(at):
         loads[name] = pltpu.make_async_copy(bg_ref.at[at[name]], bg.at[at[name]], load.at[n])
         loads[name].start()
-    kept = pltpu.make_async_copy(x_ref, held.at[own], keep)
-    kept.start()
-    pb_ref[...] = jnp.zeros_like(pb_ref)
     greet(ids)
     ship, started = shipper(send, recv, ids)
     x0 = ship(x_ref.at[parts[0]], held.at[own, parts[0]], "x")
@@ -273,43 +289,45 @@
     x1 = ship(x_ref.at[parts[1]], held.at[own, parts[1]], "x")
     y0 = ship(x_ref.at[parts[0]], held.at[own, parts[0]], "y")
     s0 = ship(x_ref, held.at[own], "s")
+    pb_ref[...] = jnp.zeros_like(pb_ref)
+    kept = []
 
     def units(name):
         rank = at[name]
         src = x_ref if name == "o" else held.at[rank]
+        copy = pltpu.make_async_copy(src, all_ref.at[rank], keep.at[len(kept)])
+        copy.start()
+        kept.append(copy)
         loads[name].wait()
-        def body(cols):
-            pre = jnp.dot(src[...], w1_ref[:, cols], preferred_element_type=single) + b_ref[:, cols]
-            square = pre * pre
-            bend = jnp.tanh(0.7978845608028654 * (pre + 0.044715 * (pre * square)))
-            rise = 0.5 * (1.0 + bend)
-            hid_ref[rank, :, cols] = (pre * rise).astype(bfloat)
-            slope = rise + (0.5 * 0.7978845608028654) * pre * (1.0 - bend * bend) * (1.0 + 3 * 0.044715 * square)
-            grad = (dot_nt(bg[rank], w2_ref[cols, :]) * slope).astype(bfloat)
-            pg_ref[rank, :, cols] = grad
-            pb_ref[:, cols] += jnp.sum(grad.astype(single), axis=0, keepdims=True)
-        tiles(0, F, body)
-
-    def term(name, cols):
-        return dot_nt(pg_ref[at[name]], w1_ref[cols, :])
-    order = ("d", "x", "y", "o")
-    twin = {"d": "ds", "x": "xs", "y": "ys", "o": "s"}
-    def to_sibling(j):
-        def fill(cols):
-            sib_out[j, :, cols] = term(twin[order[j]], cols).astype(bfloat)
-        tiles(0, D, fill)
-        return ship(sib_out.at[j], sib_in.at[j], "s")
-    def pair(j, cols):
-        return term(order[j], cols) + sib_in[j, :, cols].astype(single)
-    def local(h, cols):
-        return pl.ds(pl.multiple_of(cols.start - h * mid, TILE), TILE)
-    def put(j, h, extra=None):
-        def fill(cols):
-            value = pair(j, cols)
-            if extra is not None:
-                value = value + landed[extra, :, local(h, cols)].astype(single)
-            stage[j, h, :, local(h, cols)] = value.astype(bfloat)
-        tiles(h * mid, (h + 1) * mid, fill)
+        hidden_units(src, bg.at[rank], w1_ref, w2_ref, b_ref, hid_ref, pg_ref, pb_ref, rank)
+
+    def weigh(name, last=False):
+        wide = 256
+
+        def add(total, out, here, pairs):
+            term = sum(dot_tn(left, right) for left, right in pairs)
+            if name == "o":
+                total[here, :] = term
+            elif last:
+                out[here, :] = (total[here, :] + term).astype(bfloat)
+            else:
+                total[here, :] += term
+
+        both = [(n, at[n]) for n in (name, TWIN[name])]
+
+        def down(i, _):
+            here = pl.ds(pl.multiple_of(i * wide, wide), wide)
+            add(down_sum, down_ref, here, [(hid_ref[r, :, here], bg[r]) for n, r in both])
+            return 0
+
+        def up(i, _):
+            here = pl.ds(pl.multiple_of(i * wide, wide), wide)
+            tokens = [(x_ref[:, here] if n == "o" else held[r, :, here], pg_ref[r]) for n, r in both]
+            add(up_sum, up_ref, here, tokens)
+            return 0
+
+        lax.fori_loop(0, hid_ref.shape[2] // wide, down, 0)
+        lax.fori_loop(0, x_ref.shape[1] // wide, up, 0)
 
     units("o")
     s0.wait_recv()
@@ -318,7 +336,7 @@
     ry = ship(held.at[at["x"], parts[0]], held.at[at["x"], parts[0]], "y")
     y1.wait_recv()
     rx = ship(held.at[at["y"], parts[1]], held.at[at["y"], parts[1]], "x")
-    own_sib = to_sibling(3)
+    weigh("o")
     x1.wait_recv()
     sx = ship(held.at[at["x"]], held.at[at["x"]], "s")
     y0.wait_recv()
@@ -326,21 +344,79 @@
     units("x")
     sx.wait_recv()
     units("xs")
-    x_sib = to_sibling(1)
     units("y")
     sy.wait_recv()
     units("ys")
-    y_sib = to_sibling(2)
+    weigh("x")
     ry.wait_recv()
     rx.wait_recv()
     sd = ship(held.at[at["d"]], held.at[at["d"]], "s")
-    x_sib.wait_recv()
-    put(1, 0)
-    x_a = ship(stage.at[1, 0], landed.at[2], "x")
-    y_sib.wait_recv()
-    put(2, 1)
-    y_b = ship(stage.at[2, 1], landed.at[3], "y")
+    weigh("y")
+    units("d")
     sd.wait_recv()
+    units("ds")
+    weigh("d", last=True)
+    for copy in started:
+        copy.wait_send()
+    for copy in kept:
+        copy.wait()
+
+
+def last_units_kernel(
+    all_ref, bg_ref, pg1_ref, w1a_ref, w1_ref, w2_ref, b_ref, hid_ref, pb_ref, r_ref, down_ref, up_ref,
+    held, bg, pg_ref, sib_out, sib_in, stage, landed, send, recv, load, load_b,
+):
+    ids, at = plane_place()
+    ranks, tok, D = held.shape
+    F = w1_ref.shape[1]
+    mid = D // 2
+    names = ("ds", "d", "xs", "x", "ys", "y", "s", "o")
+    loads = {}
+    for n, name in enumerate(names):
+        loads[name] = [
+            pltpu.make_async_copy(all_ref.at[at[name]], held.at[at[name]], load.at[n]),
+            pltpu.make_async_copy(bg_ref.at[at[name]], bg.at[at[name]], load_b.at[n]),
+        ]
+        for copy in loads[name]:
+            copy.start()
+    greet(ids)
+    ship, started = shipper(send, recv, ids)
+    pb_ref[...] = jnp.zeros_like(pb_ref)
+
+    def units(name):
+        for copy in loads[name]:
+            copy.wait()
+        rank = at[name]
+        hidden_units(held.at[rank], bg.at[rank], w1_ref, w2_ref, b_ref, hid_ref, pg_ref, pb_ref, rank)
+
+    def term(name, cols):
+        rank = at[name]
+        return dot_nt(pg1_ref[rank], w1a_ref[cols, :]) + dot_nt(pg_ref[rank], w1_ref[cols, :])
+
+    order = ("d", "x", "y", "o")
+
+    def to_sibling(j):
+        def fill(cols):
+            sib_out[j, :, cols] = term(TWIN[order[j]], cols).astype(bfloat)
+
+        tiles(0, D, fill)
+        return ship(sib_out.at[j], sib_in.at[j], "s")
+
+    def pair(j, cols):
+        return term(order[j], cols) + sib_in[j, :, cols].astype(single)
+
+    def local(h, cols):
+        return pl.ds(pl.multiple_of(cols.start - h * mid, TILE), TILE)
+
+    def put(j, h, extra=None):
+        def fill(cols):
+            value = pair(j, cols)
+            if extra is not None:
+                value = value + landed[extra, :, local(h, cols)].astype(single)
+            stage[j, h, :, local(h, cols)] = value.astype(bfloat)
+
+        tiles(h * mid, (h + 1) * mid, fill)
+
     units("ds")
     d_sib = to_sibling(0)
     units("d")
@@ -349,54 +425,101 @@
     d_a = ship(stage.at[0, 0], landed.at[0], "x")
     put(0, 1)
     d_b = ship(stage.at[0, 1], landed.at[1], "y")
-    own_sib.wait_recv()
-    def first(cols):
-        r_ref[:, cols] = pair(3, cols)
-    tiles(0, D, first)
-
-    kept.wait()
-    wide = rows_out.shape[1]
-    def grads(out_ref, count, value):
-        def step(i, _):
-            slot = lax.rem(i, 2)
-            here = pl.ds(pl.multiple_of(i * wide, wide), wide)
-            copy = pltpu.make_async_copy(rows_out.at[slot, :, pl.ds(0, out_ref.shape[1])], out_ref.at[here], store.at[slot])
-            @pl.when(i >= 2)
-            def _():
-                copy.wait()
-            rows_out[slot, :, : out_ref.shape[1]] = value(here).astype(bfloat)
-            copy.start()
-            return 0
-        lax.fori_loop(0, count, step, 0)
-        for slot in range(2):
-            pltpu.make_async_copy(rows_out.at[slot, :, pl.ds(0, out_ref.shape[1])], out_ref.at[pl.ds(0, wide)], store.at[slot]).wait()
-    ranks = held.shape[0]
-    grads(down_ref, F // wide, lambda cols: dot_tn(hid_ref[:, :, cols].reshape(ranks * tok, wide), bg[...].reshape(ranks * tok, D)))
+    units("xs")
+    x_sib = to_sibling(1)
+    units("x")
+    x_sib.wait_recv()
+    put(1, 0)
+    x_a = ship(stage.at[1, 0], landed.at[2], "x")
+    units("ys")
+    y_sib = to_sibling(2)
+    units("y")
+    y_sib.wait_recv()
+    put(2, 1)
+    y_b = ship(stage.at[2, 1], landed.at[3], "y")
     d_b.wait_recv()
     put(1, 1, extra=1)
     x_b = ship(stage.at[1, 1], landed.at[5], "x")
     d_a.wait_recv()
     put(2, 0, extra=0)
     y_a = ship(stage.at[2, 0], landed.at[4], "y")
-    grads(up_ref, D // wide, lambda cols: dot_tn(held[:, :, cols].reshape(ranks * tok, wide), pg_ref[...].reshape(ranks * tok, F)))
+    units("s")
+    own_sib = to_sibling(3)
+    units("o")
+    own_sib.wait_recv()
+
+    def first(cols):
+        r_ref[:, cols] = pair(3, cols)
+
+    tiles(0, D, first)
+
+    wide = 256
+
+    def grads(out_ref, count, value):
+        def step(i, _):
+            here = pl.ds(pl.multiple_of(i * wide, wide), wide)
+            out_ref[here, :] = value(here).astype(bfloat)
+            return 0
+
+        lax.fori_loop(0, count, step, 0)
+
+    rows = ranks * tok
+    grads(down_ref, F // wide, lambda c: dot_tn(hid_ref[:, :, c].reshape(rows, wide), bg[...].reshape(rows, D)))
+    grads(up_ref, D // wide, lambda c: dot_tn(held[:, :, c].reshape(rows, wide), pg_ref[...].reshape(rows, F)))
     for copy in (x_a, y_b, x_b, y_a):
         copy.wait_recv()
     for h, (n, m) in enumerate(((2, 4), (3, 5))):
+
         def add(cols, h=h, n=n, m=m):
             c = local(h, cols)
             r_ref[:, cols] = r_ref[:, cols] + landed[n, :, c].astype(single) + landed[m, :, c].astype(single)
+
         tiles(h * mid, (h + 1) * mid, add)
     for copy in started:
         copy.wait_send()
 
-def feed_forward(x, bg, w1, w2, bias, cid):
+
+def first_units(x, bg, w1, w2, bias, cid):
     ranks = 8
     tok, D = x.shape
     F = w1.shape[1]
     anywhere = pl.BlockSpec(memory_space=pl.ANY)
     inside = pl.BlockSpec(memory_space=pltpu.VMEM)
-    hid, pb, r, down, up = pl.pallas_call(
-        ffn_kernel,
+    return pl.pallas_call(
+        first_units_kernel,
+        out_shape=[
+            jax.ShapeDtypeStruct((ranks, tok, D), bfloat),
+            jax.ShapeDtypeStruct((ranks, tok, F), bfloat),
+            jax.ShapeDtypeStruct((ranks, tok, F), bfloat),
+            jax.ShapeDtypeStruct((1, F), single),
+            jax.ShapeDtypeStruct((F, D), bfloat),
+            jax.ShapeDtypeStruct((D, F), bfloat),
+        ],
+        in_specs=[inside, anywhere, inside, inside, inside],
+        out_specs=[anywhere, inside, inside, inside, inside, inside],
+        scratch_shapes=[
+            pltpu.VMEM((ranks, tok, D), bfloat),
+            pltpu.VMEM((ranks, tok, D), bfloat),
+            pltpu.VMEM((F, D), single),
+            pltpu.VMEM((D, F), single),
+            pltpu.SemaphoreType.DMA((10,)),
+            pltpu.SemaphoreType.DMA((10,)),
+            pltpu.SemaphoreType.DMA((8,)),
+            pltpu.SemaphoreType.DMA((8,)),
+        ],
+        compiler_params=pltpu.CompilerParams(collective_id=cid, has_side_effects=True, vmem_limit_bytes=62 << 20),
+        cost_estimate=pl.CostEstimate(flops=1 << 30, bytes_accessed=160 << 20, transcendentals=0),
+        name="first_units",
+    )(x, bg, w1, w2, bias)
+
+
+def last_units(rows, bg, pg, w1a, w1, w2, bias, cid):
+    ranks, tok, D = rows.shape
+    F = w1.shape[1]
+    anywhere = pl.BlockSpec(memory_space=pl.ANY)
+    inside = pl.BlockSpec(memory_space=pltpu.VMEM)
+    return pl.pallas_call(
+        last_units_kernel,
         out_shape=[
             jax.ShapeDtypeStruct((ranks, tok, F), bfloat),
             jax.ShapeDtypeStruct((1, F), single),
@@ -404,8 +527,8 @@
             jax.ShapeDtypeStruct((F, D), bfloat),
             jax.ShapeDtypeStruct((D, F), bfloat),
         ],
-        in_specs=[inside, anywhere, inside, inside, inside],
-        out_specs=[inside, inside, inside, anywhere, anywhere],
+        in_specs=[anywhere, anywhere, inside, inside, inside, inside, inside],
+        out_specs=[inside] * 5,
         scratch_shapes=[
             pltpu.VMEM((ranks, tok, D), bfloat),
             pltpu.VMEM((ranks, tok, D), bfloat),
@@ -414,18 +537,15 @@
             pltpu.VMEM((4, tok, D), bfloat),
             pltpu.VMEM((3, 2, tok, D // 2), bfloat),
             pltpu.VMEM((6, tok, D // 2), bfloat),
-            pltpu.VMEM((2, 128, D), bfloat),
-            pltpu.SemaphoreType.DMA((20,)),
-            pltpu.SemaphoreType.DMA((20,)),
-            pltpu.SemaphoreType.DMA,
+            pltpu.SemaphoreType.DMA((10,)),
+            pltpu.SemaphoreType.DMA((10,)),
             pltpu.SemaphoreType.DMA((8,)),
-            pltpu.SemaphoreType.DMA((2,)),
+            pltpu.SemaphoreType.DMA((8,)),
         ],
-        compiler_params=pltpu.CompilerParams(collective_id=cid, has_side_effects=True, vmem_limit_bytes=63 << 20),
-        cost_estimate=pl.CostEstimate(flops=1 << 30, bytes_accessed=256 << 20, transcendentals=0),
-        name="feed_forward",
-    )(x, bg.reshape(ranks, tok, D), w1, w2, bias)
-    return hid.reshape(ranks * tok, F), pb[0], r, down, up
+        compiler_params=pltpu.CompilerParams(collective_id=cid, has_side_effects=True, vmem_limit_bytes=62 << 20),
+        cost_estimate=pl.CostEstimate(flops=1 << 30, bytes_accessed=160 << 20, transcendentals=0),
+        name="last_units",
+    )(rows, bg, pg, w1a, w1, w2, bias)
 
 
 def windows(span):
@@ -619,6 +739,27 @@
 
     count = lengths.shape[1]
     upto = jnp.arange(count)[:, None] <= jnp.arange(count)[None, :]
+    def to_ranks(matrix):
+        lead = matrix.shape[:-1]
+        if whole_heads:
+            matrix = matrix.reshape(*lead, B, Z, X, rows_dev)
+            k = len(lead)
+            return matrix.transpose(k, k + 2, *range(k), k + 1, k + 3).reshape(R, *lead, cols)
+        return jnp.moveaxis(matrix.reshape(*lead, R, cols), -2, 0)
+
+    def from_ranks(parts):
+        if whole_heads:
+            parts = parts.reshape(B, X, -1, Z, rows_dev)
+            return parts.transpose(2, 0, 3, 1, 4).reshape(-1, D)
+        return parts.transpose(1, 0, 2).reshape(-1, D)
+
+    def mine(vector):
+        return lax.dynamic_index_in_dim(to_ranks(vector), rank, 0, keepdims=False)
+
+    qkv_parts = jnp.concatenate([to_ranks(q_weight), to_ranks(k_weight), to_ranks(v_weight)], axis=2)
+    qkv_mine = lax.all_to_all(qkv_parts, PLANE, split_axis=0, concat_axis=0, tiled=True)
+    qkv_mine = qkv_mine.reshape(D // Z, 3 * cols)
+    qkv_mine, fc2_bias = lax.optimization_barrier((qkv_mine, fc2_bias))
     small = [ln1_gain, ln1_bias, q_bias, v_bias, o_bias, ln2_gain, ln2_bias, fc2_bias]
     pack = jnp.concatenate([v.astype(single) for v in (*small, fc1_bias, lengths[0])])
     pad = -pack.shape[0] % 128
@@ -637,40 +778,14 @@
     starts = jnp.max(jnp.where(ends[:, None, :] <= places[None, :, None], ends[:, None, :], 0), axis=2)
     starts = starts - (at_z - 1) * span
 
-    def to_ranks(matrix):
-        lead = matrix.shape[:-1]
-        if whole_heads:
-            matrix = matrix.reshape(*lead, B, Z, X, rows_dev)
-            k = len(lead)
-            return matrix.transpose(k, k + 2, *range(k), k + 1, k + 3).reshape(R, *lead, cols)
-        return jnp.moveaxis(matrix.reshape(*lead, R, cols), -2, 0)
-
-    def from_ranks(parts):
-        if whole_heads:
-            parts = parts.reshape(B, X, -1, Z, rows_dev)
-            return parts.transpose(2, 0, 3, 1, 4).reshape(-1, D)
-        return parts.transpose(1, 0, 2).reshape(-1, D)
-
-    def mine(vector):
-        return lax.dynamic_index_in_dim(to_ranks(vector), rank, 0, keepdims=False)
-
-    gain_one, q_weight, k_weight, v_weight = lax.optimization_barrier((gain_one, q_weight, k_weight, v_weight))
-    if whole_heads:
-        weight_o = lax.all_gather(o_weight, "z", axis=0, tiled=True)
-    else:
-        weight_o = lax.dynamic_slice_in_dim(lax.all_gather(o_weight, ALL, axis=0, tiled=True), rank * cols, cols, 0)
-    qkv_parts = jnp.concatenate([to_ranks(q_weight), to_ranks(k_weight), to_ranks(v_weight)], axis=2)
-    qkv_mine = lax.all_to_all(qkv_parts, PLANE, split_axis=0, concat_axis=0, tiled=True)
-    qkv_mine = qkv_mine.reshape(D // Z, 3 * cols)
-
     def feature_rows(mine):
         full = lax.all_gather(mine, "z", axis=0, tiled=True)
         return full.reshape(Z, B, X, rows_dev, -1).transpose(1, 0, 2, 3, 4).reshape(D, -1)
 
     weight_kv = feature_rows(qkv_mine[:, cols:])
     bias_kv = jnp.concatenate([jnp.zeros((cols,), single), mine(bias_v)])
+    bias_one, query_mine, o_weight = lax.optimization_barrier((bias_one, qkv_mine[:, :cols], o_weight))
     normed_low = layer_norm(local, gain_one, bias_one).astype(bfloat)
-    normed_low, weight_o = lax.optimization_barrier((normed_low, weight_o))
     fast = (B, X) == (4, 2)
 
     def gather_plane(rows, cid, name):
@@ -686,17 +801,21 @@
 
     def reduce_plane(left, weight, turned, cid, name):
         if fast:
-            return dot_reduce(left, weight, turned, cid, name)
+            return dot_reduce([left], [weight], turned, cid, name)
         terms = (dot_nt if turned else dot)(left, weight).astype(bfloat)
         return lax.psum_scatter(terms, PLANE, scatter_dimension=0, tiled=True).astype(single)
 
     normed_all = gather_plane(normed_low, 0, "gather_normed")
-    normed_all, weight_kv, query_mine, fc1_weight, fc2_weight = lax.optimization_barrier(
-        (normed_all, weight_kv, qkv_mine[:, :cols], fc1_weight, fc2_weight)
-    )
+    units = fc1_bias.shape[0] // 2
+    up_one, down_one = fc1_weight[:, :units], fc2_weight[:units]
+    normed_all, weight_kv, up_one, down_one = lax.optimization_barrier((normed_all, weight_kv, up_one, down_one))
     weight_q = feature_rows(query_mine)
-    weight_up = lax.all_gather(fc1_weight, "z", axis=1, tiled=True)
-    weight_down = lax.all_gather(fc2_weight, "z", axis=0, tiled=True)
+    if whole_heads:
+        weight_o = lax.all_gather(o_weight, "z", axis=0, tiled=True)
+    else:
+        weight_o = lax.dynamic_slice_in_dim(lax.all_gather(o_weight, ALL, axis=0, tiled=True), rank * cols, cols, 0)
+    up_one = lax.all_gather(up_one, "z", axis=1, tiled=True)
+    down_one = lax.all_gather(down_one, "z", axis=0, tiled=True)
     key_value = (dot(normed_all, weight_kv) + bias_kv).astype(bfloat)
     up = [(i, i + 1) for i in range(Z - 1)]
     down = [(i + 1, i) for i in range(Z - 1)]
@@ -711,26 +830,52 @@
     before, query = lax.optimization_barrier((before, query))
     starts = starts.reshape(B * span, 1)
     context = attention_forward(starts, query, key_value, before, B)
+    context, up_two, down_two = lax.optimization_barrier((context, fc1_weight[:, units:], fc2_weight[units:]))
+    up_two = lax.all_gather(up_two, "z", axis=1, tiled=True)
+    down_two = lax.all_gather(down_two, "z", axis=0, tiled=True)
 
     attended = reduce_plane(context, weight_o, False, 1, "attended") + bias_o
     middle = local + active * attended
     normed_two = layer_norm(middle, gain_two, bias_two).astype(bfloat)
+    bias_up = bias_up.reshape(Z, 2, units)
+    bias_up = [bias_up[:, i].reshape(1, Z * units) for i in range(2)]
+
+    def sum_halves(left, right, turned, cid, name):
+        if fast:
+            return dot_reduce(left, right, turned, cid, name)
+        terms = sum((dot_nt if turned else dot)(a, w) for a, w in zip(left, right)).astype(bfloat)
+        return lax.psum_scatter(terms, PLANE, scatter_dimension=0, tiled=True).astype(single)
+
+    def sum_z(down_grad, up_grad):
+        down_grad = lax.psum_scatter(down_grad, "z", scatter_dimension=0, tiled=True)
+        return down_grad, lax.psum_scatter(up_grad, "z", scatter_dimension=1, tiled=True)
+
     if fast:
-        hidden, up_b_grad, normed_two_grad, down_w_grad, up_w_grad = feed_forward(
-            normed_two, branch_all, weight_up, weight_down, bias_up[None], 2
+        branch_rows = branch_all.reshape(R, tok, D)
+        two_all, hidden_one, pre_one, bias_one_up, down_grad, up_grad = first_units(
+            normed_two, branch_rows, up_one, down_one, bias_up[0], 2
         )
+        shards_one = sum_z(down_grad, up_grad)
+        hidden_two, bias_two_up, normed_two_grad, down_grad, up_grad = last_units(
+            two_all, branch_rows, pre_one, up_one, up_two, down_two, bias_up[1], 3
+        )
+        shards_two = sum_z(down_grad, up_grad)
+        up_b_halves = [bias_one_up[0], bias_two_up[0]]
     else:
         two_all = gather_plane(normed_two, 2, "gather_two")
-        hidden_pre = dot(two_all, weight_up) + bias_up
-        gelu_value, gelu_pull = jax.vjp(partial(jax.nn.gelu, approximate=True), hidden_pre)
-        hidden = gelu_value.astype(bfloat)
-        pre_grad = gelu_pull(dot_nt(branch_all, weight_down))[0].astype(bfloat)
-        down_w_grad = dot_tn(hidden, branch_all).astype(bfloat)
-        up_w_grad = dot_tn(two_all, pre_grad).astype(bfloat)
-        up_b_grad = column_sums(pre_grad)
-        normed_two_grad = reduce_plane(pre_grad, weight_up, True, 3, "up_grad")
-    down_w_shard = lax.psum_scatter(down_w_grad, "z", scatter_dimension=0, tiled=True)
-    up_w_shard = lax.psum_scatter(up_w_grad, "z", scatter_dimension=1, tiled=True)
+
+        def half_units(weight_up, weight_down, bias):
+            hidden, gelu_pull = jax.vjp(partial(jax.nn.gelu, approximate=True), dot(two_all, weight_up) + bias)
+            hidden = hidden.astype(bfloat)
+            pre_grad = gelu_pull(dot_nt(branch_all, weight_down))[0].astype(bfloat)
+            grads = dot_tn(hidden, branch_all).astype(bfloat), dot_tn(two_all, pre_grad).astype(bfloat)
+            return hidden, pre_grad, sum_z(*grads)
+
+        hidden_one, pre_one, shards_one = half_units(up_one, down_one, bias_up[0])
+        hidden_two, pre_two, shards_two = half_units(up_two, down_two, bias_up[1])
+        up_b_halves = [column_sums(pre_one), column_sums(pre_two)]
+        normed_two_grad = sum_halves([pre_one, pre_two], [up_one, up_two], True, 3, "up_grad")
+    up_b_grad = jnp.stack([half.reshape(Z, units) for half in up_b_halves], axis=1).reshape(-1)
 
     middle_part, gain_two_grad, bias_two_grad = norm_backward(middle, normed_two_grad, gain_two)
     middle_grad = cotangent + middle_part
@@ -739,13 +884,13 @@
     attended_all, context_grad = gather_plane_dot(
         attended_grad, weight_o, jnp.zeros((1, cols), single), bfloat, True, 5, "attended_grad"
     )
-    context_grad, down_w_shard = lax.optimization_barrier((context_grad, down_w_shard))
+    context_grad, shards_one = lax.optimization_barrier((context_grad, shards_one))
     out_w_grad = dot_tn(context, attended_all)
     query_grad, edge, pair = attention_backward(starts, query, key_value, before, context_grad, B)
-    hidden, edge, pair = lax.optimization_barrier((hidden, edge, pair))
+    hidden_one, edge, pair = lax.optimization_barrier((hidden_one, edge, pair))
     after = lax.ppermute(edge, "z", down)
-    branch = reduce_plane(hidden, weight_down, False, 4, "down")
-    branch, after, up_w_shard = lax.optimization_barrier((branch, after, up_w_shard))
+    branch = sum_halves([hidden_one, hidden_two], [down_one, down_two], False, 4, "down")
+    branch, after, shards_two = lax.optimization_barrier((branch, after, shards_two))
     outputs = middle + active * (branch + bias_down)
     pair_grad = (pair + after.astype(single)).astype(bfloat)
     qkv_grad = jnp.concatenate([query_grad, pair_grad], axis=1)
@@ -799,9 +944,9 @@
         sums[2],
         sums[3],
         sums[4],
-        up_w_shard.astype(single),
+        jnp.concatenate([shards_one[1], shards_two[1]], axis=1).astype(single),
         up_b_shard,
-        down_w_shard.astype(single),
+        jnp.concatenate([shards_one[0], shards_two[0]], axis=0).astype(single),
         sums[5],
     )
 

time: 754 us -> 716 us (0.950)
  waiting for transfers between devices: 158 us -> 104 us
  Pallas kernels: 408 us -> 428 us
  blocking collectives: 32.9 us -> 17.2 us
  local copies, waits for them, and re-layouts: 38.9 us -> 47.5 us
    reduce_scatter x2, waiting for transfers between devices: 48 us -> 0.01 us  [sum_z(): lax.psum_scatter(down_grad, 'z', scatter_dimension=0, tiled=True)]
    all_gather x2 -> x4, waiting for transfers between devices: 62.7 us -> 43.5 us  [the longest x1 34.1 us: on_device(): down_two = lax.all_gather(down_two, 'z', axis=0, tiled=True)]
    all_to_all x1 -> x0, blocking collectives: 18.3 us -> none  [on_device(): lax.all_to_all(jnp.broadcast_to(pack, (R * Z, pack.shape[0])), ALL, split...]
    pallas_call x4 -> x5, Pallas kernels: 239 us -> 257 us  [the longest x3 147 us: dot_reduce(): pl.pallas_call(functools.partial(reduce_kernel, turned, len(left)), out_s...]
    ppermute x1, waiting for transfers between devices: 7.49 us -> 19.3 us  [on_device(): after = lax.ppermute(edge, 'z', down)]
  transfers between devices with their start and end apart: 14 -> 19, of which waited for: 8 -> 7; matrix products, arithmetic and copies ran while one was open for 13% -> 15% of each run, Pallas kernels for 42% -> 60%
where the time goes in v6:
time: 716 us; the launch traced here: 708 us
  Pallas kernels  428 us (60%)
  waiting for transfers between devices  104 us (15%)
  local copies, waits for them, and re-layouts  47.5 us (7%)
  other arithmetic  39.8 us (6%)
  matrix products  33 us (5%)
  starting transfers between devices  22.7 us (3%)
  blocking collectives  17.2 us (2%)
  between operations  16.4 us (2%)
    pallas_call x3, Pallas kernels, dot_reduce(): pl.pallas_call(functools.partial(reduce_kernel, turned, len(left)), out_s...  147 us
    pallas_call x3, Pallas kernels, plane_gather(): pl.pallas_call(functools.partial(gather_kernel, body_of, len(ins), len(ou...  124 us
    pallas_call x1, Pallas kernels, last_units(): pl.pallas_call(last_units_kernel, out_shape=[jax.ShapeDtypeStruct((ranks,...  55.2 us
    pallas_call x1, Pallas kernels, first_units(): pl.pallas_call(first_units_kernel, out_shape=[jax.ShapeDtypeStruct((ranks...  54.2 us
    all_gather x1, waiting for transfers between devices, on_device(): down_two = lax.all_gather(down_two, 'z', axis=0, tiled=True)  34.1 us
    pallas_call x1, Pallas kernels, attend_back(): pl.pallas_call(attend_back_kernel, grid=(groups,), out_shape=[jax.ShapeDt...  33.5 us
    ppermute x1, waiting for transfers between devices, on_device(): after = lax.ppermute(edge, 'z', down)  19.3 us
    ppermute x1, waiting for transfers between devices, on_device(): before = lax.ppermute(key_value, 'z', up)  17.3 us
  transfers between devices with their start and end apart: 19, of which 7 were waited for; matrix products, arithmetic and copies ran while one was open for 15% of the time, Pallas kernels for 60%

profile of v6, /device:TPU:0, one launch (start us, length us, event | category | flops | bytes accessed | tf_op | source)
XLA Modules:
  0.0 707.7 jit_solution(4103185368105346710)
XLA Ops:
  11.5 17.2 %all_to_all.37 = bf16[8,64,768]{2,1,0:T(8,128)(2,1)S(1)} all-to-all(bf16[8,64,768]{2,1,0:T(8,128)(2,1)S(1)} %pad_maximum_fusion.2), channel_id=1, replica_groups=mesh['b'=4,'z'=4,'x'=2] {'b','x'}, dimensions={0} | all-to-all | bytes 1572864 | tf_op jit(solution)/shard_map/all_to_all | solution.py:760
  30.4 4.4 all-to-all-start.1
  35.7 6.9 all-to-all-done.1
  48.4 40.4 %gather_normed.1 = bf16[8,256,2048]{2,1,0:T(8,128)(2,1)} custom-call(bf16[256,2048]{1,0:T(8,128)(2,1)} %fusion.10.x_ref), custom_call_target="tpu_custom_call" | custom-call | flops 1073741824 | bytes 134217728 | tf_op jit(solution)/shard_map/gather_normed/pallas_call | solution.py:108
  95.6 8.6 %add_convert_fusion.1.k_ref.v_ref = bf16[2048,512]{1,0:T(8,128)(2,1)S(1)} fusion(bf16[2048,2048]{1,0:T(8,128)(2,1)} %bitcast.138, bf16[2048,512]{1,0:T(8,128)(2,1)} %bitcast.136, f32[512]{0:T(512)S(1)} %concatenate.29), kind=kOutput, calls=%fused_computation.2 | convolution fusion | flops 4297064448 | bytes 12584960 | tf_op jit(solution)/shard_map/dot_general | solution.py:220
  112.5 42.0 %gather_branch.1 = bf16[8,256,2048]{2,1,0:T(8,128)(2,1)} custom-call(bf16[256,2048]{1,0:T(8,128)(2,1)} %get-tuple-element.67.x_ref), custom_call_target="tpu_custom_call" | custom-call | flops 1073741824 | bytes 134217728 | tf_op jit(solution)/shard_map/gather_branch/pallas_call | solution.py:108
  154.5 7.3 %fusion.2.q_ref = bf16[2048,256]{1,0:T(8,128)(2,1)} fusion(bf16[2048,2048]{1,0:T(8,128)(2,1)} %bitcast.139, bf16[2048,256]{1,0:T(8,128)(2,1)} %bitcast.146, f32[256]{0:T(256)S(1)} %bitcast.175), kind=kOutput, calls=%fused_computation.11 | convolution fusion | flops 2148532224 | bytes 10486784 | tf_op jit(solution)/shard_map/dot_general | solution.py:220
  161.8 17.3 %collective-permute-done.kb_ref.vb_ref = bf16[2048,512]{1,0:T(8,128)(2,1)} collective-permute-done((bf16[2048,512]{1,0:T(8,128)(2,1)S(1)}, bf16[2048,512]{1,0:T(8,128)(2,1)}, u32[]{:S(2)}, u32[]{:S(2)}) %collective-permute-start) | collective-permute-done | bytes 2097184 | tf_op jit(solution)/shard_map/ppermute | solution.py:826
  179.1 13.1 %attend.1 = bf16[2048,256]{1,0:T(8,128)(2,1)} custom-call(s32[2048,1]{1,0:T(8,128)} %bitcast.134, bf16[2048,256]{1,0:T(8,128)(2,1)} %fusion.2.q_ref, bf16[2048,512]{1,0:T(8,128)(2,1)} %copy-done.3, bf16[2048,512]{1,0:T(8,128)(2,1)} %copy-done.3, bf16[2048,512]{1,0:T(8,128)(2,1)} %collective-permute-done.kb_ref.vb_ref, ...), custom_call_target="tpu_custom_call" | custom-call | tf_op jit(solution)/shard_map/attend/pallas_call | solution.py:626
  194.4 45.4 %attended.1 = f32[256,2048]{1,0:T(8,128)} custom-call(bf16[8,256,256]{2,1,0:T(8,128)(2,1)} %bitcast.131, bf16[256,2048]{1,0:T(8,128)(2,1)} %all-gather.12.cloned.1.call-done.refs_1_.refs_0_), custom_call_target="tpu_custom_call" | custom-call | flops 1073741824 | bytes 134217728 | tf_op jit(solution)/shard_map/attended/pallas_call | solution.py:207
  244.7 9.4 %all-gather.16.cloned.1.call-done.w2_ref.refs_2_ = bf16[512,2048]{1,0:T(8,128)(2,1)} async-done(((bf16[128,2048]{1,0:T(8,128)(2,1)}), bf16[512,2048]{1,0:T(8,128)(2,1)}) %all-gather.16.cloned.1.call-update) | async-done | bytes 2097168 | tf_op jit(solution)/shard_map/all_gather | solution.py:818
  254.1 54.2 %first_units.1 = (bf16[8,256,2048]{2,1,0:T(8,128)(2,1)}, bf16[8,256,512]{2,1,0:T(8,128)(2,1)}, bf16[8,256,512]{2,1,0:T(8,128)(2,1)}, f32[1,512]{1,0:T(1,128)}, b...) custom-call(bf16[256,2048]{1,0:T(8,128)(2,1)} %add_convert_fusion.3.x_ref, bf16[8,256,2048]{2,1,0:T(8,128)(2,1)} %gather_branch.1, ...), custom_call_target="tpu_custom_call" | custom-call | flops 1073741824 | bytes 167772160 | tf_op jit(solution)/shard_map/first_units/pallas_call | solution.py:488
  313.1 34.1 %all-gather.20.cloned.1.call-done.w2_ref.refs_3_ = bf16[512,2048]{1,0:T(8,128)(2,1)} async-done(((bf16[128,2048]{1,0:T(8,128)(2,1)}), bf16[512,2048]{1,0:T(8,128)(2,1)}) %all-gather.20.cloned.1.call-update) | async-done | bytes 2097168 | tf_op jit(solution)/shard_map/all_gather | solution.py:835
  347.2 55.2 %last_units.1 = (bf16[8,256,512]{2,1,0:T(8,128)(2,1)}, f32[1,512]{1,0:T(1,128)}, f32[256,2048]{1,0:T(8,128)}, bf16[512,2048]{1,0:T(8,128)(2,1)}, bf16[2048,512]{1,0:T(8,128)(2,1)}) custom-call(bf16[8,256,2048]{2,1,0:T(8,128)(2,1)} %get-tuple-element.78.all_ref, bf16[8,256,2048]{2,1,0:T(8,128)(2,1)} %gather_branch.1, ...), custom_call_target="tpu_custom_call" | custom-call | flops 1073741824 | bytes 167772160 | tf_op jit(solution)/shard_map/last_units/pallas_call | solution.py:521
  413.9 42.0 %attended_grad.1 = (bf16[8,256,2048]{2,1,0:T(8,128)(2,1)}, bf16[8,256,256]{2,1,0:T(8,128)(2,1)}) custom-call(bf16[256,2048]{1,0:T(8,128)(2,1)} %get-tuple-element.116.x_ref, bf16[256,2048]{1,0:T(8,128)(2,1)} %all-gather.12.cloned.1.call-done.refs_1_.refs_0_, f32[1,256]{1,0:T(1,128)} %broadcast_in_dim.42.refs_1_), custom_call_target="tpu_custom_call" | custom-call | flops 1073741824 | bytes 134217728 | tf_op jit(solution)/shard_map/attended_grad/pallas_call | solution.py:108
  457.9 33.5 %attend_back.1 = (bf16[2048,256]{1,0:T(8,128)(2,1)}, bf16[2048,512]{1,0:T(8,128)(2,1)}, f32[2048,512]{1,0:T(8,128)}) custom-call(s32[2048,1]{1,0:T(8,128)} %bitcast.135, bf16[2048,256]{1,0:T(8,128)(2,1)} %fusion.2.q_ref, bf16[2048,512]{1,0:T(8,128)(2,1)} %copy-done.3, bf16[2048,512]{1,0:T(8,128)(2,1)} %copy-done.3, ...), custom_call_target="tpu_custom_call" | custom-call | tf_op jit(solution)/shard_map/attend_back/pallas_call | solution.py:639
  492.8 7.0 convolution_convert_fusion.1
  499.9 51.7 %down.1 = f32[256,2048]{1,0:T(8,128)} custom-call(bf16[8,256,512]{2,1,0:T(8,128)(2,1)} %get-tuple-element.89.refs_0_, bf16[8,256,512]{2,1,0:T(8,128)(2,1)} %get-tuple-element.90.refs_1_, bf16[512,2048]{1,0:T(8,128)(2,1)} %all-gather.16.cloned.1.call-done.w2_ref.refs_2_, bf16[512,2048]{1,0:T(8,128)(2,1)} %all-gather.20.cloned.1.call-done.w2_ref.refs_3_), custom_call_target="tpu_custom_call" | custom-call | flops 1073741824 | bytes 134217728 | tf_op jit(solution)/shard_map/down/pallas_call | solution.py:207
  553.7 19.3 %collective-permute-done.1 = bf16[2048,512]{1,0:T(8,128)(2,1)} collective-permute-done((bf16[2048,512]{1,0:T(8,128)(2,1)}, bf16[2048,512]{1,0:T(8,128)(2,1)}, u32[]{:S(2)}, u32[]{:S(2)}) %collective-permute-start.1) | collective-permute-done | bytes 2097184 | tf_op jit(solution)/shard_map/ppermute | solution.py:891
  576.7 10.1 %convolution_convert_fusion = bf16[2048,768]{1,0:T(8,128)(2,1)S(1)} fusion(bf16[2048,2048]{1,0:T(8,128)(2,1)} %bitcast.140, bf16[2048,512]{1,0:T(8,128)(2,1)S(1)} %add_convert_fusion, bf16[2048,256]{1,0:T(8,128)(2,1)S(1)} %copy-done.8), kind=kOutput, calls=%fused_computation.3 | convolution fusion | flops 6450315264 | bytes 14680064 | tf_op jit(solution)/shard_map/dot_general | solution.py:224
  605.2 50.0 %qkv_grad.1 = f32[256,2048]{1,0:T(8,128)} custom-call(bf16[8,256,768]{2,1,0:T(8,128)(2,1)} %bitcast.133, bf16[2048,768]{1,0:T(8,128)(2,1)} %pad_maximum_fusion.1.refs_1_), custom_call_target="tpu_custom_call" | custom-call | flops 1073741824 | bytes 134217728 | tf_op jit(solution)/shard_map/qkv_grad/pallas_call | solution.py:207
  663.8 4.8 all-to-all-start.2
  670.2 5.6 all-to-all-done.2
  682.9 8.7 %all-to-all-done.3 = bf16[8,64,768]{2,1,0:T(8,128)(2,1)S(1)} async-done(((bf16[8,64,768]{2,1,0:T(8,128)(2,1)}), bf16[8,64,768]{2,1,0:T(8,128)(2,1)S(1)}, u32[]{:S(2)}, u32[]{:S(2)}) %all-to-all-start.3) | async-done | bytes 786464 | tf_op jit(solution)/shard_map/all_to_all | solution.py:913
  (219 shorter events, 103.2 us)
Async XLA Ops:
  7.2 81.6 %all-gather.8.cloned.1.call-start = ((), (), s32[]{:S(2)}) async-start(), calls=%async_computation.11 | async-start | bytes 2621440 | tf_op jit(solution)/shard_map/all_gather | solution.py:782
  11.3 18.3 %copy-start.21 = (bf16[64]{0:T(256)(128)(2,1)S(1)}, bf16[64]{0:T(256)(128)(2,1)}, u32[]{:S(2)}) copy-start(bf16[64]{0:T(256)(128)(2,1)} %param.25) | copy-start | bytes 388
  11.3 18.3 %copy-start.22 = (bf16[64]{0:T(256)(128)(2,1)S(1)}, bf16[64]{0:T(256)(128)(2,1)}, u32[]{:S(2)}) copy-start(bf16[64]{0:T(256)(128)(2,1)} %param.26) | copy-start | bytes 388
  11.3 18.3 %copy-start.23 = (bf16[64]{0:T(256)(128)(2,1)S(1)}, bf16[64]{0:T(256)(128)(2,1)}, u32[]{:S(2)}) copy-start(bf16[64]{0:T(256)(128)(2,1)} %param.28) | copy-start | bytes 388
  11.5 31.3 %copy-start.2 = (bf16[1,256,2048]{2,1,0:T(8,128)(2,1)S(1)}, bf16[1,256,2048]{2,1,0:T(8,128)(2,1)}, u32[]{:S(2)}) copy-start(bf16[1,256,2048]{2,1,0:T(8,128)(2,1)} %param.20) | copy-start | bytes 3145732
  30.4 12.1 %all-to-all-start.1 = ((f32[32,1,896]{2,1,0:T(1,128)}), f32[32,1,896]{2,1,0:T(1,128)S(1)}, u32[]{:S(2)}, u32[]{:S(2)}) async-start(f32[32,1,896]{2,1,0:T(1,128)} %broadcast_in_dim.38), calls=%async_computation.1 | async-start | bytes 229376 | tf_op jit(solution)/shard_map/all_to_all | solution.py:767
  34.9 75.3 %all-gather.10.cloned.1.call-start = ((), (), s32[]{:S(2)}) async-start(), calls=%async_computation.12 | async-start | bytes 1310720 | tf_op jit(solution)/shard_map/all_gather | solution.py:782
  42.7 151.6 %all-gather.12.cloned.1.call-start = ((), (), s32[]{:S(2)}) async-start(), calls=%async_computation.13 | async-start | bytes 1310720 | tf_op jit(solution)/shard_map/all_gather | solution.py:814
  43.5 201.2 %all-gather.14.cloned.1.call-start = ((), (), s32[]{:S(2)}) async-start(), calls=%async_computation.14 | async-start | bytes 2621440 | tf_op jit(solution)/shard_map/all_gather | solution.py:817
  92.0 162.1 %all-gather.16.cloned.1.call-start = ((), (), s32[]{:S(2)}) async-start(), calls=%async_computation.15 | async-start | bytes 2621440 | tf_op jit(solution)/shard_map/all_gather | solution.py:818
  95.5 217.6 %all-gather.18.cloned.1.call-start = ((), (), s32[]{:S(2)}) async-start(), calls=%async_computation.16 | async-start | bytes 2621440 | tf_op jit(solution)/shard_map/all_gather | solution.py:834
  104.2 50.3 %copy-start.3 = (bf16[2048,512]{1,0:T(8,128)(2,1)}, bf16[2048,512]{1,0:T(8,128)(2,1)S(1)}, u32[]{:S(2)}) copy-start(bf16[2048,512]{1,0:T(8,128)(2,1)S(1)} %add_convert_fusion.1.k_ref.v_ref) | copy-start | bytes 6291460
  104.2 74.9 %collective-permute-start = (bf16[2048,512]{1,0:T(8,128)(2,1)S(1)}, bf16[2048,512]{1,0:T(8,128)(2,1)}, u32[]{:S(2)}, u32[]{:S(2)}) collective-permute-start(bf16[2048,512]{1,0:T(8,128)(2,1)S(1)} %add_convert_fusion.1.k_ref.v_ref), channel_id=1, source_target_pairs={{0,2},{2,4},{4,6},{1,3},{3,5},{5,7},{8,10},{10,12},{12,14},{9,11},... | collective-permute-start | bytes 6291464 | tf_op jit(solution)/shard_map/ppermute | solution.py:826
  192.2 155.1 %all-gather.20.cloned.1.call-start = ((), (), s32[]{:S(2)}) async-start(), calls=%async_computation.17 | async-start | bytes 2621440 | tf_op jit(solution)/shard_map/all_gather | solution.py:835
  192.9 263.0 %reduce-scatter.19.cloned.1.call-start = ((), (), s32[]{:S(2)}) async-start(), calls=%async_computation.22 | async-start | bytes 2621440
  312.3 145.6 %reduce-scatter.11.cloned.1.call-start = ((), (), s32[]{:S(2)}) async-start(), calls=%async_computation.18 | async-start | bytes 2621440 | tf_op jit(solution)/shard_map/reduce_scatter | solution.py:850
  313.1 238.6 %reduce-scatter.21.cloned.1.call-start = ((), (), s32[]{:S(2)}) async-start(), calls=%async_computation.23 | async-start | bytes 2621440
  406.4 166.6 %reduce-scatter.13.cloned.1.call-start = ((), (), s32[]{:S(2)}) async-start(), calls=%async_computation.19 | async-start | bytes 2621440 | tf_op jit(solution)/shard_map/reduce_scatter | solution.py:850
  407.1 185.7 %reduce-scatter.17.cloned.1.call-start = ((), (), s32[]{:S(2)}) async-start(), calls=%async_computation.21 | async-start | bytes 1310720 | tf_op jit(solution)/shard_map/reduce_scatter | solution.py:917
  491.5 81.5 %collective-permute-start.1 = (bf16[2048,512]{1,0:T(8,128)(2,1)}, bf16[2048,512]{1,0:T(8,128)(2,1)}, u32[]{:S(2)}, u32[]{:S(2)}) collective-permute-start(bf16[2048,512]{1,0:T(8,128)(2,1)} %get-tuple-element.91), channel_id=1, source_target_pairs={{2,0},{4,2},{6,4},{3,1},{5,3},{7,5},{10,8},{12,10},{14,12},{11,9},... | collective-permute-start | bytes 6291464 | tf_op jit(solution)/shard_map/ppermute | solution.py:891
  499.8 176.0 %reduce-scatter.15.cloned.1.call-start = ((), (), s32[]{:S(2)}) async-start(), calls=%async_computation.20 | async-start | bytes 3932160 | tf_op jit(solution)/shard_map/reduce_scatter | solution.py:912
  597.9 65.9 %all-to-all-start.4 = ((f32[4,1,384]{2,1,0:T(1,128)}), f32[4,1,384]{2,1,0:T(1,128)S(1)}, u32[]{:S(2)}, u32[]{:S(2)}) async-start(f32[4,1,384]{2,1,0:T(1,128)} %all_to_all.30), calls=%async_computation.7 | async-start | bytes 12288 | tf_op jit(solution)/shard_map/all_to_all | solution.py:906
  663.8 12.0 %all-to-all-start.2 = ((f32[32,1,384]{2,1,0:T(1,128)}), f32[32,1,384]{2,1,0:T(1,128)S(1)}, u32[]{:S(2)}, u32[]{:S(2)}) async-start(f32[32,1,384]{2,1,0:T(1,128)} %all_to_all.27), calls=%async_computation.4 | async-start | bytes 98304 | tf_op jit(solution)/shard_map/all_to_all | solution.py:906
  675.8 15.8 %all-to-all-start.3 = ((bf16[8,64,768]{2,1,0:T(8,128)(2,1)}), bf16[8,64,768]{2,1,0:T(8,128)(2,1)S(1)}, u32[]{:S(2)}, u32[]{:S(2)}) async-start(bf16[8,64,768]{2,1,0:T(8,128)(2,1)} %bitcast.157), calls=%async_computation.6 | async-start | bytes 1572864 | tf_op jit(solution)/shard_map/all_to_all | solution.py:913
  (26 other events, 227.0 us)
Sparse Core Ops, SparseCore 0:
  29.6 46.0 all-gather.7
  77.8 26.6 all-gather.9
  106.1 41.4 all-gather.11
  149.6 55.7 all-gather.13
  206.8 47.2 all-gather.15
  256.1 44.7 all-gather.17
  303.0 44.1 all-gather.19
  349.5 42.4 reduce-scatter.18
  394.4 43.1 reduce-scatter.10
  439.8 43.1 reduce-scatter.20
  485.4 72.2 reduce-scatter.12
  560.4 29.8 reduce-scatter.16
  592.8 59.1 reduce-scatter.14

commit v7 on v6

--- a/solution.py
+++ b/solution.py
@@ -151,13 +151,15 @@
     def term(rank, cols):
         if turned:
             return sum(dot_nt(a[rank], w[cols, :]) for a, w in zip(left, right))
-        return sum(dot(a[rank], w[:, cols]) for a, w in zip(left, right))
+        rows = [w[:, 1, :, cols].reshape(-1, TILE) if len(w.shape) == 4 else w[:, cols] for w in right]
+        return sum(dot(a[rank], w) for a, w in zip(left, rows))
     order = ("d", "x", "y", "o")
     twin = {"d": "ds", "x": "xs", "y": "ys", "o": "s"}
     sib = []
-    for j, d in enumerate(order):
-        def fill(cols, j=j, d=d):
-            sib_out[j, :, cols] = term(at[twin[d]], cols).astype(bfloat)
+    def to_sibling():
+        j = len(sib)
+        def fill(cols):
+            sib_out[j, :, cols] = term(at[twin[order[j]]], cols).astype(bfloat)
         tiles(0, D, fill)
         sib.append(ship(sib_out.at[j], sib_in.at[j], "s"))
     def pair(j, cols):
@@ -171,17 +173,21 @@
                 value = value + landed[extra, :, local(h, cols)].astype(single)
             stage[j, h, :, local(h, cols)] = value.astype(bfloat)
         tiles(h * mid, (h + 1) * mid, fill)
+    to_sibling()
+    to_sibling()
     sib[0].wait_recv()
     put(0, 0)
     d_a = ship(stage.at[0, 0], landed.at[0], "x")
     put(0, 1)
     d_b = ship(stage.at[0, 1], landed.at[1], "y")
+    to_sibling()
     sib[1].wait_recv()
     put(1, 0)
     x_a = ship(stage.at[1, 0], landed.at[2], "x")
     sib[2].wait_recv()
     put(2, 1)
     y_b = ship(stage.at[2, 1], landed.at[3], "y")
+    to_sibling()
     sib[3].wait_recv()
     def first(cols):
         out_ref[:, cols] = pair(3, cols)
@@ -202,7 +208,7 @@
 
 def dot_reduce(left, right, turned, cid, name):
     ranks = 8
-    D = right[0].shape[0] if turned else right[0].shape[1]
+    D = right[0].shape[0] if turned else right[0].shape[-1]
     tok = left[0].size // left[0].shape[-1] // ranks
     return pl.pallas_call(
         functools.partial(reduce_kernel, turned, len(left)),
@@ -257,21 +263,26 @@
 TWIN = {"o": "s", "x": "xs", "y": "ys", "d": "ds"}
 
 
-def hidden_units(src, branch, w1_ref, w2_ref, b_ref, hid_ref, pg_ref, pb_ref, rank):
-    pre = jnp.dot(src[...], w1_ref[...], preferred_element_type=single) + b_ref[...]
+def unit_rows(w_ref, i):
+    parts, _, units, D = w_ref.shape
+    return w_ref[:, i].reshape(parts * units, D)
+
+
+def hidden_units(src, branch, w_ref, b_ref, hid_ref, pg_ref, pb_ref, rank):
+    pre = dot_nt(src[...], unit_rows(w_ref, 0)) + b_ref[...]
     square = pre * pre
     bend = jnp.tanh(0.7978845608028654 * (pre + 0.044715 * (pre * square)))
     rise = 0.5 * (1.0 + bend)
     hid_ref[rank] = (pre * rise).astype(bfloat)
     slope = rise + (0.5 * 0.7978845608028654) * pre * (1.0 - bend * bend) * (1.0 + 3 * 0.044715 * square)
-    grad = (dot_nt(branch[...], w2_ref[...]) * slope).astype(bfloat)
+    grad = (dot_nt(branch[...], unit_rows(w_ref, 1)) * slope).astype(bfloat)
     pg_ref[rank] = grad
     pb_ref[...] += jnp.sum(grad.astype(single), axis=0, keepdims=True)
 
 
 def first_units_kernel(
-    x_ref, bg_ref, w1_ref, w2_ref, b_ref, all_ref, hid_ref, pg_ref, pb_ref, down_ref, up_ref,
-    held, bg, down_sum, up_sum, send, recv, keep, load,
+    x_ref, bg_ref, w_ref, b_ref, all_ref, hid_ref, pg_ref, pb_ref, grad_ref,
+    held, bg, total, send, recv, keep, load,
 ):
     ids, at = plane_place()
     tok = x_ref.shape[0]
@@ -299,35 +310,30 @@
         copy.start()
         kept.append(copy)
         loads[name].wait()
-        hidden_units(src, bg.at[rank], w1_ref, w2_ref, b_ref, hid_ref, pg_ref, pb_ref, rank)
+        hidden_units(src, bg.at[rank], w_ref, b_ref, hid_ref, pg_ref, pb_ref, rank)
 
     def weigh(name, last=False):
-        wide = 256
-
-        def add(total, out, here, pairs):
-            term = sum(dot_tn(left, right) for left, right in pairs)
-            if name == "o":
-                total[here, :] = term
-            elif last:
-                out[here, :] = (total[here, :] + term).astype(bfloat)
-            else:
-                total[here, :] += term
-
-        both = [(n, at[n]) for n in (name, TWIN[name])]
-
-        def down(i, _):
-            here = pl.ds(pl.multiple_of(i * wide, wide), wide)
-            add(down_sum, down_ref, here, [(hid_ref[r, :, here], bg[r]) for n, r in both])
+        units_at = grad_ref.shape[2]
+        per = 256 // units_at
+
+        def rows(i, _):
+            here = pl.ds(pl.multiple_of(i * 256, 256), 256)
+            owners = pl.ds(i * per, per)
+            for j, left in enumerate((pg_ref, hid_ref)):
+                term = 0
+                for n in (name, TWIN[name]):
+                    right = bg[at[n]] if j else (x_ref[...] if n == "o" else held[at[n]])
+                    term = term + dot_tn(left[at[n], :, here], right)
+                term = term.reshape(per, units_at, -1)
+                if name == "o":
+                    total[owners, j] = term
+                elif last:
+                    grad_ref[owners, j] = (total[owners, j] + term).astype(bfloat)
+                else:
+                    total[owners, j] += term
             return 0
 
-        def up(i, _):
-            here = pl.ds(pl.multiple_of(i * wide, wide), wide)
-            tokens = [(x_ref[:, here] if n == "o" else held[r, :, here], pg_ref[r]) for n, r in both]
-            add(up_sum, up_ref, here, tokens)
-            return 0
-
-        lax.fori_loop(0, hid_ref.shape[2] // wide, down, 0)
-        lax.fori_loop(0, x_ref.shape[1] // wide, up, 0)
+        lax.fori_loop(0, hid_ref.shape[2] // 256, rows, 0)
 
     units("o")
     s0.wait_recv()
@@ -363,12 +369,11 @@
 
 
 def last_units_kernel(
-    all_ref, bg_ref, pg1_ref, w1a_ref, w1_ref, w2_ref, b_ref, hid_ref, pb_ref, r_ref, down_ref, up_ref,
+    all_ref, bg_ref, pg1_ref, w1_ref, w_ref, b_ref, hid_ref, pb_ref, r_ref, grad_ref,
     held, bg, pg_ref, sib_out, sib_in, stage, landed, send, recv, load, load_b,
 ):
     ids, at = plane_place()
     ranks, tok, D = held.shape
-    F = w1_ref.shape[1]
     mid = D // 2
     names = ("ds", "d", "xs", "x", "ys", "y", "s", "o")
     loads = {}
@@ -387,11 +392,12 @@
         for copy in loads[name]:
             copy.wait()
         rank = at[name]
-        hidden_units(held.at[rank], bg.at[rank], w1_ref, w2_ref, b_ref, hid_ref, pg_ref, pb_ref, rank)
+        hidden_units(held.at[rank], bg.at[rank], w_ref, b_ref, hid_ref, pg_ref, pb_ref, rank)
 
     def term(name, cols):
         rank = at[name]
-        return dot_nt(pg1_ref[rank], w1a_ref[cols, :]) + dot_nt(pg_ref[rank], w1_ref[cols, :])
+        first, second = [w[:, 0, :, cols].reshape(-1, TILE) for w in (w1_ref, w_ref)]
+        return dot(pg1_ref[rank], first) + dot(pg_ref[rank], second)
 
     order = ("d", "x", "y", "o")
 
@@ -453,19 +459,19 @@
 
     tiles(0, D, first)
 
-    wide = 256
-
-    def grads(out_ref, count, value):
-        def step(i, _):
-            here = pl.ds(pl.multiple_of(i * wide, wide), wide)
-            out_ref[here, :] = value(here).astype(bfloat)
-            return 0
-
-        lax.fori_loop(0, count, step, 0)
-
-    rows = ranks * tok
-    grads(down_ref, F // wide, lambda c: dot_tn(hid_ref[:, :, c].reshape(rows, wide), bg[...].reshape(rows, D)))
-    grads(up_ref, D // wide, lambda c: dot_tn(held[:, :, c].reshape(rows, wide), pg_ref[...].reshape(rows, F)))
+    units_at = grad_ref.shape[2]
+    per = 256 // units_at
+    tokens = ranks * tok
+
+    def grads(i, _):
+        here = pl.ds(pl.multiple_of(i * 256, 256), 256)
+        owners = pl.ds(i * per, per)
+        for j, (left, right) in enumerate(((pg_ref, held), (hid_ref, bg))):
+            value = dot_tn(left[:, :, here].reshape(tokens, 256), right[...].reshape(tokens, D))
+            grad_ref[owners, j] = value.astype(bfloat).reshape(per, units_at, D)
+        return 0
+
+    lax.fori_loop(0, hid_ref.shape[2] // 256, grads, 0)
     for copy in (x_a, y_b, x_b, y_a):
         copy.wait_recv()
     for h, (n, m) in enumerate(((2, 4), (3, 5))):
@@ -479,10 +485,10 @@
         copy.wait_send()
 
 
-def first_units(x, bg, w1, w2, bias, cid):
+def first_units(x, bg, w, bias, cid):
     ranks = 8
     tok, D = x.shape
-    F = w1.shape[1]
+    F = bias.shape[1]
     anywhere = pl.BlockSpec(memory_space=pl.ANY)
     inside = pl.BlockSpec(memory_space=pltpu.VMEM)
     return pl.pallas_call(
@@ -492,16 +498,14 @@
             jax.ShapeDtypeStruct((ranks, tok, F), bfloat),
             jax.ShapeDtypeStruct((ranks, tok, F), bfloat),
             jax.ShapeDtypeStruct((1, F), single),
-            jax.ShapeDtypeStruct((F, D), bfloat),
-            jax.ShapeDtypeStruct((D, F), bfloat),
+            jax.ShapeDtypeStruct(w.shape, bfloat),
         ],
-        in_specs=[inside, anywhere, inside, inside, inside],
-        out_specs=[anywhere, inside, inside, inside, inside, inside],
+        in_specs=[inside, anywhere, inside, inside],
+        out_specs=[anywhere, inside, inside, inside, inside],
         scratch_shapes=[
             pltpu.VMEM((ranks, tok, D), bfloat),
             pltpu.VMEM((ranks, tok, D), bfloat),
-            pltpu.VMEM((F, D), single),
-            pltpu.VMEM((D, F), single),
+            pltpu.VMEM(w.shape, single),
             pltpu.SemaphoreType.DMA((10,)),
             pltpu.SemaphoreType.DMA((10,)),
             pltpu.SemaphoreType.DMA((8,)),
@@ -510,12 +514,12 @@
         compiler_params=pltpu.CompilerParams(collective_id=cid, has_side_effects=True, vmem_limit_bytes=62 << 20),
         cost_estimate=pl.CostEstimate(flops=1 << 30, bytes_accessed=160 << 20, transcendentals=0),
         name="first_units",
-    )(x, bg, w1, w2, bias)
-
-
-def last_units(rows, bg, pg, w1a, w1, w2, bias, cid):
+    )(x, bg, w, bias)
+
+
+def last_units(rows, bg, pg, w1, w, bias, cid):
     ranks, tok, D = rows.shape
-    F = w1.shape[1]
+    F = bias.shape[1]
     anywhere = pl.BlockSpec(memory_space=pl.ANY)
     inside = pl.BlockSpec(memory_space=pltpu.VMEM)
     return pl.pallas_call(
@@ -524,11 +528,10 @@
             jax.ShapeDtypeStruct((ranks, tok, F), bfloat),
             jax.ShapeDtypeStruct((1, F), single),
             jax.ShapeDtypeStruct((tok, D), single),
-            jax.ShapeDtypeStruct((F, D), bfloat),
-            jax.ShapeDtypeStruct((D, F), bfloat),
+            jax.ShapeDtypeStruct(w.shape, bfloat),
         ],
-        in_specs=[anywhere, anywhere, inside, inside, inside, inside, inside],
-        out_specs=[inside] * 5,
+        in_specs=[anywhere, anywhere, inside, inside, inside, inside],
+        out_specs=[inside] * 4,
         scratch_shapes=[
             pltpu.VMEM((ranks, tok, D), bfloat),
             pltpu.VMEM((ranks, tok, D), bfloat),
@@ -545,7 +548,7 @@
         compiler_params=pltpu.CompilerParams(collective_id=cid, has_side_effects=True, vmem_limit_bytes=62 << 20),
         cost_estimate=pl.CostEstimate(flops=1 << 30, bytes_accessed=160 << 20, transcendentals=0),
         name="last_units",
-    )(rows, bg, pg, w1a, w1, w2, bias)
+    )(rows, bg, pg, w1, w, bias)
 
 
 def windows(span):
@@ -756,6 +759,10 @@
     def mine(vector):
         return lax.dynamic_index_in_dim(to_ranks(vector), rank, 0, keepdims=False)
 
+    if whole_heads:
+        weight_o = lax.all_gather(o_weight, "z", axis=0, tiled=True)
+    else:
+        weight_o = lax.dynamic_slice_in_dim(lax.all_gather(o_weight, ALL, axis=0, tiled=True), rank * cols, cols, 0)
     qkv_parts = jnp.concatenate([to_ranks(q_weight), to_ranks(k_weight), to_ranks(v_weight)], axis=2)
     qkv_mine = lax.all_to_all(qkv_parts, PLANE, split_axis=0, concat_axis=0, tiled=True)
     qkv_mine = qkv_mine.reshape(D // Z, 3 * cols)
@@ -784,7 +791,7 @@
 
     weight_kv = feature_rows(qkv_mine[:, cols:])
     bias_kv = jnp.concatenate([jnp.zeros((cols,), single), mine(bias_v)])
-    bias_one, query_mine, o_weight = lax.optimization_barrier((bias_one, qkv_mine[:, :cols], o_weight))
+    bias_one, query_mine, weight_o = lax.optimization_barrier((bias_one, qkv_mine[:, :cols], weight_o))
     normed_low = layer_norm(local, gain_one, bias_one).astype(bfloat)
     fast = (B, X) == (4, 2)
 
@@ -807,15 +814,14 @@
 
     normed_all = gather_plane(normed_low, 0, "gather_normed")
     units = fc1_bias.shape[0] // 2
-    up_one, down_one = fc1_weight[:, :units], fc2_weight[:units]
-    normed_all, weight_kv, up_one, down_one = lax.optimization_barrier((normed_all, weight_kv, up_one, down_one))
+    halves = [jnp.concatenate([fc1_weight.T[i : i + units], fc2_weight[i : i + units]]) for i in (0, units)]
+
+    def gather_units(mine):
+        return lax.all_gather(mine, "z", axis=0, tiled=True).reshape(Z, 2, units, D)
+
+    normed_all, weight_kv, unit_one = lax.optimization_barrier((normed_all, weight_kv, halves[0]))
     weight_q = feature_rows(query_mine)
-    if whole_heads:
-        weight_o = lax.all_gather(o_weight, "z", axis=0, tiled=True)
-    else:
-        weight_o = lax.dynamic_slice_in_dim(lax.all_gather(o_weight, ALL, axis=0, tiled=True), rank * cols, cols, 0)
-    up_one = lax.all_gather(up_one, "z", axis=1, tiled=True)
-    down_one = lax.all_gather(down_one, "z", axis=0, tiled=True)
+    unit_one = gather_units(unit_one)
     key_value = (dot(normed_all, weight_kv) + bias_kv).astype(bfloat)
     up = [(i, i + 1) for i in range(Z - 1)]
     down = [(i + 1, i) for i in range(Z - 1)]
@@ -830,9 +836,8 @@
     before, query = lax.optimization_barrier((before, query))
     starts = starts.reshape(B * span, 1)
     context = attention_forward(starts, query, key_value, before, B)
-    context, up_two, down_two = lax.optimization_barrier((context, fc1_weight[:, units:], fc2_weight[units:]))
-    up_two = lax.all_gather(up_two, "z", axis=1, tiled=True)
-    down_two = lax.all_gather(down_two, "z", axis=0, tiled=True)
+    context, unit_two = lax.optimization_barrier((context, halves[1]))
+    unit_two = gather_units(unit_two)
 
     attended = reduce_plane(context, weight_o, False, 1, "attended") + bias_o
     middle = local + active * attended
@@ -846,35 +851,34 @@
         terms = sum((dot_nt if turned else dot)(a, w) for a, w in zip(left, right)).astype(bfloat)
         return lax.psum_scatter(terms, PLANE, scatter_dimension=0, tiled=True).astype(single)
 
-    def sum_z(down_grad, up_grad):
-        down_grad = lax.psum_scatter(down_grad, "z", scatter_dimension=0, tiled=True)
-        return down_grad, lax.psum_scatter(up_grad, "z", scatter_dimension=1, tiled=True)
+    def sum_z(grads):
+        return lax.psum_scatter(grads.reshape(Z * 2 * units, D), "z", scatter_dimension=0, tiled=True)
 
     if fast:
         branch_rows = branch_all.reshape(R, tok, D)
-        two_all, hidden_one, pre_one, bias_one_up, down_grad, up_grad = first_units(
-            normed_two, branch_rows, up_one, down_one, bias_up[0], 2
+        two_all, hidden_one, pre_one, bias_one_up, grads = first_units(normed_two, branch_rows, unit_one, bias_up[0], 2)
+        shard_one = sum_z(grads)
+        hidden_two, bias_two_up, normed_two_grad, grads = last_units(
+            two_all, branch_rows, pre_one, unit_one, unit_two, bias_up[1], 3
         )
-        shards_one = sum_z(down_grad, up_grad)
-        hidden_two, bias_two_up, normed_two_grad, down_grad, up_grad = last_units(
-            two_all, branch_rows, pre_one, up_one, up_two, down_two, bias_up[1], 3
-        )
-        shards_two = sum_z(down_grad, up_grad)
+        shard_two = sum_z(grads)
         up_b_halves = [bias_one_up[0], bias_two_up[0]]
     else:
         two_all = gather_plane(normed_two, 2, "gather_two")
 
-        def half_units(weight_up, weight_down, bias):
-            hidden, gelu_pull = jax.vjp(partial(jax.nn.gelu, approximate=True), dot(two_all, weight_up) + bias)
+        def half_units(weights, bias):
+            weight_up, weight_down = [weights[:, i].reshape(Z * units, D) for i in (0, 1)]
+            hidden, gelu_pull = jax.vjp(partial(jax.nn.gelu, approximate=True), dot_nt(two_all, weight_up) + bias)
             hidden = hidden.astype(bfloat)
             pre_grad = gelu_pull(dot_nt(branch_all, weight_down))[0].astype(bfloat)
-            grads = dot_tn(hidden, branch_all).astype(bfloat), dot_tn(two_all, pre_grad).astype(bfloat)
-            return hidden, pre_grad, sum_z(*grads)
-
-        hidden_one, pre_one, shards_one = half_units(up_one, down_one, bias_up[0])
-        hidden_two, pre_two, shards_two = half_units(up_two, down_two, bias_up[1])
+            grads = dot_tn(pre_grad, two_all), dot_tn(hidden, branch_all)
+            grads = jnp.stack([g.astype(bfloat).reshape(Z, units, D) for g in grads], axis=1)
+            return hidden, pre_grad, sum_z(grads), weight_up, weight_down
+
+        hidden_one, pre_one, shard_one, up_one, down_one = half_units(unit_one, bias_up[0])
+        hidden_two, pre_two, shard_two, up_two, down_two = half_units(unit_two, bias_up[1])
         up_b_halves = [column_sums(pre_one), column_sums(pre_two)]
-        normed_two_grad = sum_halves([pre_one, pre_two], [up_one, up_two], True, 3, "up_grad")
+        normed_two_grad = sum_halves([pre_one, pre_two], [up_one, up_two], False, 3, "up_grad")
     up_b_grad = jnp.stack([half.reshape(Z, units) for half in up_b_halves], axis=1).reshape(-1)
 
     middle_part, gain_two_grad, bias_two_grad = norm_backward(middle, normed_two_grad, gain_two)
@@ -884,20 +888,23 @@
     attended_all, context_grad = gather_plane_dot(
         attended_grad, weight_o, jnp.zeros((1, cols), single), bfloat, True, 5, "attended_grad"
     )
-    context_grad, shards_one = lax.optimization_barrier((context_grad, shards_one))
+    context_grad, shard_one = lax.optimization_barrier((context_grad, shard_one))
     out_w_grad = dot_tn(context, attended_all)
     query_grad, edge, pair = attention_backward(starts, query, key_value, before, context_grad, B)
-    hidden_one, edge, pair = lax.optimization_barrier((hidden_one, edge, pair))
+    hidden_one, edge, pair, query_grad = lax.optimization_barrier((hidden_one, edge, pair, query_grad))
     after = lax.ppermute(edge, "z", down)
-    branch = sum_halves([hidden_one, hidden_two], [down_one, down_two], False, 4, "down")
-    branch, after, shards_two = lax.optimization_barrier((branch, after, shards_two))
+    query_w_grad = dot_tn(normed_all, query_grad).astype(bfloat)
+    hidden_one, query_w_grad, out_w_grad = lax.optimization_barrier((hidden_one, query_w_grad, out_w_grad))
+    downs = [unit_one, unit_two] if fast else [down_one, down_two]
+    branch = sum_halves([hidden_one, hidden_two], downs, False, 4, "down")
+    branch, after, shard_two = lax.optimization_barrier((branch, after, shard_two))
     outputs = middle + active * (branch + bias_down)
     pair_grad = (pair + after.astype(single)).astype(bfloat)
-    qkv_grad = jnp.concatenate([query_grad, pair_grad], axis=1)
-    weight_qkv = jnp.concatenate([weight_q, weight_kv], axis=1)
-    normed_grad = reduce_plane(qkv_grad, weight_qkv, True, 6, "qkv_grad")
-    qkv_w_grad = dot_tn(normed_all, qkv_grad)
-    qkv_b_grad = column_sums(qkv_grad)
+    pair_w_grad = dot_tn(normed_all, pair_grad).astype(bfloat)
+    pair_grad, pair_w_grad = lax.optimization_barrier((pair_grad, pair_w_grad))
+    normed_grad = sum_halves([query_grad, pair_grad], [weight_q, weight_kv], True, 6, "qkv_grad")
+    query_b_grad = column_sums(query_grad)
+    value_b_grad = column_sums(pair_grad[:, cols:])
     input_part, gain_one_grad, bias_one_grad = norm_backward(local, normed_grad, gain_one)
     input_grad = middle_grad + input_part
 
@@ -907,15 +914,18 @@
         widths = [v.shape[0] // parts for v in vectors]
         return [summed[sum(widths[:i]) : sum(widths[: i + 1])] for i in range(len(widths))]
 
-    qkv_w_grad = qkv_w_grad.astype(bfloat).reshape(B, Z, X, rows_dev, 3 * cols)
-    qkv_w_grad = qkv_w_grad.transpose(1, 0, 2, 3, 4).reshape(D, 3 * cols)
-    qkv_w_grad = lax.psum_scatter(qkv_w_grad, "z", scatter_dimension=0, tiled=True)
-    qkv_w_grad = lax.all_to_all(qkv_w_grad.reshape(R, rows_dev, 3 * cols), PLANE, split_axis=0, concat_axis=0, tiled=True)
-    qkv_w_grad = qkv_w_grad.astype(single)
-    q_w_shard, k_w_shard, v_w_shard = [from_ranks(qkv_w_grad[..., i * cols : (i + 1) * cols]) for i in range(3)]
+    def feature_shard(grads):
+        width = grads.shape[1]
+        grads = grads.reshape(B, Z, X, rows_dev, width).transpose(1, 0, 2, 3, 4).reshape(D, width)
+        grads = lax.psum_scatter(grads, "z", scatter_dimension=0, tiled=True)
+        grads = lax.all_to_all(grads.reshape(R, rows_dev, width), PLANE, split_axis=0, concat_axis=0, tiled=True)
+        return [from_ranks(grads[..., i : i + cols]).astype(single) for i in range(0, width, cols)]
+
+    [q_w_shard] = feature_shard(query_w_grad)
+    k_w_shard, v_w_shard = feature_shard(pair_w_grad)
     if whole_heads:
         out_w_shard = lax.psum_scatter(out_w_grad.astype(bfloat), "z", scatter_dimension=0, tiled=True).astype(single)
-        q_b_shard, v_b_shard, up_b_shard = sum_to_owners([qkv_b_grad[:cols], qkv_b_grad[2 * cols :], up_b_grad], "z", Z)
+        q_b_shard, v_b_shard, up_b_shard = sum_to_owners([query_b_grad, value_b_grad, up_b_grad], "z", Z)
     else:
 
         def placed(rows):
@@ -924,8 +934,8 @@
             return lax.psum_scatter(full, ALL, scatter_dimension=0, tiled=True).astype(single)
 
         out_w_shard = placed(out_w_grad.astype(bfloat))
-        q_b_shard = placed(qkv_b_grad[:cols])
-        v_b_shard = placed(qkv_b_grad[2 * cols :])
+        q_b_shard = placed(query_b_grad)
+        v_b_shard = placed(value_b_grad)
         [up_b_shard] = sum_to_owners([up_b_grad], "z", Z)
     sums = sum_to_owners(
         [gain_one_grad, bias_one_grad, out_b_grad, gain_two_grad, bias_two_grad, down_b_grad], ALL, R * Z
@@ -944,9 +954,9 @@
         sums[2],
         sums[3],
         sums[4],
-        jnp.concatenate([shards_one[1], shards_two[1]], axis=1).astype(single),
+        jnp.concatenate([shard_one[:units], shard_two[:units]]).T.astype(single),
         up_b_shard,
-        jnp.concatenate([shards_one[0], shards_two[0]], axis=0).astype(single),
+        jnp.concatenate([shard_one[units:], shard_two[units:]]).astype(single),
         sums[5],
     )
 

time: 716 us -> 690 us (0.964)
  waiting for transfers between devices: 104 us -> 79.5 us
  Pallas kernels: 428 us -> 420 us
    all_gather x4 -> x2, waiting for transfers between devices: 43.5 us -> 9.32 us  [gather_units(): return lax.all_gather(mine, 'z', axis=0, tiled=True).reshape(Z, 2, units, D)]
    ppermute x1, waiting for transfers between devices: 19.3 us -> 33.3 us  [on_device(): after = lax.ppermute(edge, 'z', down)]
    convert_element_type x0 -> x9, local copies, waits for them, and re-layouts: none -> 9.04 us  [feature_shard(): from_ranks(grads[..., i:i + cols]).astype(single)]
    dot_general x2 -> x3, matrix products: 17.1 us -> 22.5 us  [dot_tn(): lax.dot_general(left, right, (((0,), (0,)), ((), ())), preferred_element_...]
  transfers between devices with their start and end apart: 19 -> 17, of which waited for: 7 -> 7; matrix products, arithmetic and copies ran while one was open for 15% -> 16% of each run, Pallas kernels for 60% -> 62%
where the time goes in v7:
time: 690 us; the launch traced here: 682 us
  Pallas kernels  420 us (61%)
  waiting for transfers between devices  79.5 us (12%)
  local copies, waits for them, and re-layouts  45.3 us (7%)
  matrix products  38.1 us (6%)
  other arithmetic  37.7 us (5%)
  starting transfers between devices  27.4 us (4%)
  blocking collectives  17 us (2%)
  between operations  16.6 us (2%)
    pallas_call x3, Pallas kernels, dot_reduce(): pl.pallas_call(functools.partial(reduce_kernel, turned, len(left)), out_s...  143 us
    pallas_call x3, Pallas kernels, plane_gather(): pl.pallas_call(functools.partial(gather_kernel, body_of, len(ins), len(ou...  124 us
    pallas_call x1, Pallas kernels, last_units(): pl.pallas_call(last_units_kernel, out_shape=[jax.ShapeDtypeStruct((ranks,...  54.8 us
    pallas_call x1, Pallas kernels, first_units(): pl.pallas_call(first_units_kernel, out_shape=[jax.ShapeDtypeStruct((ranks...  50.4 us
    pallas_call x1, Pallas kernels, attend_back(): pl.pallas_call(attend_back_kernel, grid=(groups,), out_shape=[jax.ShapeDt...  34 us
    ppermute x1, waiting for transfers between devices, on_device(): after = lax.ppermute(edge, 'z', down)  33.3 us
    dot_general x3, matrix products, dot_tn(): lax.dot_general(left, right, (((0,), (0,)), ((), ())), preferred_element_...  22.5 us
    ppermute x1, waiting for transfers between devices, on_device(): before = lax.ppermute(key_value, 'z', up)  18.3 us
  transfers between devices with their start and end apart: 17, of which 7 were waited for; matrix products, arithmetic and copies ran while one was open for 16% of the time, Pallas kernels for 62%

profile of v7, /device:TPU:0, one launch (start us, length us, event | category | flops | bytes accessed | tf_op | source)
XLA Modules:
  0.0 681.5 jit_solution(2882728601840046621)
XLA Ops:
  12.0 17.0 %all_to_all.42 = bf16[8,64,768]{2,1,0:T(8,128)(2,1)S(1)} all-to-all(bf16[8,64,768]{2,1,0:T(8,128)(2,1)S(1)} %pad_maximum_fusion.2), channel_id=1, replica_groups=mesh['b'=4,'z'=4,'x'=2] {'b','x'}, dimensions={0} | all-to-all | bytes 1572864 | tf_op jit(solution)/shard_map/all_to_all | solution.py:767
  33.6 4.4 all-to-all-start.1
  39.2 6.4 all-to-all-done.1
  50.8 40.4 %gather_normed.1 = bf16[8,256,2048]{2,1,0:T(8,128)(2,1)} custom-call(bf16[256,2048]{1,0:T(8,128)(2,1)} %fusion.10.x_ref), custom_call_target="tpu_custom_call" | custom-call | flops 1073741824 | bytes 134217728 | tf_op jit(solution)/shard_map/gather_normed/pallas_call | solution.py:108
  98.0 8.5 %add_convert_fusion.1.k_ref.v_ref = bf16[2048,512]{1,0:T(8,128)(2,1)S(1)} fusion(bf16[2048,2048]{1,0:T(8,128)(2,1)} %bitcast.152, bf16[2048,512]{1,0:T(8,128)(2,1)} %bitcast.157, f32[512]{0:T(512)S(1)} %concatenate.30), kind=kOutput, calls=%fused_computation.1 | convolution fusion | flops 4297064448 | bytes 12584960 | tf_op jit(solution)/shard_map/dot_general | solution.py:226
  120.0 41.8 %gather_branch.1 = bf16[8,256,2048]{2,1,0:T(8,128)(2,1)} custom-call(bf16[256,2048]{1,0:T(8,128)(2,1)} %get-tuple-element.67.x_ref), custom_call_target="tpu_custom_call" | custom-call | flops 1073741824 | bytes 134217728 | tf_op jit(solution)/shard_map/gather_branch/pallas_call | solution.py:108
  161.9 7.1 %fusion.2.q_ref = bf16[2048,256]{1,0:T(8,128)(2,1)} fusion(bf16[2048,2048]{1,0:T(8,128)(2,1)} %bitcast.153, bf16[2048,256]{1,0:T(8,128)(2,1)} %bitcast.166, f32[256]{0:T(256)S(1)} %bitcast.196), kind=kOutput, calls=%fused_computation.8 | convolution fusion | flops 2148532224 | bytes 10486784 | tf_op jit(solution)/shard_map/dot_general | solution.py:226
  169.0 18.3 %collective-permute-done.kb_ref.vb_ref = bf16[2048,512]{1,0:T(8,128)(2,1)} collective-permute-done((bf16[2048,512]{1,0:T(8,128)(2,1)S(1)}, bf16[2048,512]{1,0:T(8,128)(2,1)}, u32[]{:S(2)}, u32[]{:S(2)}) %collective-permute-start) | collective-permute-done | bytes 2097184 | tf_op jit(solution)/shard_map/ppermute | solution.py:832
  187.3 13.1 %attend.1 = bf16[2048,256]{1,0:T(8,128)(2,1)} custom-call(s32[2048,1]{1,0:T(8,128)} %bitcast.150, bf16[2048,256]{1,0:T(8,128)(2,1)} %fusion.2.q_ref, bf16[2048,512]{1,0:T(8,128)(2,1)} %copy-done.3, bf16[2048,512]{1,0:T(8,128)(2,1)} %copy-done.3, bf16[2048,512]{1,0:T(8,128)(2,1)} %collective-permute-done.kb_ref.vb_ref, ...), custom_call_target="tpu_custom_call" | custom-call | tf_op jit(solution)/shard_map/attend/pallas_call | solution.py:629
  201.8 45.6 %attended.1 = f32[256,2048]{1,0:T(8,128)} custom-call(bf16[8,256,256]{2,1,0:T(8,128)(2,1)} %bitcast.148, bf16[256,2048]{1,0:T(8,128)(2,1)} %all-gather.6.cloned.1.call-done.refs_1_.refs_0_), custom_call_target="tpu_custom_call" | custom-call | flops 1073741824 | bytes 134217728 | tf_op jit(solution)/shard_map/attended/pallas_call | solution.py:213
  252.2 50.4 %first_units.1 = (bf16[8,256,2048]{2,1,0:T(8,128)(2,1)}, bf16[8,256,512]{2,1,0:T(8,128)(2,1)}, bf16[8,256,512]{2,1,0:T(8,128)(2,1)}, f32[1,512]{1,0:T(1,128)}, bf16[4,2,128,2048]{3,2,1,0:T(8,128)(2,1)}) custom-call(bf16[256,2048]{1,0:T(8,128)(2,1)} %add_convert_fusion.3.x_ref, bf16[8,256,2048]{2,1,0:T(8,128)(2,1)} %gather_branch.1, ...), custom_call_target="tpu_custom_call" | custom-call | flops 1073741824 | bytes 167772160 | tf_op jit(solution)/shard_map/first_units/pallas_call | solution.py:494
  302.6 9.3 %all-gather.14.cloned.1.call-done = bf16[1024,2048]{1,0:T(8,128)(2,1)} async-done(((bf16[256,2048]{1,0:T(8,128)(2,1)}), bf16[1024,2048]{1,0:T(8,128)(2,1)}) %all-gather.14.cloned.1.call-update) | async-done | bytes 4194320 | tf_op jit(solution)/shard_map/all_gather | solution.py:820
  312.0 54.8 %last_units.1 = (bf16[8,256,512]{2,1,0:T(8,128)(2,1)}, f32[1,512]{1,0:T(1,128)}, f32[256,2048]{1,0:T(8,128)}, bf16[4,2,128,2048]{3,2,1,0:T(8,128)(2,1)}) custom-call(bf16[8,256,2048]{2,1,0:T(8,128)(2,1)} %get-tuple-element.77.all_ref, bf16[8,256,2048]{2,1,0:T(8,128)(2,1)} %gather_branch.1, bf16[8,256,512]{2,1,0:T(8,128)(2,1)} %get-tuple-element.78.pg1_ref, ...), custom_call_target="tpu_custom_call" | custom-call | flops 1073741824 | bytes 167772160 | tf_op jit(solution)/shard_map/last_units/pallas_call | solution.py:525
  374.4 41.9 %attended_grad.1 = (bf16[8,256,2048]{2,1,0:T(8,128)(2,1)}, bf16[8,256,256]{2,1,0:T(8,128)(2,1)}) custom-call(bf16[256,2048]{1,0:T(8,128)(2,1)} %get-tuple-element.201.x_ref, bf16[256,2048]{1,0:T(8,128)(2,1)} %all-gather.6.cloned.1.call-done.refs_1_.refs_0_, f32[1,256]{1,0:T(1,128)} %broadcast_in_dim.42.refs_1_), custom_call_target="tpu_custom_call" | custom-call | flops 1073741824 | bytes 134217728 | tf_op jit(solution)/shard_map/attended_grad/pallas_call | solution.py:108
  416.3 34.0 %attend_back.1 = (bf16[2048,256]{1,0:T(8,128)(2,1)}, bf16[2048,512]{1,0:T(8,128)(2,1)}, f32[2048,512]{1,0:T(8,128)}) custom-call(s32[2048,1]{1,0:T(8,128)} %bitcast.151, bf16[2048,256]{1,0:T(8,128)(2,1)} %fusion.2.q_ref, bf16[2048,512]{1,0:T(8,128)(2,1)} %copy-done.3, bf16[2048,512]{1,0:T(8,128)(2,1)} %copy-done.3, ...), custom_call_target="tpu_custom_call" | custom-call | tf_op jit(solution)/shard_map/attend_back/pallas_call | solution.py:642
  451.6 7.1 %fusion.32 = bf16[256,2048]{1,0:T(8,128)(2,1)} fusion(bf16[2048,256]{1,0:T(8,128)(2,1)} %attend.1, bf16[2048,2048]{1,0:T(8,128)(2,1)} %bitcast.145), kind=kOutput, calls=%fused_computation.89 | convolution fusion | flops 2147483648 | bytes 10485760 | tf_op jit(solution)/shard_map/dot_general | solution.py:230
  458.7 6.1 convolution_convert_fusion.1
  466.0 50.3 %down.1 = f32[256,2048]{1,0:T(8,128)} custom-call(bf16[8,256,512]{2,1,0:T(8,128)(2,1)} %get-tuple-element.90.refs_0_, bf16[8,256,512]{2,1,0:T(8,128)(2,1)} %get-tuple-element.91.refs_1_, bf16[4,2,128,2048]{3,2,1,0:T(8,128)(2,1)} %bitcast.144, bf16[4,2,128,2048]{3,2,1,0:T(8,128)(2,1)} %bitcast.147), custom_call_target="tpu_custom_call" | custom-call | flops 1073741824 | bytes 134217728 | tf_op jit(solution)/shard_map/down/pallas_call | solution.py:213
  516.4 33.3 %collective-permute-done.1 = bf16[2048,512]{1,0:T(8,128)(2,1)} collective-permute-done((bf16[2048,512]{1,0:T(8,128)(2,1)}, bf16[2048,512]{1,0:T(8,128)(2,1)}, u32[]{:S(2)}, u32[]{:S(2)}) %collective-permute-start.1) | collective-permute-done | bytes 2097184 | tf_op jit(solution)/shard_map/ppermute | solution.py:895
  553.2 9.2 %convolution_convert_fusion = bf16[2048,512]{1,0:T(8,128)(2,1)S(1)} fusion(bf16[2048,2048]{1,0:T(8,128)(2,1)} %bitcast.155, bf16[2048,512]{1,0:T(8,128)(2,1)S(1)} %add_convert_fusion), kind=kOutput, calls=%fused_computation.2 | convolution fusion | flops 4296015872 | bytes 12582912 | tf_op jit(solution)/shard_map/dot_general | solution.py:230
  574.9 47.6 %qkv_grad.1 = f32[256,2048]{1,0:T(8,128)} custom-call(bf16[8,256,256]{2,1,0:T(8,128)(2,1)} %bitcast.168, bf16[8,256,512]{2,1,0:T(8,128)(2,1)} %bitcast.149, bf16[2048,256]{1,0:T(8,128)(2,1)} %bitcast.167, bf16[2048,512]{1,0:T(8,128)(2,1)} %bitcast.158), custom_call_target="tpu_custom_call" | custom-call | flops 1073741824 | bytes 134217728 | tf_op jit(solution)/shard_map/qkv_grad/pallas_call | solution.py:213
  631.1 5.0 all-to-all-start.2
  638.2 5.1 all-to-all-done.2
  648.4 4.8 all-to-all-done.3
  (228 shorter events, 103.2 us)
Async XLA Ops:
  7.2 39.2 %all-gather.6.cloned.1.call-start = ((), (), s32[]{:S(2)}) async-start(), calls=%async_computation.11 | async-start | bytes 1310720 | tf_op jit(solution)/shard_map/all_gather | solution.py:763
  7.9 83.3 %all-gather.8.cloned.1.call-start = ((), (), s32[]{:S(2)}) async-start(), calls=%async_computation.12 | async-start | bytes 2621440 | tf_op jit(solution)/shard_map/all_gather | solution.py:789
  33.6 12.1 %all-to-all-start.1 = ((f32[32,1,896]{2,1,0:T(1,128)}), f32[32,1,896]{2,1,0:T(1,128)S(1)}, u32[]{:S(2)}, u32[]{:S(2)}) async-start(f32[32,1,896]{2,1,0:T(1,128)} %broadcast_in_dim.38), calls=%async_computation.1 | async-start | bytes 229376 | tf_op jit(solution)/shard_map/all_to_all | solution.py:774
  38.0 79.7 %all-gather.10.cloned.1.call-start = ((), (), s32[]{:S(2)}) async-start(), calls=%async_computation.13 | async-start | bytes 1310720 | tf_op jit(solution)/shard_map/all_gather | solution.py:789
  46.5 205.8 %all-gather.12.cloned.1.call-start = ((), (), s32[]{:S(2)}) async-start(), calls=%async_computation.14 | async-start | bytes 5242880 | tf_op jit(solution)/shard_map/all_gather | solution.py:820
  94.6 217.4 %all-gather.14.cloned.1.call-start = ((), (), s32[]{:S(2)}) async-start(), calls=%async_computation.15 | async-start | bytes 5242880 | tf_op jit(solution)/shard_map/all_gather | solution.py:820
  106.5 55.3 %copy-start.3 = (bf16[2048,512]{1,0:T(8,128)(2,1)}, bf16[2048,512]{1,0:T(8,128)(2,1)S(1)}, u32[]{:S(2)}) copy-start(bf16[2048,512]{1,0:T(8,128)(2,1)S(1)} %add_convert_fusion.1.k_ref.v_ref) | copy-start | bytes 6291460
  106.6 80.7 %collective-permute-start = (bf16[2048,512]{1,0:T(8,128)(2,1)S(1)}, bf16[2048,512]{1,0:T(8,128)(2,1)}, u32[]{:S(2)}, u32[]{:S(2)}) collective-permute-start(bf16[2048,512]{1,0:T(8,128)(2,1)S(1)} %add_convert_fusion.1.k_ref.v_ref), channel_id=1, source_target_pairs={{0,2},{2,4},{4,6},{1,3},{3,5},{5,7},{8,10},{10,12},{12,14},{9,11},... | collective-permute-start | bytes 6291464 | tf_op jit(solution)/shard_map/ppermute | solution.py:832
  187.3 13.7 %copy-start.16 = (f32[32,64]{1,0:T(8,128)S(1)}, f32[32,64]{1,0:T(8,128)}, u32[]{:S(2)}) copy-start(f32[32,64]{1,0:T(8,128)} %get-tuple-element.220) | copy-start | bytes 24580
  187.3 13.8 %copy-start.15 = (f32[32,64]{1,0:T(8,128)S(1)}, f32[32,64]{1,0:T(8,128)}, u32[]{:S(2)}) copy-start(f32[32,64]{1,0:T(8,128)} %get-tuple-element.219) | copy-start | bytes 24580
  200.4 215.9 %reduce-scatter.6.cloned.1.call-start = ((), (), s32[]{:S(2)}) async-start(), calls=%async_computation.16 | async-start | bytes 5242880 | tf_op jit(solution)/shard_map/reduce_scatter | solution.py:855
  201.8 45.6 %copy-start.22 = (f32[1,256]{1,0:T(1,128)S(1)}, f32[1,256]{1,0:T(1,128)}, u32[]{:S(2)}) copy-start(f32[1,256]{1,0:T(1,128)} %copy-done.21) | copy-start | bytes 3076
  302.6 247.0 %reduce-scatter.8.cloned.1.call-start = ((), (), s32[]{:S(2)}) async-start(), calls=%async_computation.17 | async-start | bytes 5242880 | tf_op jit(solution)/shard_map/reduce_scatter | solution.py:855
  366.9 271.3 %reduce-scatter.10.cloned.1.call-start = ((), (), s32[]{:S(2)}) async-start(), calls=%async_computation.18 | async-start | bytes 1310720 | tf_op jit(solution)/shard_map/reduce_scatter | solution.py:920
  450.3 99.4 %collective-permute-start.1 = (bf16[2048,512]{1,0:T(8,128)(2,1)}, bf16[2048,512]{1,0:T(8,128)(2,1)}, u32[]{:S(2)}, u32[]{:S(2)}) collective-permute-start(bf16[2048,512]{1,0:T(8,128)(2,1)} %get-tuple-element.92), channel_id=1, source_target_pairs={{2,0},{4,2},{6,4},{3,1},{5,3},{7,5},{10,8},{12,10},{14,12},{11,9},... | collective-permute-start | bytes 6291464 | tf_op jit(solution)/shard_map/ppermute | solution.py:895
  466.0 187.2 %reduce-scatter.12.cloned.1.call-start = ((), (), s32[]{:S(2)}) async-start(), calls=%async_computation.19 | async-start | bytes 2621440 | tf_op jit(solution)/shard_map/reduce_scatter | solution.py:920
  564.0 96.7 %reduce-scatter.14.cloned.1.call-start = ((), (), s32[]{:S(2)}) async-start(), calls=%async_computation.20 | async-start | bytes 1310720 | tf_op jit(solution)/shard_map/reduce_scatter | solution.py:927
  570.8 60.3 %all-to-all-start.4 = ((f32[4,1,384]{2,1,0:T(1,128)}), f32[4,1,384]{2,1,0:T(1,128)S(1)}, u32[]{:S(2)}, u32[]{:S(2)}) async-start(f32[4,1,384]{2,1,0:T(1,128)} %all_to_all.33), calls=%async_computation.7 | async-start | bytes 12288 | tf_op jit(solution)/shard_map/all_to_all | solution.py:913
  574.9 47.6 %copy-start.20 = (f32[256]{0:T(256)S(1)}, f32[256]{0:T(256)}, u32[]{:S(2)}) copy-start(f32[256]{0:T(256)} %copy-done.18) | copy-start | bytes 3076
  574.9 47.6 %copy-start.24 = (f32[256]{0:T(256)S(1)}, f32[256]{0:T(256)}, u32[]{:S(2)}) copy-start(f32[256]{0:T(256)} %copy-done.23) | copy-start | bytes 3076
  630.2 16.6 %copy-start.11 = (bf16[128,2048]{1,0:T(8,128)(2,1)S(1)}, bf16[128,2048]{1,0:T(8,128)(2,1)}, u32[]{:S(2)}) copy-start(bf16[128,2048]{1,0:T(8,128)(2,1)} %get-tuple-element.207) | copy-start | bytes 1572868
  631.1 12.3 %all-to-all-start.2 = ((f32[32,1,384]{2,1,0:T(1,128)}), f32[32,1,384]{2,1,0:T(1,128)S(1)}, u32[]{:S(2)}, u32[]{:S(2)}) async-start(f32[32,1,384]{2,1,0:T(1,128)} %all_to_all.30), calls=%async_computation.4 | async-start | bytes 98304 | tf_op jit(solution)/shard_map/all_to_all | solution.py:913
  643.3 9.8 %all-to-all-start.3 = ((bf16[8,64,256]{2,1,0:T(8,128)(2,1)}), bf16[8,64,256]{2,1,0:T(8,128)(2,1)S(1)}, u32[]{:S(2)}, u32[]{:S(2)}) async-start(bf16[8,64,256]{2,1,0:T(8,128)(2,1)} %bitcast.181), calls=%async_computation.6 | async-start | bytes 524288 | tf_op jit(solution)/shard_map/all_to_all | solution.py:921
  653.1 14.1 %all-to-all-start.5 = ((bf16[8,64,512]{2,1,0:T(8,128)(2,1)}), bf16[8,64,512]{2,1,0:T(8,128)(2,1)}, u32[]{:S(2)}, u32[]{:S(2)}) async-start(bf16[8,64,512]{2,1,0:T(8,128)(2,1)} %bitcast.180), calls=%async_computation.9 | async-start | bytes 1048576 | tf_op jit(solution)/shard_map/all_to_all | solution.py:921
  (31 other events, 94.9 us)
Sparse Core Ops, SparseCore 0:
  9.6 30.6 all-gather.5
  42.4 45.4 all-gather.7
  90.0 27.6 all-gather.9
  119.2 107.2 all-gather.11
  227.9 84.0 all-gather.13
  314.1 95.2 reduce-scatter.5
  411.8 87.8 reduce-scatter.7
  501.9 47.5 reduce-scatter.9
  564.1 44.3 reduce-scatter.11
  610.7 26.4 reduce-scatter.13

commit v8 on v7

--- a/solution.py
+++ b/solution.py
@@ -551,6 +551,146 @@
     )(rows, bg, pg, w1, w, bias)
 
 
+def everyone(width):
+    b, z, x = lax.axis_index("b"), lax.axis_index("z"), lax.axis_index("x")
+    rank, me = b * 2 + x, (b * 4 + z) * 2 + x
+
+    def in_plane(i):
+        other = lax.rem(rank + i, 8)
+        return other, (other // 2, z, lax.rem(other, 2))
+
+    def anywhere(i):
+        other = lax.rem(me + i, width)
+        return other, (other // 8, lax.rem(other // 2, 4), lax.rem(other, 2))
+
+    return rank, me, in_plane, anywhere
+
+
+def exchange(blocks, landed, rows, gathered, same_row, sems):
+    plane_send, plane_recv, all_send, all_recv = sems
+    width = gathered.shape[0]
+    rank, me, in_plane, anywhere = everyone(width)
+    barrier = pltpu.get_barrier_semaphore()
+
+    def each(count, body):
+        def step(i, _):
+            body(i)
+            return 0
+
+        lax.fori_loop(1, count, step, 0)
+
+    each(width, lambda i: pl.semaphore_signal(barrier, inc=1, device_id=anywhere(i)[1], device_id_type=MESH))
+    pl.semaphore_wait(barrier, width - 1)
+
+    def block(i):
+        other, device = in_plane(i)
+        return pltpu.make_async_remote_copy(
+            src_ref=blocks.at[other], dst_ref=landed.at[rank], send_sem=plane_send.at[i], recv_sem=plane_recv.at[i],
+            device_id=device, device_id_type=MESH,
+        )
+
+    def row(i):
+        other, device = anywhere(i)
+        return pltpu.make_async_remote_copy(
+            src_ref=rows.at[0] if same_row else rows.at[other], dst_ref=gathered.at[me],
+            send_sem=all_send.at[i], recv_sem=all_recv.at[i], device_id=device, device_id_type=MESH,
+        )
+
+    each(8, lambda i: block(i).start())
+    each(width, lambda i: row(i).start())
+    landed[rank] = blocks[rank]
+    gathered[me] = rows[0] if same_row else rows[me]
+    each(width, lambda i: row(i).wait())
+    each(8, lambda i: block(i).wait())
+
+
+def head_at(rank, i):
+    return (rank // 2 * 4 + i) * 2 + rank % 2
+
+
+def spread_kernel(q_ref, k_ref, v_ref, pack_ref, q_out, kv_out, pack_out, blocks, landed, gathered, *sems):
+    cols = q_out.shape[2]
+    for rank in range(8):
+        for part, ref in enumerate((q_ref, k_ref, v_ref)):
+            heads = [ref[:, head_at(rank, i) * HEAD_DIM : (head_at(rank, i) + 1) * HEAD_DIM] for i in range(4)]
+            blocks[rank, :, part * cols : (part + 1) * cols] = jnp.concatenate(heads, axis=1)
+    exchange(blocks, landed, pack_ref, gathered, True, sems)
+    q_out[...] = landed[:, :, :cols]
+    kv_out[...] = landed[:, :, cols:]
+    pack_out[...] = gathered[...]
+
+
+def settle_kernel(w_ref, rows_ref, q_out, k_out, v_out, sums_ref, landed, gathered, *sems):
+    cols = w_ref.shape[2] // 3
+    exchange(w_ref, landed, rows_ref, gathered, False, sems)
+    for part, out in enumerate((q_out, k_out, v_out)):
+        for pair in range(out.shape[1] // 128):
+            sides = []
+            for head in (2 * pair, 2 * pair + 1):
+                rank, i = head // 8 * 2 + head % 2, head // 2 % 4
+                at = part * cols + i * HEAD_DIM
+                sides.append(landed[rank, :, at : at + HEAD_DIM])
+            out[:, pair * 128 : (pair + 1) * 128] = jnp.concatenate(sides, axis=1).astype(single)
+    sums_ref[...] = jnp.sum(gathered[...], axis=0)
+
+
+def exchange_call(kernel, out_shape, args, blocks, landed, gathered, cid, name):
+    inside = pl.BlockSpec(memory_space=pltpu.VMEM)
+    width = gathered[0]
+    return pl.pallas_call(
+        kernel,
+        out_shape=out_shape,
+        in_specs=[inside] * len(args),
+        out_specs=[inside] * len(out_shape),
+        scratch_shapes=blocks
+        + [
+            pltpu.VMEM(landed, bfloat),
+            pltpu.VMEM(gathered, single),
+            pltpu.SemaphoreType.DMA((8,)),
+            pltpu.SemaphoreType.DMA((8,)),
+            pltpu.SemaphoreType.DMA((width,)),
+            pltpu.SemaphoreType.DMA((width,)),
+        ],
+        compiler_params=pltpu.CompilerParams(collective_id=cid, has_side_effects=True, vmem_limit_bytes=32 << 20),
+        cost_estimate=pl.CostEstimate(flops=1 << 20, bytes_accessed=32 << 20, transcendentals=0),
+        name=name,
+    )(*args)
+
+
+def spread(q, k, v, pack, devices, cid):
+    rows, D = q.shape
+    cols = D // 8
+    return exchange_call(
+        spread_kernel,
+        [
+            jax.ShapeDtypeStruct((8, rows, cols), bfloat),
+            jax.ShapeDtypeStruct((8, rows, 2 * cols), bfloat),
+            jax.ShapeDtypeStruct((devices, 1, pack.shape[0]), single),
+        ],
+        (q, k, v, pack[None, None]),
+        [pltpu.VMEM((8, rows, 3 * cols), bfloat)],
+        (8, rows, 3 * cols),
+        (devices, 1, pack.shape[0]),
+        cid,
+        "spread",
+    )
+
+
+def settle(weights, rows, cid):
+    _, tall, wide = weights.shape
+    D = wide // 3 * 8
+    return exchange_call(
+        settle_kernel,
+        [jax.ShapeDtypeStruct((tall, D), single)] * 3 + [jax.ShapeDtypeStruct((1, rows.shape[1]), single)],
+        (weights, rows[:, None]),
+        [],
+        weights.shape,
+        (rows.shape[0], 1, rows.shape[1]),
+        cid,
+        "settle",
+    )
+
+
 def windows(span):
     block = span // 2
     return [(i * block, i * block + block + span) for i in range(2)]
@@ -735,6 +875,7 @@
     cols = D // R
     heads = cols // HEAD_DIM
     whole_heads = rows_dev % HEAD_DIM == 0
+    fast = (B, Z, X, rows_dev) == (4, 4, 2, HEAD_DIM)
 
     group_active = (exit_layers[0] > layer_index[0]).astype(single)
     active_total = jnp.sum(group_active)
@@ -763,15 +904,18 @@
         weight_o = lax.all_gather(o_weight, "z", axis=0, tiled=True)
     else:
         weight_o = lax.dynamic_slice_in_dim(lax.all_gather(o_weight, ALL, axis=0, tiled=True), rank * cols, cols, 0)
-    qkv_parts = jnp.concatenate([to_ranks(q_weight), to_ranks(k_weight), to_ranks(v_weight)], axis=2)
-    qkv_mine = lax.all_to_all(qkv_parts, PLANE, split_axis=0, concat_axis=0, tiled=True)
-    qkv_mine = qkv_mine.reshape(D // Z, 3 * cols)
-    qkv_mine, fc2_bias = lax.optimization_barrier((qkv_mine, fc2_bias))
     small = [ln1_gain, ln1_bias, q_bias, v_bias, o_bias, ln2_gain, ln2_bias, fc2_bias]
     pack = jnp.concatenate([v.astype(single) for v in (*small, fc1_bias, lengths[0])])
-    pad = -pack.shape[0] % 128
-    pack = jnp.concatenate([pack, jnp.zeros((pad,), single)])
-    pack = lax.all_to_all(jnp.broadcast_to(pack, (R * Z, pack.shape[0])), ALL, split_axis=0, concat_axis=0, tiled=True)
+    pack = jnp.concatenate([pack, jnp.zeros((-pack.shape[0] % 128,), single)])
+    if fast:
+        query_mine, pair_mine, pack = spread(q_weight, k_weight, v_weight, pack, R * Z, 8)
+        query_mine, pair_mine, pack = query_mine.reshape(-1, cols), pair_mine.reshape(-1, 2 * cols), pack[:, 0]
+    else:
+        qkv_parts = jnp.concatenate([to_ranks(q_weight), to_ranks(k_weight), to_ranks(v_weight)], axis=2)
+        qkv_mine = lax.all_to_all(qkv_parts, PLANE, split_axis=0, concat_axis=0, tiled=True).reshape(D // Z, 3 * cols)
+        query_mine, pair_mine = qkv_mine[:, :cols], qkv_mine[:, cols:]
+        pack = jnp.broadcast_to(pack, (R * Z, pack.shape[0]))
+        pack = lax.all_to_all(pack, ALL, split_axis=0, concat_axis=0, tiled=True)
     vectors = [pack[:, i * rows_dev : (i + 1) * rows_dev].reshape(-1) for i in range(len(small))]
     gain_one, bias_one, bias_q, bias_v, bias_o, gain_two, bias_two, bias_down = vectors
     pack = pack.reshape(B, Z, X, -1)[..., len(small) * rows_dev :]
@@ -789,11 +933,10 @@
         full = lax.all_gather(mine, "z", axis=0, tiled=True)
         return full.reshape(Z, B, X, rows_dev, -1).transpose(1, 0, 2, 3, 4).reshape(D, -1)
 
-    weight_kv = feature_rows(qkv_mine[:, cols:])
+    weight_kv = feature_rows(pair_mine)
     bias_kv = jnp.concatenate([jnp.zeros((cols,), single), mine(bias_v)])
-    bias_one, query_mine, weight_o = lax.optimization_barrier((bias_one, qkv_mine[:, :cols], weight_o))
+    bias_one, query_mine, weight_o = lax.optimization_barrier((bias_one, query_mine, weight_o))
     normed_low = layer_norm(local, gain_one, bias_one).astype(bfloat)
-    fast = (B, X) == (4, 2)
 
     def gather_plane(rows, cid, name):
         if fast:
@@ -914,18 +1057,30 @@
         widths = [v.shape[0] // parts for v in vectors]
         return [summed[sum(widths[:i]) : sum(widths[: i + 1])] for i in range(len(widths))]
 
-    def feature_shard(grads):
-        width = grads.shape[1]
-        grads = grads.reshape(B, Z, X, rows_dev, width).transpose(1, 0, 2, 3, 4).reshape(D, width)
-        grads = lax.psum_scatter(grads, "z", scatter_dimension=0, tiled=True)
-        grads = lax.all_to_all(grads.reshape(R, rows_dev, width), PLANE, split_axis=0, concat_axis=0, tiled=True)
-        return [from_ranks(grads[..., i : i + cols]).astype(single) for i in range(0, width, cols)]
-
-    [q_w_shard] = feature_shard(query_w_grad)
-    k_w_shard, v_w_shard = feature_shard(pair_w_grad)
+    qkv_w_grad = jnp.concatenate([query_w_grad, pair_w_grad], axis=1)
+    qkv_w_grad = qkv_w_grad.reshape(B, Z, X, rows_dev, 3 * cols).transpose(1, 0, 2, 3, 4).reshape(D, 3 * cols)
+    qkv_w_grad = lax.psum_scatter(qkv_w_grad, "z", scatter_dimension=0, tiled=True).reshape(R, rows_dev, 3 * cols)
+    device_sums = [gain_one_grad, bias_one_grad, out_b_grad, gain_two_grad, bias_two_grad, down_b_grad]
+    if fast:
+        rank_sums = jnp.concatenate([v.reshape(Z, -1) for v in (query_b_grad, value_b_grad, up_b_grad)], axis=1)
+        here = (jnp.arange(R) == rank).reshape(B, 1, X, 1)
+        rank_sums = jnp.where(here, rank_sums[None, :, None, :], 0.0).reshape(R * Z, -1)
+        rows = jnp.concatenate([v.reshape(R * Z, -1) for v in device_sums] + [rank_sums], axis=1)
+        q_w_shard, k_w_shard, v_w_shard, summed = settle(qkv_w_grad, rows, 9)
+        sums = [summed[0, i * rows_dev : (i + 1) * rows_dev] for i in range(len(device_sums) + 2)]
+        q_b_shard, v_b_shard = sums[len(device_sums) :]
+        up_b_shard = summed[0, (len(device_sums) + 2) * rows_dev :]
+    else:
+        qkv_w_grad = lax.all_to_all(qkv_w_grad, PLANE, split_axis=0, concat_axis=0, tiled=True)
+        q_w_shard, k_w_shard, v_w_shard = [
+            from_ranks(qkv_w_grad[..., i : i + cols]).astype(single) for i in range(0, 3 * cols, cols)
+        ]
+        sums = sum_to_owners(device_sums, ALL, R * Z)
+        [up_b_shard] = sum_to_owners([up_b_grad], "z", Z)
     if whole_heads:
         out_w_shard = lax.psum_scatter(out_w_grad.astype(bfloat), "z", scatter_dimension=0, tiled=True).astype(single)
-        q_b_shard, v_b_shard, up_b_shard = sum_to_owners([query_b_grad, value_b_grad, up_b_grad], "z", Z)
+        if not fast:
+            q_b_shard, v_b_shard = sum_to_owners([query_b_grad, value_b_grad], "z", Z)
     else:
 
         def placed(rows):
@@ -936,10 +1091,6 @@
         out_w_shard = placed(out_w_grad.astype(bfloat))
         q_b_shard = placed(query_b_grad)
         v_b_shard = placed(value_b_grad)
-        [up_b_shard] = sum_to_owners([up_b_grad], "z", Z)
-    sums = sum_to_owners(
-        [gain_one_grad, bias_one_grad, out_b_grad, gain_two_grad, bias_two_grad, down_b_grad], ALL, R * Z
-    )
     return (
         outputs.astype(bfloat)[None],
         input_grad.astype(bfloat)[None],

time: 690 us -> 667 us (0.967)
  Pallas kernels: 420 us -> 457 us
  starting transfers between devices: 27.4 us -> 5.04 us
  blocking collectives: 17 us -> 0 us
  local copies, waits for them, and re-layouts: 45.3 us -> 35.9 us
  waiting for transfers between devices: 79.5 us -> 72.3 us
    pallas_call x0 -> x2, Pallas kernels: none -> 37.4 us  [exchange_call(): pl.pallas_call(kernel, out_shape=out_shape, in_specs=[inside] * len(args)...]
    all_to_all x5 -> x0, starting transfers between devices: 21.4 us -> none  [the longest x2 9.17 us: sum_to_owners(): lax.all_to_all(split, axes, split_axis=0, concat_axis=0, tiled=True)]
    all_to_all x1 -> x0, blocking collectives: 17 us -> none  [on_device(): lax.all_to_all(qkv_parts, PLANE, split_axis=0, concat_axis=0, tiled=True)]
    all_to_all x5 -> x0, waiting for transfers between devices: 16.4 us -> none  [the longest x1 6.42 us: on_device(): lax.all_to_all(jnp.broadcast_to(pack, (R * Z, pack.shape[0])), ALL, split...]
    convert_element_type x9 -> x0, local copies, waits for them, and re-layouts: 9.04 us -> none  [feature_shard(): from_ranks(grads[..., i:i + cols]).astype(single)]
    unnamed x82 -> x50, local copies, waits for them, and re-layouts: 7.63 us -> 16.1 us
    ppermute x1, waiting for transfers between devices: 18.3 us -> 26.4 us  [on_device(): before = lax.ppermute(key_value, 'z', up)]
  transfers between devices with their start and end apart: 17 -> 11, of which waited for: 7 -> 5; matrix products, arithmetic and copies ran while one was open for 16% -> 15% of each run, Pallas kernels for 62% -> 66%
where the time goes in v8:
time: 667 us; the launch traced here: 662 us
  Pallas kernels  457 us (69%)
  waiting for transfers between devices  72.3 us (11%)
  matrix products  39.8 us (6%)
  other arithmetic  36.1 us (5%)
  local copies, waits for them, and re-layouts  35.9 us (5%)
  between operations  16.3 us (2%)
    pallas_call x3, Pallas kernels, dot_reduce(): pl.pallas_call(functools.partial(reduce_kernel, turned, len(left)), out_s...  143 us
    pallas_call x3, Pallas kernels, plane_gather(): pl.pallas_call(functools.partial(gather_kernel, body_of, len(ins), len(ou...  123 us
    pallas_call x1, Pallas kernels, last_units(): pl.pallas_call(last_units_kernel, out_shape=[jax.ShapeDtypeStruct((ranks,...  54.7 us
    pallas_call x1, Pallas kernels, first_units(): pl.pallas_call(first_units_kernel, out_shape=[jax.ShapeDtypeStruct((ranks...  51.8 us
    pallas_call x2, Pallas kernels, exchange_call(): pl.pallas_call(kernel, out_shape=out_shape, in_specs=[inside] * len(args)...  37.4 us
    pallas_call x1, Pallas kernels, attend_back(): pl.pallas_call(attend_back_kernel, grid=(groups,), out_shape=[jax.ShapeDt...  33.7 us
    ppermute x1, waiting for transfers between devices, on_device(): after = lax.ppermute(edge, 'z', down)  30.5 us
    ppermute x1, waiting for transfers between devices, on_device(): before = lax.ppermute(key_value, 'z', up)  26.4 us
  transfers between devices with their start and end apart: 11, of which 5 were waited for; matrix products, arithmetic and copies ran while one was open for 15% of the time, Pallas kernels for 66%

profile of v8, /device:TPU:0, one launch (start us, length us, event | category | flops | bytes accessed | tf_op | source)
XLA Modules:
  0.0 661.9 jit_solution(11213114079891619684)
XLA Ops:
  8.6 6.1 concatenate.27
  17.6 20.5 %spread.1 = (bf16[8,64,256]{2,1,0:T(8,128)(2,1)}, bf16[8,64,512]{2,1,0:T(8,128)(2,1)}, f32[32,1,896]{2,1,0:T(1,128)S(1)}) custom-call(bf16[64,2048]{1,0:T(8,128)(2,1)S(1)} %copy-done.1, bf16[64,2048]{1,0:T(8,128)(2,1)S(1)} %copy-done.2, bf16[64,2048]{1,0:T(8,128)(2,1)S(1)} %copy-done.3, f32[1,1,896]{2,1,0:T(1,128)S(1)} %broadcast_in_dim.96.pack_ref), custom_call_target="tpu_custom_call" | custom-call | flops 1048576 | bytes 33554432 | tf_op jit(solution)/shard_map/spread/pallas_call | solution.py:640
  47.7 40.8 %gather_normed.1 = bf16[8,256,2048]{2,1,0:T(8,128)(2,1)} custom-call(bf16[256,2048]{1,0:T(8,128)(2,1)} %fusion.10.x_ref), custom_call_target="tpu_custom_call" | custom-call | flops 1073741824 | bytes 134217728 | tf_op jit(solution)/shard_map/gather_normed/pallas_call | solution.py:108
  96.3 9.3 %add_convert_fusion.1.k_ref.v_ref = bf16[2048,512]{1,0:T(8,128)(2,1)} fusion(bf16[2048,2048]{1,0:T(8,128)(2,1)} %bitcast.159, bf16[2048,512]{1,0:T(8,128)(2,1)S(1)} %bitcast.163, f32[512]{0:T(512)S(1)} %concatenate.29), kind=kOutput, calls=%fused_computation.1 | convolution fusion | flops 4297064448 | bytes 12584960 | tf_op jit(solution)/shard_map/dot_general | solution.py:226
  105.5 3.2 collective-permute-start
  110.9 40.4 %gather_branch.1 = bf16[8,256,2048]{2,1,0:T(8,128)(2,1)} custom-call(bf16[256,2048]{1,0:T(8,128)(2,1)} %get-tuple-element.73.x_ref), custom_call_target="tpu_custom_call" | custom-call | flops 1073741824 | bytes 134217728 | tf_op jit(solution)/shard_map/gather_branch/pallas_call | solution.py:108
  152.7 7.1 %fusion.2.q_ref = bf16[2048,256]{1,0:T(8,128)(2,1)} fusion(bf16[2048,2048]{1,0:T(8,128)(2,1)} %bitcast.160, bf16[2048,256]{1,0:T(8,128)(2,1)S(1)} %bitcast.168, f32[256]{0:T(256)S(1)} %bitcast.192), kind=kOutput, calls=%fused_computation.9 | convolution fusion | flops 2148532224 | bytes 10486784 | tf_op jit(solution)/shard_map/dot_general | solution.py:226
  159.8 26.4 %collective-permute-done.kb_ref.vb_ref = bf16[2048,512]{1,0:T(8,128)(2,1)} collective-permute-done((bf16[2048,512]{1,0:T(8,128)(2,1)}, bf16[2048,512]{1,0:T(8,128)(2,1)}, u32[]{:S(2)}, u32[]{:S(2)}) %collective-permute-start) | collective-permute-done | bytes 2097184 | tf_op jit(solution)/shard_map/ppermute | solution.py:975
  186.3 13.1 %attend.1 = bf16[2048,256]{1,0:T(8,128)(2,1)} custom-call(s32[2048,1]{1,0:T(8,128)} %bitcast.157, bf16[2048,256]{1,0:T(8,128)(2,1)} %fusion.2.q_ref, bf16[2048,512]{1,0:T(8,128)(2,1)} %add_convert_fusion.1.k_ref.v_ref, bf16[2048,512]{1,0:T(8,128)(2,1)} %add_convert_fusion.1.k_ref.v_ref, bf16[2048,512]{1,0:T(8,128)(2,1)} %collective-permute-done.kb_ref.vb_ref, ...), custom_call_target="tpu_custom_call" | custom-call | tf_op jit(solution)/shard_map/attend/pallas_call | solution.py:769
  200.5 44.1 %attended.1 = f32[256,2048]{1,0:T(8,128)} custom-call(bf16[8,256,256]{2,1,0:T(8,128)(2,1)} %bitcast.153, bf16[256,2048]{1,0:T(8,128)(2,1)} %all-gather.6.cloned.1.call-done.refs_1_.refs_0_), custom_call_target="tpu_custom_call" | custom-call | flops 1073741824 | bytes 134217728 | tf_op jit(solution)/shard_map/attended/pallas_call | solution.py:213
  249.4 51.8 %first_units.1 = (bf16[8,256,2048]{2,1,0:T(8,128)(2,1)}, bf16[8,256,512]{2,1,0:T(8,128)(2,1)}, bf16[8,256,512]{2,1,0:T(8,128)(2,1)}, f32[1,512]{1,0:T(1,128)}, bf16[4,2,128,2048]{3,2,1,0:T(8,128)(2,1)}) custom-call(bf16[256,2048]{1,0:T(8,128)(2,1)} %add_convert_fusion.3.x_ref, bf16[8,256,2048]{2,1,0:T(8,128)(2,1)} %gather_branch.1, ...), custom_call_target="tpu_custom_call" | custom-call | flops 1073741824 | bytes 167772160 | tf_op jit(solution)/shard_map/first_units/pallas_call | solution.py:494
  301.3 10.7 %all-gather.14.cloned.1.call-done = bf16[1024,2048]{1,0:T(8,128)(2,1)} async-done(((bf16[256,2048]{1,0:T(8,128)(2,1)}), bf16[1024,2048]{1,0:T(8,128)(2,1)}) %all-gather.14.cloned.1.call-update) | async-done | bytes 4194320 | tf_op jit(solution)/shard_map/all_gather | solution.py:963
  311.9 54.7 %last_units.1 = (bf16[8,256,512]{2,1,0:T(8,128)(2,1)}, f32[1,512]{1,0:T(1,128)}, f32[256,2048]{1,0:T(8,128)}, bf16[4,2,128,2048]{3,2,1,0:T(8,128)(2,1)}) custom-call(bf16[8,256,2048]{2,1,0:T(8,128)(2,1)} %get-tuple-element.83.all_ref, bf16[8,256,2048]{2,1,0:T(8,128)(2,1)} %gather_branch.1, bf16[8,256,512]{2,1,0:T(8,128)(2,1)} %get-tuple-element.84.pg1_ref, ...), custom_call_target="tpu_custom_call" | custom-call | flops 1073741824 | bytes 167772160 | tf_op jit(solution)/shard_map/last_units/pallas_call | solution.py:525
  374.2 42.0 %attended_grad.1 = (bf16[8,256,2048]{2,1,0:T(8,128)(2,1)}, bf16[8,256,256]{2,1,0:T(8,128)(2,1)}) custom-call(bf16[256,2048]{1,0:T(8,128)(2,1)} %get-tuple-element.177.x_ref, bf16[256,2048]{1,0:T(8,128)(2,1)} %all-gather.6.cloned.1.call-done.refs_1_.refs_0_, f32[1,256]{1,0:T(1,128)} %broadcast_in_dim.100.refs_1_), custom_call_target="tpu_custom_call" | custom-call | flops 1073741824 | bytes 134217728 | tf_op jit(solution)/shard_map/attended_grad/pallas_call | solution.py:108
  416.3 33.7 %attend_back.1 = (bf16[2048,256]{1,0:T(8,128)(2,1)}, bf16[2048,512]{1,0:T(8,128)(2,1)}, f32[2048,512]{1,0:T(8,128)}) custom-call(s32[2048,1]{1,0:T(8,128)} %bitcast.158, bf16[2048,256]{1,0:T(8,128)(2,1)} %fusion.2.q_ref, bf16[2048,512]{1,0:T(8,128)(2,1)} %add_convert_fusion.1.k_ref.v_ref, bf16[2048,512]{1,0:T(8,128)(2,1)} %add_convert_fusion.1.k_ref.v_ref, ...), custom_call_target="tpu_custom_call" | custom-call | tf_op jit(solution)/shard_map/attend_back/pallas_call | solution.py:782
  451.2 7.0 %fusion.30 = bf16[256,2048]{1,0:T(8,128)(2,1)} fusion(bf16[2048,256]{1,0:T(8,128)(2,1)} %attend.1, bf16[2048,2048]{1,0:T(8,128)(2,1)} %bitcast.150), kind=kOutput, calls=%fused_computation.93 | convolution fusion | flops 2147483648 | bytes 10485760 | tf_op jit(solution)/shard_map/dot_general | solution.py:230
  458.3 7.2 %convolution_convert_fusion.1 = bf16[2048,256]{1,0:T(8,128)(2,1)} fusion(bf16[2048,2048]{1,0:T(8,128)(2,1)} %bitcast.161, bf16[2048,256]{1,0:T(8,128)(2,1)} %get-tuple-element.94), kind=kOutput, calls=%fused_computation.10 | convolution fusion | flops 2148007936 | bytes 10485760 | tf_op jit(solution)/shard_map/dot_general | solution.py:230
  465.5 50.1 %down.1 = f32[256,2048]{1,0:T(8,128)} custom-call(bf16[8,256,512]{2,1,0:T(8,128)(2,1)} %get-tuple-element.96.refs_0_, bf16[8,256,512]{2,1,0:T(8,128)(2,1)} %get-tuple-element.97.refs_1_, bf16[4,2,128,2048]{3,2,1,0:T(8,128)(2,1)} %bitcast.149, bf16[4,2,128,2048]{3,2,1,0:T(8,128)(2,1)} %bitcast.152), custom_call_target="tpu_custom_call" | custom-call | flops 1073741824 | bytes 134217728 | tf_op jit(solution)/shard_map/down/pallas_call | solution.py:213
  515.6 30.5 %collective-permute-done.1 = bf16[2048,512]{1,0:T(8,128)(2,1)} collective-permute-done((bf16[2048,512]{1,0:T(8,128)(2,1)}, bf16[2048,512]{1,0:T(8,128)(2,1)}, u32[]{:S(2)}, u32[]{:S(2)}) %collective-permute-start.1) | collective-permute-done | bytes 2097184 | tf_op jit(solution)/shard_map/ppermute | solution.py:1038
  546.1 3.6 add_convert_fusion
  549.7 9.2 %convolution_convert_fusion = bf16[2048,512]{1,0:T(8,128)(2,1)S(1)} fusion(bf16[2048,2048]{1,0:T(8,128)(2,1)} %bitcast.162, bf16[2048,512]{1,0:T(8,128)(2,1)S(1)} %add_convert_fusion), kind=kOutput, calls=%fused_computation.3 | convolution fusion | flops 4296015872 | bytes 12582912 | tf_op jit(solution)/shard_map/dot_general | solution.py:230
  568.0 2.9 copy.64
  572.7 48.5 %qkv_grad.1 = f32[256,2048]{1,0:T(8,128)} custom-call(bf16[8,256,256]{2,1,0:T(8,128)(2,1)} %bitcast.170, bf16[8,256,512]{2,1,0:T(8,128)(2,1)} %bitcast.154, bf16[2048,256]{1,0:T(8,128)(2,1)} %bitcast.169, bf16[2048,512]{1,0:T(8,128)(2,1)} %bitcast.164), custom_call_target="tpu_custom_call" | custom-call | flops 1073741824 | bytes 134217728 | tf_op jit(solution)/shard_map/qkv_grad/pallas_call | solution.py:213
  634.5 16.8 %settle.1 = (f32[64,2048]{1,0:T(8,128)S(1)}, f32[64,2048]{1,0:T(8,128)S(1)}, f32[64,2048]{1,0:T(8,128)S(1)}, f32[1,768]{1,0:T(1,128)S(1)}) custom-call(bf16[8,64,768]{2,1,0:T(8,128)(2,1)S(1)} %bitcast.146, f32[32,1,768]{2,1,0:T(1,128)S(1)} %broadcast_in_dim.109.rows_ref), custom_call_target="tpu_custom_call" | custom-call | flops 1048576 | bytes 33554432 | tf_op jit(solution)/shard_map/settle/pallas_call | solution.py:640
  (164 shorter events, 65.9 us)
Async XLA Ops:
  7.2 36.1 %all-gather.6.cloned.1.call-start = ((), (), s32[]{:S(2)}) async-start(), calls=%async_computation.4 | async-start | bytes 1310720 | tf_op jit(solution)/shard_map/all_gather | solution.py:904
  7.9 81.8 %all-gather.8.cloned.1.call-start = ((), (), s32[]{:S(2)}) async-start(), calls=%async_computation.5 | async-start | bytes 2621440 | tf_op jit(solution)/shard_map/all_gather | solution.py:933
  17.6 22.3 %copy-start.6 = (bf16[1,256,2048]{2,1,0:T(8,128)(2,1)S(1)}, bf16[1,256,2048]{2,1,0:T(8,128)(2,1)}, u32[]{:S(2)}) copy-start(bf16[1,256,2048]{2,1,0:T(8,128)(2,1)} %param.20) | copy-start | bytes 3145732
  38.1 113.3 %all-gather.10.cloned.1.call-start = ((), (), s32[]{:S(2)}) async-start(), calls=%async_computation.6 | async-start | bytes 1310720 | tf_op jit(solution)/shard_map/all_gather | solution.py:933
  43.3 206.1 %all-gather.12.cloned.1.call-start = ((), (), s32[]{:S(2)}) async-start(), calls=%async_computation.7 | async-start | bytes 5242880 | tf_op jit(solution)/shard_map/all_gather | solution.py:963
  89.7 2.7 copy-start.17
  91.5 14.0 %copy-start.11 = (bf16[4,4,2,64,512]{4,3,2,1,0:T(8,128)(2,1)}, bf16[4,4,2,64,512]{4,3,2,1,0:T(8,128)(2,1)S(1)}, u32[]{:S(2)}) copy-start(bf16[4,4,2,64,512]{4,3,2,1,0:T(8,128)(2,1)S(1)} %copy.55) | copy-start | bytes 6291460
  91.5 220.4 %all-gather.14.cloned.1.call-start = ((), (), s32[]{:S(2)}) async-start(), calls=%async_computation.8 | async-start | bytes 5242880 | tf_op jit(solution)/shard_map/all_gather | solution.py:963
  105.5 80.8 %collective-permute-start = (bf16[2048,512]{1,0:T(8,128)(2,1)}, bf16[2048,512]{1,0:T(8,128)(2,1)}, u32[]{:S(2)}, u32[]{:S(2)}) collective-permute-start(bf16[2048,512]{1,0:T(8,128)(2,1)} %add_convert_fusion.1.k_ref.v_ref), channel_id=1, source_target_pairs={{0,2},{2,4},{4,6},{1,3},{3,5},{5,7},{8,10},{10,12},{12,14},{9,11},... | collective-permute-start | bytes 6291464 | tf_op jit(solution)/shard_map/ppermute | solution.py:975
  152.7 7.1 %copy-start.14 = (bf16[4,4,2,64,256]{4,3,2,1,0:T(8,128)(2,1)}, bf16[4,4,2,64,256]{4,3,2,1,0:T(8,128)(2,1)S(1)}, u32[]{:S(2)}) copy-start(bf16[4,4,2,64,256]{4,3,2,1,0:T(8,128)(2,1)S(1)} %copy.58) | copy-start | bytes 3145732
  199.4 216.9 %reduce-scatter.5.cloned.1.call-start = ((), (), s32[]{:S(2)}) async-start(), calls=%async_computation.9 | async-start | bytes 5242880 | tf_op jit(solution)/shard_map/reduce_scatter | solution.py:998
  301.2 244.9 %reduce-scatter.7.cloned.1.call-start = ((), (), s32[]{:S(2)}) async-start(), calls=%async_computation.10 | async-start | bytes 5242880 | tf_op jit(solution)/shard_map/reduce_scatter | solution.py:998
  366.7 1.6 copy-start.5
  366.7 257.5 %reduce-scatter.11.cloned.1.call-start = ((), (), s32[]{:S(2)}) async-start(), calls=%async_computation.12 | async-start | bytes 1310720 | tf_op jit(solution)/shard_map/reduce_scatter | solution.py:1081
  368.3 2.7 copy-start.10
  368.3 2.7 copy-start.13
  449.9 96.2 %collective-permute-start.1 = (bf16[2048,512]{1,0:T(8,128)(2,1)}, bf16[2048,512]{1,0:T(8,128)(2,1)}, u32[]{:S(2)}, u32[]{:S(2)}) collective-permute-start(bf16[2048,512]{1,0:T(8,128)(2,1)} %get-tuple-element.98), channel_id=1, source_target_pairs={{2,0},{4,2},{6,4},{3,1},{5,3},{7,5},{10,8},{12,10},{14,12},{11,9},... | collective-permute-start | bytes 6291464 | tf_op jit(solution)/shard_map/ppermute | solution.py:1038
  465.5 167.9 %reduce-scatter.9.cloned.1.call-start = ((), (), s32[]{:S(2)}) async-start(), calls=%async_computation.11 | async-start | bytes 3932160 | tf_op jit(solution)/shard_map/reduce_scatter | solution.py:1062
  549.7 9.3 %copy-start.8 = (bf16[2048,512]{1,0:T(8,128)(2,1)}, bf16[2048,512]{1,0:T(8,128)(2,1)S(1)}, u32[]{:S(2)}) copy-start(bf16[2048,512]{1,0:T(8,128)(2,1)S(1)} %add_convert_fusion) | copy-start | bytes 6291460
  549.7 9.3 %copy-start.16 = (bf16[2048,256]{1,0:T(8,128)(2,1)S(1)}, bf16[2048,256]{1,0:T(8,128)(2,1)}, u32[]{:S(2)}) copy-start(bf16[2048,256]{1,0:T(8,128)(2,1)} %convolution_convert_fusion.1) | copy-start | bytes 3145732
  563.3 2.2 copy-start.15
  624.2 4.7 copy-start.9
  629.0 2.0 copy-start.7
  629.0 2.6 copy-start.12
  (7 other events, 6.6 us)
Sparse Core Ops, SparseCore 0:
  9.6 33.6 all-gather.5
  44.8 44.7 all-gather.7
  91.3 30.4 all-gather.9
  123.2 104.4 all-gather.11
  229.1 82.8 all-gather.13
  314.1 91.7 reduce-scatter.4
  408.3 85.7 reduce-scatter.6
  497.0 47.5 reduce-scatter.10
  561.2 60.6 reduce-scatter.8

commit v9 on v8

--- a/solution.py
+++ b/solution.py
@@ -1060,6 +1060,7 @@
     qkv_w_grad = jnp.concatenate([query_w_grad, pair_w_grad], axis=1)
     qkv_w_grad = qkv_w_grad.reshape(B, Z, X, rows_dev, 3 * cols).transpose(1, 0, 2, 3, 4).reshape(D, 3 * cols)
     qkv_w_grad = lax.psum_scatter(qkv_w_grad, "z", scatter_dimension=0, tiled=True).reshape(R, rows_dev, 3 * cols)
+    qkv_w_grad, out_w_grad = lax.optimization_barrier((qkv_w_grad, out_w_grad))
     device_sums = [gain_one_grad, bias_one_grad, out_b_grad, gain_two_grad, bias_two_grad, down_b_grad]
     if fast:
         rank_sums = jnp.concatenate([v.reshape(Z, -1) for v in (query_b_grad, value_b_grad, up_b_grad)], axis=1)

time: 667 us -> 658 us (0.987)
  waiting for transfers between devices: 72.3 us -> 64.1 us
    ppermute x1, waiting for transfers between devices: 30.5 us -> 14.1 us  [on_device(): after = lax.ppermute(edge, 'z', down)]
    unnamed x50 -> x56, local copies, waits for them, and re-layouts: 16.1 us -> 15.2 us
  transfers between devices with their start and end apart: 11 -> 11, of which waited for: 5 -> 7; matrix products, arithmetic and copies ran while one was open for 15% -> 13% of each run, Pallas kernels for 66% -> 70%
where the time goes in v9:
time: 658 us; the launch traced here: 653 us
  Pallas kernels  458 us (70%)
  waiting for transfers between devices  64.1 us (10%)
  matrix products  39.3 us (6%)
  other arithmetic  34.9 us (5%)
  local copies, waits for them, and re-layouts  34.9 us (5%)
  between operations  16.3 us (2%)
    pallas_call x3, Pallas kernels, dot_reduce(): pl.pallas_call(functools.partial(reduce_kernel, turned, len(left)), out_s...  143 us
    pallas_call x3, Pallas kernels, plane_gather(): pl.pallas_call(functools.partial(gather_kernel, body_of, len(ins), len(ou...  123 us
    pallas_call x1, Pallas kernels, last_units(): pl.pallas_call(last_units_kernel, out_shape=[jax.ShapeDtypeStruct((ranks,...  54.7 us
    pallas_call x1, Pallas kernels, first_units(): pl.pallas_call(first_units_kernel, out_shape=[jax.ShapeDtypeStruct((ranks...  51.8 us
    pallas_call x2, Pallas kernels, exchange_call(): pl.pallas_call(kernel, out_shape=out_shape, in_specs=[inside] * len(args)...  38.5 us
    pallas_call x1, Pallas kernels, attend_back(): pl.pallas_call(attend_back_kernel, grid=(groups,), out_shape=[jax.ShapeDt...  33.8 us
    ppermute x1, waiting for transfers between devices, on_device(): before = lax.ppermute(key_value, 'z', up)  26.4 us
    dot_general x3, matrix products, dot_tn(): lax.dot_general(left, right, (((0,), (0,)), ((), ())), preferred_element_...  23 us
  transfers between devices with their start and end apart: 11, of which 7 were waited for; matrix products, arithmetic and copies ran while one was open for 13% of the time, Pallas kernels for 70%

profile of v9, /device:TPU:0, one launch (start us, length us, event | category | flops | bytes accessed | tf_op | source)
XLA Modules:
  0.0 652.5 jit_solution(4811675542199862521)
XLA Ops:
  8.6 6.1 concatenate.27
  17.6 20.5 %spread.1 = (bf16[8,64,256]{2,1,0:T(8,128)(2,1)}, bf16[8,64,512]{2,1,0:T(8,128)(2,1)}, f32[32,1,896]{2,1,0:T(1,128)S(1)}) custom-call(bf16[64,2048]{1,0:T(8,128)(2,1)S(1)} %copy-done.1, bf16[64,2048]{1,0:T(8,128)(2,1)S(1)} %copy-done.2, bf16[64,2048]{1,0:T(8,128)(2,1)S(1)} %copy-done.3, f32[1,1,896]{2,1,0:T(1,128)S(1)} %broadcast_in_dim.96.pack_ref), custom_call_target="tpu_custom_call" | custom-call | flops 1048576 | bytes 33554432 | tf_op jit(solution)/shard_map/spread/pallas_call | solution.py:640
  47.7 40.8 %gather_normed.1 = bf16[8,256,2048]{2,1,0:T(8,128)(2,1)} custom-call(bf16[256,2048]{1,0:T(8,128)(2,1)} %fusion.10.x_ref), custom_call_target="tpu_custom_call" | custom-call | flops 1073741824 | bytes 134217728 | tf_op jit(solution)/shard_map/gather_normed/pallas_call | solution.py:108
  96.3 9.3 %add_convert_fusion.1.k_ref.v_ref = bf16[2048,512]{1,0:T(8,128)(2,1)} fusion(bf16[2048,2048]{1,0:T(8,128)(2,1)} %bitcast.159, bf16[2048,512]{1,0:T(8,128)(2,1)S(1)} %bitcast.163, f32[512]{0:T(512)S(1)} %concatenate.29), kind=kOutput, calls=%fused_computation.1 | convolution fusion | flops 4297064448 | bytes 12584960 | tf_op jit(solution)/shard_map/dot_general | solution.py:226
  111.0 40.4 %gather_branch.1 = bf16[8,256,2048]{2,1,0:T(8,128)(2,1)} custom-call(bf16[256,2048]{1,0:T(8,128)(2,1)} %get-tuple-element.75.x_ref), custom_call_target="tpu_custom_call" | custom-call | flops 1073741824 | bytes 134217728 | tf_op jit(solution)/shard_map/gather_branch/pallas_call | solution.py:108
  152.8 7.1 %fusion.2.q_ref = bf16[2048,256]{1,0:T(8,128)(2,1)} fusion(bf16[2048,2048]{1,0:T(8,128)(2,1)} %bitcast.160, bf16[2048,256]{1,0:T(8,128)(2,1)S(1)} %bitcast.168, f32[256]{0:T(256)S(1)} %bitcast.192), kind=kOutput, calls=%fused_computation.9 | convolution fusion | flops 2148532224 | bytes 10486784 | tf_op jit(solution)/shard_map/dot_general | solution.py:226
  159.9 26.4 %collective-permute-done.kb_ref.vb_ref = bf16[2048,512]{1,0:T(8,128)(2,1)} collective-permute-done((bf16[2048,512]{1,0:T(8,128)(2,1)}, bf16[2048,512]{1,0:T(8,128)(2,1)}, u32[]{:S(2)}, u32[]{:S(2)}) %collective-permute-start) | collective-permute-done | bytes 2097184 | tf_op jit(solution)/shard_map/ppermute | solution.py:975
  186.3 13.1 %attend.1 = bf16[2048,256]{1,0:T(8,128)(2,1)} custom-call(s32[2048,1]{1,0:T(8,128)} %bitcast.157, bf16[2048,256]{1,0:T(8,128)(2,1)} %fusion.2.q_ref, bf16[2048,512]{1,0:T(8,128)(2,1)} %add_convert_fusion.1.k_ref.v_ref, bf16[2048,512]{1,0:T(8,128)(2,1)} %add_convert_fusion.1.k_ref.v_ref, bf16[2048,512]{1,0:T(8,128)(2,1)} %collective-permute-done.kb_ref.vb_ref, ...), custom_call_target="tpu_custom_call" | custom-call | tf_op jit(solution)/shard_map/attend/pallas_call | solution.py:769
  200.5 44.0 %attended.1 = f32[256,2048]{1,0:T(8,128)} custom-call(bf16[8,256,256]{2,1,0:T(8,128)(2,1)} %bitcast.153, bf16[256,2048]{1,0:T(8,128)(2,1)} %all-gather.6.cloned.1.call-done.refs_1_.refs_0_), custom_call_target="tpu_custom_call" | custom-call | flops 1073741824 | bytes 134217728 | tf_op jit(solution)/shard_map/attended/pallas_call | solution.py:213
  249.3 51.8 %first_units.1 = (bf16[8,256,2048]{2,1,0:T(8,128)(2,1)}, bf16[8,256,512]{2,1,0:T(8,128)(2,1)}, bf16[8,256,512]{2,1,0:T(8,128)(2,1)}, f32[1,512]{1,0:T(1,128)}, bf16[4,2,128,2048]{3,2,1,0:T(8,128)(2,1)}) custom-call(bf16[256,2048]{1,0:T(8,128)(2,1)} %add_convert_fusion.3.x_ref, bf16[8,256,2048]{2,1,0:T(8,128)(2,1)} %gather_branch.1, ...), custom_call_target="tpu_custom_call" | custom-call | flops 1073741824 | bytes 167772160 | tf_op jit(solution)/shard_map/first_units/pallas_call | solution.py:494
  301.2 10.8 %all-gather.14.cloned.1.call-done = bf16[1024,2048]{1,0:T(8,128)(2,1)} async-done(((bf16[256,2048]{1,0:T(8,128)(2,1)}), bf16[1024,2048]{1,0:T(8,128)(2,1)}) %all-gather.14.cloned.1.call-update) | async-done | bytes 4194320 | tf_op jit(solution)/shard_map/all_gather | solution.py:963
  311.9 54.7 %last_units.1 = (bf16[8,256,512]{2,1,0:T(8,128)(2,1)}, f32[1,512]{1,0:T(1,128)}, f32[256,2048]{1,0:T(8,128)}, bf16[4,2,128,2048]{3,2,1,0:T(8,128)(2,1)}) custom-call(bf16[8,256,2048]{2,1,0:T(8,128)(2,1)} %get-tuple-element.85.all_ref, bf16[8,256,2048]{2,1,0:T(8,128)(2,1)} %gather_branch.1, bf16[8,256,512]{2,1,0:T(8,128)(2,1)} %get-tuple-element.86.pg1_ref, ...), custom_call_target="tpu_custom_call" | custom-call | flops 1073741824 | bytes 167772160 | tf_op jit(solution)/shard_map/last_units/pallas_call | solution.py:525
  374.1 42.0 %attended_grad.1 = (bf16[8,256,2048]{2,1,0:T(8,128)(2,1)}, bf16[8,256,256]{2,1,0:T(8,128)(2,1)}) custom-call(bf16[256,2048]{1,0:T(8,128)(2,1)} %get-tuple-element.181.x_ref, bf16[256,2048]{1,0:T(8,128)(2,1)} %all-gather.6.cloned.1.call-done.refs_1_.refs_0_, f32[1,256]{1,0:T(1,128)} %broadcast_in_dim.100.refs_1_), custom_call_target="tpu_custom_call" | custom-call | flops 1073741824 | bytes 134217728 | tf_op jit(solution)/shard_map/attended_grad/pallas_call | solution.py:108
  416.2 33.8 %attend_back.1 = (bf16[2048,256]{1,0:T(8,128)(2,1)}, bf16[2048,512]{1,0:T(8,128)(2,1)}, f32[2048,512]{1,0:T(8,128)}) custom-call(s32[2048,1]{1,0:T(8,128)} %bitcast.158, bf16[2048,256]{1,0:T(8,128)(2,1)} %fusion.2.q_ref, bf16[2048,512]{1,0:T(8,128)(2,1)} %add_convert_fusion.1.k_ref.v_ref, bf16[2048,512]{1,0:T(8,128)(2,1)} %add_convert_fusion.1.k_ref.v_ref, ...), custom_call_target="tpu_custom_call" | custom-call | tf_op jit(solution)/shard_map/attend_back/pallas_call | solution.py:782
  451.3 6.8 %fusion.30 = bf16[256,2048]{1,0:T(8,128)(2,1)} fusion(bf16[2048,256]{1,0:T(8,128)(2,1)S(1)} %copy-done.9, bf16[2048,2048]{1,0:T(8,128)(2,1)} %bitcast.150), kind=kOutput, calls=%fused_computation.93 | convolution fusion | flops 2147483648 | bytes 10485760 | tf_op jit(solution)/shard_map/dot_general | solution.py:230
  458.1 6.9 %convolution_convert_fusion.1 = bf16[2048,256]{1,0:T(8,128)(2,1)} fusion(bf16[2048,2048]{1,0:T(8,128)(2,1)} %bitcast.161, bf16[2048,256]{1,0:T(8,128)(2,1)S(1)} %copy-done.17), kind=kOutput, calls=%fused_computation.10 | convolution fusion | flops 2148007936 | bytes 10485760 | tf_op jit(solution)/shard_map/dot_general | solution.py:230
  465.0 50.1 %down.1 = f32[256,2048]{1,0:T(8,128)} custom-call(bf16[8,256,512]{2,1,0:T(8,128)(2,1)} %get-tuple-element.98.refs_0_, bf16[8,256,512]{2,1,0:T(8,128)(2,1)} %get-tuple-element.99.refs_1_, bf16[4,2,128,2048]{3,2,1,0:T(8,128)(2,1)} %bitcast.149, bf16[4,2,128,2048]{3,2,1,0:T(8,128)(2,1)} %bitcast.152), custom_call_target="tpu_custom_call" | custom-call | flops 1073741824 | bytes 134217728 | tf_op jit(solution)/shard_map/down/pallas_call | solution.py:213
  515.1 14.1 %collective-permute-done.1 = bf16[2048,512]{1,0:T(8,128)(2,1)} collective-permute-done((bf16[2048,512]{1,0:T(8,128)(2,1)}, bf16[2048,512]{1,0:T(8,128)(2,1)}, u32[]{:S(2)}, u32[]{:S(2)}) %collective-permute-start.1) | collective-permute-done | bytes 2097184 | tf_op jit(solution)/shard_map/ppermute | solution.py:1038
  529.2 3.6 add_convert_fusion
  532.8 9.2 %convolution_convert_fusion = bf16[2048,512]{1,0:T(8,128)(2,1)S(1)} fusion(bf16[2048,2048]{1,0:T(8,128)(2,1)} %bitcast.162, bf16[2048,512]{1,0:T(8,128)(2,1)S(1)} %add_convert_fusion), kind=kOutput, calls=%fused_computation.3 | convolution fusion | flops 4296015872 | bytes 12582912 | tf_op jit(solution)/shard_map/dot_general | solution.py:230
  554.8 48.7 %qkv_grad.1 = f32[256,2048]{1,0:T(8,128)} custom-call(bf16[8,256,256]{2,1,0:T(8,128)(2,1)} %bitcast.170, bf16[8,256,512]{2,1,0:T(8,128)(2,1)} %bitcast.154, bf16[2048,256]{1,0:T(8,128)(2,1)} %bitcast.169, bf16[2048,512]{1,0:T(8,128)(2,1)} %bitcast.164), custom_call_target="tpu_custom_call" | custom-call | flops 1073741824 | bytes 134217728 | tf_op jit(solution)/shard_map/qkv_grad/pallas_call | solution.py:213
  606.5 3.8 reduce-scatter.9.cloned.1.call-done
  617.7 18.0 %settle.1 = (f32[64,2048]{1,0:T(8,128)S(1)}, f32[64,2048]{1,0:T(8,128)S(1)}, f32[64,2048]{1,0:T(8,128)S(1)}, f32[1,768]{1,0:T(1,128)S(1)}) custom-call(bf16[8,64,768]{2,1,0:T(8,128)(2,1)S(1)} %bitcast.146, f32[32,1,768]{2,1,0:T(1,128)S(1)} %broadcast_in_dim.109.rows_ref), custom_call_target="tpu_custom_call" | custom-call | flops 1048576 | bytes 33554432 | tf_op jit(solution)/shard_map/settle/pallas_call | solution.py:640
  636.8 4.5 reduce-scatter.11.cloned.1.call-done
  (170 shorter events, 69.8 us)
Async XLA Ops:
  7.2 36.1 %all-gather.6.cloned.1.call-start = ((), (), s32[]{:S(2)}) async-start(), calls=%async_computation.4 | async-start | bytes 1310720 | tf_op jit(solution)/shard_map/all_gather | solution.py:904
  7.9 81.8 %all-gather.8.cloned.1.call-start = ((), (), s32[]{:S(2)}) async-start(), calls=%async_computation.5 | async-start | bytes 2621440 | tf_op jit(solution)/shard_map/all_gather | solution.py:933
  17.6 22.3 %copy-start.7 = (bf16[1,256,2048]{2,1,0:T(8,128)(2,1)S(1)}, bf16[1,256,2048]{2,1,0:T(8,128)(2,1)}, u32[]{:S(2)}) copy-start(bf16[1,256,2048]{2,1,0:T(8,128)(2,1)} %param.20) | copy-start | bytes 3145732
  38.1 113.3 %all-gather.10.cloned.1.call-start = ((), (), s32[]{:S(2)}) async-start(), calls=%async_computation.6 | async-start | bytes 1310720 | tf_op jit(solution)/shard_map/all_gather | solution.py:933
  43.3 206.0 %all-gather.12.cloned.1.call-start = ((), (), s32[]{:S(2)}) async-start(), calls=%async_computation.7 | async-start | bytes 5242880 | tf_op jit(solution)/shard_map/all_gather | solution.py:963
  89.7 2.7 copy-start.20
  91.5 14.0 %copy-start.13 = (bf16[4,4,2,64,512]{4,3,2,1,0:T(8,128)(2,1)}, bf16[4,4,2,64,512]{4,3,2,1,0:T(8,128)(2,1)S(1)}, u32[]{:S(2)}) copy-start(bf16[4,4,2,64,512]{4,3,2,1,0:T(8,128)(2,1)S(1)} %copy.55) | copy-start | bytes 6291460
  91.5 220.4 %all-gather.14.cloned.1.call-start = ((), (), s32[]{:S(2)}) async-start(), calls=%async_computation.8 | async-start | bytes 5242880 | tf_op jit(solution)/shard_map/all_gather | solution.py:963
  105.5 80.8 %collective-permute-start = (bf16[2048,512]{1,0:T(8,128)(2,1)}, bf16[2048,512]{1,0:T(8,128)(2,1)}, u32[]{:S(2)}, u32[]{:S(2)}) collective-permute-start(bf16[2048,512]{1,0:T(8,128)(2,1)} %add_convert_fusion.1.k_ref.v_ref), channel_id=1, source_target_pairs={{0,2},{2,4},{4,6},{1,3},{3,5},{5,7},{8,10},{10,12},{12,14},{9,11},... | collective-permute-start | bytes 6291464 | tf_op jit(solution)/shard_map/ppermute | solution.py:975
  152.8 7.1 %copy-start.16 = (bf16[4,4,2,64,256]{4,3,2,1,0:T(8,128)(2,1)}, bf16[4,4,2,64,256]{4,3,2,1,0:T(8,128)(2,1)S(1)}, u32[]{:S(2)}) copy-start(bf16[4,4,2,64,256]{4,3,2,1,0:T(8,128)(2,1)S(1)} %copy.58) | copy-start | bytes 3145732
  199.4 216.8 %reduce-scatter.5.cloned.1.call-start = ((), (), s32[]{:S(2)}) async-start(), calls=%async_computation.9 | async-start | bytes 5242880 | tf_op jit(solution)/shard_map/reduce_scatter | solution.py:998
  301.1 228.0 %reduce-scatter.7.cloned.1.call-start = ((), (), s32[]{:S(2)}) async-start(), calls=%async_computation.10 | async-start | bytes 5242880 | tf_op jit(solution)/shard_map/reduce_scatter | solution.py:998
  366.7 243.6 %reduce-scatter.9.cloned.1.call-start = ((), (), s32[]{:S(2)}) async-start(), calls=%async_computation.11 | async-start | bytes 3932160 | tf_op jit(solution)/shard_map/reduce_scatter | solution.py:1062
  368.2 2.7 copy-start.12
  368.2 2.7 copy-start.15
  416.2 35.1 %copy-start.9 = (bf16[2048,256]{1,0:T(8,128)(2,1)S(1)}, bf16[2048,256]{1,0:T(8,128)(2,1)}, u32[]{:S(2)}) copy-start(bf16[2048,256]{1,0:T(8,128)(2,1)} %attend.1) | copy-start | bytes 3145732
  450.0 79.2 %collective-permute-start.1 = (bf16[2048,512]{1,0:T(8,128)(2,1)}, bf16[2048,512]{1,0:T(8,128)(2,1)}, u32[]{:S(2)}, u32[]{:S(2)}) collective-permute-start(bf16[2048,512]{1,0:T(8,128)(2,1)} %get-tuple-element.100), channel_id=1, source_target_pairs={{2,0},{4,2},{6,4},{3,1},{5,3},{7,5},{10,8},{12,10},{14,12},{11,9},... | collective-permute-start | bytes 6291464 | tf_op jit(solution)/shard_map/ppermute | solution.py:1038
  451.3 6.8 %copy-start.17 = (bf16[2048,256]{1,0:T(8,128)(2,1)S(1)}, bf16[2048,256]{1,0:T(8,128)(2,1)}, u32[]{:S(2)}) copy-start(bf16[2048,256]{1,0:T(8,128)(2,1)} %get-tuple-element.96) | copy-start | bytes 3145732
  532.8 21.5 %copy-start.10 = (bf16[2048,512]{1,0:T(8,128)(2,1)}, bf16[2048,512]{1,0:T(8,128)(2,1)S(1)}, u32[]{:S(2)}) copy-start(bf16[2048,512]{1,0:T(8,128)(2,1)S(1)} %add_convert_fusion) | copy-start | bytes 6291460
  532.8 9.3 %copy-start.19 = (bf16[2048,256]{1,0:T(8,128)(2,1)S(1)}, bf16[2048,256]{1,0:T(8,128)(2,1)}, u32[]{:S(2)}) copy-start(bf16[2048,256]{1,0:T(8,128)(2,1)} %convolution_convert_fusion.1) | copy-start | bytes 3145732
  544.1 97.2 %reduce-scatter.11.cloned.1.call-start = ((), (), s32[]{:S(2)}) async-start(), calls=%async_computation.12 | async-start | bytes 1310720 | tf_op jit(solution)/shard_map/reduce_scatter | solution.py:1082
  610.3 3.0 copy-start.11
  610.3 3.0 copy-start.6
  613.3 2.6 copy-start.14
  (10 other events, 13.1 us)
Sparse Core Ops, SparseCore 0:
  9.6 33.6 all-gather.5
  44.8 44.7 all-gather.7
  91.3 30.4 all-gather.9
  123.2 104.3 all-gather.11
  229.1 82.8 all-gather.13
  314.1 91.6 reduce-scatter.4
  408.2 85.7 reduce-scatter.6
  544.3 65.9 reduce-scatter.8
  612.6 28.7 reduce-scatter.10

commit v10 on v9

--- a/solution.py
+++ b/solution.py
@@ -50,9 +50,10 @@
         return 0
     lax.fori_loop(lo // TILE, hi // TILE, step, 0)
 
-def gather_kernel(body_of, n_in, n_out, x_ref, *refs):
+def gather_kernel(body_of, beside, n_in, n_out, x_ref, *refs):
     ins = refs[:n_in]; all_ref = refs[n_in]; outs = refs[n_in + 1 : n_in + 1 + n_out]
-    held, send, recv, keep = refs[n_in + 1 + n_out :]
+    held, send, recv, keep, *more = refs[n_in + 1 + n_out :]
+    work = None if beside is None else beside(ins, outs, more)
     ids, at = plane_place()
     half = x_ref.shape[0] // 2
     parts = (pl.ds(0, half), pl.ds(half, half))
@@ -83,6 +84,8 @@
     ry = ship(held.at[at["x"], parts[0]], held.at[at["x"], parts[0]], "y")
     y1.wait_recv()
     rx = ship(held.at[at["y"], parts[1]], held.at[at["y"], parts[1]], "x")
+    if work is not None:
+        work()
     x1.wait_recv()
     sx = ship(held.at[at["x"]], held.at[at["x"]], "s")
     y0.wait_recv()
@@ -103,26 +106,26 @@
 
 def vmem(n): return [pl.BlockSpec(memory_space=pltpu.VMEM)] * n
 
-def plane_gather(x, ins, out_types, body_of, cid, name, ranks=8):
+def plane_gather(x, ins, out_types, body_of, cid, name, ranks=8, beside=None, far=(), more=()):
     tok, D = x.shape
     res = pl.pallas_call(
-        functools.partial(gather_kernel, body_of, len(ins), len(out_types)),
+        functools.partial(gather_kernel, body_of, beside, len(ins) + len(far), len(out_types)),
         out_shape=[jax.ShapeDtypeStruct((ranks, tok, D), x.dtype), *out_types],
-        in_specs=vmem(1 + len(ins)),
+        in_specs=vmem(1 + len(ins)) + [pl.BlockSpec(memory_space=pl.ANY)] * len(far),
         out_specs=[pl.BlockSpec(memory_space=pl.ANY)] + vmem(len(out_types)),
-        scratch_shapes=[pltpu.VMEM((ranks, tok, D), x.dtype), pltpu.SemaphoreType.DMA((10,)), pltpu.SemaphoreType.DMA((10,)), pltpu.SemaphoreType.DMA((8,))],
+        scratch_shapes=[pltpu.VMEM((ranks, tok, D), x.dtype), pltpu.SemaphoreType.DMA((10,)), pltpu.SemaphoreType.DMA((10,)), pltpu.SemaphoreType.DMA((8,)), *more],
         compiler_params=pltpu.CompilerParams(collective_id=cid, has_side_effects=True, vmem_limit_bytes=60 << 20),
         cost_estimate=pl.CostEstimate(flops=1 << 30, bytes_accessed=128 << 20, transcendentals=0),
         name=name,
-    )(x, *ins)
+    )(x, *ins, *far)
     return res[0].reshape(ranks * tok, D), *res[1:]
 
-def gather_dot(x, w, bias, out_dtype, turned, cid, name):
+def gather_dot(x, w, bias, out_dtype, turned, cid, name, extra_out=(), **beside):
     ranks, tok, D = 8, *x.shape
     N = w.shape[0] if turned else w.shape[1]
     tile = min(N, 512) if N % 512 == 0 else 256
     def body(rank, src, ins, outs):
-        w_ref, b_ref = ins
+        w_ref, b_ref = ins[:2]
         def step(i, _):
             cols = pl.ds(pl.multiple_of(i * tile, tile), tile)
             if turned:
@@ -132,8 +135,9 @@
             outs[0][rank, :, cols] = (y + b_ref[:, cols]).astype(out_dtype)
             return 0
         lax.fori_loop(0, N // tile, step, 0)
-    all_, y = plane_gather(x, (w, bias), [jax.ShapeDtypeStruct((ranks, tok, N), out_dtype)], body, cid, name)
-    return all_, y.reshape(ranks * tok, N)
+    types = [jax.ShapeDtypeStruct((ranks, tok, N), out_dtype), *extra_out]
+    all_, y, *rest = plane_gather(x, (w, bias), types, body, cid, name, **beside)
+    return all_, y.reshape(ranks * tok, N), *rest
 
 def reduce_kernel(turned, pairs, *refs):
     left, right = refs[:pairs], refs[pairs : 2 * pairs]
@@ -155,49 +159,49 @@
         return sum(dot(a[rank], w) for a, w in zip(left, rows))
     order = ("d", "x", "y", "o")
     twin = {"d": "ds", "x": "xs", "y": "ys", "o": "s"}
-    sib = []
-    def to_sibling():
-        j = len(sib)
+    sib = {}
+    def to_sibling(j, h):
         def fill(cols):
-            sib_out[j, :, cols] = term(at[twin[order[j]]], cols).astype(bfloat)
-        tiles(0, D, fill)
-        sib.append(ship(sib_out.at[j], sib_in.at[j], "s"))
-    def pair(j, cols):
-        return term(at[order[j]], cols) + sib_in[j, :, cols].astype(single)
+            sib_out[j, h, :, local(h, cols)] = term(at[twin[order[j]]], cols).astype(bfloat)
+        tiles(h * mid, (h + 1) * mid, fill)
+        sib[j, h] = ship(sib_out.at[j, h], sib_in.at[j, h], "s")
     def local(h, cols):
         return pl.ds(pl.multiple_of(cols.start - h * mid, TILE), TILE)
+    def pair(j, h, cols):
+        return term(at[order[j]], cols) + sib_in[j, h, :, local(h, cols)].astype(single)
     def put(j, h, extra=None):
+        sib[j, h].wait_recv()
         def fill(cols):
-            value = pair(j, cols)
+            value = pair(j, h, cols)
             if extra is not None:
                 value = value + landed[extra, :, local(h, cols)].astype(single)
             stage[j, h, :, local(h, cols)] = value.astype(bfloat)
         tiles(h * mid, (h + 1) * mid, fill)
-    to_sibling()
-    to_sibling()
-    sib[0].wait_recv()
+    to_sibling(0, 0)
+    to_sibling(0, 1)
     put(0, 0)
     d_a = ship(stage.at[0, 0], landed.at[0], "x")
     put(0, 1)
     d_b = ship(stage.at[0, 1], landed.at[1], "y")
-    to_sibling()
-    sib[1].wait_recv()
+    to_sibling(1, 0)
+    to_sibling(2, 1)
     put(1, 0)
     x_a = ship(stage.at[1, 0], landed.at[2], "x")
-    sib[2].wait_recv()
     put(2, 1)
     y_b = ship(stage.at[2, 1], landed.at[3], "y")
-    to_sibling()
-    sib[3].wait_recv()
-    def first(cols):
-        out_ref[:, cols] = pair(3, cols)
-    tiles(0, D, first)
+    for j, h in ((1, 1), (2, 0), (3, 0), (3, 1)):
+        to_sibling(j, h)
     d_b.wait_recv()
     put(1, 1, extra=1)
     x_b = ship(stage.at[1, 1], landed.at[5], "x")
     d_a.wait_recv()
     put(2, 0, extra=0)
     y_a = ship(stage.at[2, 0], landed.at[4], "y")
+    for h in range(2):
+        sib[3, h].wait_recv()
+        def first(cols, h=h):
+            out_ref[:, cols] = pair(3, h, cols)
+        tiles(h * mid, (h + 1) * mid, first)
     x_a.wait_recv(); y_b.wait_recv(); x_b.wait_recv(); y_a.wait_recv()
     for h, (n, m) in enumerate(((2, 4), (3, 5))):
         def add(cols, h=h, n=n, m=m):
@@ -214,8 +218,8 @@
         functools.partial(reduce_kernel, turned, len(left)),
         out_shape=jax.ShapeDtypeStruct((tok, D), single),
         in_specs=vmem(2 * len(left)), out_specs=vmem(1)[0],
-        scratch_shapes=[pltpu.VMEM((4, tok, D), bfloat), pltpu.VMEM((4, tok, D), bfloat), pltpu.VMEM((3, 2, tok, D // 2), bfloat), pltpu.VMEM((6, tok, D // 2), bfloat),
-            pltpu.SemaphoreType.DMA((10,)), pltpu.SemaphoreType.DMA((10,))],
+        scratch_shapes=[pltpu.VMEM((4, 2, tok, D // 2), bfloat), pltpu.VMEM((4, 2, tok, D // 2), bfloat), pltpu.VMEM((3, 2, tok, D // 2), bfloat), pltpu.VMEM((6, tok, D // 2), bfloat),
+            pltpu.SemaphoreType.DMA((14,)), pltpu.SemaphoreType.DMA((14,))],
         compiler_params=pltpu.CompilerParams(collective_id=cid, has_side_effects=True, vmem_limit_bytes=60 << 20),
         cost_estimate=pl.CostEstimate(flops=1 << 30, bytes_accessed=128 << 20, transcendentals=0),
         name=name,
@@ -369,8 +373,8 @@
 
 
 def last_units_kernel(
-    all_ref, bg_ref, pg1_ref, w1_ref, w_ref, b_ref, hid_ref, pb_ref, r_ref, grad_ref,
-    held, bg, pg_ref, sib_out, sib_in, stage, landed, send, recv, load, load_b,
+    all_ref, bg_ref, pg1_ref, w1_ref, w_ref, b_ref, hid_ref, pg_ref, pb_ref, r_ref,
+    held, bg, sib_out, sib_in, stage, landed, send, recv, load, load_b,
 ):
     ids, at = plane_place()
     ranks, tok, D = held.shape
@@ -459,19 +463,6 @@
 
     tiles(0, D, first)
 
-    units_at = grad_ref.shape[2]
-    per = 256 // units_at
-    tokens = ranks * tok
-
-    def grads(i, _):
-        here = pl.ds(pl.multiple_of(i * 256, 256), 256)
-        owners = pl.ds(i * per, per)
-        for j, (left, right) in enumerate(((pg_ref, held), (hid_ref, bg))):
-            value = dot_tn(left[:, :, here].reshape(tokens, 256), right[...].reshape(tokens, D))
-            grad_ref[owners, j] = value.astype(bfloat).reshape(per, units_at, D)
-        return 0
-
-    lax.fori_loop(0, hid_ref.shape[2] // 256, grads, 0)
     for copy in (x_a, y_b, x_b, y_a):
         copy.wait_recv()
     for h, (n, m) in enumerate(((2, 4), (3, 5))):
@@ -526,16 +517,15 @@
         last_units_kernel,
         out_shape=[
             jax.ShapeDtypeStruct((ranks, tok, F), bfloat),
+            jax.ShapeDtypeStruct((ranks, tok, F), bfloat),
             jax.ShapeDtypeStruct((1, F), single),
             jax.ShapeDtypeStruct((tok, D), single),
-            jax.ShapeDtypeStruct(w.shape, bfloat),
         ],
         in_specs=[anywhere, anywhere, inside, inside, inside, inside],
         out_specs=[inside] * 4,
         scratch_shapes=[
             pltpu.VMEM((ranks, tok, D), bfloat),
             pltpu.VMEM((ranks, tok, D), bfloat),
-            pltpu.VMEM((ranks, tok, F), bfloat),
             pltpu.VMEM((4, tok, D), bfloat),
             pltpu.VMEM((4, tok, D), bfloat),
             pltpu.VMEM((3, 2, tok, D // 2), bfloat),
@@ -549,6 +539,42 @@
         cost_estimate=pl.CostEstimate(flops=1 << 30, bytes_accessed=160 << 20, transcendentals=0),
         name="last_units",
     )(rows, bg, pg, w1, w, bias)
+
+
+def attended_grads(x, w, tokens, cid):
+    two, bg, hid, pg = tokens
+    ranks, tok, D = two.shape
+    F = hid.shape[2]
+    units_at = (4, 2, F // 4, D)[2]
+    per = 256 // units_at
+
+    def beside(ins, outs, more):
+        *inside, load = more
+        loads = [pltpu.make_async_copy(ref, buf, load.at[n]) for n, (ref, buf) in enumerate(zip(ins[2:], inside))]
+        for copy in loads:
+            copy.start()
+
+        def work():
+            for copy in loads:
+                copy.wait()
+            two_in, bg_in, hid_in, pg_in = inside
+
+            def step(i, _):
+                here = pl.ds(pl.multiple_of(i * 256, 256), 256)
+                for j, (left, right) in enumerate(((pg_in, two_in), (hid_in, bg_in))):
+                    value = dot_tn(left[:, :, here].reshape(ranks * tok, 256), right[...].reshape(ranks * tok, D))
+                    outs[1][pl.ds(i * per, per), j] = value.astype(bfloat).reshape(per, units_at, D)
+                return 0
+
+            lax.fori_loop(0, F // 256, step, 0)
+
+        return work
+
+    return gather_dot(
+        x, w, jnp.zeros((1, w.shape[0]), single), bfloat, True, cid, "attended_grad",
+        extra_out=[jax.ShapeDtypeStruct((4, 2, F // 4, D), bfloat)], beside=beside, far=tokens,
+        more=[pltpu.VMEM(t.shape, bfloat) for t in tokens] + [pltpu.SemaphoreType.DMA((4,))],
+    )
 
 
 def everyone(width):
@@ -943,12 +969,6 @@
             return plane_gather(rows, (), [], None, cid, name)[0]
         return lax.all_gather(rows, PLANE, axis=0, tiled=True)
 
-    def gather_plane_dot(rows, weight, shift, out_type, turned, cid, name):
-        if fast:
-            return gather_dot(rows, weight, shift, out_type, turned, cid, name)
-        rows = lax.all_gather(rows, PLANE, axis=0, tiled=True)
-        return rows, ((dot_nt if turned else dot)(rows, weight) + shift).astype(out_type)
-
     def reduce_plane(left, weight, turned, cid, name):
         if fast:
             return dot_reduce([left], [weight], turned, cid, name)
@@ -1001,10 +1021,9 @@
         branch_rows = branch_all.reshape(R, tok, D)
         two_all, hidden_one, pre_one, bias_one_up, grads = first_units(normed_two, branch_rows, unit_one, bias_up[0], 2)
         shard_one = sum_z(grads)
-        hidden_two, bias_two_up, normed_two_grad, grads = last_units(
+        hidden_two, pre_two, bias_two_up, normed_two_grad = last_units(
             two_all, branch_rows, pre_one, unit_one, unit_two, bias_up[1], 3
         )
-        shard_two = sum_z(grads)
         up_b_halves = [bias_one_up[0], bias_two_up[0]]
     else:
         two_all = gather_plane(normed_two, 2, "gather_two")
@@ -1028,9 +1047,14 @@
     middle_grad = cotangent + middle_part
     attended_grad = (active * middle_grad).astype(bfloat)
     out_b_grad = column_sums(attended_grad)
-    attended_all, context_grad = gather_plane_dot(
-        attended_grad, weight_o, jnp.zeros((1, cols), single), bfloat, True, 5, "attended_grad"
-    )
+    if fast:
+        attended_all, context_grad, grads = attended_grads(
+            attended_grad, weight_o, (two_all, branch_rows, hidden_two, pre_two), 5
+        )
+        shard_two = sum_z(grads)
+    else:
+        attended_all = gather_plane(attended_grad, 5, "attended_grad")
+        context_grad = dot_nt(attended_all, weight_o).astype(bfloat)
     context_grad, shard_one = lax.optimization_barrier((context_grad, shard_one))
     out_w_grad = dot_tn(context, attended_all)
     query_grad, edge, pair = attention_backward(starts, query, key_value, before, context_grad, B)
@@ -1040,13 +1064,17 @@
     hidden_one, query_w_grad, out_w_grad = lax.optimization_barrier((hidden_one, query_w_grad, out_w_grad))
     downs = [unit_one, unit_two] if fast else [down_one, down_two]
     branch = sum_halves([hidden_one, hidden_two], downs, False, 4, "down")
-    branch, after, shard_two = lax.optimization_barrier((branch, after, shard_two))
+    up_w_shard = jnp.concatenate([shard_one[:units], shard_two[:units]]).T.astype(single)
+    down_w_shard = jnp.concatenate([shard_one[units:], shard_two[units:]]).astype(single)
+    query_b_grad = column_sums(query_grad)
+    branch, after, up_w_shard, down_w_shard, query_b_grad, query_w_grad = lax.optimization_barrier(
+        (branch, after, up_w_shard, down_w_shard, query_b_grad, query_w_grad)
+    )
     outputs = middle + active * (branch + bias_down)
     pair_grad = (pair + after.astype(single)).astype(bfloat)
     pair_w_grad = dot_tn(normed_all, pair_grad).astype(bfloat)
     pair_grad, pair_w_grad = lax.optimization_barrier((pair_grad, pair_w_grad))
     normed_grad = sum_halves([query_grad, pair_grad], [weight_q, weight_kv], True, 6, "qkv_grad")
-    query_b_grad = column_sums(query_grad)
     value_b_grad = column_sums(pair_grad[:, cols:])
     input_part, gain_one_grad, bias_one_grad = norm_backward(local, normed_grad, gain_one)
     input_grad = middle_grad + input_part
@@ -1106,9 +1134,9 @@
         sums[2],
         sums[3],
         sums[4],
-        jnp.concatenate([shard_one[:units], shard_two[:units]]).T.astype(single),
+        up_w_shard,
         up_b_shard,
-        jnp.concatenate([shard_one[units:], shard_two[units:]]).astype(single),
+        down_w_shard,
         sums[5],
     )
 

time: 658 us -> 677 us (1.029)
  waiting for transfers between devices: 64.1 us -> 89.4 us
    reduce_scatter x2, waiting for transfers between devices: 0.02 us -> 19.7 us  [sum_z(): lax.psum_scatter(grads.reshape(Z * 2 * units, D), 'z', scatter_dimension=...]
    ppermute x1, waiting for transfers between devices: 26.4 us -> 14.5 us  [on_device(): before = lax.ppermute(key_value, 'z', up)]
    all_gather x2, waiting for transfers between devices: 1.18 us -> 11.9 us  [feature_rows(): full = lax.all_gather(mine, 'z', axis=0, tiled=True)]
    unnamed x56 -> x52, local copies, waits for them, and re-layouts: 15.2 us -> 13.6 us
  transfers between devices with their start and end apart: 11 -> 11, of which waited for: 7 -> 9; matrix products, arithmetic and copies ran while one was open for 13% -> 12% of each run, Pallas kernels for 70% -> 68%
where the time goes in v10:
time: 677 us; the launch traced here: 672 us
  Pallas kernels  455 us (67%)
  waiting for transfers between devices  89.4 us (13%)
  matrix products  39.1 us (6%)
  other arithmetic  35.4 us (5%)
  local copies, waits for them, and re-layouts  31.6 us (5%)
  between operations  16.1 us (2%)
    pallas_call x3, Pallas kernels, dot_reduce(): pl.pallas_call(functools.partial(reduce_kernel, turned, len(left)), out_s...  138 us
    pallas_call x3, Pallas kernels, plane_gather(): pl.pallas_call(functools.partial(gather_kernel, body_of, beside, len(ins)...  126 us
    pallas_call x1, Pallas kernels, last_units(): pl.pallas_call(last_units_kernel, out_shape=[jax.ShapeDtypeStruct((ranks,...  54.8 us
    pallas_call x1, Pallas kernels, first_units(): pl.pallas_call(first_units_kernel, out_shape=[jax.ShapeDtypeStruct((ranks...  51.5 us
    pallas_call x2, Pallas kernels, exchange_call(): pl.pallas_call(kernel, out_shape=out_shape, in_specs=[inside] * len(args)...  37.1 us
    pallas_call x1, Pallas kernels, attend_back(): pl.pallas_call(attend_back_kernel, grid=(groups,), out_shape=[jax.ShapeDt...  33.7 us
    dot_general x3, matrix products, dot_tn(): lax.dot_general(left, right, (((0,), (0,)), ((), ())), preferred_element_...  23.1 us
    reduce_scatter x2, waiting for transfers between devices, sum_z(): lax.psum_scatter(grads.reshape(Z * 2 * units, D), 'z', scatter_dimension=...  19.7 us
  transfers between devices with their start and end apart: 11, of which 9 were waited for; matrix products, arithmetic and copies ran while one was open for 12% of the time, Pallas kernels for 68%

profile of v10, /device:TPU:0, one launch (start us, length us, event | category | flops | bytes accessed | tf_op | source)
XLA Modules:
  0.0 671.8 jit_solution(6624987603605695568)
XLA Ops:
  8.6 6.1 concatenate.27
  17.6 20.5 %spread.1 = (bf16[8,64,256]{2,1,0:T(8,128)(2,1)}, bf16[8,64,512]{2,1,0:T(8,128)(2,1)}, f32[32,1,896]{2,1,0:T(1,128)S(1)}) custom-call(bf16[64,2048]{1,0:T(8,128)(2,1)S(1)} %copy-done.1, bf16[64,2048]{1,0:T(8,128)(2,1)S(1)} %copy-done.2, bf16[64,2048]{1,0:T(8,128)(2,1)S(1)} %copy-done.3, f32[1,1,896]{2,1,0:T(1,128)S(1)} %broadcast_in_dim.96.pack_ref), custom_call_target="tpu_custom_call" | custom-call | flops 1048576 | bytes 33554432 | tf_op jit(solution)/shard_map/spread/pallas_call | solution.py:666
  47.7 40.8 %gather_normed.1 = bf16[8,256,2048]{2,1,0:T(8,128)(2,1)} custom-call(bf16[256,2048]{1,0:T(8,128)(2,1)} %fusion.10.x_ref), custom_call_target="tpu_custom_call" | custom-call | flops 1073741824 | bytes 134217728 | tf_op jit(solution)/shard_map/gather_normed/pallas_call | solution.py:111
  96.2 9.3 %add_convert_fusion.1.k_ref.v_ref = bf16[2048,512]{1,0:T(8,128)(2,1)} fusion(bf16[2048,2048]{1,0:T(8,128)(2,1)} %bitcast.159, bf16[2048,512]{1,0:T(8,128)(2,1)S(1)} %bitcast.163, f32[512]{0:T(512)S(1)} %concatenate.29), kind=kOutput, calls=%fused_computation.1 | convolution fusion | flops 4297064448 | bytes 12584960 | tf_op jit(solution)/shard_map/dot_general | solution.py:230
  111.1 10.8 %all-gather.10.cloned.1.call-done = bf16[2048,256]{1,0:T(8,128)(2,1)} async-done(((bf16[512,256]{1,0:T(8,128)(2,1)}), bf16[2048,256]{1,0:T(8,128)(2,1)}) %all-gather.10.cloned.1.call-update) | async-done | bytes 1048592 | tf_op jit(solution)/shard_map/all_gather | solution.py:959
  123.2 41.9 %gather_branch.1 = bf16[8,256,2048]{2,1,0:T(8,128)(2,1)} custom-call(bf16[256,2048]{1,0:T(8,128)(2,1)} %get-tuple-element.79.x_ref), custom_call_target="tpu_custom_call" | custom-call | flops 1073741824 | bytes 134217728 | tf_op jit(solution)/shard_map/gather_branch/pallas_call | solution.py:111
  165.1 6.7 %fusion.2.q_ref = bf16[2048,256]{1,0:T(8,128)(2,1)} fusion(bf16[2048,2048]{1,0:T(8,128)(2,1)} %bitcast.160, bf16[2048,256]{1,0:T(8,128)(2,1)S(1)} %bitcast.168, f32[256]{0:T(256)S(1)} %bitcast.192), kind=kOutput, calls=%fused_computation.9 | convolution fusion | flops 2148532224 | bytes 10486784 | tf_op jit(solution)/shard_map/dot_general | solution.py:230
  171.8 14.5 %collective-permute-done.kb_ref.vb_ref = bf16[2048,512]{1,0:T(8,128)(2,1)} collective-permute-done((bf16[2048,512]{1,0:T(8,128)(2,1)}, bf16[2048,512]{1,0:T(8,128)(2,1)}, u32[]{:S(2)}, u32[]{:S(2)}) %collective-permute-start) | collective-permute-done | bytes 2097184 | tf_op jit(solution)/shard_map/ppermute | solution.py:995
  186.3 13.1 %attend.1 = bf16[2048,256]{1,0:T(8,128)(2,1)} custom-call(s32[2048,1]{1,0:T(8,128)} %bitcast.157, bf16[2048,256]{1,0:T(8,128)(2,1)} %fusion.2.q_ref, bf16[2048,512]{1,0:T(8,128)(2,1)} %add_convert_fusion.1.k_ref.v_ref, bf16[2048,512]{1,0:T(8,128)(2,1)} %add_convert_fusion.1.k_ref.v_ref, bf16[2048,512]{1,0:T(8,128)(2,1)} %collective-permute-done.kb_ref.vb_ref, ...), custom_call_target="tpu_custom_call" | custom-call | tf_op jit(solution)/shard_map/attend/pallas_call | solution.py:795
  200.8 43.2 %attended.1 = f32[256,2048]{1,0:T(8,128)} custom-call(bf16[8,256,256]{2,1,0:T(8,128)(2,1)} %bitcast.153, bf16[256,2048]{1,0:T(8,128)(2,1)} %all-gather.6.cloned.1.call-done.refs_1_.refs_0_), custom_call_target="tpu_custom_call" | custom-call | flops 1073741824 | bytes 134217728 | tf_op jit(solution)/shard_map/attended/pallas_call | solution.py:217
  249.0 51.5 %first_units.1 = (bf16[8,256,2048]{2,1,0:T(8,128)(2,1)}, bf16[8,256,512]{2,1,0:T(8,128)(2,1)}, bf16[8,256,512]{2,1,0:T(8,128)(2,1)}, f32[1,512]{1,0:T(1,128)}, bf16[4,2,128,2048]{3,2,1,0:T(8,128)(2,1)}) custom-call(bf16[256,2048]{1,0:T(8,128)(2,1)} %add_convert_fusion.3.x_ref, bf16[8,256,2048]{2,1,0:T(8,128)(2,1)} %gather_branch.1, ...), custom_call_target="tpu_custom_call" | custom-call | flops 1073741824 | bytes 167772160 | tf_op jit(solution)/shard_map/first_units/pallas_call | solution.py:485
  300.6 11.3 %all-gather.14.cloned.1.call-done = bf16[1024,2048]{1,0:T(8,128)(2,1)} async-done(((bf16[256,2048]{1,0:T(8,128)(2,1)}), bf16[1024,2048]{1,0:T(8,128)(2,1)}) %all-gather.14.cloned.1.call-update) | async-done | bytes 4194320 | tf_op jit(solution)/shard_map/all_gather | solution.py:983
  311.9 54.8 %last_units.1 = (bf16[8,256,512]{2,1,0:T(8,128)(2,1)}, bf16[8,256,512]{2,1,0:T(8,128)(2,1)}, f32[1,512]{1,0:T(1,128)}, f32[256,2048]{1,0:T(8,128)}) custom-call(bf16[8,256,2048]{2,1,0:T(8,128)(2,1)} %get-tuple-element.89.all_ref.refs_2_, bf16[8,256,2048]{2,1,0:T(8,128)(2,1)} %gather_branch.1, bf16[8,256,512]{2,1,0:T(8,128)(2,1)} %get-tuple-element.90.pg1_ref, ...), custom_call_target="tpu_custom_call" | custom-call | flops 1073741824 | bytes 167772160 | tf_op jit(solution)/shard_map/last_units/pallas_call | solution.py:516
  374.8 43.3 %attended_grad.1 = (bf16[8,256,2048]{2,1,0:T(8,128)(2,1)}, bf16[8,256,256]{2,1,0:T(8,128)(2,1)}, bf16[4,2,128,2048]{3,2,1,0:T(8,128)(2,1)}) custom-call(bf16[256,2048]{1,0:T(8,128)(2,1)} %get-tuple-element.189.x_ref, bf16[256,2048]{1,0:T(8,128)(2,1)} %all-gather.6.cloned.1.call-done.refs_1_.refs_0_, f32[1,256]{1,0:T(1,128)} %broadcast_in_dim.100.refs_1_, ...), custom_call_target="tpu_custom_call" | custom-call | flops 1073741824 | bytes 134217728 | tf_op jit(solution)/shard_map/attended_grad/pallas_call | solution.py:111
  419.3 6.7 fusion.30
  426.0 33.7 %attend_back.1 = (bf16[2048,256]{1,0:T(8,128)(2,1)}, bf16[2048,512]{1,0:T(8,128)(2,1)}, f32[2048,512]{1,0:T(8,128)}) custom-call(s32[2048,1]{1,0:T(8,128)} %bitcast.158, bf16[2048,256]{1,0:T(8,128)(2,1)} %fusion.2.q_ref, bf16[2048,512]{1,0:T(8,128)(2,1)} %add_convert_fusion.1.k_ref.v_ref, bf16[2048,512]{1,0:T(8,128)(2,1)} %add_convert_fusion.1.k_ref.v_ref, ...), custom_call_target="tpu_custom_call" | custom-call | tf_op jit(solution)/shard_map/attend_back/pallas_call | solution.py:808
  461.0 7.1 %convolution_convert_fusion.1 = bf16[2048,256]{1,0:T(8,128)(2,1)} fusion(bf16[2048,2048]{1,0:T(8,128)(2,1)} %bitcast.161, bf16[2048,256]{1,0:T(8,128)(2,1)} %get-tuple-element.102), kind=kOutput, calls=%fused_computation.10 | convolution fusion | flops 2148007936 | bytes 10485760 | tf_op jit(solution)/shard_map/dot_general | solution.py:234
  468.1 48.5 %down.1 = f32[256,2048]{1,0:T(8,128)} custom-call(bf16[8,256,512]{2,1,0:T(8,128)(2,1)} %get-tuple-element.104.refs_0_, bf16[8,256,512]{2,1,0:T(8,128)(2,1)} %get-tuple-element.93.refs_4_.refs_1_, bf16[4,2,128,2048]{3,2,1,0:T(8,128)(2,1)} %bitcast.149, bf16[4,2,128,2048]{3,2,1,0:T(8,128)(2,1)} %bitcast.152), custom_call_target="tpu_custom_call" | custom-call | flops 1073741824 | bytes 134217728 | tf_op jit(solution)/shard_map/down/pallas_call | solution.py:217
  517.0 19.7 %reduce-scatter.7.cloned.1.call-done = bf16[256,2048]{1,0:T(8,128)(2,1)} async-done(((bf16[1024,2048]{1,0:T(8,128)(2,1)}), bf16[256,2048]{1,0:T(8,128)(2,1)}) %reduce-scatter.7.cloned.1.call-update) | async-done | bytes 1048592 | tf_op jit(solution)/shard_map/reduce_scatter | solution.py:1018
  541.1 14.1 %collective-permute-done.1 = bf16[2048,512]{1,0:T(8,128)(2,1)} collective-permute-done((bf16[2048,512]{1,0:T(8,128)(2,1)}, bf16[2048,512]{1,0:T(8,128)(2,1)}, u32[]{:S(2)}, u32[]{:S(2)}) %collective-permute-start.1) | collective-permute-done | bytes 2097184 | tf_op jit(solution)/shard_map/ppermute | solution.py:1062
  557.7 9.2 %convolution_convert_fusion = bf16[2048,512]{1,0:T(8,128)(2,1)S(1)} fusion(bf16[2048,2048]{1,0:T(8,128)(2,1)} %bitcast.162, bf16[2048,512]{1,0:T(8,128)(2,1)S(1)} %add_convert_fusion), kind=kOutput, calls=%fused_computation.3 | convolution fusion | flops 4296015872 | bytes 12582912 | tf_op jit(solution)/shard_map/dot_general | solution.py:234
  570.1 46.8 %qkv_grad.1 = f32[256,2048]{1,0:T(8,128)} custom-call(bf16[8,256,256]{2,1,0:T(8,128)(2,1)} %bitcast.170, bf16[8,256,512]{2,1,0:T(8,128)(2,1)} %bitcast.154, bf16[2048,256]{1,0:T(8,128)(2,1)} %bitcast.169, bf16[2048,512]{1,0:T(8,128)(2,1)} %bitcast.164), custom_call_target="tpu_custom_call" | custom-call | flops 1073741824 | bytes 134217728 | tf_op jit(solution)/shard_map/qkv_grad/pallas_call | solution.py:217
  619.5 10.2 %reduce-scatter.9.cloned.1.call-done = bf16[512,768]{1,0:T(8,128)(2,1)} async-done(((bf16[2048,768]{1,0:T(8,128)(2,1)}), bf16[512,768]{1,0:T(8,128)(2,1)}) %reduce-scatter.9.cloned.1.call-update) | async-done | bytes 786448 | tf_op jit(solution)/shard_map/reduce_scatter | solution.py:1090
  638.7 16.6 %settle.1 = (f32[64,2048]{1,0:T(8,128)S(1)}, f32[64,2048]{1,0:T(8,128)S(1)}, f32[64,2048]{1,0:T(8,128)S(1)}, f32[1,768]{1,0:T(1,128)S(1)}) custom-call(bf16[8,64,768]{2,1,0:T(8,128)(2,1)S(1)} %bitcast.146, f32[32,1,768]{2,1,0:T(1,128)S(1)} %broadcast_in_dim.109.rows_ref), custom_call_target="tpu_custom_call" | custom-call | flops 1048576 | bytes 33554432 | tf_op jit(solution)/shard_map/settle/pallas_call | solution.py:666
  (166 shorter events, 75.4 us)
Async XLA Ops:
  7.2 36.1 %all-gather.6.cloned.1.call-start = ((), (), s32[]{:S(2)}) async-start(), calls=%async_computation.4 | async-start | bytes 1310720 | tf_op jit(solution)/shard_map/all_gather | solution.py:930
  7.9 81.8 %all-gather.8.cloned.1.call-start = ((), (), s32[]{:S(2)}) async-start(), calls=%async_computation.5 | async-start | bytes 2621440 | tf_op jit(solution)/shard_map/all_gather | solution.py:959
  17.6 22.3 %copy-start.6 = (bf16[1,256,2048]{2,1,0:T(8,128)(2,1)S(1)}, bf16[1,256,2048]{2,1,0:T(8,128)(2,1)}, u32[]{:S(2)}) copy-start(bf16[1,256,2048]{2,1,0:T(8,128)(2,1)} %param.20) | copy-start | bytes 3145732
  38.1 83.7 %all-gather.10.cloned.1.call-start = ((), (), s32[]{:S(2)}) async-start(), calls=%async_computation.6 | async-start | bytes 1310720 | tf_op jit(solution)/shard_map/all_gather | solution.py:959
  43.3 205.7 %all-gather.12.cloned.1.call-start = ((), (), s32[]{:S(2)}) async-start(), calls=%async_computation.7 | async-start | bytes 5242880 | tf_op jit(solution)/shard_map/all_gather | solution.py:983
  89.7 2.7 copy-start.18
  91.5 14.0 %copy-start.11 = (bf16[4,4,2,64,512]{4,3,2,1,0:T(8,128)(2,1)}, bf16[4,4,2,64,512]{4,3,2,1,0:T(8,128)(2,1)S(1)}, u32[]{:S(2)}) copy-start(bf16[4,4,2,64,512]{4,3,2,1,0:T(8,128)(2,1)S(1)} %copy.55) | copy-start | bytes 6291460
  91.5 220.4 %all-gather.14.cloned.1.call-start = ((), (), s32[]{:S(2)}) async-start(), calls=%async_computation.8 | async-start | bytes 5242880 | tf_op jit(solution)/shard_map/all_gather | solution.py:983
  105.5 80.8 %collective-permute-start = (bf16[2048,512]{1,0:T(8,128)(2,1)}, bf16[2048,512]{1,0:T(8,128)(2,1)}, u32[]{:S(2)}, u32[]{:S(2)}) collective-permute-start(bf16[2048,512]{1,0:T(8,128)(2,1)} %add_convert_fusion.1.k_ref.v_ref), channel_id=1, source_target_pairs={{0,2},{2,4},{4,6},{1,3},{3,5},{5,7},{8,10},{10,12},{12,14},{9,11},... | collective-permute-start | bytes 6291464 | tf_op jit(solution)/shard_map/ppermute | solution.py:995
  123.1 41.9 %copy-start.14 = (bf16[4,4,2,64,256]{4,3,2,1,0:T(8,128)(2,1)}, bf16[4,4,2,64,256]{4,3,2,1,0:T(8,128)(2,1)S(1)}, u32[]{:S(2)}) copy-start(bf16[4,4,2,64,256]{4,3,2,1,0:T(8,128)(2,1)S(1)} %copy.58) | copy-start | bytes 3145732
  199.4 226.6 %reduce-scatter.5.cloned.1.call-start = ((), (), s32[]{:S(2)}) async-start(), calls=%async_computation.9 | async-start | bytes 5242880 | tf_op jit(solution)/shard_map/reduce_scatter | solution.py:1018
  300.6 236.0 %reduce-scatter.7.cloned.1.call-start = ((), (), s32[]{:S(2)}) async-start(), calls=%async_computation.10 | async-start | bytes 5242880 | tf_op jit(solution)/shard_map/reduce_scatter | solution.py:1018
  366.7 3.3 copy-start.5
  366.7 3.6 copy-start.10
  418.1 211.7 %reduce-scatter.9.cloned.1.call-start = ((), (), s32[]{:S(2)}) async-start(), calls=%async_computation.11 | async-start | bytes 3932160 | tf_op jit(solution)/shard_map/reduce_scatter | solution.py:1090
  459.7 95.5 %collective-permute-start.1 = (bf16[2048,512]{1,0:T(8,128)(2,1)}, bf16[2048,512]{1,0:T(8,128)(2,1)}, u32[]{:S(2)}, u32[]{:S(2)}) collective-permute-start(bf16[2048,512]{1,0:T(8,128)(2,1)} %get-tuple-element.105), channel_id=1, source_target_pairs={{2,0},{4,2},{6,4},{3,1},{5,3},{7,5},{10,8},{12,10},{14,12},{11,9},... | collective-permute-start | bytes 6291464 | tf_op jit(solution)/shard_map/ppermute | solution.py:1062
  468.1 48.5 %copy-start.15 = (bf16[2048,256]{1,0:T(8,128)(2,1)S(1)}, bf16[2048,256]{1,0:T(8,128)(2,1)}, u32[]{:S(2)}) copy-start(bf16[2048,256]{1,0:T(8,128)(2,1)} %get-tuple-element.102) | copy-start | bytes 3145732
  468.1 48.8 %copy-start.16 = (bf16[256,2048]{1,0:T(8,128)(2,1)S(1)}, bf16[256,2048]{1,0:T(8,128)(2,1)}, u32[]{:S(2)}) copy-start(bf16[256,2048]{1,0:T(8,128)(2,1)} %reduce-scatter.5.cloned.1.call-done) | copy-start | bytes 3145732
  537.9 17.2 %copy-start.13 = (f32[2048,512]{1,0:T(8,128)S(1)}, f32[2048,512]{1,0:T(8,128)}, u32[]{:S(2)}) copy-start(f32[2048,512]{1,0:T(8,128)} %get-tuple-element.110) | copy-start | bytes 12582916
  557.6 12.0 %copy-start.9 = (bf16[2048,512]{1,0:T(8,128)(2,1)}, bf16[2048,512]{1,0:T(8,128)(2,1)S(1)}, u32[]{:S(2)}) copy-start(bf16[2048,512]{1,0:T(8,128)(2,1)S(1)} %add_convert_fusion) | copy-start | bytes 6291460
  557.6 9.3 %copy-start.17 = (bf16[2048,256]{1,0:T(8,128)(2,1)S(1)}, bf16[2048,256]{1,0:T(8,128)(2,1)}, u32[]{:S(2)}) copy-start(bf16[2048,256]{1,0:T(8,128)(2,1)} %convolution_convert_fusion.1) | copy-start | bytes 3145732
  569.0 91.8 %reduce-scatter.11.cloned.1.call-start = ((), (), s32[]{:S(2)}) async-start(), calls=%async_computation.12 | async-start | bytes 1310720 | tf_op jit(solution)/shard_map/reduce_scatter | solution.py:1110
  633.2 3.6 copy-start.7
  633.2 3.6 copy-start.12
  (8 other events, 8.6 us)
Sparse Core Ops, SparseCore 0:
  9.6 33.6 all-gather.5
  44.8 44.7 all-gather.7
  91.3 30.5 all-gather.9
  123.2 104.3 all-gather.11
  229.1 82.8 all-gather.13
  314.1 91.1 reduce-scatter.4
  418.2 118.3 reduce-scatter.6
  569.2 60.5 reduce-scatter.8
  632.0 28.7 reduce-scatter.10

commit v11 on v9

--- a/solution.py
+++ b/solution.py
@@ -155,49 +155,49 @@
         return sum(dot(a[rank], w) for a, w in zip(left, rows))
     order = ("d", "x", "y", "o")
     twin = {"d": "ds", "x": "xs", "y": "ys", "o": "s"}
-    sib = []
-    def to_sibling():
-        j = len(sib)
+    sib = {}
+    def to_sibling(j, h):
         def fill(cols):
-            sib_out[j, :, cols] = term(at[twin[order[j]]], cols).astype(bfloat)
-        tiles(0, D, fill)
-        sib.append(ship(sib_out.at[j], sib_in.at[j], "s"))
-    def pair(j, cols):
-        return term(at[order[j]], cols) + sib_in[j, :, cols].astype(single)
+            sib_out[j, h, :, local(h, cols)] = term(at[twin[order[j]]], cols).astype(bfloat)
+        tiles(h * mid, (h + 1) * mid, fill)
+        sib[j, h] = ship(sib_out.at[j, h], sib_in.at[j, h], "s")
     def local(h, cols):
         return pl.ds(pl.multiple_of(cols.start - h * mid, TILE), TILE)
+    def pair(j, h, cols):
+        return term(at[order[j]], cols) + sib_in[j, h, :, local(h, cols)].astype(single)
     def put(j, h, extra=None):
+        sib[j, h].wait_recv()
         def fill(cols):
-            value = pair(j, cols)
+            value = pair(j, h, cols)
             if extra is not None:
                 value = value + landed[extra, :, local(h, cols)].astype(single)
             stage[j, h, :, local(h, cols)] = value.astype(bfloat)
         tiles(h * mid, (h + 1) * mid, fill)
-    to_sibling()
-    to_sibling()
-    sib[0].wait_recv()
+    to_sibling(0, 0)
+    to_sibling(0, 1)
     put(0, 0)
     d_a = ship(stage.at[0, 0], landed.at[0], "x")
     put(0, 1)
     d_b = ship(stage.at[0, 1], landed.at[1], "y")
-    to_sibling()
-    sib[1].wait_recv()
+    to_sibling(1, 0)
+    to_sibling(2, 1)
     put(1, 0)
     x_a = ship(stage.at[1, 0], landed.at[2], "x")
-    sib[2].wait_recv()
     put(2, 1)
     y_b = ship(stage.at[2, 1], landed.at[3], "y")
-    to_sibling()
-    sib[3].wait_recv()
-    def first(cols):
-        out_ref[:, cols] = pair(3, cols)
-    tiles(0, D, first)
+    for j, h in ((1, 1), (2, 0), (3, 0), (3, 1)):
+        to_sibling(j, h)
     d_b.wait_recv()
     put(1, 1, extra=1)
     x_b = ship(stage.at[1, 1], landed.at[5], "x")
     d_a.wait_recv()
     put(2, 0, extra=0)
     y_a = ship(stage.at[2, 0], landed.at[4], "y")
+    for h in range(2):
+        sib[3, h].wait_recv()
+        def first(cols, h=h):
+            out_ref[:, cols] = pair(3, h, cols)
+        tiles(h * mid, (h + 1) * mid, first)
     x_a.wait_recv(); y_b.wait_recv(); x_b.wait_recv(); y_a.wait_recv()
     for h, (n, m) in enumerate(((2, 4), (3, 5))):
         def add(cols, h=h, n=n, m=m):
@@ -214,8 +214,8 @@
         functools.partial(reduce_kernel, turned, len(left)),
         out_shape=jax.ShapeDtypeStruct((tok, D), single),
         in_specs=vmem(2 * len(left)), out_specs=vmem(1)[0],
-        scratch_shapes=[pltpu.VMEM((4, tok, D), bfloat), pltpu.VMEM((4, tok, D), bfloat), pltpu.VMEM((3, 2, tok, D // 2), bfloat), pltpu.VMEM((6, tok, D // 2), bfloat),
-            pltpu.SemaphoreType.DMA((10,)), pltpu.SemaphoreType.DMA((10,))],
+        scratch_shapes=[pltpu.VMEM((4, 2, tok, D // 2), bfloat), pltpu.VMEM((4, 2, tok, D // 2), bfloat), pltpu.VMEM((3, 2, tok, D // 2), bfloat), pltpu.VMEM((6, tok, D // 2), bfloat),
+            pltpu.SemaphoreType.DMA((14,)), pltpu.SemaphoreType.DMA((14,))],
         compiler_params=pltpu.CompilerParams(collective_id=cid, has_side_effects=True, vmem_limit_bytes=60 << 20),
         cost_estimate=pl.CostEstimate(flops=1 << 30, bytes_accessed=128 << 20, transcendentals=0),
         name=name,
@@ -696,6 +696,8 @@
     return [(i * block, i * block + block + span) for i in range(2)]
 
 def key_window(before, own, lo, hi, span):
+    if lo >= span:
+        return own[lo - span : hi - span]
     return jnp.concatenate([before[lo:span], own[0 : hi - span]], axis=0)
 
 def hidden_bias(start_ref, i, block, lo, hi, span):
@@ -704,16 +706,26 @@
     start = start_ref[i * block : (i + 1) * block, :]
     return jnp.where((keys >= start) & (keys <= rows), 0.0, -1e30).astype(single)
 
-def attend_kernel(start_ref, q_ref, k_ref, v_ref, kb_ref, vb_ref, out_ref):
+def each_window(first_ref, span, body):
+    block = span // 2
+    for i, (lo, hi) in enumerate(windows(span)):
+        begins = first_ref[pl.program_id(0) * 2 + i]
+        pl.when(begins >= lo + block)(functools.partial(body, i, lo + block, hi))
+        pl.when(begins < lo + block)(functools.partial(body, i, lo, hi))
+
+
+def attend_kernel(first_ref, start_ref, q_ref, k_ref, v_ref, kb_ref, vb_ref, out_ref):
     span, cols = q_ref.shape
     block = span // 2
-    lane = lax.broadcasted_iota(jnp.int32, (block, cols), 1) // HEAD_DIM
-    for i, (lo, hi) in enumerate(windows(span)):
+
+    def body(i, lo, hi):
+        lane = lax.broadcasted_iota(jnp.int32, (block, cols), 1) // HEAD_DIM
         rows = pl.ds(i * block, block)
         bias = hidden_bias(start_ref, i, block, lo, hi, span)
         keys = key_window(kb_ref, k_ref, lo, hi, span)
         vals = key_window(vb_ref, v_ref, lo, hi, span)
         query = q_ref[rows, :] * jnp.asarray(HEAD_DIM ** (-0.5), bfloat)
+
         def head(h, total):
             mine = lane == h
             scores = dot_nt(jnp.where(mine, query, 0), keys) + bias
@@ -721,23 +733,31 @@
             part = jnp.dot(weights.astype(bfloat), vals, preferred_element_type=single)
             part = part * (1.0 / jnp.sum(weights, axis=1, keepdims=True))
             return jnp.where(mine, part, total)
+
         total = lax.fori_loop(0, cols // HEAD_DIM, head, jnp.zeros((block, cols), single), unroll=True)
         out_ref[rows, :] = total.astype(bfloat)
 
-def attend_back_kernel(start_ref, q_ref, k_ref, v_ref, kb_ref, vb_ref, do_ref, dq_ref, edge_ref, pair_ref, dk, dv):
+    each_window(first_ref, span, body)
+
+
+def attend_back_kernel(
+    first_ref, start_ref, q_ref, k_ref, v_ref, kb_ref, vb_ref, do_ref, dq_ref, edge_ref, pair_ref, dk, dv
+):
     span, cols = q_ref.shape
     block = span // 2
     scale = HEAD_DIM ** (-0.5)
     dk[...] = jnp.zeros_like(dk)
     dv[...] = jnp.zeros_like(dv)
-    lane = lax.broadcasted_iota(jnp.int32, (block, cols), 1) // HEAD_DIM
-    for i, (lo, hi) in enumerate(windows(span)):
+
+    def body(i, lo, hi):
+        lane = lax.broadcasted_iota(jnp.int32, (block, cols), 1) // HEAD_DIM
         rows = pl.ds(i * block, block)
         bias = hidden_bias(start_ref, i, block, lo, hi, span)
         keys = key_window(kb_ref, k_ref, lo, hi, span)
         vals = key_window(vb_ref, v_ref, lo, hi, span)
         query = q_ref[rows, :] * jnp.asarray(scale, bfloat)
         grad = do_ref[rows, :]
+
         def head(h, total):
             mine = lane == h
             query_h = jnp.where(mine, query, 0)
@@ -752,43 +772,62 @@
             dk[lo:hi, :] += dot_tn(score_grad, query_h)
             part = jnp.dot(score_grad, keys, preferred_element_type=single)
             return jnp.where(mine, part, total)
+
         total = lax.fori_loop(0, cols // HEAD_DIM, head, jnp.zeros((block, cols), single), unroll=True)
         dq_ref[rows, :] = (total * scale).astype(bfloat)
+
+    each_window(first_ref, span, body)
     edge_ref[:, :cols] = dk[:span, :].astype(bfloat)
     edge_ref[:, cols:] = dv[:span, :].astype(bfloat)
     pair_ref[:, :cols] = dk[span:, :]
     pair_ref[:, cols:] = dv[span:, :]
 
+
+def block_starts(starts, groups):
+    return starts.reshape(groups * 2, -1)[:, 0]
+
+
 def attention_specs(span, cols):
     def at(j):
-        return pl.BlockSpec((span, cols), lambda g: (g, j))
-    return [pl.BlockSpec((span, 1), lambda g: (g, 0)), at(0), at(0), at(1), at(0), at(1)]
+        return pl.BlockSpec((span, cols), lambda g, _: (g, j))
+    return [pl.BlockSpec((span, 1), lambda g, _: (g, 0)), at(0), at(0), at(1), at(0), at(1)]
 
 def attend(starts, query, key_value, before, groups):
     span, cols = query.shape[0] // groups, query.shape[1]
     return pl.pallas_call(
         attend_kernel,
-        grid=(groups,),
         out_shape=jax.ShapeDtypeStruct((groups * span, cols), bfloat),
-        in_specs=attention_specs(span, cols),
-        out_specs=pl.BlockSpec((span, cols), lambda g: (g, 0)),
+        grid_spec=pltpu.PrefetchScalarGridSpec(
+            num_scalar_prefetch=1,
+            grid=(groups,),
+            in_specs=attention_specs(span, cols),
+            out_specs=pl.BlockSpec((span, cols), lambda g, _: (g, 0)),
+        ),
         compiler_params=pltpu.CompilerParams(vmem_limit_bytes=60 << 20),
         name="attend",
-    )(starts, query, key_value, key_value, before, before)
+    )(block_starts(starts, groups), starts, query, key_value, key_value, before, before)
 
 def attend_back(starts, query, key_value, before, grad, groups):
     span, cols = query.shape[0] // groups, query.shape[1]
     rows = groups * span
     return pl.pallas_call(
         attend_back_kernel,
-        grid=(groups,),
-        out_shape=[jax.ShapeDtypeStruct((rows, cols), bfloat), jax.ShapeDtypeStruct((rows, 2 * cols), bfloat), jax.ShapeDtypeStruct((rows, 2 * cols), single)],
-        in_specs=attention_specs(span, cols) + [pl.BlockSpec((span, cols), lambda g: (g, 0))],
-        out_specs=[pl.BlockSpec((span, cols), lambda g: (g, 0))] + [pl.BlockSpec((span, 2 * cols), lambda g: (g, 0))] * 2,
-        scratch_shapes=[pltpu.VMEM((2 * span, cols), single)] * 2,
+        out_shape=[
+            jax.ShapeDtypeStruct((rows, cols), bfloat),
+            jax.ShapeDtypeStruct((rows, 2 * cols), bfloat),
+            jax.ShapeDtypeStruct((rows, 2 * cols), single),
+        ],
+        grid_spec=pltpu.PrefetchScalarGridSpec(
+            num_scalar_prefetch=1,
+            grid=(groups,),
+            in_specs=attention_specs(span, cols) + [pl.BlockSpec((span, cols), lambda g, _: (g, 0))],
+            out_specs=[pl.BlockSpec((span, cols), lambda g, _: (g, 0))]
+            + [pl.BlockSpec((span, 2 * cols), lambda g, _: (g, 0))] * 2,
+            scratch_shapes=[pltpu.VMEM((2 * span, cols), single)] * 2,
+        ),
         compiler_params=pltpu.CompilerParams(vmem_limit_bytes=60 << 20),
         name="attend_back",
-    )(starts, query, key_value, key_value, before, before, grad)
+    )(block_starts(starts, groups), starts, query, key_value, key_value, before, before, grad)
 
 
 def attention_heads(starts, query, key_value, before, groups):

time: 658 us -> 653 us (level)
  Pallas kernels: 458 us -> 447 us
    unnamed x56 -> x60, local copies, waits for them, and re-layouts: 15.2 us -> 16.1 us
  transfers between devices with their start and end apart: 11 -> 11, of which waited for: 7 -> 7; matrix products, arithmetic and copies ran while one was open for 13% -> 13% of each run, Pallas kernels for 70% -> 69%
where the time goes in v11:
time: 653 us; the launch traced here: 647 us
  Pallas kernels  447 us (68%)
  waiting for transfers between devices  68.2 us (10%)
  matrix products  38.2 us (6%)
  local copies, waits for them, and re-layouts  38 us (6%)
  other arithmetic  33.6 us (5%)
  between operations  16.2 us (2%)
    pallas_call x3, Pallas kernels, dot_reduce(): pl.pallas_call(functools.partial(reduce_kernel, turned, len(left)), out_s...  138 us
    pallas_call x3, Pallas kernels, plane_gather(): pl.pallas_call(functools.partial(gather_kernel, body_of, len(ins), len(ou...  123 us
    pallas_call x1, Pallas kernels, last_units(): pl.pallas_call(last_units_kernel, out_shape=[jax.ShapeDtypeStruct((ranks,...  54.9 us
    pallas_call x1, Pallas kernels, first_units(): pl.pallas_call(first_units_kernel, out_shape=[jax.ShapeDtypeStruct((ranks...  51.3 us
    pallas_call x2, Pallas kernels, exchange_call(): pl.pallas_call(kernel, out_shape=out_shape, in_specs=[inside] * len(args)...  37.2 us
    pallas_call x1, Pallas kernels, attend_back(): pl.pallas_call(attend_back_kernel, out_shape=[jax.ShapeDtypeStruct((rows,...  30.4 us
    ppermute x1, waiting for transfers between devices, on_device(): before = lax.ppermute(key_value, 'z', up)  25.7 us
    dot_general x3, matrix products, dot_tn(): lax.dot_general(left, right, (((0,), (0,)), ((), ())), preferred_element_...  22.9 us
  transfers between devices with their start and end apart: 11, of which 7 were waited for; matrix products, arithmetic and copies ran while one was open for 13% of the time, Pallas kernels for 69%

profile of v11, /device:TPU:0, one launch (start us, length us, event | category | flops | bytes accessed | tf_op | source)
XLA Modules:
  0.0 646.9 jit_solution(376299172158360221)
XLA Ops:
  8.6 6.1 concatenate.27
  17.6 20.5 %spread.1 = (bf16[8,64,256]{2,1,0:T(8,128)(2,1)}, bf16[8,64,512]{2,1,0:T(8,128)(2,1)}, f32[32,1,896]{2,1,0:T(1,128)S(1)}) custom-call(bf16[64,2048]{1,0:T(8,128)(2,1)S(1)} %copy-done.1, bf16[64,2048]{1,0:T(8,128)(2,1)S(1)} %copy-done.2, bf16[64,2048]{1,0:T(8,128)(2,1)S(1)} %copy-done.3, f32[1,1,896]{2,1,0:T(1,128)S(1)} %broadcast_in_dim.96.pack_ref), custom_call_target="tpu_custom_call" | custom-call | flops 1048576 | bytes 33554432 | tf_op jit(solution)/shard_map/spread/pallas_call | solution.py:640
  47.7 40.8 %gather_normed.1 = bf16[8,256,2048]{2,1,0:T(8,128)(2,1)} custom-call(bf16[256,2048]{1,0:T(8,128)(2,1)} %fusion.10.x_ref), custom_call_target="tpu_custom_call" | custom-call | flops 1073741824 | bytes 134217728 | tf_op jit(solution)/shard_map/gather_normed/pallas_call | solution.py:108
  97.6 8.2 %add_convert_fusion.1.k_ref.v_ref = bf16[2048,512]{1,0:T(8,128)(2,1)S(1)} fusion(bf16[2048,2048]{1,0:T(8,128)(2,1)} %bitcast.159, bf16[2048,512]{1,0:T(8,128)(2,1)S(1)} %bitcast.164, f32[512]{0:T(512)S(1)} %concatenate.29), kind=kOutput, calls=%fused_computation.1 | convolution fusion | flops 4297064448 | bytes 12584960 | tf_op jit(solution)/shard_map/dot_general | solution.py:226
  105.8 3.5 collective-permute-start
  111.7 40.3 %gather_branch.1 = bf16[8,256,2048]{2,1,0:T(8,128)(2,1)} custom-call(bf16[256,2048]{1,0:T(8,128)(2,1)} %get-tuple-element.75.x_ref), custom_call_target="tpu_custom_call" | custom-call | flops 1073741824 | bytes 134217728 | tf_op jit(solution)/shard_map/gather_branch/pallas_call | solution.py:108
  153.4 7.1 %fusion.2.q_ref = bf16[2048,256]{1,0:T(8,128)(2,1)} fusion(bf16[2048,2048]{1,0:T(8,128)(2,1)} %bitcast.160, bf16[2048,256]{1,0:T(8,128)(2,1)S(1)} %bitcast.168, f32[256]{0:T(256)S(1)} %bitcast.192), kind=kOutput, calls=%fused_computation.9 | convolution fusion | flops 2148532224 | bytes 10486784 | tf_op jit(solution)/shard_map/dot_general | solution.py:226
  160.5 25.7 %collective-permute-done.kb_ref.vb_ref = bf16[2048,512]{1,0:T(8,128)(2,1)} collective-permute-done((bf16[2048,512]{1,0:T(8,128)(2,1)S(1)}, bf16[2048,512]{1,0:T(8,128)(2,1)}, u32[]{:S(2)}, u32[]{:S(2)}) %collective-permute-start) | collective-permute-done | bytes 2097184 | tf_op jit(solution)/shard_map/ppermute | solution.py:1014
  186.3 12.1 %attend.1 = bf16[2048,256]{1,0:T(8,128)(2,1)} custom-call(s32[8]{0:T(128)} %slice_reduce_fusion.first_ref, s32[2048,1]{1,0:T(8,128)} %bitcast.157, bf16[2048,256]{1,0:T(8,128)(2,1)} %fusion.2.q_ref, bf16[2048,512]{1,0:T(8,128)(2,1)} %copy-done.8, bf16[2048,512]{1,0:T(8,128)(2,1)} %copy-done.8, bf16[2048,512]{1,0:T(8,128)(2,1)} %collective-permute-done.kb_ref.vb_ref, ...), custom_call_target="tpu_custom_call" | custom-call | tf_op jit(solution)/shard_map/attend/pallas_call | solution.py:797
  199.8 43.1 %attended.1 = f32[256,2048]{1,0:T(8,128)} custom-call(bf16[8,256,256]{2,1,0:T(8,128)(2,1)} %bitcast.153, bf16[256,2048]{1,0:T(8,128)(2,1)} %all-gather.6.cloned.1.call-done.refs_1_.refs_0_), custom_call_target="tpu_custom_call" | custom-call | flops 1073741824 | bytes 134217728 | tf_op jit(solution)/shard_map/attended/pallas_call | solution.py:213
  247.8 51.3 %first_units.1 = (bf16[8,256,2048]{2,1,0:T(8,128)(2,1)}, bf16[8,256,512]{2,1,0:T(8,128)(2,1)}, bf16[8,256,512]{2,1,0:T(8,128)(2,1)}, f32[1,512]{1,0:T(1,128)}, bf16[4,2,128,2048]{3,2,1,0:T(8,128)(2,1)}) custom-call(bf16[256,2048]{1,0:T(8,128)(2,1)} %add_convert_fusion.3.x_ref, bf16[8,256,2048]{2,1,0:T(8,128)(2,1)} %gather_branch.1, ...), custom_call_target="tpu_custom_call" | custom-call | flops 1073741824 | bytes 167772160 | tf_op jit(solution)/shard_map/first_units/pallas_call | solution.py:494
  299.2 12.8 %all-gather.14.cloned.1.call-done = bf16[1024,2048]{1,0:T(8,128)(2,1)} async-done(((bf16[256,2048]{1,0:T(8,128)(2,1)}), bf16[1024,2048]{1,0:T(8,128)(2,1)}) %all-gather.14.cloned.1.call-update) | async-done | bytes 4194320 | tf_op jit(solution)/shard_map/all_gather | solution.py:1002
  312.0 54.9 %last_units.1 = (bf16[8,256,512]{2,1,0:T(8,128)(2,1)}, f32[1,512]{1,0:T(1,128)}, f32[256,2048]{1,0:T(8,128)}, bf16[4,2,128,2048]{3,2,1,0:T(8,128)(2,1)}) custom-call(bf16[8,256,2048]{2,1,0:T(8,128)(2,1)} %get-tuple-element.85.all_ref, bf16[8,256,2048]{2,1,0:T(8,128)(2,1)} %gather_branch.1, bf16[8,256,512]{2,1,0:T(8,128)(2,1)} %get-tuple-element.86.pg1_ref, ...), custom_call_target="tpu_custom_call" | custom-call | flops 1073741824 | bytes 167772160 | tf_op jit(solution)/shard_map/last_units/pallas_call | solution.py:525
  374.4 42.0 %attended_grad.1 = (bf16[8,256,2048]{2,1,0:T(8,128)(2,1)}, bf16[8,256,256]{2,1,0:T(8,128)(2,1)}) custom-call(bf16[256,2048]{1,0:T(8,128)(2,1)} %get-tuple-element.198.x_ref, bf16[256,2048]{1,0:T(8,128)(2,1)} %all-gather.6.cloned.1.call-done.refs_1_.refs_0_, f32[1,256]{1,0:T(1,128)} %broadcast_in_dim.100.refs_1_), custom_call_target="tpu_custom_call" | custom-call | flops 1073741824 | bytes 134217728 | tf_op jit(solution)/shard_map/attended_grad/pallas_call | solution.py:108
  416.4 30.4 %attend_back.1 = (bf16[2048,256]{1,0:T(8,128)(2,1)}, bf16[2048,512]{1,0:T(8,128)(2,1)}, f32[2048,512]{1,0:T(8,128)}) custom-call(s32[8]{0:T(128)} %slice_reduce_fusion.first_ref, s32[2048,1]{1,0:T(8,128)} %bitcast.158, bf16[2048,256]{1,0:T(8,128)(2,1)} %fusion.2.q_ref, bf16[2048,512]{1,0:T(8,128)(2,1)} %copy-done.8, bf16[2048,512]{1,0:T(8,128)(2,1)} %copy-done.8, ...), custom_call_target="tpu_custom_call" | custom-call | tf_op jit(solution)/shard_map/attend_back/pallas_call | solution.py:813
  448.1 6.8 %fusion.30 = bf16[256,2048]{1,0:T(8,128)(2,1)} fusion(bf16[2048,256]{1,0:T(8,128)(2,1)S(1)} %copy-done.10, bf16[2048,2048]{1,0:T(8,128)(2,1)} %bitcast.150), kind=kOutput, calls=%fused_computation.94 | convolution fusion | flops 2147483648 | bytes 10485760 | tf_op jit(solution)/shard_map/dot_general | solution.py:230
  454.9 6.9 %convolution_convert_fusion.1 = bf16[2048,256]{1,0:T(8,128)(2,1)} fusion(bf16[2048,2048]{1,0:T(8,128)(2,1)} %bitcast.161, bf16[2048,256]{1,0:T(8,128)(2,1)S(1)} %copy-done.19), kind=kOutput, calls=%fused_computation.10 | convolution fusion | flops 2148007936 | bytes 10485760 | tf_op jit(solution)/shard_map/dot_general | solution.py:230
  461.8 48.1 %down.1 = f32[256,2048]{1,0:T(8,128)} custom-call(bf16[8,256,512]{2,1,0:T(8,128)(2,1)} %get-tuple-element.98.refs_0_, bf16[8,256,512]{2,1,0:T(8,128)(2,1)} %get-tuple-element.99.refs_1_, bf16[4,2,128,2048]{3,2,1,0:T(8,128)(2,1)} %bitcast.149, bf16[4,2,128,2048]{3,2,1,0:T(8,128)(2,1)} %bitcast.152), custom_call_target="tpu_custom_call" | custom-call | flops 1073741824 | bytes 134217728 | tf_op jit(solution)/shard_map/down/pallas_call | solution.py:213
  509.9 18.0 %collective-permute-done.1 = bf16[2048,512]{1,0:T(8,128)(2,1)} collective-permute-done((bf16[2048,512]{1,0:T(8,128)(2,1)}, bf16[2048,512]{1,0:T(8,128)(2,1)}, u32[]{:S(2)}, u32[]{:S(2)}) %collective-permute-start.1) | collective-permute-done | bytes 2097184 | tf_op jit(solution)/shard_map/ppermute | solution.py:1077
  527.9 3.6 add_convert_fusion
  531.5 9.2 %convolution_convert_fusion = bf16[2048,512]{1,0:T(8,128)(2,1)S(1)} fusion(bf16[2048,2048]{1,0:T(8,128)(2,1)} %bitcast.162, bf16[2048,512]{1,0:T(8,128)(2,1)S(1)} %add_convert_fusion), kind=kOutput, calls=%fused_computation.3 | convolution fusion | flops 4296015872 | bytes 12582912 | tf_op jit(solution)/shard_map/dot_general | solution.py:230
  553.7 46.8 %qkv_grad.1 = f32[256,2048]{1,0:T(8,128)} custom-call(bf16[8,256,256]{2,1,0:T(8,128)(2,1)} %bitcast.170, bf16[8,256,512]{2,1,0:T(8,128)(2,1)} %bitcast.154, bf16[2048,256]{1,0:T(8,128)(2,1)} %bitcast.169, bf16[2048,512]{1,0:T(8,128)(2,1)} %bitcast.163), custom_call_target="tpu_custom_call" | custom-call | flops 1073741824 | bytes 134217728 | tf_op jit(solution)/shard_map/qkv_grad/pallas_call | solution.py:213
  612.1 16.7 %settle.1 = (f32[64,2048]{1,0:T(8,128)S(1)}, f32[64,2048]{1,0:T(8,128)S(1)}, f32[64,2048]{1,0:T(8,128)S(1)}, f32[1,768]{1,0:T(1,128)S(1)}) custom-call(bf16[8,64,768]{2,1,0:T(8,128)(2,1)S(1)} %bitcast.146, f32[32,1,768]{2,1,0:T(1,128)S(1)} %broadcast_in_dim.109.rows_ref), custom_call_target="tpu_custom_call" | custom-call | flops 1048576 | bytes 33554432 | tf_op jit(solution)/shard_map/settle/pallas_call | solution.py:640
  629.9 5.8 reduce-scatter.11.cloned.1.call-done
  (177 shorter events, 69.9 us)
Async XLA Ops:
  7.2 36.1 %all-gather.6.cloned.1.call-start = ((), (), s32[]{:S(2)}) async-start(), calls=%async_computation.4 | async-start | bytes 1310720 | tf_op jit(solution)/shard_map/all_gather | solution.py:943
  7.9 81.8 %all-gather.8.cloned.1.call-start = ((), (), s32[]{:S(2)}) async-start(), calls=%async_computation.5 | async-start | bytes 2621440 | tf_op jit(solution)/shard_map/all_gather | solution.py:972
  17.6 22.4 %copy-start.7 = (bf16[1,256,2048]{2,1,0:T(8,128)(2,1)S(1)}, bf16[1,256,2048]{2,1,0:T(8,128)(2,1)}, u32[]{:S(2)}) copy-start(bf16[1,256,2048]{2,1,0:T(8,128)(2,1)} %param.20) | copy-start | bytes 3145732
  38.1 113.9 %all-gather.10.cloned.1.call-start = ((), (), s32[]{:S(2)}) async-start(), calls=%async_computation.6 | async-start | bytes 1310720 | tf_op jit(solution)/shard_map/all_gather | solution.py:972
  43.3 204.5 %all-gather.12.cloned.1.call-start = ((), (), s32[]{:S(2)}) async-start(), calls=%async_computation.7 | async-start | bytes 5242880 | tf_op jit(solution)/shard_map/all_gather | solution.py:1002
  89.7 4.5 copy-start.22
  89.7 5.9 copy-start.16
  92.9 219.0 %all-gather.14.cloned.1.call-start = ((), (), s32[]{:S(2)}) async-start(), calls=%async_computation.8 | async-start | bytes 5242880 | tf_op jit(solution)/shard_map/all_gather | solution.py:1002
  105.7 46.3 %copy-start.8 = (bf16[2048,512]{1,0:T(8,128)(2,1)}, bf16[2048,512]{1,0:T(8,128)(2,1)S(1)}, u32[]{:S(2)}) copy-start(bf16[2048,512]{1,0:T(8,128)(2,1)S(1)} %add_convert_fusion.1.k_ref.v_ref) | copy-start | bytes 6291460
  105.8 80.5 %collective-permute-start = (bf16[2048,512]{1,0:T(8,128)(2,1)S(1)}, bf16[2048,512]{1,0:T(8,128)(2,1)}, u32[]{:S(2)}, u32[]{:S(2)}) collective-permute-start(bf16[2048,512]{1,0:T(8,128)(2,1)S(1)} %add_convert_fusion.1.k_ref.v_ref), channel_id=1, source_target_pairs={{0,2},{2,4},{4,6},{1,3},{3,5},{5,7},{8,10},{10,12},{12,14},{9,11},... | collective-permute-start | bytes 6291464 | tf_op jit(solution)/shard_map/ppermute | solution.py:1014
  153.4 7.1 %copy-start.18 = (bf16[4,4,2,64,256]{4,3,2,1,0:T(8,128)(2,1)}, bf16[4,4,2,64,256]{4,3,2,1,0:T(8,128)(2,1)S(1)}, u32[]{:S(2)}) copy-start(bf16[4,4,2,64,256]{4,3,2,1,0:T(8,128)(2,1)S(1)} %copy.69) | copy-start | bytes 3145732
  198.4 218.1 %reduce-scatter.5.cloned.1.call-start = ((), (), s32[]{:S(2)}) async-start(), calls=%async_computation.9 | async-start | bytes 5242880 | tf_op jit(solution)/shard_map/reduce_scatter | solution.py:1037
  299.1 228.8 %reduce-scatter.7.cloned.1.call-start = ((), (), s32[]{:S(2)}) async-start(), calls=%async_computation.10 | async-start | bytes 5242880 | tf_op jit(solution)/shard_map/reduce_scatter | solution.py:1037
  366.9 237.7 %reduce-scatter.9.cloned.1.call-start = ((), (), s32[]{:S(2)}) async-start(), calls=%async_computation.11 | async-start | bytes 3932160 | tf_op jit(solution)/shard_map/reduce_scatter | solution.py:1101
  368.5 2.7 copy-start.13
  368.5 2.7 copy-start.17
  416.4 31.7 %copy-start.10 = (bf16[2048,256]{1,0:T(8,128)(2,1)S(1)}, bf16[2048,256]{1,0:T(8,128)(2,1)}, u32[]{:S(2)}) copy-start(bf16[2048,256]{1,0:T(8,128)(2,1)} %attend.1) | copy-start | bytes 3145732
  446.8 81.1 %collective-permute-start.1 = (bf16[2048,512]{1,0:T(8,128)(2,1)}, bf16[2048,512]{1,0:T(8,128)(2,1)}, u32[]{:S(2)}, u32[]{:S(2)}) collective-permute-start(bf16[2048,512]{1,0:T(8,128)(2,1)} %get-tuple-element.100), channel_id=1, source_target_pairs={{2,0},{4,2},{6,4},{3,1},{5,3},{7,5},{10,8},{12,10},{14,12},{11,9},... | collective-permute-start | bytes 6291464 | tf_op jit(solution)/shard_map/ppermute | solution.py:1077
  448.1 6.8 %copy-start.19 = (bf16[2048,256]{1,0:T(8,128)(2,1)S(1)}, bf16[2048,256]{1,0:T(8,128)(2,1)}, u32[]{:S(2)}) copy-start(bf16[2048,256]{1,0:T(8,128)(2,1)} %get-tuple-element.96) | copy-start | bytes 3145732
  531.5 21.7 %copy-start.11 = (bf16[2048,512]{1,0:T(8,128)(2,1)}, bf16[2048,512]{1,0:T(8,128)(2,1)S(1)}, u32[]{:S(2)}) copy-start(bf16[2048,512]{1,0:T(8,128)(2,1)S(1)} %add_convert_fusion) | copy-start | bytes 6291460
  531.5 9.3 %copy-start.21 = (bf16[2048,256]{1,0:T(8,128)(2,1)S(1)}, bf16[2048,256]{1,0:T(8,128)(2,1)}, u32[]{:S(2)}) copy-start(bf16[2048,256]{1,0:T(8,128)(2,1)} %convolution_convert_fusion.1) | copy-start | bytes 3145732
  542.9 92.9 %reduce-scatter.11.cloned.1.call-start = ((), (), s32[]{:S(2)}) async-start(), calls=%async_computation.12 | async-start | bytes 1310720 | tf_op jit(solution)/shard_map/reduce_scatter | solution.py:1121
  604.7 3.0 copy-start.12
  604.7 3.0 copy-start.6
  (12 other events, 17.8 us)
Sparse Core Ops, SparseCore 0:
  9.6 33.6 all-gather.5
  44.8 44.7 all-gather.7
  91.3 30.2 all-gather.9
  123.0 104.6 all-gather.11
  229.1 82.8 all-gather.13
  314.1 90.3 reduce-scatter.4
  406.9 88.1 reduce-scatter.6
  543.0 61.6 reduce-scatter.8
  607.0 28.7 reduce-scatter.10

commit v12 on v11

--- a/solution.py
+++ b/solution.py
@@ -783,6 +783,56 @@
     pair_ref[:, cols:] = dv[span:, :]
 
 
+def pair_grads_kernel(pair_ref, after_ref, normed_ref, query_w_ref, grad_ref, weight_ref, bias_ref):
+    block = pl.program_id(0)
+    cols = query_w_ref.shape[1]
+    rows = weight_ref.shape[3]
+
+    @pl.when(block == 0)
+    def _():
+        grad = (pair_ref[...] + after_ref[...].astype(single)).astype(bfloat)
+        grad_ref[...] = grad
+        bias_ref[...] = jnp.sum(grad[:, cols:].astype(single), axis=0, keepdims=True)
+
+    value = dot_tn(normed_ref[...], grad_ref[...]).astype(bfloat)
+    xs = weight_ref.shape[2]
+    for z in range(weight_ref.shape[0]):
+        for x in range(xs):
+            here = slice((z * xs + x) * rows, (z * xs + x + 1) * rows)
+            weight_ref[z, 0, x, :, :cols] = query_w_ref[here, :]
+            weight_ref[z, 0, x, :, cols:] = value[here, :]
+
+
+def pair_grads(pair, after, normed, query_w, B, Z, X):
+    tokens, wide = pair.shape
+    D = normed.shape[1]
+    per = D // B
+    rows = per // (Z * X)
+    cols = query_w.shape[1]
+    return pl.pallas_call(
+        pair_grads_kernel,
+        grid=(B,),
+        out_shape=[
+            jax.ShapeDtypeStruct((tokens, wide), bfloat),
+            jax.ShapeDtypeStruct((Z, B, X, rows, cols + wide), bfloat),
+            jax.ShapeDtypeStruct((1, wide - cols), single),
+        ],
+        in_specs=[
+            pl.BlockSpec((tokens, wide), lambda b: (0, 0)),
+            pl.BlockSpec((tokens, wide), lambda b: (0, 0)),
+            pl.BlockSpec((tokens, per), lambda b: (0, b)),
+            pl.BlockSpec((per, cols), lambda b: (b, 0)),
+        ],
+        out_specs=[
+            pl.BlockSpec((tokens, wide), lambda b: (0, 0)),
+            pl.BlockSpec((Z, 1, X, rows, cols + wide), lambda b: (0, b, 0, 0, 0)),
+            pl.BlockSpec((1, wide - cols), lambda b: (0, 0)),
+        ],
+        compiler_params=pltpu.CompilerParams(vmem_limit_bytes=48 << 20),
+        name="pair_grads",
+    )(pair, after, normed, query_w)
+
+
 def block_starts(starts, groups):
     return starts.reshape(groups * 2, -1)[:, 0]
 
@@ -1080,15 +1130,20 @@
     downs = [unit_one, unit_two] if fast else [down_one, down_two]
     branch = sum_halves([hidden_one, hidden_two], downs, False, 4, "down")
     branch, after, shard_two = lax.optimization_barrier((branch, after, shard_two))
-    outputs = middle + active * (branch + bias_down)
-    pair_grad = (pair + after.astype(single)).astype(bfloat)
-    pair_w_grad = dot_tn(normed_all, pair_grad).astype(bfloat)
-    pair_grad, pair_w_grad = lax.optimization_barrier((pair_grad, pair_w_grad))
+    if fast:
+        pair_grad, qkv_w_grad, value_b_grad = pair_grads(pair, after, normed_all, query_w_grad, B, Z, X)
+        value_b_grad = value_b_grad[0]
+    else:
+        pair_grad = (pair + after.astype(single)).astype(bfloat)
+        pair_w_grad = dot_tn(normed_all, pair_grad).astype(bfloat)
+        qkv_w_grad = jnp.concatenate([query_w_grad, pair_w_grad], axis=1)
+        qkv_w_grad = qkv_w_grad.reshape(B, Z, X, rows_dev, 3 * cols).transpose(1, 0, 2, 3, 4)
+        value_b_grad = column_sums(pair_grad[:, cols:])
+    qkv_w_grad = qkv_w_grad.reshape(D, 3 * cols)
+    qkv_w_grad = lax.psum_scatter(qkv_w_grad, "z", scatter_dimension=0, tiled=True).reshape(R, rows_dev, 3 * cols)
     normed_grad = sum_halves([query_grad, pair_grad], [weight_q, weight_kv], True, 6, "qkv_grad")
     query_b_grad = column_sums(query_grad)
-    value_b_grad = column_sums(pair_grad[:, cols:])
     input_part, gain_one_grad, bias_one_grad = norm_backward(local, normed_grad, gain_one)
-    input_grad = middle_grad + input_part
 
     def sum_to_owners(vectors, axes, parts):
         split = jnp.concatenate([v.reshape(parts, -1) for v in vectors], axis=1)
@@ -1096,9 +1151,6 @@
         widths = [v.shape[0] // parts for v in vectors]
         return [summed[sum(widths[:i]) : sum(widths[: i + 1])] for i in range(len(widths))]
 
-    qkv_w_grad = jnp.concatenate([query_w_grad, pair_w_grad], axis=1)
-    qkv_w_grad = qkv_w_grad.reshape(B, Z, X, rows_dev, 3 * cols).transpose(1, 0, 2, 3, 4).reshape(D, 3 * cols)
-    qkv_w_grad = lax.psum_scatter(qkv_w_grad, "z", scatter_dimension=0, tiled=True).reshape(R, rows_dev, 3 * cols)
     qkv_w_grad, out_w_grad = lax.optimization_barrier((qkv_w_grad, out_w_grad))
     device_sums = [gain_one_grad, bias_one_grad, out_b_grad, gain_two_grad, bias_two_grad, down_b_grad]
     if fast:
@@ -1131,6 +1183,8 @@
         out_w_shard = placed(out_w_grad.astype(bfloat))
         q_b_shard = placed(query_b_grad)
         v_b_shard = placed(value_b_grad)
+    outputs = middle + active * (branch + bias_down)
+    input_grad = middle_grad + input_part
     return (
         outputs.astype(bfloat)[None],
         input_grad.astype(bfloat)[None],

time: 653 us -> 649 us (level)
  matrix products: 38.2 us -> 28.2 us
  Pallas kernels: 447 us -> 457 us
    pallas_call x0 -> x1, Pallas kernels: none -> 10.2 us  [pair_grads(): pl.pallas_call(pair_grads_kernel, grid=(B,), out_shape=[jax.ShapeDtypeStr...]
    dot_general x3 -> x2, matrix products: 22.9 us -> 12.9 us  [dot_tn(): lax.dot_general(left, right, (((0,), (0,)), ((), ())), preferred_element_...]
    unnamed x60 -> x62, local copies, waits for them, and re-layouts: 16.1 us -> 16.7 us
  transfers between devices with their start and end apart: 11 -> 11, of which waited for: 7 -> 7; matrix products, arithmetic and copies ran while one was open for 13% -> 12% of each run, Pallas kernels for 69% -> 70%
where the time goes in v12:
time: 649 us; the launch traced here: 643 us
  Pallas kernels  457 us (70%)
  waiting for transfers between devices  72.4 us (11%)
  local copies, waits for them, and re-layouts  35.8 us (6%)
  matrix products  28.2 us (4%)
  other arithmetic  27.6 us (4%)
  between operations  16.2 us (2%)
    pallas_call x3, Pallas kernels, dot_reduce(): pl.pallas_call(functools.partial(reduce_kernel, turned, len(left)), out_s...  138 us
    pallas_call x3, Pallas kernels, plane_gather(): pl.pallas_call(functools.partial(gather_kernel, body_of, len(ins), len(ou...  123 us
    pallas_call x1, Pallas kernels, last_units(): pl.pallas_call(last_units_kernel, out_shape=[jax.ShapeDtypeStruct((ranks,...  54.9 us
    pallas_call x1, Pallas kernels, first_units(): pl.pallas_call(first_units_kernel, out_shape=[jax.ShapeDtypeStruct((ranks...  51.3 us
    pallas_call x2, Pallas kernels, exchange_call(): pl.pallas_call(kernel, out_shape=out_shape, in_specs=[inside] * len(args)...  37.2 us
    pallas_call x1, Pallas kernels, attend_back(): pl.pallas_call(attend_back_kernel, out_shape=[jax.ShapeDtypeStruct((rows,...  30.4 us
    ppermute x1, waiting for transfers between devices, on_device(): before = lax.ppermute(key_value, 'z', up)  25.8 us
    ppermute x1, waiting for transfers between devices, on_device(): after = lax.ppermute(edge, 'z', down)  19.2 us
  transfers between devices with their start and end apart: 11, of which 7 were waited for; matrix products, arithmetic and copies ran while one was open for 12% of the time, Pallas kernels for 70%

profile of v12, /device:TPU:0, one launch (start us, length us, event | category | flops | bytes accessed | tf_op | source)
XLA Modules:
  0.0 642.9 jit_solution(604536709134991212)
XLA Ops:
  8.6 6.1 concatenate.24
  17.6 20.5 %spread.1 = (bf16[8,64,256]{2,1,0:T(8,128)(2,1)}, bf16[8,64,512]{2,1,0:T(8,128)(2,1)}, f32[32,1,896]{2,1,0:T(1,128)S(1)}) custom-call(bf16[64,2048]{1,0:T(8,128)(2,1)S(1)} %copy-done.2, bf16[64,2048]{1,0:T(8,128)(2,1)S(1)} %copy-done.3, bf16[64,2048]{1,0:T(8,128)(2,1)S(1)} %copy-done.4, f32[1,1,896]{2,1,0:T(1,128)S(1)} %broadcast_in_dim.96.pack_ref), custom_call_target="tpu_custom_call" | custom-call | flops 1048576 | bytes 33554432 | tf_op jit(solution)/shard_map/spread/pallas_call | solution.py:640
  47.7 40.8 %gather_normed.1 = bf16[8,256,2048]{2,1,0:T(8,128)(2,1)} custom-call(bf16[256,2048]{1,0:T(8,128)(2,1)} %fusion.10.x_ref), custom_call_target="tpu_custom_call" | custom-call | flops 1073741824 | bytes 134217728 | tf_op jit(solution)/shard_map/gather_normed/pallas_call | solution.py:108
  97.6 8.2 %add_convert_fusion.k_ref.v_ref = bf16[2048,512]{1,0:T(8,128)(2,1)S(1)} fusion(bf16[2048,2048]{1,0:T(8,128)(2,1)} %bitcast.146, bf16[2048,512]{1,0:T(8,128)(2,1)S(1)} %bitcast.157, f32[512]{0:T(512)S(1)} %concatenate.26), kind=kOutput, calls=%fused_computation | convolution fusion | flops 4297064448 | bytes 12584960 | tf_op jit(solution)/shard_map/dot_general | solution.py:226
  105.8 3.5 collective-permute-start
  111.7 40.3 %gather_branch.1 = bf16[8,256,2048]{2,1,0:T(8,128)(2,1)} custom-call(bf16[256,2048]{1,0:T(8,128)(2,1)} %get-tuple-element.76.x_ref), custom_call_target="tpu_custom_call" | custom-call | flops 1073741824 | bytes 134217728 | tf_op jit(solution)/shard_map/gather_branch/pallas_call | solution.py:108
  153.4 7.1 %fusion.2.q_ref = bf16[2048,256]{1,0:T(8,128)(2,1)} fusion(bf16[2048,2048]{1,0:T(8,128)(2,1)} %bitcast.147, bf16[2048,256]{1,0:T(8,128)(2,1)S(1)} %bitcast.161, f32[256]{0:T(256)S(1)} %bitcast.186), kind=kOutput, calls=%fused_computation.6 | convolution fusion | flops 2148532224 | bytes 10486784 | tf_op jit(solution)/shard_map/dot_general | solution.py:226
  160.5 25.8 %collective-permute-done.kb_ref.vb_ref = bf16[2048,512]{1,0:T(8,128)(2,1)} collective-permute-done((bf16[2048,512]{1,0:T(8,128)(2,1)S(1)}, bf16[2048,512]{1,0:T(8,128)(2,1)}, u32[]{:S(2)}, u32[]{:S(2)}) %collective-permute-start) | collective-permute-done | bytes 2097184 | tf_op jit(solution)/shard_map/ppermute | solution.py:1064
  186.3 12.1 %attend.1 = bf16[2048,256]{1,0:T(8,128)(2,1)} custom-call(s32[8]{0:T(128)} %slice_reduce_fusion.first_ref, s32[2048,1]{1,0:T(8,128)} %bitcast.154, bf16[2048,256]{1,0:T(8,128)(2,1)} %fusion.2.q_ref, bf16[2048,512]{1,0:T(8,128)(2,1)} %copy-done.10, bf16[2048,512]{1,0:T(8,128)(2,1)} %copy-done.10, bf16[2048,512]{1,0:T(8,128)(2,1)} %collective-permute-done.kb_ref.vb_ref, ...), custom_call_target="tpu_custom_call" | custom-call | tf_op jit(solution)/shard_map/attend/pallas_call | solution.py:847
  199.8 43.1 %attended.1 = f32[256,2048]{1,0:T(8,128)} custom-call(bf16[8,256,256]{2,1,0:T(8,128)(2,1)} %bitcast.153, bf16[256,2048]{1,0:T(8,128)(2,1)} %all-gather.6.cloned.1.call-done.refs_1_.refs_0_), custom_call_target="tpu_custom_call" | custom-call | flops 1073741824 | bytes 134217728 | tf_op jit(solution)/shard_map/attended/pallas_call | solution.py:213
  247.8 51.3 %first_units.1 = (bf16[8,256,2048]{2,1,0:T(8,128)(2,1)}, bf16[8,256,512]{2,1,0:T(8,128)(2,1)}, bf16[8,256,512]{2,1,0:T(8,128)(2,1)}, f32[1,512]{1,0:T(1,128)}, bf16[4,2,128,2048]{3,2,1,0:T(8,128)(2,1)}) custom-call(bf16[256,2048]{1,0:T(8,128)(2,1)} %add_convert_fusion.2.x_ref, bf16[8,256,2048]{2,1,0:T(8,128)(2,1)} %gather_branch.1, ...), custom_call_target="tpu_custom_call" | custom-call | flops 1073741824 | bytes 167772160 | tf_op jit(solution)/shard_map/first_units/pallas_call | solution.py:494
  299.1 12.8 %all-gather.14.cloned.1.call-done = bf16[1024,2048]{1,0:T(8,128)(2,1)} async-done(((bf16[256,2048]{1,0:T(8,128)(2,1)}), bf16[1024,2048]{1,0:T(8,128)(2,1)}) %all-gather.14.cloned.1.call-update) | async-done | bytes 4194320 | tf_op jit(solution)/shard_map/all_gather | solution.py:1052
  312.0 54.9 %last_units.1 = (bf16[8,256,512]{2,1,0:T(8,128)(2,1)}, f32[1,512]{1,0:T(1,128)}, f32[256,2048]{1,0:T(8,128)}, bf16[4,2,128,2048]{3,2,1,0:T(8,128)(2,1)}) custom-call(bf16[8,256,2048]{2,1,0:T(8,128)(2,1)} %get-tuple-element.86.all_ref, bf16[8,256,2048]{2,1,0:T(8,128)(2,1)} %gather_branch.1, bf16[8,256,512]{2,1,0:T(8,128)(2,1)} %get-tuple-element.87.pg1_ref, ...), custom_call_target="tpu_custom_call" | custom-call | flops 1073741824 | bytes 167772160 | tf_op jit(solution)/shard_map/last_units/pallas_call | solution.py:525
  374.4 42.1 %attended_grad.1 = (bf16[8,256,2048]{2,1,0:T(8,128)(2,1)}, bf16[8,256,256]{2,1,0:T(8,128)(2,1)}) custom-call(bf16[256,2048]{1,0:T(8,128)(2,1)} %get-tuple-element.200.x_ref, bf16[256,2048]{1,0:T(8,128)(2,1)} %all-gather.6.cloned.1.call-done.refs_1_.refs_0_, f32[1,256]{1,0:T(1,128)} %broadcast_in_dim.100.refs_1_), custom_call_target="tpu_custom_call" | custom-call | flops 1073741824 | bytes 134217728 | tf_op jit(solution)/shard_map/attended_grad/pallas_call | solution.py:108
  416.6 30.4 %attend_back.1 = (bf16[2048,256]{1,0:T(8,128)(2,1)}, bf16[2048,512]{1,0:T(8,128)(2,1)}, f32[2048,512]{1,0:T(8,128)}) custom-call(s32[8]{0:T(128)} %slice_reduce_fusion.first_ref, s32[2048,1]{1,0:T(8,128)} %bitcast.155, bf16[2048,256]{1,0:T(8,128)(2,1)} %fusion.2.q_ref, bf16[2048,512]{1,0:T(8,128)(2,1)} %copy-done.10, bf16[2048,512]{1,0:T(8,128)(2,1)} %copy-done.10, ...), custom_call_target="tpu_custom_call" | custom-call | tf_op jit(solution)/shard_map/attend_back/pallas_call | solution.py:863
  448.2 6.7 %fusion.30 = bf16[256,2048]{1,0:T(8,128)(2,1)} fusion(bf16[2048,256]{1,0:T(8,128)(2,1)S(1)} %copy-done.12, bf16[2048,2048]{1,0:T(8,128)(2,1)} %bitcast.150), kind=kOutput, calls=%fused_computation.90 | convolution fusion | flops 2147483648 | bytes 10485760 | tf_op jit(solution)/shard_map/dot_general | solution.py:230
  455.0 6.1 convolution_convert_fusion.query_w_ref
  461.1 47.9 %down.1 = f32[256,2048]{1,0:T(8,128)} custom-call(bf16[8,256,512]{2,1,0:T(8,128)(2,1)} %get-tuple-element.99.refs_0_, bf16[8,256,512]{2,1,0:T(8,128)(2,1)} %get-tuple-element.100.refs_1_, bf16[4,2,128,2048]{3,2,1,0:T(8,128)(2,1)} %bitcast.145, bf16[4,2,128,2048]{3,2,1,0:T(8,128)(2,1)} %bitcast.152), custom_call_target="tpu_custom_call" | custom-call | flops 1073741824 | bytes 134217728 | tf_op jit(solution)/shard_map/down/pallas_call | solution.py:213
  509.1 19.2 %collective-permute-done.1.after_ref = bf16[2048,512]{1,0:T(8,128)(2,1)S(1)} collective-permute-done((bf16[2048,512]{1,0:T(8,128)(2,1)}, bf16[2048,512]{1,0:T(8,128)(2,1)S(1)}, u32[]{:S(2)}, u32[]{:S(2)}) %collective-permute-start.1) | collective-permute-done | bytes 2097184 | tf_op jit(solution)/shard_map/ppermute | solution.py:1127
  528.2 10.2 %pair_grads.1 = (bf16[2048,512]{1,0:T(8,128)(2,1)S(1)}, bf16[4,4,2,64,768]{4,3,2,1,0:T(8,128)(2,1)}, f32[1,256]{1,0:T(1,128)S(1)}) custom-call(f32[2048,512]{1,0:T(8,128)} %get-tuple-element.104.pair_ref, bf16[2048,512]{1,0:T(8,128)(2,1)S(1)} %collective-permute-done.1.after_ref, bf16[2048,2048]{1,0:T(8,128)(2,1)} %bitcast.149, ...), custom_call_target="tpu_custom_call" | custom-call | tf_op jit(solution)/shard_map/pair_grads/pallas_call | solution.py:812
  546.8 46.7 %qkv_grad.1 = f32[256,2048]{1,0:T(8,128)} custom-call(bf16[8,256,256]{2,1,0:T(8,128)(2,1)} %bitcast.163, bf16[8,256,512]{2,1,0:T(8,128)(2,1)} %bitcast.141, bf16[2048,256]{1,0:T(8,128)(2,1)} %bitcast.162, bf16[2048,512]{1,0:T(8,128)(2,1)} %bitcast.156), custom_call_target="tpu_custom_call" | custom-call | flops 1073741824 | bytes 134217728 | tf_op jit(solution)/shard_map/qkv_grad/pallas_call | solution.py:213
  596.5 4.2 reduce-scatter.9.cloned.1.call-done
  608.1 16.7 %settle.1 = (f32[64,2048]{1,0:T(8,128)S(1)}, f32[64,2048]{1,0:T(8,128)S(1)}, f32[64,2048]{1,0:T(8,128)S(1)}, f32[1,768]{1,0:T(1,128)S(1)}) custom-call(bf16[8,64,768]{2,1,0:T(8,128)(2,1)S(1)} %bitcast.142, f32[32,1,768]{2,1,0:T(1,128)S(1)} %broadcast_in_dim.109.rows_ref), custom_call_target="tpu_custom_call" | custom-call | flops 1048576 | bytes 33554432 | tf_op jit(solution)/shard_map/settle/pallas_call | solution.py:640
  625.9 5.9 reduce-scatter.11.cloned.1.call-done
  (177 shorter events, 64.2 us)
Async XLA Ops:
  7.2 36.1 %all-gather.6.cloned.1.call-start = ((), (), s32[]{:S(2)}) async-start(), calls=%async_computation.4 | async-start | bytes 1310720 | tf_op jit(solution)/shard_map/all_gather | solution.py:993
  7.9 81.8 %all-gather.8.cloned.1.call-start = ((), (), s32[]{:S(2)}) async-start(), calls=%async_computation.5 | async-start | bytes 2621440 | tf_op jit(solution)/shard_map/all_gather | solution.py:1022
  17.6 22.3 %copy-start.8 = (bf16[1,256,2048]{2,1,0:T(8,128)(2,1)S(1)}, bf16[1,256,2048]{2,1,0:T(8,128)(2,1)}, u32[]{:S(2)}) copy-start(bf16[1,256,2048]{2,1,0:T(8,128)(2,1)} %param.20) | copy-start | bytes 3145732
  38.1 113.9 %all-gather.10.cloned.1.call-start = ((), (), s32[]{:S(2)}) async-start(), calls=%async_computation.6 | async-start | bytes 1310720 | tf_op jit(solution)/shard_map/all_gather | solution.py:1022
  43.3 204.5 %all-gather.12.cloned.1.call-start = ((), (), s32[]{:S(2)}) async-start(), calls=%async_computation.7 | async-start | bytes 5242880 | tf_op jit(solution)/shard_map/all_gather | solution.py:1052
  89.7 4.5 copy-start.23
  89.7 5.9 copy-start.17
  92.9 219.0 %all-gather.14.cloned.1.call-start = ((), (), s32[]{:S(2)}) async-start(), calls=%async_computation.8 | async-start | bytes 5242880 | tf_op jit(solution)/shard_map/all_gather | solution.py:1052
  105.7 46.3 %copy-start.10 = (bf16[2048,512]{1,0:T(8,128)(2,1)}, bf16[2048,512]{1,0:T(8,128)(2,1)S(1)}, u32[]{:S(2)}) copy-start(bf16[2048,512]{1,0:T(8,128)(2,1)S(1)} %add_convert_fusion.k_ref.v_ref) | copy-start | bytes 6291460
  105.8 80.5 %collective-permute-start = (bf16[2048,512]{1,0:T(8,128)(2,1)S(1)}, bf16[2048,512]{1,0:T(8,128)(2,1)}, u32[]{:S(2)}, u32[]{:S(2)}) collective-permute-start(bf16[2048,512]{1,0:T(8,128)(2,1)S(1)} %add_convert_fusion.k_ref.v_ref), channel_id=1, source_target_pairs={{0,2},{2,4},{4,6},{1,3},{3,5},{5,7},{8,10},{10,12},{12,14},{9,11},... | collective-permute-start | bytes 6291464 | tf_op jit(solution)/shard_map/ppermute | solution.py:1064
  153.4 7.1 %copy-start.19 = (bf16[4,4,2,64,256]{4,3,2,1,0:T(8,128)(2,1)}, bf16[4,4,2,64,256]{4,3,2,1,0:T(8,128)(2,1)S(1)}, u32[]{:S(2)}) copy-start(bf16[4,4,2,64,256]{4,3,2,1,0:T(8,128)(2,1)S(1)} %copy.66) | copy-start | bytes 3145732
  198.4 218.2 %reduce-scatter.5.cloned.1.call-start = ((), (), s32[]{:S(2)}) async-start(), calls=%async_computation.9 | async-start | bytes 5242880 | tf_op jit(solution)/shard_map/reduce_scatter | solution.py:1087
  299.1 229.1 %reduce-scatter.7.cloned.1.call-start = ((), (), s32[]{:S(2)}) async-start(), calls=%async_computation.10 | async-start | bytes 5242880 | tf_op jit(solution)/shard_map/reduce_scatter | solution.py:1087
  366.9 233.8 %reduce-scatter.9.cloned.1.call-start = ((), (), s32[]{:S(2)}) async-start(), calls=%async_computation.11 | async-start | bytes 3932160 | tf_op jit(solution)/shard_map/reduce_scatter | solution.py:1143
  368.5 2.7 copy-start.14
  368.5 2.7 copy-start.18
  416.6 31.7 %copy-start.12 = (bf16[2048,256]{1,0:T(8,128)(2,1)S(1)}, bf16[2048,256]{1,0:T(8,128)(2,1)}, u32[]{:S(2)}) copy-start(bf16[2048,256]{1,0:T(8,128)(2,1)} %attend.1) | copy-start | bytes 3145732
  446.9 81.3 %collective-permute-start.1 = (bf16[2048,512]{1,0:T(8,128)(2,1)}, bf16[2048,512]{1,0:T(8,128)(2,1)S(1)}, u32[]{:S(2)}, u32[]{:S(2)}) collective-permute-start(bf16[2048,512]{1,0:T(8,128)(2,1)} %get-tuple-element.101), channel_id=1, source_target_pairs={{2,0},{4,2},{6,4},{3,1},{5,3},{7,5},{10,8},{12,10},{14,12},{11,9},... | collective-permute-start | bytes 6291464 | tf_op jit(solution)/shard_map/ppermute | solution.py:1127
  539.8 2.4 copy-start.22
  539.8 92.0 %reduce-scatter.11.cloned.1.call-start = ((), (), s32[]{:S(2)}) async-start(), calls=%async_computation.12 | async-start | bytes 1310720 | tf_op jit(solution)/shard_map/reduce_scatter | solution.py:1173
  546.8 46.7 %copy-start.9 = (bf16[1,256,2048]{2,1,0:T(8,128)(2,1)S(1)}, bf16[1,256,2048]{2,1,0:T(8,128)(2,1)}, u32[]{:S(2)}) copy-start(bf16[1,256,2048]{2,1,0:T(8,128)(2,1)} %param.20) | copy-start | bytes 3145732
  600.7 3.0 copy-start.13
  600.7 3.0 copy-start.7
  603.7 2.6 copy-start.16
  (13 other events, 17.1 us)
Sparse Core Ops, SparseCore 0:
  9.6 33.6 all-gather.5
  44.8 44.7 all-gather.7
  91.3 30.2 all-gather.9
  123.0 104.6 all-gather.11
  229.1 82.8 all-gather.13
  314.1 90.8 reduce-scatter.4
  407.3 87.2 reduce-scatter.6
  539.9 60.7 reduce-scatter.8
  603.0 28.7 reduce-scatter.10

commit v13 on v12

--- a/solution.py
+++ b/solution.py
@@ -292,7 +292,7 @@
     loads = {}
     for n, name in enumerate(at):
         loads[name] = pltpu.make_async_copy(bg_ref.at[at[name]], bg.at[at[name]], load.at[n])
-        loads[name].start()
+    loads["o"].start()
     greet(ids)
     ship, started = shipper(send, recv, ids)
     x0 = ship(x_ref.at[parts[0]], held.at[own, parts[0]], "x")
@@ -310,6 +310,10 @@
         copy.start()
         kept.append(copy)
         loads[name].wait()
+        if name == "o":
+            for other in loads:
+                if other != "o":
+                    loads[other].start()
         hidden_units(src, bg.at[rank], w_ref, b_ref, hid_ref, pg_ref, pb_ref, rank)
 
     def weigh(name, last=False):
@@ -382,6 +386,7 @@
             pltpu.make_async_copy(all_ref.at[at[name]], held.at[at[name]], load.at[n]),
             pltpu.make_async_copy(bg_ref.at[at[name]], bg.at[at[name]], load_b.at[n]),
         ]
+    for name in names[:2]:
         for copy in loads[name]:
             copy.start()
     greet(ids)
@@ -391,6 +396,10 @@
     def units(name):
         for copy in loads[name]:
             copy.wait()
+        if name == names[0]:
+            for other in names[2:]:
+                for copy in loads[other]:
+                    copy.start()
         rank = at[name]
         hidden_units(held.at[rank], bg.at[rank], w_ref, b_ref, hid_ref, pg_ref, pb_ref, rank)
 
@@ -630,7 +639,7 @@
                 rank, i = head // 8 * 2 + head % 2, head // 2 % 4
                 at = part * cols + i * HEAD_DIM
                 sides.append(landed[rank, :, at : at + HEAD_DIM])
-            out[:, pair * 128 : (pair + 1) * 128] = jnp.concatenate(sides, axis=1).astype(single)
+            out[:, pair * 128 : (pair + 1) * 128] = jnp.concatenate(sides, axis=1)
     sums_ref[...] = jnp.sum(gathered[...], axis=0)
 
 
@@ -681,7 +690,7 @@
     D = wide // 3 * 8
     return exchange_call(
         settle_kernel,
-        [jax.ShapeDtypeStruct((tall, D), single)] * 3 + [jax.ShapeDtypeStruct((1, rows.shape[1]), single)],
+        [jax.ShapeDtypeStruct((tall, D), bfloat)] * 3 + [jax.ShapeDtypeStruct((1, rows.shape[1]), single)],
         (weights, rows[:, None]),
         [],
         weights.shape,
@@ -1159,6 +1168,7 @@
         rank_sums = jnp.where(here, rank_sums[None, :, None, :], 0.0).reshape(R * Z, -1)
         rows = jnp.concatenate([v.reshape(R * Z, -1) for v in device_sums] + [rank_sums], axis=1)
         q_w_shard, k_w_shard, v_w_shard, summed = settle(qkv_w_grad, rows, 9)
+        q_w_shard, k_w_shard, v_w_shard = [t.astype(single) for t in (q_w_shard, k_w_shard, v_w_shard)]
         sums = [summed[0, i * rows_dev : (i + 1) * rows_dev] for i in range(len(device_sums) + 2)]
         q_b_shard, v_b_shard = sums[len(device_sums) :]
         up_b_shard = summed[0, (len(device_sums) + 2) * rows_dev :]

time: 649 us -> 646 us (level)
    unnamed x62 -> x59, local copies, waits for them, and re-layouts: 16.7 us -> 14.3 us
  transfers between devices with their start and end apart: 11 -> 11, of which waited for: 7 -> 7; matrix products, arithmetic and copies ran while one was open for 12% -> 13% of each run, Pallas kernels for 70% -> 70%
where the time goes in v13:
time: 646 us; the launch traced here: 640 us
  Pallas kernels  457 us (71%)
  waiting for transfers between devices  69.8 us (11%)
  local copies, waits for them, and re-layouts  33.5 us (5%)
  other arithmetic  30.1 us (5%)
  matrix products  28.2 us (4%)
  between operations  16.2 us (3%)
    pallas_call x3, Pallas kernels, dot_reduce(): pl.pallas_call(functools.partial(reduce_kernel, turned, len(left)), out_s...  138 us
    pallas_call x3, Pallas kernels, plane_gather(): pl.pallas_call(functools.partial(gather_kernel, body_of, len(ins), len(ou...  123 us
    pallas_call x1, Pallas kernels, last_units(): pl.pallas_call(last_units_kernel, out_shape=[jax.ShapeDtypeStruct((ranks,...  54.9 us
    pallas_call x1, Pallas kernels, first_units(): pl.pallas_call(first_units_kernel, out_shape=[jax.ShapeDtypeStruct((ranks...  51.3 us
    pallas_call x2, Pallas kernels, exchange_call(): pl.pallas_call(kernel, out_shape=out_shape, in_specs=[inside] * len(args)...  37.2 us
    pallas_call x1, Pallas kernels, attend_back(): pl.pallas_call(attend_back_kernel, out_shape=[jax.ShapeDtypeStruct((rows,...  30.4 us
    ppermute x1, waiting for transfers between devices, on_device(): before = lax.ppermute(key_value, 'z', up)  25.8 us
    ppermute x1, waiting for transfers between devices, on_device(): after = lax.ppermute(edge, 'z', down)  19.1 us
  transfers between devices with their start and end apart: 11, of which 7 were waited for; matrix products, arithmetic and copies ran while one was open for 13% of the time, Pallas kernels for 70%

profile of v13, /device:TPU:0, one launch (start us, length us, event | category | flops | bytes accessed | tf_op | source)
XLA Modules:
  0.0 640.5 jit_solution(6890416984107389934)
XLA Ops:
  8.6 6.1 concatenate.24
  17.6 20.5 %spread.1 = (bf16[8,64,256]{2,1,0:T(8,128)(2,1)}, bf16[8,64,512]{2,1,0:T(8,128)(2,1)}, f32[32,1,896]{2,1,0:T(1,128)S(1)}) custom-call(bf16[64,2048]{1,0:T(8,128)(2,1)S(1)} %copy-done.2, bf16[64,2048]{1,0:T(8,128)(2,1)S(1)} %copy-done.3, bf16[64,2048]{1,0:T(8,128)(2,1)S(1)} %copy-done.4, f32[1,1,896]{2,1,0:T(1,128)S(1)} %broadcast_in_dim.96.pack_ref), custom_call_target="tpu_custom_call" | custom-call | flops 1048576 | bytes 33554432 | tf_op jit(solution)/shard_map/spread/pallas_call | solution.py:649
  47.7 40.8 %gather_normed.1 = bf16[8,256,2048]{2,1,0:T(8,128)(2,1)} custom-call(bf16[256,2048]{1,0:T(8,128)(2,1)} %fusion.10.x_ref), custom_call_target="tpu_custom_call" | custom-call | flops 1073741824 | bytes 134217728 | tf_op jit(solution)/shard_map/gather_normed/pallas_call | solution.py:108
  97.6 8.2 %add_convert_fusion.k_ref.v_ref = bf16[2048,512]{1,0:T(8,128)(2,1)S(1)} fusion(bf16[2048,2048]{1,0:T(8,128)(2,1)} %bitcast.146, bf16[2048,512]{1,0:T(8,128)(2,1)S(1)} %bitcast.157, f32[512]{0:T(512)S(1)} %concatenate.26), kind=kOutput, calls=%fused_computation | convolution fusion | flops 4297064448 | bytes 12584960 | tf_op jit(solution)/shard_map/dot_general | solution.py:226
  105.8 3.5 collective-permute-start
  111.7 40.3 %gather_branch.1 = bf16[8,256,2048]{2,1,0:T(8,128)(2,1)} custom-call(bf16[256,2048]{1,0:T(8,128)(2,1)} %get-tuple-element.76.x_ref), custom_call_target="tpu_custom_call" | custom-call | flops 1073741824 | bytes 134217728 | tf_op jit(solution)/shard_map/gather_branch/pallas_call | solution.py:108
  153.4 7.1 %fusion.2.q_ref = bf16[2048,256]{1,0:T(8,128)(2,1)} fusion(bf16[2048,2048]{1,0:T(8,128)(2,1)} %bitcast.147, bf16[2048,256]{1,0:T(8,128)(2,1)S(1)} %bitcast.161, f32[256]{0:T(256)S(1)} %bitcast.186), kind=kOutput, calls=%fused_computation.6 | convolution fusion | flops 2148532224 | bytes 10486784 | tf_op jit(solution)/shard_map/dot_general | solution.py:226
  160.5 25.8 %collective-permute-done.kb_ref.vb_ref = bf16[2048,512]{1,0:T(8,128)(2,1)} collective-permute-done((bf16[2048,512]{1,0:T(8,128)(2,1)S(1)}, bf16[2048,512]{1,0:T(8,128)(2,1)}, u32[]{:S(2)}, u32[]{:S(2)}) %collective-permute-start) | collective-permute-done | bytes 2097184 | tf_op jit(solution)/shard_map/ppermute | solution.py:1073
  186.3 12.1 %attend.1 = bf16[2048,256]{1,0:T(8,128)(2,1)} custom-call(s32[8]{0:T(128)} %slice_reduce_fusion.first_ref, s32[2048,1]{1,0:T(8,128)} %bitcast.154, bf16[2048,256]{1,0:T(8,128)(2,1)} %fusion.2.q_ref, bf16[2048,512]{1,0:T(8,128)(2,1)} %copy-done.10, bf16[2048,512]{1,0:T(8,128)(2,1)} %copy-done.10, bf16[2048,512]{1,0:T(8,128)(2,1)} %collective-permute-done.kb_ref.vb_ref, ...), custom_call_target="tpu_custom_call" | custom-call | tf_op jit(solution)/shard_map/attend/pallas_call | solution.py:856
  199.8 43.1 %attended.1 = f32[256,2048]{1,0:T(8,128)} custom-call(bf16[8,256,256]{2,1,0:T(8,128)(2,1)} %bitcast.153, bf16[256,2048]{1,0:T(8,128)(2,1)} %all-gather.6.cloned.1.call-done.refs_1_.refs_0_), custom_call_target="tpu_custom_call" | custom-call | flops 1073741824 | bytes 134217728 | tf_op jit(solution)/shard_map/attended/pallas_call | solution.py:213
  247.8 51.3 %first_units.1 = (bf16[8,256,2048]{2,1,0:T(8,128)(2,1)}, bf16[8,256,512]{2,1,0:T(8,128)(2,1)}, bf16[8,256,512]{2,1,0:T(8,128)(2,1)}, f32[1,512]{1,0:T(1,128)}, bf16[4,2,128,2048]{3,2,1,0:T(8,128)(2,1)}) custom-call(bf16[256,2048]{1,0:T(8,128)(2,1)} %add_convert_fusion.2.x_ref, bf16[8,256,2048]{2,1,0:T(8,128)(2,1)} %gather_branch.1, ...), custom_call_target="tpu_custom_call" | custom-call | flops 1073741824 | bytes 167772160 | tf_op jit(solution)/shard_map/first_units/pallas_call | solution.py:503
  299.1 12.8 %all-gather.14.cloned.1.call-done = bf16[1024,2048]{1,0:T(8,128)(2,1)} async-done(((bf16[256,2048]{1,0:T(8,128)(2,1)}), bf16[1024,2048]{1,0:T(8,128)(2,1)}) %all-gather.14.cloned.1.call-update) | async-done | bytes 4194320 | tf_op jit(solution)/shard_map/all_gather | solution.py:1061
  312.0 54.9 %last_units.1 = (bf16[8,256,512]{2,1,0:T(8,128)(2,1)}, f32[1,512]{1,0:T(1,128)}, f32[256,2048]{1,0:T(8,128)}, bf16[4,2,128,2048]{3,2,1,0:T(8,128)(2,1)}) custom-call(bf16[8,256,2048]{2,1,0:T(8,128)(2,1)} %get-tuple-element.86.all_ref, bf16[8,256,2048]{2,1,0:T(8,128)(2,1)} %gather_branch.1, bf16[8,256,512]{2,1,0:T(8,128)(2,1)} %get-tuple-element.87.pg1_ref, ...), custom_call_target="tpu_custom_call" | custom-call | flops 1073741824 | bytes 167772160 | tf_op jit(solution)/shard_map/last_units/pallas_call | solution.py:534
  374.4 42.1 %attended_grad.1 = (bf16[8,256,2048]{2,1,0:T(8,128)(2,1)}, bf16[8,256,256]{2,1,0:T(8,128)(2,1)}) custom-call(bf16[256,2048]{1,0:T(8,128)(2,1)} %get-tuple-element.200.x_ref, bf16[256,2048]{1,0:T(8,128)(2,1)} %all-gather.6.cloned.1.call-done.refs_1_.refs_0_, f32[1,256]{1,0:T(1,128)} %broadcast_in_dim.100.refs_1_), custom_call_target="tpu_custom_call" | custom-call | flops 1073741824 | bytes 134217728 | tf_op jit(solution)/shard_map/attended_grad/pallas_call | solution.py:108
  416.6 30.4 %attend_back.1 = (bf16[2048,256]{1,0:T(8,128)(2,1)}, bf16[2048,512]{1,0:T(8,128)(2,1)}, f32[2048,512]{1,0:T(8,128)}) custom-call(s32[8]{0:T(128)} %slice_reduce_fusion.first_ref, s32[2048,1]{1,0:T(8,128)} %bitcast.155, bf16[2048,256]{1,0:T(8,128)(2,1)} %fusion.2.q_ref, bf16[2048,512]{1,0:T(8,128)(2,1)} %copy-done.10, bf16[2048,512]{1,0:T(8,128)(2,1)} %copy-done.10, ...), custom_call_target="tpu_custom_call" | custom-call | tf_op jit(solution)/shard_map/attend_back/pallas_call | solution.py:872
  448.3 6.7 %fusion.30 = bf16[256,2048]{1,0:T(8,128)(2,1)} fusion(bf16[2048,256]{1,0:T(8,128)(2,1)S(1)} %copy-done.12, bf16[2048,2048]{1,0:T(8,128)(2,1)} %bitcast.150), kind=kOutput, calls=%fused_computation.90 | convolution fusion | flops 2147483648 | bytes 10485760 | tf_op jit(solution)/shard_map/dot_general | solution.py:230
  455.0 6.1 convolution_convert_fusion.query_w_ref
  461.1 47.9 %down.1 = f32[256,2048]{1,0:T(8,128)} custom-call(bf16[8,256,512]{2,1,0:T(8,128)(2,1)} %get-tuple-element.99.refs_0_, bf16[8,256,512]{2,1,0:T(8,128)(2,1)} %get-tuple-element.100.refs_1_, bf16[4,2,128,2048]{3,2,1,0:T(8,128)(2,1)} %bitcast.145, bf16[4,2,128,2048]{3,2,1,0:T(8,128)(2,1)} %bitcast.152), custom_call_target="tpu_custom_call" | custom-call | flops 1073741824 | bytes 134217728 | tf_op jit(solution)/shard_map/down/pallas_call | solution.py:213
  509.1 19.1 %collective-permute-done.1.after_ref = bf16[2048,512]{1,0:T(8,128)(2,1)S(1)} collective-permute-done((bf16[2048,512]{1,0:T(8,128)(2,1)}, bf16[2048,512]{1,0:T(8,128)(2,1)S(1)}, u32[]{:S(2)}, u32[]{:S(2)}) %collective-permute-start.1) | collective-permute-done | bytes 2097184 | tf_op jit(solution)/shard_map/ppermute | solution.py:1136
  528.2 10.2 %pair_grads.1 = (bf16[2048,512]{1,0:T(8,128)(2,1)S(1)}, bf16[4,4,2,64,768]{4,3,2,1,0:T(8,128)(2,1)}, f32[1,256]{1,0:T(1,128)S(1)}) custom-call(f32[2048,512]{1,0:T(8,128)} %get-tuple-element.104.pair_ref, bf16[2048,512]{1,0:T(8,128)(2,1)S(1)} %collective-permute-done.1.after_ref, bf16[2048,2048]{1,0:T(8,128)(2,1)} %bitcast.149, ...), custom_call_target="tpu_custom_call" | custom-call | tf_op jit(solution)/shard_map/pair_grads/pallas_call | solution.py:821
  546.8 46.7 %qkv_grad.1 = f32[256,2048]{1,0:T(8,128)} custom-call(bf16[8,256,256]{2,1,0:T(8,128)(2,1)} %bitcast.163, bf16[8,256,512]{2,1,0:T(8,128)(2,1)} %bitcast.141, bf16[2048,256]{1,0:T(8,128)(2,1)} %bitcast.162, bf16[2048,512]{1,0:T(8,128)(2,1)} %bitcast.156), custom_call_target="tpu_custom_call" | custom-call | flops 1073741824 | bytes 134217728 | tf_op jit(solution)/shard_map/qkv_grad/pallas_call | solution.py:213
  596.5 4.1 reduce-scatter.9.cloned.1.call-done
  608.0 16.7 %settle.1 = (bf16[64,2048]{1,0:T(8,128)(2,1)S(1)}, bf16[64,2048]{1,0:T(8,128)(2,1)S(1)}, bf16[64,2048]{1,0:T(8,128)(2,1)S(1)}, f32[1,768]{1,0:T(1,128)S(1)}) custom-call(bf16[8,64,768]{2,1,0:T(8,128)(2,1)S(1)} %bitcast.142, f32[32,1,768]{2,1,0:T(1,128)S(1)} %broadcast_in_dim.109.rows_ref), custom_call_target="tpu_custom_call" | custom-call | flops 1048576 | bytes 33554432 | tf_op jit(solution)/shard_map/settle/pallas_call | solution.py:649
  628.3 3.4 reduce-scatter.11.cloned.1.call-done
  (177 shorter events, 64.3 us)
Async XLA Ops:
  7.2 36.1 %all-gather.6.cloned.1.call-start = ((), (), s32[]{:S(2)}) async-start(), calls=%async_computation.4 | async-start | bytes 1310720 | tf_op jit(solution)/shard_map/all_gather | solution.py:1002
  7.9 81.8 %all-gather.8.cloned.1.call-start = ((), (), s32[]{:S(2)}) async-start(), calls=%async_computation.5 | async-start | bytes 2621440 | tf_op jit(solution)/shard_map/all_gather | solution.py:1031
  17.6 22.3 %copy-start.8 = (bf16[1,256,2048]{2,1,0:T(8,128)(2,1)S(1)}, bf16[1,256,2048]{2,1,0:T(8,128)(2,1)}, u32[]{:S(2)}) copy-start(bf16[1,256,2048]{2,1,0:T(8,128)(2,1)} %param.20) | copy-start | bytes 3145732
  38.1 113.9 %all-gather.10.cloned.1.call-start = ((), (), s32[]{:S(2)}) async-start(), calls=%async_computation.6 | async-start | bytes 1310720 | tf_op jit(solution)/shard_map/all_gather | solution.py:1031
  43.3 204.5 %all-gather.12.cloned.1.call-start = ((), (), s32[]{:S(2)}) async-start(), calls=%async_computation.7 | async-start | bytes 5242880 | tf_op jit(solution)/shard_map/all_gather | solution.py:1061
  89.7 4.5 copy-start.23
  89.7 5.9 copy-start.17
  92.9 219.0 %all-gather.14.cloned.1.call-start = ((), (), s32[]{:S(2)}) async-start(), calls=%async_computation.8 | async-start | bytes 5242880 | tf_op jit(solution)/shard_map/all_gather | solution.py:1061
  105.7 46.3 %copy-start.10 = (bf16[2048,512]{1,0:T(8,128)(2,1)}, bf16[2048,512]{1,0:T(8,128)(2,1)S(1)}, u32[]{:S(2)}) copy-start(bf16[2048,512]{1,0:T(8,128)(2,1)S(1)} %add_convert_fusion.k_ref.v_ref) | copy-start | bytes 6291460
  105.8 80.5 %collective-permute-start = (bf16[2048,512]{1,0:T(8,128)(2,1)S(1)}, bf16[2048,512]{1,0:T(8,128)(2,1)}, u32[]{:S(2)}, u32[]{:S(2)}) collective-permute-start(bf16[2048,512]{1,0:T(8,128)(2,1)S(1)} %add_convert_fusion.k_ref.v_ref), channel_id=1, source_target_pairs={{0,2},{2,4},{4,6},{1,3},{3,5},{5,7},{8,10},{10,12},{12,14},{9,11},... | collective-permute-start | bytes 6291464 | tf_op jit(solution)/shard_map/ppermute | solution.py:1073
  153.4 7.1 %copy-start.19 = (bf16[4,4,2,64,256]{4,3,2,1,0:T(8,128)(2,1)}, bf16[4,4,2,64,256]{4,3,2,1,0:T(8,128)(2,1)S(1)}, u32[]{:S(2)}) copy-start(bf16[4,4,2,64,256]{4,3,2,1,0:T(8,128)(2,1)S(1)} %copy.66) | copy-start | bytes 3145732
  198.4 218.2 %reduce-scatter.5.cloned.1.call-start = ((), (), s32[]{:S(2)}) async-start(), calls=%async_computation.9 | async-start | bytes 5242880 | tf_op jit(solution)/shard_map/reduce_scatter | solution.py:1096
  299.1 229.1 %reduce-scatter.7.cloned.1.call-start = ((), (), s32[]{:S(2)}) async-start(), calls=%async_computation.10 | async-start | bytes 5242880 | tf_op jit(solution)/shard_map/reduce_scatter | solution.py:1096
  366.9 233.7 %reduce-scatter.9.cloned.1.call-start = ((), (), s32[]{:S(2)}) async-start(), calls=%async_computation.11 | async-start | bytes 3932160 | tf_op jit(solution)/shard_map/reduce_scatter | solution.py:1152
  368.5 2.7 copy-start.14
  368.5 2.7 copy-start.18
  416.6 31.7 %copy-start.12 = (bf16[2048,256]{1,0:T(8,128)(2,1)S(1)}, bf16[2048,256]{1,0:T(8,128)(2,1)}, u32[]{:S(2)}) copy-start(bf16[2048,256]{1,0:T(8,128)(2,1)} %attend.1) | copy-start | bytes 3145732
  446.9 81.3 %collective-permute-start.1 = (bf16[2048,512]{1,0:T(8,128)(2,1)}, bf16[2048,512]{1,0:T(8,128)(2,1)S(1)}, u32[]{:S(2)}, u32[]{:S(2)}) collective-permute-start(bf16[2048,512]{1,0:T(8,128)(2,1)} %get-tuple-element.101), channel_id=1, source_target_pairs={{2,0},{4,2},{6,4},{3,1},{5,3},{7,5},{10,8},{12,10},{14,12},{11,9},... | collective-permute-start | bytes 6291464 | tf_op jit(solution)/shard_map/ppermute | solution.py:1136
  539.8 2.4 copy-start.22
  539.8 91.9 %reduce-scatter.11.cloned.1.call-start = ((), (), s32[]{:S(2)}) async-start(), calls=%async_computation.12 | async-start | bytes 1310720 | tf_op jit(solution)/shard_map/reduce_scatter | solution.py:1183
  546.8 46.7 %copy-start.9 = (bf16[1,256,2048]{2,1,0:T(8,128)(2,1)S(1)}, bf16[1,256,2048]{2,1,0:T(8,128)(2,1)}, u32[]{:S(2)}) copy-start(bf16[1,256,2048]{2,1,0:T(8,128)(2,1)} %param.20) | copy-start | bytes 3145732
  600.6 3.0 copy-start.7
  600.6 3.0 copy-start.13
  603.6 2.6 copy-start.16
  (13 other events, 17.1 us)
Sparse Core Ops, SparseCore 0:
  9.6 33.6 all-gather.5
  44.8 44.7 all-gather.7
  91.3 30.2 all-gather.9
  123.0 104.6 all-gather.11
  229.1 82.8 all-gather.13
  314.1 90.8 reduce-scatter.4
  407.3 87.2 reduce-scatter.6
  539.9 60.6 reduce-scatter.8
  602.9 28.7 reduce-scatter.10

commit v14 on v13

--- a/solution.py
+++ b/solution.py
@@ -1031,9 +1031,9 @@
         full = lax.all_gather(mine, "z", axis=0, tiled=True)
         return full.reshape(Z, B, X, rows_dev, -1).transpose(1, 0, 2, 3, 4).reshape(D, -1)
 
-    weight_kv = feature_rows(pair_mine)
+    weight_all = feature_rows(jnp.concatenate([query_mine, pair_mine], axis=1))
     bias_kv = jnp.concatenate([jnp.zeros((cols,), single), mine(bias_v)])
-    bias_one, query_mine, weight_o = lax.optimization_barrier((bias_one, query_mine, weight_o))
+    bias_one, weight_o = lax.optimization_barrier((bias_one, weight_o))
     normed_low = layer_norm(local, gain_one, bias_one).astype(bfloat)
 
     def gather_plane(rows, cid, name):
@@ -1060,8 +1060,8 @@
     def gather_units(mine):
         return lax.all_gather(mine, "z", axis=0, tiled=True).reshape(Z, 2, units, D)
 
-    normed_all, weight_kv, unit_one = lax.optimization_barrier((normed_all, weight_kv, halves[0]))
-    weight_q = feature_rows(query_mine)
+    normed_all, weight_all, unit_one = lax.optimization_barrier((normed_all, weight_all, halves[0]))
+    weight_q, weight_kv = weight_all[:, :cols], weight_all[:, cols:]
     unit_one = gather_units(unit_one)
     key_value = (dot(normed_all, weight_kv) + bias_kv).astype(bfloat)
     up = [(i, i + 1) for i in range(Z - 1)]

time: 646 us -> 667 us (1.033)
  waiting for transfers between devices: 69.8 us -> 85.6 us
    all_gather x2 -> x1, waiting for transfers between devices: 1.18 us -> 22.3 us  [feature_rows(): full = lax.all_gather(mine, 'z', axis=0, tiled=True)]
    ppermute x1, waiting for transfers between devices: 25.8 us -> 38.7 us  [on_device(): before = lax.ppermute(key_value, 'z', up)]
    all_gather x2, waiting for transfers between devices: 12.8 us -> 0.02 us  [gather_units(): return lax.all_gather(mine, 'z', axis=0, tiled=True).reshape(Z, 2, units, D)]
    unnamed x59 -> x57, local copies, waits for them, and re-layouts: 14.3 us -> 14.4 us
  transfers between devices with their start and end apart: 11 -> 10, of which waited for: 7 -> 5; matrix products, arithmetic and copies ran while one was open for 13% -> 12% of each run, Pallas kernels for 70% -> 68%
where the time goes in v14:
time: 667 us; the launch traced here: 660 us
  Pallas kernels  456 us (68%)
  waiting for transfers between devices  85.6 us (13%)
  local copies, waits for them, and re-layouts  35.7 us (5%)
  other arithmetic  32.2 us (5%)
  matrix products  29.1 us (4%)
  between operations  16.5 us (2%)
    pallas_call x3, Pallas kernels, dot_reduce(): pl.pallas_call(functools.partial(reduce_kernel, turned, len(left)), out_s...  138 us
    pallas_call x3, Pallas kernels, plane_gather(): pl.pallas_call(functools.partial(gather_kernel, body_of, len(ins), len(ou...  124 us
    pallas_call x1, Pallas kernels, last_units(): pl.pallas_call(last_units_kernel, out_shape=[jax.ShapeDtypeStruct((ranks,...  53.9 us
    pallas_call x1, Pallas kernels, first_units(): pl.pallas_call(first_units_kernel, out_shape=[jax.ShapeDtypeStruct((ranks...  51.2 us
    ppermute x1, waiting for transfers between devices, on_device(): before = lax.ppermute(key_value, 'z', up)  38.7 us
    pallas_call x2, Pallas kernels, exchange_call(): pl.pallas_call(kernel, out_shape=out_shape, in_specs=[inside] * len(args)...  36.6 us
    pallas_call x1, Pallas kernels, attend_back(): pl.pallas_call(attend_back_kernel, out_shape=[jax.ShapeDtypeStruct((rows,...  30.4 us
    all_gather x1, waiting for transfers between devices, feature_rows(): full = lax.all_gather(mine, 'z', axis=0, tiled=True)  22.3 us
  transfers between devices with their start and end apart: 10, of which 5 were waited for; matrix products, arithmetic and copies ran while one was open for 12% of the time, Pallas kernels for 68%

profile of v14, /device:TPU:0, one launch (start us, length us, event | category | flops | bytes accessed | tf_op | source)
XLA Modules:
  0.0 660.5 jit_solution(10609422256538353340)
XLA Ops:
  8.6 6.1 concatenate.27
  17.6 19.7 %spread.1 = (bf16[8,64,256]{2,1,0:T(8,128)(2,1)S(1)}, bf16[8,64,512]{2,1,0:T(8,128)(2,1)S(1)}, f32[32,1,896]{2,1,0:T(1,128)S(1)}) custom-call(bf16[64,2048]{1,0:T(8,128)(2,1)S(1)} %copy-done.2, bf16[64,2048]{1,0:T(8,128)(2,1)S(1)} %copy-done.3, bf16[64,2048]{1,0:T(8,128)(2,1)S(1)} %copy-done.4, f32[1,1,896]{2,1,0:T(1,128)S(1)} %broadcast_in_dim.96.pack_ref), custom_call_target="tpu_custom_call" | custom-call | flops 1048576 | bytes 33554432 | tf_op jit(solution)/shard_map/spread/pallas_call | solution.py:649
  44.7 40.8 %gather_normed.1 = bf16[8,256,2048]{2,1,0:T(8,128)(2,1)} custom-call(bf16[256,2048]{1,0:T(8,128)(2,1)} %fusion.10.x_ref), custom_call_target="tpu_custom_call" | custom-call | flops 1073741824 | bytes 134217728 | tf_op jit(solution)/shard_map/gather_normed/pallas_call | solution.py:108
  85.5 22.3 %all-gather.7.cloned.1.call-done = bf16[2048,768]{1,0:T(8,128)(2,1)} async-done(((bf16[512,768]{1,0:T(8,128)(2,1)}), bf16[2048,768]{1,0:T(8,128)(2,1)}) %all-gather.7.cloned.1.call-update) | async-done | bytes 3145744 | tf_op jit(solution)/shard_map/all_gather | solution.py:1031
  107.8 4.0 copy.61
  115.4 9.2 %add_convert_fusion.k_ref.v_ref = bf16[2048,512]{1,0:T(8,128)(2,1)S(1)} fusion(bf16[2048,2048]{1,0:T(8,128)(2,1)} %bitcast.142, f32[512]{0:T(512)S(1)} %concatenate.30, bf16[2048,768]{1,0:T(8,128)(2,1)} %bitcast.150), kind=kOutput, calls=%fused_computation | convolution fusion | flops 4297064448 | bytes 12584960 | tf_op jit(solution)/shard_map/dot_general | solution.py:226
  124.6 2.9 collective-permute-start
  130.3 40.6 %gather_branch.1 = bf16[8,256,2048]{2,1,0:T(8,128)(2,1)} custom-call(bf16[256,2048]{1,0:T(8,128)(2,1)} %get-tuple-element.75.x_ref), custom_call_target="tpu_custom_call" | custom-call | flops 1073741824 | bytes 134217728 | tf_op jit(solution)/shard_map/gather_branch/pallas_call | solution.py:108
  170.9 6.9 %fusion.2.q_ref = bf16[2048,256]{1,0:T(8,128)(2,1)} fusion(bf16[2048,2048]{1,0:T(8,128)(2,1)} %bitcast.143, f32[256]{0:T(256)S(1)} %bitcast.181, bf16[2048,768]{1,0:T(8,128)(2,1)} %bitcast.151), kind=kOutput, calls=%fused_computation.6 | convolution fusion | flops 2148532224 | bytes 10486784 | tf_op jit(solution)/shard_map/dot_general | solution.py:226
  177.8 38.7 %collective-permute-done.kb_ref.vb_ref = bf16[2048,512]{1,0:T(8,128)(2,1)} collective-permute-done((bf16[2048,512]{1,0:T(8,128)(2,1)S(1)}, bf16[2048,512]{1,0:T(8,128)(2,1)}, u32[]{:S(2)}, u32[]{:S(2)}) %collective-permute-start) | collective-permute-done | bytes 2097184 | tf_op jit(solution)/shard_map/ppermute | solution.py:1073
  216.5 12.1 %attend.1 = bf16[2048,256]{1,0:T(8,128)(2,1)} custom-call(s32[8]{0:T(128)} %slice_reduce_fusion.first_ref, s32[2048,1]{1,0:T(8,128)} %bitcast.154, bf16[2048,256]{1,0:T(8,128)(2,1)} %fusion.2.q_ref, bf16[2048,512]{1,0:T(8,128)(2,1)} %copy-done.10, bf16[2048,512]{1,0:T(8,128)(2,1)} %copy-done.10, bf16[2048,512]{1,0:T(8,128)(2,1)} %collective-permute-done.kb_ref.vb_ref, ...), custom_call_target="tpu_custom_call" | custom-call | tf_op jit(solution)/shard_map/attend/pallas_call | solution.py:856
  230.0 43.0 %attended.1 = f32[256,2048]{1,0:T(8,128)} custom-call(bf16[8,256,256]{2,1,0:T(8,128)(2,1)} %bitcast.149, bf16[256,2048]{1,0:T(8,128)(2,1)} %all-gather.5.cloned.1.call-done.refs_1_.refs_0_), custom_call_target="tpu_custom_call" | custom-call | flops 1073741824 | bytes 134217728 | tf_op jit(solution)/shard_map/attended/pallas_call | solution.py:213
  277.9 51.2 %first_units.1 = (bf16[8,256,2048]{2,1,0:T(8,128)(2,1)}, bf16[8,256,512]{2,1,0:T(8,128)(2,1)}, bf16[8,256,512]{2,1,0:T(8,128)(2,1)}, f32[1,512]{1,0:T(1,128)}, bf16[4,2,128,2048]{3,2,1,0:T(8,128)(2,1)}) custom-call(bf16[256,2048]{1,0:T(8,128)(2,1)} %add_convert_fusion.2.x_ref, bf16[8,256,2048]{2,1,0:T(8,128)(2,1)} %gather_branch.1, ...), custom_call_target="tpu_custom_call" | custom-call | flops 1073741824 | bytes 167772160 | tf_op jit(solution)/shard_map/first_units/pallas_call | solution.py:503
  329.2 53.9 %last_units.1 = (bf16[8,256,512]{2,1,0:T(8,128)(2,1)}, f32[1,512]{1,0:T(1,128)}, f32[256,2048]{1,0:T(8,128)}, bf16[4,2,128,2048]{3,2,1,0:T(8,128)(2,1)}) custom-call(bf16[8,256,2048]{2,1,0:T(8,128)(2,1)} %get-tuple-element.84.all_ref, bf16[8,256,2048]{2,1,0:T(8,128)(2,1)} %gather_branch.1, bf16[8,256,512]{2,1,0:T(8,128)(2,1)} %get-tuple-element.85.pg1_ref, ...), custom_call_target="tpu_custom_call" | custom-call | flops 1073741824 | bytes 167772160 | tf_op jit(solution)/shard_map/last_units/pallas_call | solution.py:534
  390.6 42.6 %attended_grad.1 = (bf16[8,256,2048]{2,1,0:T(8,128)(2,1)}, bf16[8,256,256]{2,1,0:T(8,128)(2,1)}) custom-call(bf16[256,2048]{1,0:T(8,128)(2,1)} %get-tuple-element.198.x_ref, bf16[256,2048]{1,0:T(8,128)(2,1)} %all-gather.5.cloned.1.call-done.refs_1_.refs_0_, f32[1,256]{1,0:T(1,128)} %broadcast_in_dim.100.refs_1_), custom_call_target="tpu_custom_call" | custom-call | flops 1073741824 | bytes 134217728 | tf_op jit(solution)/shard_map/attended_grad/pallas_call | solution.py:108
  433.3 30.4 %attend_back.1 = (bf16[2048,256]{1,0:T(8,128)(2,1)}, bf16[2048,512]{1,0:T(8,128)(2,1)}, f32[2048,512]{1,0:T(8,128)}) custom-call(s32[8]{0:T(128)} %slice_reduce_fusion.first_ref, s32[2048,1]{1,0:T(8,128)} %bitcast.155, bf16[2048,256]{1,0:T(8,128)(2,1)} %fusion.2.q_ref, bf16[2048,512]{1,0:T(8,128)(2,1)} %copy-done.10, bf16[2048,512]{1,0:T(8,128)(2,1)} %copy-done.10, ...), custom_call_target="tpu_custom_call" | custom-call | tf_op jit(solution)/shard_map/attend_back/pallas_call | solution.py:872
  465.0 6.8 %fusion.32 = bf16[256,2048]{1,0:T(8,128)(2,1)} fusion(bf16[2048,256]{1,0:T(8,128)(2,1)S(1)} %copy-done.12, bf16[2048,2048]{1,0:T(8,128)(2,1)} %bitcast.146), kind=kOutput, calls=%fused_computation.93 | convolution fusion | flops 2147483648 | bytes 10485760 | tf_op jit(solution)/shard_map/dot_general | solution.py:230
  471.8 6.2 convolution_convert_fusion.query_w_ref
  478.0 48.2 %down.1 = f32[256,2048]{1,0:T(8,128)} custom-call(bf16[8,256,512]{2,1,0:T(8,128)(2,1)} %get-tuple-element.97.refs_0_, bf16[8,256,512]{2,1,0:T(8,128)(2,1)} %get-tuple-element.98.refs_1_, bf16[4,2,128,2048]{3,2,1,0:T(8,128)(2,1)} %bitcast.141, bf16[4,2,128,2048]{3,2,1,0:T(8,128)(2,1)} %bitcast.148), custom_call_target="tpu_custom_call" | custom-call | flops 1073741824 | bytes 134217728 | tf_op jit(solution)/shard_map/down/pallas_call | solution.py:213
  526.2 21.8 %collective-permute-done.1.after_ref = bf16[2048,512]{1,0:T(8,128)(2,1)S(1)} collective-permute-done((bf16[2048,512]{1,0:T(8,128)(2,1)}, bf16[2048,512]{1,0:T(8,128)(2,1)S(1)}, u32[]{:S(2)}, u32[]{:S(2)}) %collective-permute-start.1) | collective-permute-done | bytes 2097184 | tf_op jit(solution)/shard_map/ppermute | solution.py:1136
  548.0 10.2 %pair_grads.1 = (bf16[2048,512]{1,0:T(8,128)(2,1)S(1)}, bf16[4,4,2,64,768]{4,3,2,1,0:T(8,128)(2,1)}, f32[1,256]{1,0:T(1,128)S(1)}) custom-call(f32[2048,512]{1,0:T(8,128)} %get-tuple-element.102.pair_ref, bf16[2048,512]{1,0:T(8,128)(2,1)S(1)} %collective-permute-done.1.after_ref, bf16[2048,2048]{1,0:T(8,128)(2,1)} %bitcast.145, ...), custom_call_target="tpu_custom_call" | custom-call | tf_op jit(solution)/shard_map/pair_grads/pallas_call | solution.py:821
  572.7 46.7 %qkv_grad.1 = f32[256,2048]{1,0:T(8,128)} custom-call(bf16[8,256,256]{2,1,0:T(8,128)(2,1)} %bitcast.159, bf16[8,256,512]{2,1,0:T(8,128)(2,1)} %bitcast.135, bf16[2048,256]{1,0:T(8,128)(2,1)} %slice.108.refs_2_, bf16[2048,512]{1,0:T(8,128)(2,1)} %slice.106.refs_3_), custom_call_target="tpu_custom_call" | custom-call | flops 1073741824 | bytes 134217728 | tf_op jit(solution)/shard_map/qkv_grad/pallas_call | solution.py:213
  622.6 2.9 maximum_convert_fusion
  629.9 16.9 %settle.1 = (bf16[64,2048]{1,0:T(8,128)(2,1)S(1)}, bf16[64,2048]{1,0:T(8,128)(2,1)S(1)}, bf16[64,2048]{1,0:T(8,128)(2,1)S(1)}, f32[1,768]{1,0:T(1,128)S(1)}) custom-call(bf16[8,64,768]{2,1,0:T(8,128)(2,1)S(1)} %bitcast.136, f32[32,1,768]{2,1,0:T(1,128)S(1)} %broadcast_in_dim.109.rows_ref), custom_call_target="tpu_custom_call" | custom-call | flops 1048576 | bytes 33554432 | tf_op jit(solution)/shard_map/settle/pallas_call | solution.py:649
  (173 shorter events, 59.9 us)
Async XLA Ops:
  7.2 36.1 %all-gather.5.cloned.1.call-start = ((), (), s32[]{:S(2)}) async-start(), calls=%async_computation.4 | async-start | bytes 1310720 | tf_op jit(solution)/shard_map/all_gather | solution.py:1002
  7.9 99.9 %all-gather.7.cloned.1.call-start = ((), (), s32[]{:S(2)}) async-start(), calls=%async_computation.5 | async-start | bytes 3932160 | tf_op jit(solution)/shard_map/all_gather | solution.py:1031
  17.6 20.9 %copy-start.19 = (bf16[2048,256]{1,0:T(8,128)(2,1)S(1)}, bf16[2048,256]{1,0:T(8,128)(2,1)}, u32[]{:S(2)}) copy-start(bf16[2048,256]{1,0:T(8,128)(2,1)} %param.36) | copy-start | bytes 3145732
  38.2 239.7 %all-gather.9.cloned.1.call-start = ((), (), s32[]{:S(2)}) async-start(), calls=%async_computation.6 | async-start | bytes 5242880 | tf_op jit(solution)/shard_map/all_gather | solution.py:1061
  107.8 4.9 copy-start.22
  107.8 6.2 copy-start.17
  111.8 217.4 %all-gather.11.cloned.1.call-start = ((), (), s32[]{:S(2)}) async-start(), calls=%async_computation.7 | async-start | bytes 5242880 | tf_op jit(solution)/shard_map/all_gather | solution.py:1061
  124.6 46.3 %copy-start.10 = (bf16[2048,512]{1,0:T(8,128)(2,1)}, bf16[2048,512]{1,0:T(8,128)(2,1)S(1)}, u32[]{:S(2)}) copy-start(bf16[2048,512]{1,0:T(8,128)(2,1)S(1)} %add_convert_fusion.k_ref.v_ref) | copy-start | bytes 6291460
  124.6 91.9 %collective-permute-start = (bf16[2048,512]{1,0:T(8,128)(2,1)S(1)}, bf16[2048,512]{1,0:T(8,128)(2,1)}, u32[]{:S(2)}, u32[]{:S(2)}) collective-permute-start(bf16[2048,512]{1,0:T(8,128)(2,1)S(1)} %add_convert_fusion.k_ref.v_ref), channel_id=1, source_target_pairs={{0,2},{2,4},{4,6},{1,3},{3,5},{5,7},{8,10},{10,12},{12,14},{9,11},... | collective-permute-start | bytes 6291464 | tf_op jit(solution)/shard_map/ppermute | solution.py:1073
  228.6 204.7 %reduce-scatter.5.cloned.1.call-start = ((), (), s32[]{:S(2)}) async-start(), calls=%async_computation.8 | async-start | bytes 5242880 | tf_op jit(solution)/shard_map/reduce_scatter | solution.py:1096
  329.1 218.9 %reduce-scatter.7.cloned.1.call-start = ((), (), s32[]{:S(2)}) async-start(), calls=%async_computation.9 | async-start | bytes 5242880 | tf_op jit(solution)/shard_map/reduce_scatter | solution.py:1096
  383.2 239.4 %reduce-scatter.9.cloned.1.call-start = ((), (), s32[]{:S(2)}) async-start(), calls=%async_computation.10 | async-start | bytes 3932160 | tf_op jit(solution)/shard_map/reduce_scatter | solution.py:1152
  384.7 2.7 copy-start.15
  384.7 2.7 copy-start.18
  433.3 31.7 %copy-start.12 = (bf16[2048,256]{1,0:T(8,128)(2,1)S(1)}, bf16[2048,256]{1,0:T(8,128)(2,1)}, u32[]{:S(2)}) copy-start(bf16[2048,256]{1,0:T(8,128)(2,1)} %attend.1) | copy-start | bytes 3145732
  463.7 84.3 %collective-permute-start.1 = (bf16[2048,512]{1,0:T(8,128)(2,1)}, bf16[2048,512]{1,0:T(8,128)(2,1)S(1)}, u32[]{:S(2)}, u32[]{:S(2)}) collective-permute-start(bf16[2048,512]{1,0:T(8,128)(2,1)} %get-tuple-element.99), channel_id=1, source_target_pairs={{2,0},{4,2},{6,4},{3,1},{5,3},{7,5},{10,8},{12,10},{14,12},{11,9},... | collective-permute-start | bytes 6291464 | tf_op jit(solution)/shard_map/ppermute | solution.py:1136
  559.5 1.9 copy-start.13
  559.5 91.9 %reduce-scatter.11.cloned.1.call-start = ((), (), s32[]{:S(2)}) async-start(), calls=%async_computation.11 | async-start | bytes 1310720 | tf_op jit(solution)/shard_map/reduce_scatter | solution.py:1183
  564.0 4.2 copy-start.21
  572.7 46.8 %copy-start.9 = (bf16[1,256,2048]{2,1,0:T(8,128)(2,1)S(1)}, bf16[1,256,2048]{2,1,0:T(8,128)(2,1)}, u32[]{:S(2)}) copy-start(bf16[1,256,2048]{2,1,0:T(8,128)(2,1)} %param.20) | copy-start | bytes 3145732
  622.5 3.0 copy-start.7
  622.6 3.0 copy-start.14
  625.5 2.0 copy-start.11
  625.5 2.6 copy-start.16
  (11 other events, 13.9 us)
Sparse Core Ops, SparseCore 0:
  9.6 33.6 all-gather.4
  45.4 62.3 all-gather.6
  111.9 120.0 all-gather.8
  233.5 95.0 all-gather.10
  330.7 94.1 reduce-scatter.4
  427.1 89.0 reduce-scatter.6
  559.7 60.6 reduce-scatter.8
  622.7 28.6 reduce-scatter.10

commit v15 on v13

--- a/solution.py
+++ b/solution.py
@@ -788,8 +788,8 @@
     each_window(first_ref, span, body)
     edge_ref[:, :cols] = dk[:span, :].astype(bfloat)
     edge_ref[:, cols:] = dv[:span, :].astype(bfloat)
-    pair_ref[:, :cols] = dk[span:, :]
-    pair_ref[:, cols:] = dv[span:, :]
+    pair_ref[:, :cols] = dk[span:, :].astype(bfloat)
+    pair_ref[:, cols:] = dv[span:, :].astype(bfloat)
 
 
 def pair_grads_kernel(pair_ref, after_ref, normed_ref, query_w_ref, grad_ref, weight_ref, bias_ref):
@@ -799,7 +799,7 @@
 
     @pl.when(block == 0)
     def _():
-        grad = (pair_ref[...] + after_ref[...].astype(single)).astype(bfloat)
+        grad = (pair_ref[...].astype(single) + after_ref[...].astype(single)).astype(bfloat)
         grad_ref[...] = grad
         bias_ref[...] = jnp.sum(grad[:, cols:].astype(single), axis=0, keepdims=True)
 
@@ -874,7 +874,7 @@
         out_shape=[
             jax.ShapeDtypeStruct((rows, cols), bfloat),
             jax.ShapeDtypeStruct((rows, 2 * cols), bfloat),
-            jax.ShapeDtypeStruct((rows, 2 * cols), single),
+            jax.ShapeDtypeStruct((rows, 2 * cols), bfloat),
         ],
         grid_spec=pltpu.PrefetchScalarGridSpec(
             num_scalar_prefetch=1,

time: 646 us -> 646 us (level)
    unnamed x59 -> x63, local copies, waits for them, and re-layouts: 14.3 us -> 14.4 us
where the time goes in v15:
time: 646 us; the launch traced here: 640 us
  Pallas kernels  456 us (71%)
  waiting for transfers between devices  69.7 us (11%)
  local copies, waits for them, and re-layouts  33.6 us (5%)
  other arithmetic  30.1 us (5%)
  matrix products  28 us (4%)
  between operations  16.3 us (3%)
    pallas_call x3, Pallas kernels, dot_reduce(): pl.pallas_call(functools.partial(reduce_kernel, turned, len(left)), out_s...  138 us
    pallas_call x3, Pallas kernels, plane_gather(): pl.pallas_call(functools.partial(gather_kernel, body_of, len(ins), len(ou...  123 us
    pallas_call x1, Pallas kernels, last_units(): pl.pallas_call(last_units_kernel, out_shape=[jax.ShapeDtypeStruct((ranks,...  54.9 us
    pallas_call x1, Pallas kernels, first_units(): pl.pallas_call(first_units_kernel, out_shape=[jax.ShapeDtypeStruct((ranks...  51.3 us
    pallas_call x2, Pallas kernels, exchange_call(): pl.pallas_call(kernel, out_shape=out_shape, in_specs=[inside] * len(args)...  37.2 us
    pallas_call x1, Pallas kernels, attend_back(): pl.pallas_call(attend_back_kernel, out_shape=[jax.ShapeDtypeStruct((rows,...  30.1 us
    ppermute x1, waiting for transfers between devices, on_device(): before = lax.ppermute(key_value, 'z', up)  25.7 us
    ppermute x1, waiting for transfers between devices, on_device(): after = lax.ppermute(edge, 'z', down)  19.1 us
  transfers between devices with their start and end apart: 11, of which 7 were waited for; matrix products, arithmetic and copies ran while one was open for 13% of the time, Pallas kernels for 70%

profile of v15, /device:TPU:0, one launch (start us, length us, event | category | flops | bytes accessed | tf_op | source)
XLA Modules:
  0.0 639.7 jit_solution(11864043582188800720)
XLA Ops:
  8.6 6.1 concatenate.24
  17.6 20.5 %spread.1 = (bf16[8,64,256]{2,1,0:T(8,128)(2,1)}, bf16[8,64,512]{2,1,0:T(8,128)(2,1)}, f32[32,1,896]{2,1,0:T(1,128)S(1)}) custom-call(bf16[64,2048]{1,0:T(8,128)(2,1)S(1)} %copy-done.3, bf16[64,2048]{1,0:T(8,128)(2,1)S(1)} %copy-done.4, bf16[64,2048]{1,0:T(8,128)(2,1)S(1)} %copy-done.5, f32[1,1,896]{2,1,0:T(1,128)S(1)} %broadcast_in_dim.96.pack_ref), custom_call_target="tpu_custom_call" | custom-call | flops 1048576 | bytes 33554432 | tf_op jit(solution)/shard_map/spread/pallas_call | solution.py:649
  47.7 40.8 %gather_normed.1 = bf16[8,256,2048]{2,1,0:T(8,128)(2,1)} custom-call(bf16[256,2048]{1,0:T(8,128)(2,1)} %fusion.10.x_ref), custom_call_target="tpu_custom_call" | custom-call | flops 1073741824 | bytes 134217728 | tf_op jit(solution)/shard_map/gather_normed/pallas_call | solution.py:108
  97.6 8.2 %add_convert_fusion.k_ref.v_ref = bf16[2048,512]{1,0:T(8,128)(2,1)S(1)} fusion(bf16[2048,2048]{1,0:T(8,128)(2,1)} %bitcast.146, bf16[2048,512]{1,0:T(8,128)(2,1)S(1)} %bitcast.157, f32[512]{0:T(512)S(1)} %concatenate.26), kind=kOutput, calls=%fused_computation | convolution fusion | flops 4297064448 | bytes 12584960 | tf_op jit(solution)/shard_map/dot_general | solution.py:226
  105.8 3.5 collective-permute-start
  111.7 40.3 %gather_branch.1 = bf16[8,256,2048]{2,1,0:T(8,128)(2,1)} custom-call(bf16[256,2048]{1,0:T(8,128)(2,1)} %get-tuple-element.76.x_ref), custom_call_target="tpu_custom_call" | custom-call | flops 1073741824 | bytes 134217728 | tf_op jit(solution)/shard_map/gather_branch/pallas_call | solution.py:108
  153.4 7.1 %fusion.2.q_ref = bf16[2048,256]{1,0:T(8,128)(2,1)} fusion(bf16[2048,2048]{1,0:T(8,128)(2,1)} %bitcast.147, bf16[2048,256]{1,0:T(8,128)(2,1)S(1)} %bitcast.161, f32[256]{0:T(256)S(1)} %bitcast.186), kind=kOutput, calls=%fused_computation.6 | convolution fusion | flops 2148532224 | bytes 10486784 | tf_op jit(solution)/shard_map/dot_general | solution.py:226
  160.5 25.7 %collective-permute-done.kb_ref.vb_ref = bf16[2048,512]{1,0:T(8,128)(2,1)} collective-permute-done((bf16[2048,512]{1,0:T(8,128)(2,1)S(1)}, bf16[2048,512]{1,0:T(8,128)(2,1)}, u32[]{:S(2)}, u32[]{:S(2)}) %collective-permute-start) | collective-permute-done | bytes 2097184 | tf_op jit(solution)/shard_map/ppermute | solution.py:1073
  186.3 12.1 %attend.1 = bf16[2048,256]{1,0:T(8,128)(2,1)} custom-call(s32[8]{0:T(128)} %slice_reduce_fusion.first_ref, s32[2048,1]{1,0:T(8,128)} %bitcast.154, bf16[2048,256]{1,0:T(8,128)(2,1)} %fusion.2.q_ref, bf16[2048,512]{1,0:T(8,128)(2,1)} %copy-done.11, bf16[2048,512]{1,0:T(8,128)(2,1)} %copy-done.11, bf16[2048,512]{1,0:T(8,128)(2,1)} %collective-permute-done.kb_ref.vb_ref, ...), custom_call_target="tpu_custom_call" | custom-call | tf_op jit(solution)/shard_map/attend/pallas_call | solution.py:856
  199.8 43.1 %attended.1 = f32[256,2048]{1,0:T(8,128)} custom-call(bf16[8,256,256]{2,1,0:T(8,128)(2,1)} %bitcast.153, bf16[256,2048]{1,0:T(8,128)(2,1)} %all-gather.6.cloned.1.call-done.refs_1_.refs_0_), custom_call_target="tpu_custom_call" | custom-call | flops 1073741824 | bytes 134217728 | tf_op jit(solution)/shard_map/attended/pallas_call | solution.py:213
  247.8 51.3 %first_units.1 = (bf16[8,256,2048]{2,1,0:T(8,128)(2,1)}, bf16[8,256,512]{2,1,0:T(8,128)(2,1)}, bf16[8,256,512]{2,1,0:T(8,128)(2,1)}, f32[1,512]{1,0:T(1,128)}, bf16[4,2,128,2048]{3,2,1,0:T(8,128)(2,1)}) custom-call(bf16[256,2048]{1,0:T(8,128)(2,1)} %add_convert_fusion.2.x_ref, bf16[8,256,2048]{2,1,0:T(8,128)(2,1)} %gather_branch.1, ...), custom_call_target="tpu_custom_call" | custom-call | flops 1073741824 | bytes 167772160 | tf_op jit(solution)/shard_map/first_units/pallas_call | solution.py:503
  299.1 12.8 %all-gather.14.cloned.1.call-done = bf16[1024,2048]{1,0:T(8,128)(2,1)} async-done(((bf16[256,2048]{1,0:T(8,128)(2,1)}), bf16[1024,2048]{1,0:T(8,128)(2,1)}) %all-gather.14.cloned.1.call-update) | async-done | bytes 4194320 | tf_op jit(solution)/shard_map/all_gather | solution.py:1061
  312.0 54.9 %last_units.1 = (bf16[8,256,512]{2,1,0:T(8,128)(2,1)}, f32[1,512]{1,0:T(1,128)}, f32[256,2048]{1,0:T(8,128)}, bf16[4,2,128,2048]{3,2,1,0:T(8,128)(2,1)}) custom-call(bf16[8,256,2048]{2,1,0:T(8,128)(2,1)} %get-tuple-element.86.all_ref, bf16[8,256,2048]{2,1,0:T(8,128)(2,1)} %gather_branch.1, bf16[8,256,512]{2,1,0:T(8,128)(2,1)} %get-tuple-element.87.pg1_ref, ...), custom_call_target="tpu_custom_call" | custom-call | flops 1073741824 | bytes 167772160 | tf_op jit(solution)/shard_map/last_units/pallas_call | solution.py:534
  374.4 42.0 %attended_grad.1 = (bf16[8,256,2048]{2,1,0:T(8,128)(2,1)}, bf16[8,256,256]{2,1,0:T(8,128)(2,1)}) custom-call(bf16[256,2048]{1,0:T(8,128)(2,1)} %get-tuple-element.200.x_ref, bf16[256,2048]{1,0:T(8,128)(2,1)} %all-gather.6.cloned.1.call-done.refs_1_.refs_0_, f32[1,256]{1,0:T(1,128)} %broadcast_in_dim.100.refs_1_), custom_call_target="tpu_custom_call" | custom-call | flops 1073741824 | bytes 134217728 | tf_op jit(solution)/shard_map/attended_grad/pallas_call | solution.py:108
  416.4 30.1 %attend_back.1 = (bf16[2048,256]{1,0:T(8,128)(2,1)}, bf16[2048,512]{1,0:T(8,128)(2,1)}, bf16[2048,512]{1,0:T(8,128)(2,1)}) custom-call(s32[8]{0:T(128)} %slice_reduce_fusion.first_ref, s32[2048,1]{1,0:T(8,128)} %bitcast.155, bf16[2048,256]{1,0:T(8,128)(2,1)} %fusion.2.q_ref, bf16[2048,512]{1,0:T(8,128)(2,1)} %copy-done.11, bf16[2048,512]{1,0:T(8,128)(2,1)} %copy-done.11, ...), custom_call_target="tpu_custom_call" | custom-call | tf_op jit(solution)/shard_map/attend_back/pallas_call | solution.py:872
  447.9 6.8 %fusion.30 = bf16[256,2048]{1,0:T(8,128)(2,1)} fusion(bf16[2048,256]{1,0:T(8,128)(2,1)S(1)} %copy-done.13, bf16[2048,2048]{1,0:T(8,128)(2,1)} %bitcast.150), kind=kOutput, calls=%fused_computation.90 | convolution fusion | flops 2147483648 | bytes 10485760 | tf_op jit(solution)/shard_map/dot_general | solution.py:230
  454.7 5.9 convolution_convert_fusion.query_w_ref
  460.6 48.2 %down.1 = f32[256,2048]{1,0:T(8,128)} custom-call(bf16[8,256,512]{2,1,0:T(8,128)(2,1)} %get-tuple-element.99.refs_0_, bf16[8,256,512]{2,1,0:T(8,128)(2,1)} %get-tuple-element.100.refs_1_, bf16[4,2,128,2048]{3,2,1,0:T(8,128)(2,1)} %bitcast.145, bf16[4,2,128,2048]{3,2,1,0:T(8,128)(2,1)} %bitcast.152), custom_call_target="tpu_custom_call" | custom-call | flops 1073741824 | bytes 134217728 | tf_op jit(solution)/shard_map/down/pallas_call | solution.py:213
  508.8 19.1 %collective-permute-done.1.after_ref = bf16[2048,512]{1,0:T(8,128)(2,1)} collective-permute-done((bf16[2048,512]{1,0:T(8,128)(2,1)}, bf16[2048,512]{1,0:T(8,128)(2,1)}, u32[]{:S(2)}, u32[]{:S(2)}) %collective-permute-start.1) | collective-permute-done | bytes 2097184 | tf_op jit(solution)/shard_map/ppermute | solution.py:1136
  527.9 9.7 %pair_grads.1 = (bf16[2048,512]{1,0:T(8,128)(2,1)S(1)}, bf16[4,4,2,64,768]{4,3,2,1,0:T(8,128)(2,1)}, f32[1,256]{1,0:T(1,128)S(1)}) custom-call(bf16[2048,512]{1,0:T(8,128)(2,1)S(1)} %copy-done.1, bf16[2048,512]{1,0:T(8,128)(2,1)} %collective-permute-done.1.after_ref, bf16[2048,2048]{1,0:T(8,128)(2,1)} %bitcast.149, ...), custom_call_target="tpu_custom_call" | custom-call | tf_op jit(solution)/shard_map/pair_grads/pallas_call | solution.py:821
  546.0 46.7 %qkv_grad.1 = f32[256,2048]{1,0:T(8,128)} custom-call(bf16[8,256,256]{2,1,0:T(8,128)(2,1)} %bitcast.163, bf16[8,256,512]{2,1,0:T(8,128)(2,1)} %bitcast.141, bf16[2048,256]{1,0:T(8,128)(2,1)} %bitcast.162, bf16[2048,512]{1,0:T(8,128)(2,1)} %bitcast.156), custom_call_target="tpu_custom_call" | custom-call | flops 1073741824 | bytes 134217728 | tf_op jit(solution)/shard_map/qkv_grad/pallas_call | solution.py:213
  595.7 4.1 reduce-scatter.9.cloned.1.call-done
  607.3 16.6 %settle.1 = (bf16[64,2048]{1,0:T(8,128)(2,1)S(1)}, bf16[64,2048]{1,0:T(8,128)(2,1)S(1)}, bf16[64,2048]{1,0:T(8,128)(2,1)S(1)}, f32[1,768]{1,0:T(1,128)S(1)}) custom-call(bf16[8,64,768]{2,1,0:T(8,128)(2,1)S(1)} %bitcast.142, f32[32,1,768]{2,1,0:T(1,128)S(1)} %broadcast_in_dim.109.rows_ref), custom_call_target="tpu_custom_call" | custom-call | flops 1048576 | bytes 33554432 | tf_op jit(solution)/shard_map/settle/pallas_call | solution.py:649
  627.6 3.4 reduce-scatter.11.cloned.1.call-done
  (181 shorter events, 64.3 us)
Async XLA Ops:
  7.2 36.1 %all-gather.6.cloned.1.call-start = ((), (), s32[]{:S(2)}) async-start(), calls=%async_computation.4 | async-start | bytes 1310720 | tf_op jit(solution)/shard_map/all_gather | solution.py:1002
  7.9 81.8 %all-gather.8.cloned.1.call-start = ((), (), s32[]{:S(2)}) async-start(), calls=%async_computation.5 | async-start | bytes 2621440 | tf_op jit(solution)/shard_map/all_gather | solution.py:1031
  17.6 22.4 %copy-start.9 = (bf16[1,256,2048]{2,1,0:T(8,128)(2,1)S(1)}, bf16[1,256,2048]{2,1,0:T(8,128)(2,1)}, u32[]{:S(2)}) copy-start(bf16[1,256,2048]{2,1,0:T(8,128)(2,1)} %param.20) | copy-start | bytes 3145732
  38.1 113.9 %all-gather.10.cloned.1.call-start = ((), (), s32[]{:S(2)}) async-start(), calls=%async_computation.6 | async-start | bytes 1310720 | tf_op jit(solution)/shard_map/all_gather | solution.py:1031
  43.3 204.5 %all-gather.12.cloned.1.call-start = ((), (), s32[]{:S(2)}) async-start(), calls=%async_computation.7 | async-start | bytes 5242880 | tf_op jit(solution)/shard_map/all_gather | solution.py:1061
  89.7 4.5 copy-start.25
  89.7 5.9 copy-start.18
  92.9 219.0 %all-gather.14.cloned.1.call-start = ((), (), s32[]{:S(2)}) async-start(), calls=%async_computation.8 | async-start | bytes 5242880 | tf_op jit(solution)/shard_map/all_gather | solution.py:1061
  105.7 46.3 %copy-start.11 = (bf16[2048,512]{1,0:T(8,128)(2,1)}, bf16[2048,512]{1,0:T(8,128)(2,1)S(1)}, u32[]{:S(2)}) copy-start(bf16[2048,512]{1,0:T(8,128)(2,1)S(1)} %add_convert_fusion.k_ref.v_ref) | copy-start | bytes 6291460
  105.8 80.5 %collective-permute-start = (bf16[2048,512]{1,0:T(8,128)(2,1)S(1)}, bf16[2048,512]{1,0:T(8,128)(2,1)}, u32[]{:S(2)}, u32[]{:S(2)}) collective-permute-start(bf16[2048,512]{1,0:T(8,128)(2,1)S(1)} %add_convert_fusion.k_ref.v_ref), channel_id=1, source_target_pairs={{0,2},{2,4},{4,6},{1,3},{3,5},{5,7},{8,10},{10,12},{12,14},{9,11},... | collective-permute-start | bytes 6291464 | tf_op jit(solution)/shard_map/ppermute | solution.py:1073
  153.4 7.1 %copy-start.20 = (bf16[4,4,2,64,256]{4,3,2,1,0:T(8,128)(2,1)}, bf16[4,4,2,64,256]{4,3,2,1,0:T(8,128)(2,1)S(1)}, u32[]{:S(2)}) copy-start(bf16[4,4,2,64,256]{4,3,2,1,0:T(8,128)(2,1)S(1)} %copy.66) | copy-start | bytes 3145732
  198.4 218.0 %reduce-scatter.5.cloned.1.call-start = ((), (), s32[]{:S(2)}) async-start(), calls=%async_computation.9 | async-start | bytes 5242880 | tf_op jit(solution)/shard_map/reduce_scatter | solution.py:1096
  299.1 228.8 %reduce-scatter.7.cloned.1.call-start = ((), (), s32[]{:S(2)}) async-start(), calls=%async_computation.10 | async-start | bytes 5242880 | tf_op jit(solution)/shard_map/reduce_scatter | solution.py:1096
  366.9 232.9 %reduce-scatter.9.cloned.1.call-start = ((), (), s32[]{:S(2)}) async-start(), calls=%async_computation.11 | async-start | bytes 3932160 | tf_op jit(solution)/shard_map/reduce_scatter | solution.py:1152
  368.5 2.7 copy-start.15
  368.5 2.7 copy-start.19
  416.4 31.5 %copy-start.13 = (bf16[2048,256]{1,0:T(8,128)(2,1)S(1)}, bf16[2048,256]{1,0:T(8,128)(2,1)}, u32[]{:S(2)}) copy-start(bf16[2048,256]{1,0:T(8,128)(2,1)} %attend.1) | copy-start | bytes 3145732
  446.5 81.3 %collective-permute-start.1 = (bf16[2048,512]{1,0:T(8,128)(2,1)}, bf16[2048,512]{1,0:T(8,128)(2,1)}, u32[]{:S(2)}, u32[]{:S(2)}) collective-permute-start(bf16[2048,512]{1,0:T(8,128)(2,1)} %get-tuple-element.101), channel_id=1, source_target_pairs={{2,0},{4,2},{6,4},{3,1},{5,3},{7,5},{10,8},{12,10},{14,12},{11,9},... | collective-permute-start | bytes 6291464 | tf_op jit(solution)/shard_map/ppermute | solution.py:1136
  447.9 6.8 %copy-start.21 = (bf16[2048,256]{1,0:T(8,128)(2,1)S(1)}, bf16[2048,256]{1,0:T(8,128)(2,1)}, u32[]{:S(2)}) copy-start(bf16[2048,256]{1,0:T(8,128)(2,1)} %get-tuple-element.97) | copy-start | bytes 3145732
  460.6 67.3 %copy-start.1 = (bf16[2048,512]{1,0:T(8,128)(2,1)S(1)}, bf16[2048,512]{1,0:T(8,128)(2,1)}, u32[]{:S(2)}) copy-start(bf16[2048,512]{1,0:T(8,128)(2,1)} %get-tuple-element.104.pair_ref) | copy-start | bytes 6291460
  539.0 91.9 %reduce-scatter.11.cloned.1.call-start = ((), (), s32[]{:S(2)}) async-start(), calls=%async_computation.12 | async-start | bytes 1310720 | tf_op jit(solution)/shard_map/reduce_scatter | solution.py:1183
  546.0 46.7 %copy-start.10 = (bf16[1,256,2048]{2,1,0:T(8,128)(2,1)S(1)}, bf16[1,256,2048]{2,1,0:T(8,128)(2,1)}, u32[]{:S(2)}) copy-start(bf16[1,256,2048]{2,1,0:T(8,128)(2,1)} %param.20) | copy-start | bytes 3145732
  599.9 3.0 copy-start.8
  599.9 3.0 copy-start.14
  (15 other events, 22.3 us)
Sparse Core Ops, SparseCore 0:
  9.6 33.6 all-gather.5
  44.8 44.7 all-gather.7
  91.3 30.2 all-gather.9
  123.0 104.6 all-gather.11
  229.1 82.8 all-gather.13
  314.1 90.3 reduce-scatter.4
  406.9 88.2 reduce-scatter.6
  539.1 60.6 reduce-scatter.8
  602.2 28.7 reduce-scatter.10
